TPU v7x, 256 devices: a whole 4x4x8 slice. The times are simulated.
256 devices in a mesh: fsdp: 16 (over z, x_hi), fsdpt: 16 (over x_lo, y, core).
Axes of the slice: x: 4 (x_hi: 2, x_lo: 2; x = x_hi * 2 + x_lo), y: 4, z: 8, core: 2. Of those that a mesh axis runs over, the one named last changes fastest.
Arguments:
- tokens: bfloat16 [11264, 2304], P(('fsdpt', 'fsdp')), may hold values from -24 to 24
- gate_pre: bfloat16 [11264, 18432], P('fsdpt', 'fsdp'), may hold values from -6 to 6
- up_pre: bfloat16 [11264, 18432], P('fsdpt', 'fsdp'), may hold values from -6 to 6
- cotangent: bfloat16 [11264, 18432], P('fsdpt', 'fsdp'), may hold values from -3 to 3
- gate_weight: bfloat16 [2304, 18432], P('fsdpt', 'fsdp'), may hold values from -0.125 to 0.125
- up_weight: bfloat16 [2304, 18432], P('fsdpt', 'fsdp'), may hold values from -0.125 to 0.125
Outputs:
- input_grad: bfloat16 [11264, 2304], P(('fsdpt', 'fsdp'))
- gate_grad: bfloat16 [2304, 18432], P('fsdpt', 'fsdp')
- up_grad: bfloat16 [2304, 18432], P('fsdpt', 'fsdp')
All inputs are finite; a program needn't handle non-finite values.
Results may differ from a plain program's by a relative error of at most 0.023.
Values may be sent and summed in bfloat16 or wider, within the bound.
No kernel may reach another device: no remote copies, remote signals or barrier semaphores. Data moves between devices by JAX's collectives and lax.ppermute only.
A program may use at most 128 MiB of HBM per device.

v0:
```python
import math

import jax
import jax.numpy as jnp
from jax import lax
from jax.sharding import PartitionSpec as P


def deltas(gate_pre, up_pre, cotangent):
    g = gate_pre.astype(jnp.float32)
    u = up_pre.astype(jnp.float32)
    c = cotangent.astype(jnp.float32)
    kappa = math.sqrt(2.0 / math.pi)
    tangent = jnp.tanh(kappa * (g + 0.044715 * g * g * g))
    act = 0.5 * g * (1.0 + tangent)
    slope = 0.5 * (1.0 + tangent) + 0.5 * g * (1.0 - tangent * tangent) * kappa * (
        1.0 + 3.0 * 0.044715 * g * g
    )
    return ((c * u * slope).astype(jnp.bfloat16), (c * act).astype(jnp.bfloat16))


def times_transposed(left, piece):
    return lax.dot_general(
        left, piece, (((1,), (1,)), ((), ())), preferred_element_type=jnp.float32
    )


def input_part(gate_delta, up_delta, gate_weight, up_weight):
    partial_sums = times_transposed(
        gate_delta, lax.all_gather(gate_weight, "fsdpt", axis=0, tiled=True)
    )
    partial_sums = partial_sums + times_transposed(
        up_delta, lax.all_gather(up_weight, "fsdpt", axis=0, tiled=True)
    )
    return lax.psum_scatter(
        partial_sums.astype(jnp.bfloat16), "fsdp", scatter_dimension=0, tiled=True
    )


def weight_part(tokens, both_deltas, scale, hidden_cols):
    gathered = lax.all_gather(tokens, "fsdp", axis=0, tiled=True)
    product = lax.dot_general(
        gathered, both_deltas, (((0,), (0,)), ((), ())), preferred_element_type=jnp.float32
    )
    summed = lax.psum_scatter(
        (product * scale).astype(jnp.bfloat16), "fsdpt", scatter_dimension=0, tiled=True
    ).astype(jnp.float32)
    return (
        summed[:, :hidden_cols].astype(jnp.bfloat16),
        summed[:, hidden_cols:].astype(jnp.bfloat16),
    )


def per_device(tokens, gate_pre, up_pre, cotangent, gate_weight, up_weight):
    gate_delta, up_delta = deltas(gate_pre, up_pre, cotangent)
    both_deltas = jnp.concatenate([gate_delta, up_delta], 1)
    total_tokens = tokens.shape[0] * lax.axis_size("fsdp") * lax.axis_size("fsdpt")
    scale = 1.0 / math.sqrt(total_tokens)
    hidden_cols = gate_weight.shape[1]
    input_grad = input_part(gate_delta, up_delta, gate_weight, up_weight)
    gate_grad, up_grad = weight_part(tokens, both_deltas, scale, hidden_cols)
    return (input_grad, gate_grad, up_grad)


def solution(mesh):
    return jax.shard_map(
        per_device,
        mesh=mesh,
        in_specs=(
            P(("fsdpt", "fsdp"), None),
            P("fsdpt", "fsdp"),
            P("fsdpt", "fsdp"),
            P("fsdpt", "fsdp"),
            P("fsdpt", "fsdp"),
            P("fsdpt", "fsdp"),
        ),
        out_specs=(P(("fsdpt", "fsdp"), None), P("fsdpt", "fsdp"), P("fsdpt", "fsdp")),
        check_vma=False,
    )
```

profile of v0, /device:TPU:1, one launch (start us, length us, event | category | flops | bytes accessed | tf_op | source)
XLA Modules:
  0.0 354.7 jit_solution(9508058583427596539)
XLA Ops:
  7.2 0.7 all-gather.9.cloned.1.call-update
  7.9 0.0 all-gather.5.cloned.1.call-start
  7.9 0.7 all-gather.5.cloned.1.call-update
  8.7 0.7 all-gather.7.cloned.1.call-update
  9.4 0.0 reduce-scatter.6.cloned.1.call-start
  9.4 5.7 %fusion.10 = (bf16[704,1152]{1,0:T(8,128)(2,1)}, bf16[704,1152]{1,0:T(8,128)(2,1)}) fusion(bf16[704,1152]{1,0:T(8,128)(2,1)} %param.7, bf16[704,1152]{1,0:T(8,128)(2,1)} %param.9, bf16[704,1152]{1,0:T(8,128)(2,1)} %param.8), kind=kLoop, calls=%fused_computation.20 | loop fusion | flops 21086208 | bytes 8110080 | tf_op jit(solution)/shard_map/convert_element_type | solution.py:19
  15.1 91.6 %all-gather.9.cloned.1.call-done = bf16[16,44,2304]{2,1,0:T(8,128)(2,1)} async-done(((bf16[1,44,2304]{2,1,0:T(8,128)(2,1)}), bf16[16,44,2304]{2,1,0:T(8,128)(2,1)}) %all-gather.9.cloned.1.call-update) | async-done | bytes 3244048 | tf_op jit(solution)/shard_map/all_gather | solution.py:41
  106.7 3.0 reshape.7
  109.7 12.7 %fusion.2 = bf16[2304,2304]{0,1:T(8,128)(2,1)} fusion(bf16[704,2304]{1,0:T(8,128)(2,1)S(1)} %reshape.7, bf16[704,1152]{1,0:T(8,128)(2,1)} %get-tuple-element.12, bf16[704,1152]{1,0:T(8,128)(2,1)} %get-tuple-element.13), kind=kOutput, calls=%fused_computation.2 | convolution fusion | flops 7491354624 | bytes 17104896 | tf_op jit(solution)/shard_map/dot_general | solution.py:42
  122.5 15.4 %copy.15 = bf16[2304,2304]{1,0:T(8,128)(2,1)} copy(bf16[2304,2304]{0,1:T(8,128)(2,1)} %fusion.2) | data formatting | bytes 21233664
  137.9 13.1 %all-gather.5.cloned.1.call-done = bf16[2304,1152]{1,0:T(8,128)(2,1)} async-done(((bf16[144,1152]{1,0:T(8,128)(2,1)}), bf16[2304,1152]{1,0:T(8,128)(2,1)}) %all-gather.5.cloned.1.call-update) | async-done | bytes 5308432 | tf_op jit(solution)/shard_map/all_gather | solution.py:30
  151.0 8.8 %fusion.19 = f32[704,2304]{1,0:T(8,128)} fusion(bf16[704,1152]{1,0:T(8,128)(2,1)S(1)} %copy-done, bf16[2304,1152]{1,0:T(8,128)(2,1)} %all-gather.5.cloned.1.call-done), kind=kOutput, calls=%fused_computation.30 | convolution fusion | flops 3737124864 | bytes 13418496 | tf_op jit(solution)/shard_map/dot_general | solution.py:23
  159.8 35.2 %all-gather.7.cloned.1.call-done = bf16[2304,1152]{1,0:T(8,128)(2,1)} async-done(((bf16[144,1152]{1,0:T(8,128)(2,1)}), bf16[2304,1152]{1,0:T(8,128)(2,1)}) %all-gather.7.cloned.1.call-update) | async-done | bytes 5308432 | tf_op jit(solution)/shard_map/all_gather | solution.py:33
  195.0 9.3 %add_convert_fusion = bf16[704,2304]{1,0:T(8,128)(2,1)S(1)} fusion(f32[704,2304]{1,0:T(8,128)} %fusion.19, bf16[704,1152]{1,0:T(8,128)(2,1)} %get-tuple-element.12, bf16[2304,1152]{1,0:T(8,128)(2,1)} %all-gather.7.cloned.1.call-done), kind=kOutput, calls=%fused_computation.10 | convolution fusion | flops 3740368896 | bytes 16662528 | tf_op jit(solution)/shard_map/dot_general | solution.py:23
  204.3 98.4 %fusion = bf16[48,2304]{1,0:T(8,128)(2,1)S(1)} fusion(bf16[704,2304]{1,0:T(8,128)(2,1)S(1)} %add_convert_fusion), kind=kCustom, calls=%all-reduce-scatter | all-reduce-scatter fusion | flops 1769473 | bytes 3466240
  302.7 3.8 %collective-permute-start = (bf16[48,2304]{1,0:T(8,128)(2,1)S(1)}, bf16[48,2304]{1,0:T(8,128)(2,1)S(1)}, u32[]{:S(2)}, u32[]{:S(2)}) collective-permute-start(bf16[48,2304]{1,0:T(8,128)(2,1)S(1)} %fusion), channel_id=1, source_target_pairs={{0,16},{16,32},{32,48},{48,64},{64,80},{80,96},{96,112},{112,128},... | collective-permute-start | bytes 663560
  306.5 3.6 %collective-permute-start.1 = (bf16[12,2304]{1,0:T(8,128)(2,1)S(1)}, bf16[12,2304]{1,0:T(8,128)(2,1)S(1)}, u32[]{:S(2)}, u32[]{:S(2)}) collective-permute-start(bf16[12,2304]{1,0:T(8,128)(2,1)S(1)} %slice.12), channel_id=1, source_target_pairs={{0,32},{16,48},{32,64},{48,80},{64,96},{80,112},{96,128},{112,144}... | collective-permute-start | bytes 165896
  310.2 0.6 dynamic-slice.4
  311.4 0.1 collective-permute-done.1
  311.6 1.0 collective-permute-done
  312.6 1.1 concatenate.4
  313.7 0.7 constant_dynamic-slice_fusion
  314.4 31.8 %reduce-scatter.6.cloned.1.call-done = bf16[144,2304]{1,0:T(8,128)(2,1)} async-done(((bf16[2304,2304]{1,0:T(8,128)(2,1)}), bf16[144,2304]{1,0:T(8,128)(2,1)}) %reduce-scatter.6.cloned.1.call-update) | async-done | bytes 663568
  346.2 2.0 fusion.18
  (8 shorter events, 0.1 us)
Async XLA Ops:
  7.2 99.6 %all-gather.9.cloned.1.call-start = ((), (), s32[]{:S(2)}) async-start(), calls=%async_computation.3 | async-start | bytes 3760128 | tf_op jit(solution)/shard_map/all_gather | solution.py:41
  7.9 143.0 %all-gather.5.cloned.1.call-start = ((), (), s32[]{:S(2)}) async-start(), calls=%async_computation.1 | async-start | bytes 5640192 | tf_op jit(solution)/shard_map/all_gather | solution.py:30
  8.7 186.3 %all-gather.7.cloned.1.call-start = ((), (), s32[]{:S(2)}) async-start(), calls=%async_computation.2 | async-start | bytes 5640192 | tf_op jit(solution)/shard_map/all_gather | solution.py:33
  9.4 336.8 %reduce-scatter.6.cloned.1.call-start = ((), (), s32[]{:S(2)}) async-start(), calls=%async_computation.4 | async-start | bytes 11280384
  137.8 13.1 %copy-start = (bf16[704,1152]{1,0:T(8,128)(2,1)S(1)}, bf16[704,1152]{1,0:T(8,128)(2,1)}, u32[]{:S(2)}) copy-start(bf16[704,1152]{1,0:T(8,128)(2,1)} %get-tuple-element.13) | copy-start | bytes 4866052
  204.2 105.9 %copy-start.1 = (u32[256]{0:T(256)S(1)}, u32[256]{0:T(256)}, u32[]{:S(2)}) copy-start(u32[256]{0:T(256)} %constant.15) | copy-start | bytes 3076
  302.7 9.9 %collective-permute-start = (bf16[48,2304]{1,0:T(8,128)(2,1)S(1)}, bf16[48,2304]{1,0:T(8,128)(2,1)S(1)}, u32[]{:S(2)}, u32[]{:S(2)}) collective-permute-start(bf16[48,2304]{1,0:T(8,128)(2,1)S(1)} %fusion), channel_id=1, source_target_pairs={{0,16},{16,32},{32,48},{48,64},{64,80},{80,96},{96,112},{112,128},... | collective-permute-start | bytes 663560
  306.5 5.0 %collective-permute-start.1 = (bf16[12,2304]{1,0:T(8,128)(2,1)S(1)}, bf16[12,2304]{1,0:T(8,128)(2,1)S(1)}, u32[]{:S(2)}, u32[]{:S(2)}) collective-permute-start(bf16[12,2304]{1,0:T(8,128)(2,1)S(1)} %slice.12), channel_id=1, source_target_pairs={{0,32},{16,48},{32,64},{48,80},{64,96},{80,112},{96,128},{112,144}... | collective-permute-start | bytes 165896
Sparse Core Ops, SparseCore 0:
  10.6 96.1 all-gather.8
  108.6 42.3 all-gather.4
  152.8 42.1 all-gather.6
  197.4 148.7 reduce-scatter.5
where the time goes:
time: 358 us; the launch traced here: 355 us
  waiting for transfers between devices  175 us (49%)
  blocking collectives  98.4 us (27%)
  matrix products  30.8 us (9%)
  local copies, waits for them, and re-layouts  22.8 us (6%)
  between operations  14.5 us (4%)
  starting transfers between devices  7.62 us (2%)
  other arithmetic  5.67 us (2%)
    unnamed x1, blocking collectives  98.4 us
    all_gather x1, waiting for transfers between devices, weight_part(): gathered = lax.all_gather(tokens, 'fsdp', axis=0, tiled=True)  91.6 us
    all_gather x1, waiting for transfers between devices, input_part(): lax.all_gather(up_weight, 'fsdpt', axis=0, tiled=True)  35.2 us
    unnamed x7, waiting for transfers between devices  35 us
    unnamed x10, local copies, waits for them, and re-layouts  20.8 us
    dot_general x2, matrix products, times_transposed(): lax.dot_general(left, piece, (((1,), (1,)), ((), ())), preferred_element_...  18.1 us
    all_gather x1, waiting for transfers between devices, input_part(): lax.all_gather(gate_weight, 'fsdpt', axis=0, tiled=True)  13.1 us
    dot_general x1, matrix products, weight_part(): lax.dot_general(gathered, both_deltas, (((0,), (0,)), ((), ())), preferre...  12.7 us
  transfers between devices with their start and end apart: 6, of which 6 were waited for; matrix products, arithmetic and copies ran while one was open for 44% of the time, Pallas kernels for 0%

commit v1 on v0

v1 whole, which is shorter than its diff:
```python
import functools
import math

import jax
import jax.numpy as jnp
from jax import lax
from jax.experimental import pallas as pl
from jax.experimental.pallas import tpu as pltpu
from jax.sharding import Mesh, PartitionSpec as P

BF = jnp.bfloat16
F32 = jnp.float32
VMEM_LIMIT = 56 * 1024 * 1024


def shift(x, axis, k):
    n = lax.axis_size(axis)
    return lax.ppermute(x, axis, [(i, (i + k) % n) for i in range(n)])


def delta_body(z_ref, g_ref, u_ref, c_ref, out_ref):
    g = g_ref[0].astype(F32)
    u = u_ref[0].astype(F32)
    c = c_ref[0].astype(F32)
    kappa = math.sqrt(2.0 / math.pi)
    g2 = g * g
    tangent = jnp.tanh(kappa * (g + 0.044715 * g2 * g))
    half = 0.5 * (1.0 + tangent)
    act = g * half
    slope = half + 0.5 * g * (1.0 - tangent * tangent) * kappa * (1.0 + 3.0 * 0.044715 * g2)
    n = g.shape[1]
    out_ref[0, :, :n] = (c * u * slope).astype(BF)
    out_ref[0, :, n:] = (c * act).astype(BF)


def make_deltas(z, g, u, c):
    nz = lax.axis_size("z")
    rows, cols = g.shape[0] // nz, g.shape[1]
    spec = pl.BlockSpec((1, rows, cols), lambda k, zr: (lax.rem(k + zr[0], nz), 0, 0))
    return pl.pallas_call(
        delta_body,
        out_shape=jax.ShapeDtypeStruct((nz, rows, 2 * cols), BF),
        grid_spec=pltpu.PrefetchScalarGridSpec(
            num_scalar_prefetch=1,
            grid=(nz,),
            in_specs=[spec] * 3,
            out_specs=pl.BlockSpec((1, rows, 2 * cols), lambda k, zr: (k, 0, 0)),
        ),
        cost_estimate=pl.CostEstimate(
            flops=25 * g.size, bytes_accessed=10 * g.size, transcendentals=g.size
        ),
        name="deltas",
    )(z, *(a.reshape(nz, rows, cols) for a in (g, u, c)))


def split_body(blocks, s_ref, x_ref, mine_ref, other_ref):
    w = x_ref.shape[1] // (2 * blocks)
    x = x_ref[...].astype(F32)
    first = s_ref[0] == 0
    for j in range(blocks):
        a = x[:, 2 * j * w : (2 * j + 1) * w]
        b = x[:, (2 * j + 1) * w : (2 * j + 2) * w]
        mine_ref[:, j * w : (j + 1) * w] = jnp.where(first, a, b).astype(BF)
        other_ref[:, j * w : (j + 1) * w] = jnp.where(first, b, a).astype(BF)


def split_columns(core, x, blocks):
    rows, cols = x.shape
    return pl.pallas_call(
        functools.partial(split_body, blocks),
        out_shape=[jax.ShapeDtypeStruct((rows, cols // 2), BF)] * 2,
        in_specs=[
            pl.BlockSpec(memory_space=pltpu.SMEM),
            pl.BlockSpec(memory_space=pltpu.VMEM),
        ],
        out_specs=[pl.BlockSpec(memory_space=pltpu.VMEM)] * 2,
        name="split_columns",
    )(core, x)


def join_body(blocks, s_ref, a_ref, b_ref, out_ref):
    w = a_ref.shape[1] // blocks
    first = s_ref[0] == 0
    a = a_ref[...].astype(F32)
    b = b_ref[...].astype(F32)
    even = jnp.where(first, a, b)
    odd = jnp.where(first, b, a)
    for j in range(blocks):
        out_ref[:, 2 * j * w : (2 * j + 1) * w] = even[:, j * w : (j + 1) * w].astype(BF)
        out_ref[:, (2 * j + 1) * w : (2 * j + 2) * w] = odd[:, j * w : (j + 1) * w].astype(BF)


def join_columns(core, mine, other, blocks):
    rows, cols = mine.shape
    return pl.pallas_call(
        functools.partial(join_body, blocks),
        out_shape=jax.ShapeDtypeStruct((rows, 2 * cols), BF),
        in_specs=[
            pl.BlockSpec(memory_space=pltpu.SMEM),
            pl.BlockSpec(memory_space=pltpu.VMEM),
            pl.BlockSpec(memory_space=pltpu.VMEM),
        ],
        out_specs=pl.BlockSpec(memory_space=pltpu.VMEM),
        name="join_columns",
    )(core, mine, other)


def weight_body(scale, xm_ref, xo_ref, dm_ref, do_ref, out_ref):
    dims = (((0,), (0,)), ((), ()))
    acc = lax.dot_general(xm_ref[...], dm_ref[...], dims, preferred_element_type=F32)
    acc += lax.dot_general(xo_ref[...], do_ref[...], dims, preferred_element_type=F32)
    out_ref[...] = (acc * scale).astype(BF)


def weight_product(xm, xo, dm, do, scale, tile=256):
    rows, d = xm.shape
    cols = dm.shape[1]
    whole = pl.BlockSpec((rows, d), lambda i: (0, 0))
    part = pl.BlockSpec((rows, tile), lambda i: (0, i))
    return pl.pallas_call(
        functools.partial(weight_body, scale),
        out_shape=jax.ShapeDtypeStruct((d, cols), BF),
        grid=(cols // tile,),
        in_specs=[whole, whole, part, part],
        out_specs=pl.BlockSpec((d, tile), lambda i: (0, i)),
        compiler_params=pltpu.CompilerParams(vmem_limit_bytes=VMEM_LIMIT),
        cost_estimate=pl.CostEstimate(
            flops=4 * rows * d * cols,
            bytes_accessed=4 * rows * (d + cols) + 2 * d * cols,
            transcendentals=0,
        ),
        name="weight_product",
    )(xm, xo, dm, do)


def input_product(delta, w):
    return lax.dot_general(
        delta, w, (((1,), (1,)), ((), ())), preferred_element_type=F32
    ).astype(BF)


def gather_z(block):
    right, left = [block], [block]
    for _ in range(3):
        right.append(shift(right[-1], "z", 1))
        left.append(shift(left[-1], "z", -1))
    far = [shift(right[-1][0], "z", 1), shift(left[-1][1], "z", -1)]
    order = [block, left[1], left[2], left[3], far, right[3], right[2], right[1]]
    return [jnp.concatenate([b[i] for b in order], 0) for i in range(2)]


def add(*xs):
    total = xs[0].astype(F32)
    for x in xs[1:]:
        total = total + x.astype(F32)
    return total.astype(BF)


def scatter_z(mine, other):
    n = mine.shape[0] // 8

    def part(x, k):
        return x[k * n : (k + 1) * n]

    right = shift(part(mine, 4), "z", 1)
    left = shift(part(other, 4), "z", -1)
    right = jnp.stack([add(part(mine, 3), right), part(other, 3)])
    left = jnp.stack([part(mine, 5), add(part(other, 5), left)])
    right = shift(right, "z", 1)
    left = shift(left, "z", -1)
    for k in (2, 1):
        right = jnp.stack([add(part(mine, k), right[0]), add(part(other, k), right[1])])
        left = jnp.stack([add(part(mine, 8 - k), left[0]), add(part(other, 8 - k), left[1])])
        right = shift(right, "z", 1)
        left = shift(left, "z", -1)
    return [
        add(part(mine, 0), right[0], left[0]),
        add(part(other, 0), right[1], left[1]),
    ]


def per_device(tokens, gate_pre, up_pre, cotangent, gate_weight, up_weight):
    z = lax.axis_index("z")
    x_hi = lax.axis_index("x_hi")
    core = lax.axis_index("core").astype(jnp.int32).reshape(1)
    owners = lax.axis_size("x_lo") * lax.axis_size("y")
    total_tokens = gate_pre.shape[0] * owners * lax.axis_size("core")
    scale = 1.0 / math.sqrt(total_tokens)
    rows = tokens.shape[0]

    weights = lax.all_gather(
        jnp.concatenate([gate_weight, up_weight], 1), ("x_lo", "y"), axis=0, tiled=True
    )

    keep, give = split_columns(core, tokens, owners)
    pair = jnp.stack([keep, shift(give, "core", 1)])
    far = shift(pair, "x_hi", 1)
    block = jnp.where(
        x_hi == 0, jnp.concatenate([pair, far], 1), jnp.concatenate([far, pair], 1)
    )
    deltas_mine = make_deltas(z.astype(jnp.int32).reshape(1), gate_pre, up_pre, cotangent)
    deltas_mine = deltas_mine.reshape(gate_pre.shape[0], -1)
    deltas_other = shift(deltas_mine, "core", 1)
    x_mine, x_other = gather_z(block)

    product = weight_product(x_mine, x_other, deltas_mine, deltas_other, scale)
    grads = lax.psum_scatter(product, ("x_lo", "y"), scatter_dimension=0, tiled=True)

    sums = scatter_z(
        input_product(deltas_mine, weights), input_product(deltas_other, weights)
    )
    sums = jnp.stack(sums)
    low, high = sums[:, :rows], sums[:, rows:]
    sent = shift(jnp.where(x_hi == 0, high, low), "x_hi", 1)
    sums = add(jnp.where(x_hi == 0, low, high), sent)
    input_grad = join_columns(core, sums[0], shift(sums[1], "core", 1), owners)
    hidden = gate_weight.shape[1]
    return input_grad, grads[:, :hidden], grads[:, hidden:]


def solution(mesh):
    fine = Mesh(mesh.devices.reshape(8, 2, 2, 4, 2), ("z", "x_hi", "x_lo", "y", "core"))
    fsdp, fsdpt = ("z", "x_hi"), ("x_lo", "y", "core")
    both = P(fsdpt, fsdp)
    return jax.shard_map(
        per_device,
        mesh=fine,
        in_specs=(P(fsdpt + fsdp, None), both, both, both, both, both),
        out_specs=(P(fsdpt + fsdp, None), both, both),
        check_vma=False,
    )
```

time: 358 us -> 180 us (0.50)
  waiting for transfers between devices: 175 us -> 76.2 us
  blocking collectives: 98.4 us -> 0 us
  starting transfers between devices: 7.62 us -> 37.6 us
  Pallas kernels: 0 us -> 26.2 us
  matrix products: 30.8 us -> 12.4 us
  local copies, waits for them, and re-layouts: 22.8 us -> 5.41 us
    all_gather x3 -> x1, waiting for transfers between devices: 140 us -> 0.02 us  [per_device(): lax.all_gather(jnp.concatenate([gate_weight, up_weight], 1), ('x_lo', 'y'...]
    unnamed x1 -> x0, blocking collectives: 98.4 us -> none
    ppermute x0 -> x21, waiting for transfers between devices: none -> 76.2 us  [shift(): return lax.ppermute(x, axis, [(i, (i + k) % n) for i in range(n)])]
    ppermute x0 -> x21, starting transfers between devices: none -> 37.5 us  [shift(): return lax.ppermute(x, axis, [(i, (i + k) % n) for i in range(n)])]
    unnamed x7 -> x2, waiting for transfers between devices: 35 us -> 0.03 us
    pallas_call x0 -> x4, Pallas kernels: none -> 26.2 us  [the longest x1 14.2 us: weight_product(): pl.pallas_call(functools.partial(weight_body, scale), out_shape=jax.Shape...]
    dot_general x3 -> x2, matrix products: 30.8 us -> 12.4 us  [input_product(): lax.dot_general(delta, w, (((1,), (1,)), ((), ())), preferred_element_typ...]
    unnamed x10 -> x20, local copies, waits for them, and re-layouts: 20.8 us -> 2.64 us
  transfers between devices with their start and end apart: 6 -> 23, of which waited for: 6 -> 14; matrix products, arithmetic and copies ran while one was open for 44% -> 9% of each run, Pallas kernels for 0% -> 15%
where the time goes in v1:
time: 180 us; the launch traced here: 176 us
  waiting for transfers between devices  76.2 us (42%)
  starting transfers between devices  37.6 us (21%)
  Pallas kernels  26.2 us (15%)
  between operations  14.4 us (8%)
  matrix products  12.4 us (7%)
  local copies, waits for them, and re-layouts  5.41 us (3%)
  other arithmetic  4.3 us (2%)
    ppermute x21, waiting for transfers between devices, shift(): return lax.ppermute(x, axis, [(i, (i + k) % n) for i in range(n)])  76.2 us
    ppermute x21, starting transfers between devices, shift(): return lax.ppermute(x, axis, [(i, (i + k) % n) for i in range(n)])  37.5 us
    pallas_call x1, Pallas kernels, weight_product(): pl.pallas_call(functools.partial(weight_body, scale), out_shape=jax.Shape...  14.2 us
    dot_general x2, matrix products, input_product(): lax.dot_general(delta, w, (((1,), (1,)), ((), ())), preferred_element_typ...  12.4 us
    pallas_call x1, Pallas kernels, make_deltas(): pl.pallas_call(delta_body, out_shape=jax.ShapeDtypeStruct((nz, rows, 2 *...  7.88 us
  transfers between devices with their start and end apart: 23, of which 14 were waited for; matrix products, arithmetic and copies ran while one was open for 9% of the time, Pallas kernels for 15%

profile of v1, /device:TPU:1, one launch (start us, length us, event | category | flops | bytes accessed | tf_op | source)
XLA Modules:
  0.0 176.4 jit_solution(16471799150789609228)
XLA Ops:
  9.3 2.3 %split_columns.1 = (bf16[44,1152]{1,0:T(8,128)(2,1)}, bf16[44,1152]{1,0:T(8,128)(2,1)}) custom-call(s32[1]{0:T(128)} %bitcast.s_ref, bf16[44,2304]{1,0:T(8,128)(2,1)} %x_ref.1), custom_call_target="tpu_custom_call" | custom-call | tf_op jit(solution)/shard_map/split_columns/pallas_call | solution.py:69
  11.5 3.2 %collective-permute-start.11 = (bf16[44,1152]{1,0:T(8,128)(2,1)}, bf16[44,1152]{1,0:T(8,128)(2,1)S(1)}, u32[]{:S(2)}, u32[]{:S(2)}) collective-permute-start(bf16[44,1152]{1,0:T(8,128)(2,1)} %get-tuple-element.6), channel_id=1, source_target_pairs={{0,1},{1,0},{2,3},{3,2},{4,5},{5,4},{6,7},{7,6},{8,9},{9,8},{10,11... | collective-permute-start | bytes 304136 | tf_op jit(solution)/shard_map/ppermute | solution.py:18
  18.0 7.9 %deltas.1 = bf16[8,88,2304]{2,1,0:T(8,128)(2,1)} custom-call(s32[1]{0:T(128)} %bitcast.1.z_ref, bf16[8,88,1152]{2,1,0:T(8,128)(2,1)} %bitcast.163, bf16[8,88,1152]{2,1,0:T(8,128)(2,1)} %bitcast.164, bf16[8,88,1152]{2,1,0:T(8,128)(2,1)} %bitcast.165), custom_call_target="tpu_custom_call" | custom-call | flops 20275200 | bytes 8110080 | tf_op jit(solution)/shard_map/deltas/pallas_call | solution.py:40
  26.7 5.7 %collective-permute-start.13 = (bf16[2,88,1152]{2,1,0:T(8,128)(2,1)S(1)}, bf16[2,88,1152]{2,1,0:T(8,128)(2,1)S(1)}, u32[]{:S(2)}, u32[]{:S(2)}) collective-permute-start(bf16[2,88,1152]{2,1,0:T(8,128)(2,1)S(1)} %maximum_select_fusion), channel_id=1, source_target_pairs={{0,224},{32,0},{64,32},{96,64},{128,96},{160,128},{192,160},{224,1... | collective-permute-start | bytes 1216520 | tf_op jit(solution)/shard_map/ppermute | solution.py:18
  32.4 8.8 %collective-permute-done.13 = bf16[2,88,1152]{2,1,0:T(8,128)(2,1)S(1)} collective-permute-done((bf16[2,88,1152]{2,1,0:T(8,128)(2,1)S(1)}, bf16[2,88,1152]{2,1,0:T(8,128)(2,1)S(1)}, u32[]{:S(2)}, u32[]{:S(2)}) %collective-permute-start.13) | collective-permute-done | bytes 405536 | tf_op jit(solution)/shard_map/ppermute | solution.py:18
  41.1 3.5 %collective-permute-start.14 = (bf16[2,88,1152]{2,1,0:T(8,128)(2,1)S(1)}, bf16[2,88,1152]{2,1,0:T(8,128)(2,1)S(1)}, u32[]{:S(2)}, u32[]{:S(2)}) collective-permute-start(bf16[2,88,1152]{2,1,0:T(8,128)(2,1)S(1)} %collective-permute-done.13), channel_id=1, source_target_pairs={{0,224},{32,0},{64,32},{96,64},{128,96},{160,128},{192,160},{224,1... | collective-permute-start | bytes 1216520 | tf_op jit(solution)/shard_map/ppermute | solution.py:18
  44.7 8.0 %collective-permute-done.14 = bf16[2,88,1152]{2,1,0:T(8,128)(2,1)S(1)} collective-permute-done((bf16[2,88,1152]{2,1,0:T(8,128)(2,1)S(1)}, bf16[2,88,1152]{2,1,0:T(8,128)(2,1)S(1)}, u32[]{:S(2)}, u32[]{:S(2)}) %collective-permute-start.14) | collective-permute-done | bytes 405536 | tf_op jit(solution)/shard_map/ppermute | solution.py:18
  52.7 3.5 %collective-permute-start.15 = (bf16[2,88,1152]{2,1,0:T(8,128)(2,1)S(1)}, bf16[2,88,1152]{2,1,0:T(8,128)(2,1)S(1)}, u32[]{:S(2)}, u32[]{:S(2)}) collective-permute-start(bf16[2,88,1152]{2,1,0:T(8,128)(2,1)S(1)} %collective-permute-done.14), channel_id=1, source_target_pairs={{0,224},{32,0},{64,32},{96,64},{128,96},{160,128},{192,160},{224,1... | collective-permute-start | bytes 1216520 | tf_op jit(solution)/shard_map/ppermute | solution.py:18
  56.3 10.4 %collective-permute-done.18 = bf16[2,88,1152]{2,1,0:T(8,128)(2,1)S(1)} collective-permute-done((bf16[2,88,1152]{2,1,0:T(8,128)(2,1)S(1)}, bf16[2,88,1152]{2,1,0:T(8,128)(2,1)S(1)}, u32[]{:S(2)}, u32[]{:S(2)}) %collective-permute-start.18) | collective-permute-done | bytes 405536 | tf_op jit(solution)/shard_map/ppermute | solution.py:18
  66.8 2.9 %collective-permute-start.20 = (bf16[88,1152]{1,0:T(8,128)(2,1)S(1)}, bf16[88,1152]{1,0:T(8,128)(2,1)S(1)}, u32[]{:S(2)}, u32[]{:S(2)}) collective-permute-start(bf16[88,1152]{1,0:T(8,128)(2,1)S(1)} %slice_bitcast_fusion.3), channel_id=1, source_target_pairs={{0,224},{32,0},{64,32},{96,64},{128,96},{160,128},{192,160},{224,1... | collective-permute-start | bytes 608264 | tf_op jit(solution)/shard_map/ppermute | solution.py:18
  69.8 3.2 %collective-permute-done.19 = bf16[88,1152]{1,0:T(8,128)(2,1)S(1)} collective-permute-done((bf16[88,1152]{1,0:T(8,128)(2,1)S(1)}, bf16[88,1152]{1,0:T(8,128)(2,1)S(1)}, u32[]{:S(2)}, u32[]{:S(2)}) %collective-permute-start.19) | collective-permute-done | bytes 202784 | tf_op jit(solution)/shard_map/ppermute | solution.py:18
  74.9 14.2 %weight_product.1 = bf16[1152,2304]{1,0:T(8,128)(2,1)} custom-call(bf16[704,1152]{1,0:T(8,128)(2,1)} %copy-done.4, bf16[704,1152]{1,0:T(8,128)(2,1)} %copy-done.3, bf16[704,2304]{1,0:T(8,128)(2,1)} %bitcast.161, bf16[704,2304]{1,0:T(8,128)(2,1)} %collective-permute-done.1.do_ref), custom_call_target="tpu_custom_call" | custom-call | flops 7474249728 | bytes 15040512 | tf_op jit(solution)/shard_map/weight_product/pallas_call | solution.py:120
  89.2 8.0 %convolution_convert_fusion = bf16[704,1152]{1,0:T(8,128)(2,1)S(1)} fusion(bf16[704,2304]{1,0:T(8,128)(2,1)} %collective-permute-done.1.do_ref, bf16[1152,2304]{1,0:T(8,128)(2,1)} %all-gather.2.cloned.1.call-done), kind=kOutput, calls=%fused_computation | convolution fusion | flops 3737935872 | bytes 10174464 | tf_op jit(solution)/shard_map/dot_general | solution.py:137
  97.3 3.0 %collective-permute-start.5 = (bf16[88,1152]{1,0:T(8,128)(2,1)S(1)}, bf16[88,1152]{1,0:T(8,128)(2,1)S(1)}, u32[]{:S(2)}, u32[]{:S(2)}) collective-permute-start(bf16[88,1152]{1,0:T(8,128)(2,1)S(1)} %get-tuple-element.16), channel_id=1, source_target_pairs={{0,224},{32,0},{64,32},{96,64},{128,96},{160,128},{192,160},{224,1... | collective-permute-start | bytes 608264 | tf_op jit(solution)/shard_map/ppermute | solution.py:18
  100.2 4.4 %convolution_convert_fusion.1 = bf16[704,1152]{1,0:T(8,128)(2,1)S(1)} fusion(bf16[704,2304]{1,0:T(8,128)(2,1)S(1)} %bitcast.162, bf16[1152,2304]{1,0:T(8,128)(2,1)S(1)} %copy-done.5), kind=kOutput, calls=%fused_computation.1 | convolution fusion | flops 3737935872 | bytes 10174464 | tf_op jit(solution)/shard_map/dot_general | solution.py:137
  104.9 2.7 %collective-permute-start.6 = (bf16[2,88,1152]{2,1,0:T(8,128)(2,1)S(1)}, bf16[2,88,1152]{2,1,0:T(8,128)(2,1)S(1)}, u32[]{:S(2)}, u32[]{:S(2)}) collective-permute-start(bf16[2,88,1152]{2,1,0:T(8,128)(2,1)S(1)} %pad_maximum_fusion.4), channel_id=1, source_target_pairs={{0,224},{32,0},{64,32},{96,64},{128,96},{160,128},{192,160},{224,1... | collective-permute-start | bytes 1216520 | tf_op jit(solution)/shard_map/ppermute | solution.py:18
  107.6 3.3 %collective-permute-done = bf16[88,1152]{1,0:T(8,128)(2,1)S(1)} collective-permute-done((bf16[88,1152]{1,0:T(8,128)(2,1)S(1)}, bf16[88,1152]{1,0:T(8,128)(2,1)S(1)}, u32[]{:S(2)}, u32[]{:S(2)}) %collective-permute-start) | collective-permute-done | bytes 202784 | tf_op jit(solution)/shard_map/ppermute | solution.py:18
  112.5 7.2 %collective-permute-done.2 = bf16[2,88,1152]{2,1,0:T(8,128)(2,1)S(1)} collective-permute-done((bf16[2,88,1152]{2,1,0:T(8,128)(2,1)S(1)}, bf16[2,88,1152]{2,1,0:T(8,128)(2,1)S(1)}, u32[]{:S(2)}, u32[]{:S(2)}) %collective-permute-start.2) | collective-permute-done | bytes 405536 | tf_op jit(solution)/shard_map/ppermute | solution.py:18
  119.9 9.0 %collective-permute-done.3 = bf16[2,88,1152]{2,1,0:T(8,128)(2,1)S(1)} collective-permute-done((bf16[2,88,1152]{2,1,0:T(8,128)(2,1)S(1)}, bf16[2,88,1152]{2,1,0:T(8,128)(2,1)S(1)}, u32[]{:S(2)}, u32[]{:S(2)}) %collective-permute-start.3) | collective-permute-done | bytes 405536 | tf_op jit(solution)/shard_map/ppermute | solution.py:18
  129.2 7.1 %collective-permute-done.7 = bf16[2,88,1152]{2,1,0:T(8,128)(2,1)S(1)} collective-permute-done((bf16[2,88,1152]{2,1,0:T(8,128)(2,1)S(1)}, bf16[2,88,1152]{2,1,0:T(8,128)(2,1)S(1)}, u32[]{:S(2)}, u32[]{:S(2)}) %collective-permute-start.7) | collective-permute-done | bytes 405536 | tf_op jit(solution)/shard_map/ppermute | solution.py:18
  137.0 2.7 %collective-permute-start.8 = (bf16[2,88,1152]{2,1,0:T(8,128)(2,1)S(1)}, bf16[2,88,1152]{2,1,0:T(8,128)(2,1)S(1)}, u32[]{:S(2)}, u32[]{:S(2)}) collective-permute-start(bf16[2,88,1152]{2,1,0:T(8,128)(2,1)S(1)} %pad_maximum_fusion.6), channel_id=1, source_target_pairs={{0,224},{32,0},{64,32},{96,64},{128,96},{160,128},{192,160},{224,1... | collective-permute-start | bytes 1216520 | tf_op jit(solution)/shard_map/ppermute | solution.py:18
  139.7 5.6 %collective-permute-done.4 = bf16[2,88,1152]{2,1,0:T(8,128)(2,1)S(1)} collective-permute-done((bf16[2,88,1152]{2,1,0:T(8,128)(2,1)S(1)}, bf16[2,88,1152]{2,1,0:T(8,128)(2,1)S(1)}, u32[]{:S(2)}, u32[]{:S(2)}) %collective-permute-start.4) | collective-permute-done | bytes 405536 | tf_op jit(solution)/shard_map/ppermute | solution.py:18
  147.5 8.3 %collective-permute-done.9 = bf16[2,44,1152]{2,1,0:T(8,128)(2,1)S(1)} collective-permute-done((bf16[2,44,1152]{2,1,0:T(8,128)(2,1)S(1)}, bf16[2,44,1152]{2,1,0:T(8,128)(2,1)S(1)}, u32[]{:S(2)}, u32[]{:S(2)}) %collective-permute-start.9) | collective-permute-done | bytes 202784 | tf_op jit(solution)/shard_map/ppermute | solution.py:18
  156.6 7.6 %collective-permute-start.10 = (bf16[44,1152]{1,0:T(8,128)(2,1)S(1)}, bf16[44,1152]{1,0:T(8,128)(2,1)S(1)}, u32[]{:S(2)}, u32[]{:S(2)}) collective-permute-start(bf16[44,1152]{1,0:T(8,128)(2,1)S(1)} %get-tuple-element.37), channel_id=1, source_target_pairs={{0,1},{1,0},{2,3},{3,2},{4,5},{5,4},{6,7},{7,6},{8,9},{9,8},{10,11... | collective-permute-start | bytes 304136 | tf_op jit(solution)/shard_map/ppermute | solution.py:18
  (74 shorter events, 19.5 us)
Async XLA Ops:
  7.2 82.0 %all-gather.2.cloned.1.call-start = ((), (), s32[]{:S(2)}) async-start(), calls=%async_computation.1 | async-start | bytes 5971968 | tf_op jit(solution)/shard_map/all_gather | solution.py:191
  9.2 158.4 %reduce-scatter.2.cloned.1.call-start = ((), (), s32[]{:S(2)}) async-start(), calls=%async_computation.2 | async-start | bytes 5971968 | tf_op jit(solution)/shard_map/reduce_scatter | solution.py:207
  11.5 4.4 %collective-permute-start.11 = (bf16[44,1152]{1,0:T(8,128)(2,1)}, bf16[44,1152]{1,0:T(8,128)(2,1)S(1)}, u32[]{:S(2)}, u32[]{:S(2)}) collective-permute-start(bf16[44,1152]{1,0:T(8,128)(2,1)} %get-tuple-element.6), channel_id=1, source_target_pairs={{0,1},{1,0},{2,3},{3,2},{4,5},{5,4},{6,7},{7,6},{8,9},{9,8},{10,11... | collective-permute-start | bytes 304136 | tf_op jit(solution)/shard_map/ppermute | solution.py:18
  16.9 9.6 %collective-permute-start.12 = (bf16[2,44,1152]{2,1,0:T(8,128)(2,1)S(1)}, bf16[2,44,1152]{2,1,0:T(8,128)(2,1)S(1)}, u32[]{:S(2)}, u32[]{:S(2)}) collective-permute-start(bf16[2,44,1152]{2,1,0:T(8,128)(2,1)S(1)} %pad_maximum_fusion.8), channel_id=1, source_target_pairs={{0,16},{16,0},{1,17},{17,1},{2,18},{18,2},{3,19},{19,3},{4,20},{20... | collective-permute-start | bytes 608264 | tf_op jit(solution)/shard_map/ppermute | solution.py:18
  25.9 47.3 %collective-permute-start.1 = (bf16[704,2304]{1,0:T(8,128)(2,1)}, bf16[704,2304]{1,0:T(8,128)(2,1)}, u32[]{:S(2)}, u32[]{:S(2)}) collective-permute-start(bf16[704,2304]{1,0:T(8,128)(2,1)} %bitcast.160), channel_id=1, source_target_pairs={{0,1},{1,0},{2,3},{3,2},{4,5},{5,4},{6,7},{7,6},{8,9},{9,8},{10,11... | collective-permute-start | bytes 9732104 | tf_op jit(solution)/shard_map/ppermute | solution.py:18
  26.7 14.5 %collective-permute-start.13 = (bf16[2,88,1152]{2,1,0:T(8,128)(2,1)S(1)}, bf16[2,88,1152]{2,1,0:T(8,128)(2,1)S(1)}, u32[]{:S(2)}, u32[]{:S(2)}) collective-permute-start(bf16[2,88,1152]{2,1,0:T(8,128)(2,1)S(1)} %maximum_select_fusion), channel_id=1, source_target_pairs={{0,224},{32,0},{64,32},{96,64},{128,96},{160,128},{192,160},{224,1... | collective-permute-start | bytes 1216520 | tf_op jit(solution)/shard_map/ppermute | solution.py:18
  32.3 12.3 %collective-permute-start.16 = (bf16[2,88,1152]{2,1,0:T(8,128)(2,1)S(1)}, bf16[2,88,1152]{2,1,0:T(8,128)(2,1)S(1)}, u32[]{:S(2)}, u32[]{:S(2)}) collective-permute-start(bf16[2,88,1152]{2,1,0:T(8,128)(2,1)S(1)} %maximum_select_fusion), channel_id=1, source_target_pairs={{0,32},{32,64},{64,96},{96,128},{128,160},{160,192},{192,224},{224... | collective-permute-start | bytes 1216520 | tf_op jit(solution)/shard_map/ppermute | solution.py:18
  41.1 11.5 %collective-permute-start.14 = (bf16[2,88,1152]{2,1,0:T(8,128)(2,1)S(1)}, bf16[2,88,1152]{2,1,0:T(8,128)(2,1)S(1)}, u32[]{:S(2)}, u32[]{:S(2)}) collective-permute-start(bf16[2,88,1152]{2,1,0:T(8,128)(2,1)S(1)} %collective-permute-done.13), channel_id=1, source_target_pairs={{0,224},{32,0},{64,32},{96,64},{128,96},{160,128},{192,160},{224,1... | collective-permute-start | bytes 1216520 | tf_op jit(solution)/shard_map/ppermute | solution.py:18
  44.7 11.5 %collective-permute-start.17 = (bf16[2,88,1152]{2,1,0:T(8,128)(2,1)S(1)}, bf16[2,88,1152]{2,1,0:T(8,128)(2,1)S(1)}, u32[]{:S(2)}, u32[]{:S(2)}) collective-permute-start(bf16[2,88,1152]{2,1,0:T(8,128)(2,1)S(1)} %collective-permute-done.16), channel_id=1, source_target_pairs={{0,32},{32,64},{64,96},{96,128},{128,160},{160,192},{192,224},{224... | collective-permute-start | bytes 1216520 | tf_op jit(solution)/shard_map/ppermute | solution.py:18
  52.7 14.1 %collective-permute-start.15 = (bf16[2,88,1152]{2,1,0:T(8,128)(2,1)S(1)}, bf16[2,88,1152]{2,1,0:T(8,128)(2,1)S(1)}, u32[]{:S(2)}, u32[]{:S(2)}) collective-permute-start(bf16[2,88,1152]{2,1,0:T(8,128)(2,1)S(1)} %collective-permute-done.14), channel_id=1, source_target_pairs={{0,224},{32,0},{64,32},{96,64},{128,96},{160,128},{192,160},{224,1... | collective-permute-start | bytes 1216520 | tf_op jit(solution)/shard_map/ppermute | solution.py:18
  56.2 10.4 %collective-permute-start.18 = (bf16[2,88,1152]{2,1,0:T(8,128)(2,1)S(1)}, bf16[2,88,1152]{2,1,0:T(8,128)(2,1)S(1)}, u32[]{:S(2)}, u32[]{:S(2)}) collective-permute-start(bf16[2,88,1152]{2,1,0:T(8,128)(2,1)S(1)} %collective-permute-done.17), channel_id=1, source_target_pairs={{0,32},{32,64},{64,96},{96,128},{128,160},{160,192},{192,224},{224... | collective-permute-start | bytes 1216520 | tf_op jit(solution)/shard_map/ppermute | solution.py:18
  66.7 6.3 %collective-permute-start.19 = (bf16[88,1152]{1,0:T(8,128)(2,1)S(1)}, bf16[88,1152]{1,0:T(8,128)(2,1)S(1)}, u32[]{:S(2)}, u32[]{:S(2)}) collective-permute-start(bf16[88,1152]{1,0:T(8,128)(2,1)S(1)} %slice_bitcast_fusion.9), channel_id=1, source_target_pairs={{0,32},{32,64},{64,96},{96,128},{128,160},{160,192},{192,224},{224... | collective-permute-start | bytes 608264 | tf_op jit(solution)/shard_map/ppermute | solution.py:18
  66.8 6.2 %collective-permute-start.20 = (bf16[88,1152]{1,0:T(8,128)(2,1)S(1)}, bf16[88,1152]{1,0:T(8,128)(2,1)S(1)}, u32[]{:S(2)}, u32[]{:S(2)}) collective-permute-start(bf16[88,1152]{1,0:T(8,128)(2,1)S(1)} %slice_bitcast_fusion.3), channel_id=1, source_target_pairs={{0,224},{32,0},{64,32},{96,64},{128,96},{160,128},{192,160},{224,1... | collective-permute-start | bytes 608264 | tf_op jit(solution)/shard_map/ppermute | solution.py:18
  89.2 11.1 %copy-start = (bf16[8,88,2304]{2,1,0:T(8,128)(2,1)S(1)}, bf16[8,88,2304]{2,1,0:T(8,128)(2,1)}, u32[]{:S(2)}) copy-start(bf16[8,88,2304]{2,1,0:T(8,128)(2,1)} %deltas.1) | copy-start | bytes 9732100
  97.3 7.5 %collective-permute-start.5 = (bf16[88,1152]{1,0:T(8,128)(2,1)S(1)}, bf16[88,1152]{1,0:T(8,128)(2,1)S(1)}, u32[]{:S(2)}, u32[]{:S(2)}) collective-permute-start(bf16[88,1152]{1,0:T(8,128)(2,1)S(1)} %get-tuple-element.16), channel_id=1, source_target_pairs={{0,224},{32,0},{64,32},{96,64},{128,96},{160,128},{192,160},{224,1... | collective-permute-start | bytes 608264 | tf_op jit(solution)/shard_map/ppermute | solution.py:18
  104.7 6.3 %collective-permute-start = (bf16[88,1152]{1,0:T(8,128)(2,1)S(1)}, bf16[88,1152]{1,0:T(8,128)(2,1)S(1)}, u32[]{:S(2)}, u32[]{:S(2)}) collective-permute-start(bf16[88,1152]{1,0:T(8,128)(2,1)S(1)} %get-tuple-element.13), channel_id=1, source_target_pairs={{0,32},{32,64},{64,96},{96,128},{128,160},{160,192},{192,224},{224... | collective-permute-start | bytes 608264 | tf_op jit(solution)/shard_map/ppermute | solution.py:18
  104.9 7.6 %collective-permute-start.6 = (bf16[2,88,1152]{2,1,0:T(8,128)(2,1)S(1)}, bf16[2,88,1152]{2,1,0:T(8,128)(2,1)S(1)}, u32[]{:S(2)}, u32[]{:S(2)}) collective-permute-start(bf16[2,88,1152]{2,1,0:T(8,128)(2,1)S(1)} %pad_maximum_fusion.4), channel_id=1, source_target_pairs={{0,224},{32,0},{64,32},{96,64},{128,96},{160,128},{192,160},{224,1... | collective-permute-start | bytes 1216520 | tf_op jit(solution)/shard_map/ppermute | solution.py:18
  111.0 8.6 %collective-permute-start.2 = (bf16[2,88,1152]{2,1,0:T(8,128)(2,1)S(1)}, bf16[2,88,1152]{2,1,0:T(8,128)(2,1)S(1)}, u32[]{:S(2)}, u32[]{:S(2)}) collective-permute-start(bf16[2,88,1152]{2,1,0:T(8,128)(2,1)S(1)} %pad_maximum_fusion.1), channel_id=1, source_target_pairs={{0,32},{32,64},{64,96},{96,128},{128,160},{160,192},{192,224},{224... | collective-permute-start | bytes 1216520 | tf_op jit(solution)/shard_map/ppermute | solution.py:18
  119.9 9.1 %collective-permute-start.3 = (bf16[2,88,1152]{2,1,0:T(8,128)(2,1)S(1)}, bf16[2,88,1152]{2,1,0:T(8,128)(2,1)S(1)}, u32[]{:S(2)}, u32[]{:S(2)}) collective-permute-start(bf16[2,88,1152]{2,1,0:T(8,128)(2,1)S(1)} %pad_maximum_fusion.2), channel_id=1, source_target_pairs={{0,32},{32,64},{64,96},{96,128},{128,160},{160,192},{192,224},{224... | collective-permute-start | bytes 1216520 | tf_op jit(solution)/shard_map/ppermute | solution.py:18
  129.2 7.2 %collective-permute-start.7 = (bf16[2,88,1152]{2,1,0:T(8,128)(2,1)S(1)}, bf16[2,88,1152]{2,1,0:T(8,128)(2,1)S(1)}, u32[]{:S(2)}, u32[]{:S(2)}) collective-permute-start(bf16[2,88,1152]{2,1,0:T(8,128)(2,1)S(1)} %pad_maximum_fusion.5), channel_id=1, source_target_pairs={{0,224},{32,0},{64,32},{96,64},{128,96},{160,128},{192,160},{224,1... | collective-permute-start | bytes 1216520 | tf_op jit(solution)/shard_map/ppermute | solution.py:18
  136.6 8.7 %collective-permute-start.4 = (bf16[2,88,1152]{2,1,0:T(8,128)(2,1)S(1)}, bf16[2,88,1152]{2,1,0:T(8,128)(2,1)S(1)}, u32[]{:S(2)}, u32[]{:S(2)}) collective-permute-start(bf16[2,88,1152]{2,1,0:T(8,128)(2,1)S(1)} %pad_maximum_fusion.3), channel_id=1, source_target_pairs={{0,32},{32,64},{64,96},{96,128},{128,160},{160,192},{192,224},{224... | collective-permute-start | bytes 1216520 | tf_op jit(solution)/shard_map/ppermute | solution.py:18
  137.0 10.2 %collective-permute-start.8 = (bf16[2,88,1152]{2,1,0:T(8,128)(2,1)S(1)}, bf16[2,88,1152]{2,1,0:T(8,128)(2,1)S(1)}, u32[]{:S(2)}, u32[]{:S(2)}) collective-permute-start(bf16[2,88,1152]{2,1,0:T(8,128)(2,1)S(1)} %pad_maximum_fusion.6), channel_id=1, source_target_pairs={{0,224},{32,0},{64,32},{96,64},{128,96},{160,128},{192,160},{224,1... | collective-permute-start | bytes 1216520 | tf_op jit(solution)/shard_map/ppermute | solution.py:18
  147.4 8.4 %collective-permute-start.9 = (bf16[2,44,1152]{2,1,0:T(8,128)(2,1)S(1)}, bf16[2,44,1152]{2,1,0:T(8,128)(2,1)S(1)}, u32[]{:S(2)}, u32[]{:S(2)}) collective-permute-start(bf16[2,44,1152]{2,1,0:T(8,128)(2,1)S(1)} %broadcast_select_fusion), channel_id=1, source_target_pairs={{0,16},{16,0},{1,17},{17,1},{2,18},{18,2},{3,19},{19,3},{4,20},{20... | collective-permute-start | bytes 608264 | tf_op jit(solution)/shard_map/ppermute | solution.py:18
  156.6 8.6 %collective-permute-start.10 = (bf16[44,1152]{1,0:T(8,128)(2,1)S(1)}, bf16[44,1152]{1,0:T(8,128)(2,1)S(1)}, u32[]{:S(2)}, u32[]{:S(2)}) collective-permute-start(bf16[44,1152]{1,0:T(8,128)(2,1)S(1)} %get-tuple-element.37), channel_id=1, source_target_pairs={{0,1},{1,0},{2,3},{3,2},{4,5},{5,4},{6,7},{7,6},{8,9},{9,8},{10,11... | collective-permute-start | bytes 304136 | tf_op jit(solution)/shard_map/ppermute | solution.py:18
  (5 other events, 23.1 us)
Sparse Core Ops, SparseCore 0:
  9.8 69.3 all-gather.1
  89.3 66.7 reduce-scatter.1

commit v2 on v0

v2 whole, which is shorter than its diff:
```python
import functools
import math

import jax
import jax.numpy as jnp
from jax import lax
from jax.experimental import pallas as pl
from jax.experimental.pallas import tpu as pltpu
from jax.sharding import Mesh, PartitionSpec as P

BF = jnp.bfloat16
F32 = jnp.float32
VMEM_LIMIT = 56 * 1024 * 1024
IN_VMEM = pl.BlockSpec(memory_space=pltpu.VMEM)
IN_SMEM = pl.BlockSpec(memory_space=pltpu.SMEM)


def shift(x, axis, k):
    n = lax.axis_size(axis)
    return lax.ppermute(x, axis, [(i, (i + k) % n) for i in range(n)])


def add(*xs):
    total = xs[0].astype(F32)
    for x in xs[1:]:
        total = total + x.astype(F32)
    return total.astype(BF)


def delta_body(g_ref, u_ref, c_ref, out_ref):
    g = g_ref[...].astype(F32)
    u = u_ref[...].astype(F32)
    c = c_ref[...].astype(F32)
    kappa = math.sqrt(2.0 / math.pi)
    g2 = g * g
    tangent = jnp.tanh(kappa * (g + 0.044715 * g2 * g))
    half = 0.5 * (1.0 + tangent)
    act = g * half
    slope = half + 0.5 * g * (1.0 - tangent * tangent) * kappa * (1.0 + 3.0 * 0.044715 * g2)
    n = g.shape[1]
    out_ref[:, :n] = (c * u * slope).astype(BF)
    out_ref[:, n:] = (c * act).astype(BF)


def make_deltas(g, u, c, tile=64):
    rows, cols = g.shape
    spec = pl.BlockSpec((tile, cols), lambda i: (i, 0))
    return pl.pallas_call(
        delta_body,
        out_shape=jax.ShapeDtypeStruct((rows, 2 * cols), BF),
        grid=(rows // tile,),
        in_specs=[spec] * 3,
        out_specs=pl.BlockSpec((tile, 2 * cols), lambda i: (i, 0)),
        cost_estimate=pl.CostEstimate(
            flops=25 * g.size, bytes_accessed=10 * g.size, transcendentals=g.size
        ),
        name="deltas",
    )(g, u, c)


TOKEN_ORDER = ((1, 2), (0, 2), (1, 1), (1, 3), (0, 1), (0, 3), (1, 0), (0, 0))


def roll_blocks(blocks, y, sign):
    one = [jnp.where(y % 2 == 1, blocks[(i + sign) % 4], blocks[i]) for i in range(4)]
    return [jnp.where(y >= 2, one[(i + 2) % 4], one[i]) for i in range(4)]


def prologue_body(s_ref, x_ref, g_ref, u_ref, mine_ref, other_ref, w_ref):
    hidden = g_ref.shape[1]
    w_ref[:, :hidden] = g_ref[...]
    w_ref[:, hidden:] = u_ref[...]
    x_lo, y, core = s_ref[0], s_ref[1], s_ref[2]
    n = x_ref.shape[1] // 16
    x = x_ref[...].astype(F32)

    def ordered(parity):
        raw = [
            jnp.where(
                core == 0,
                x[:, (2 * j + parity) * n : (2 * j + parity + 1) * n],
                x[:, (2 * j + 1 - parity) * n : (2 * j + 2 - parity) * n],
            )
            for j in range(8)
        ]
        near = [jnp.where(x_lo == 0, raw[i], raw[i + 4]) for i in range(4)]
        far = [jnp.where(x_lo == 0, raw[i + 4], raw[i]) for i in range(4)]
        return roll_blocks(near, y, 1), roll_blocks(far, y, 1)

    for parity, ref in ((0, mine_ref), (1, other_ref)):
        by_a = ordered(parity)
        for j, (a, dy) in enumerate(TOKEN_ORDER):
            ref[:, j * n : (j + 1) * n] = by_a[a][dy].astype(BF)


def prologue(place, tokens, gate, up):
    rows, cols = tokens.shape
    half = jax.ShapeDtypeStruct((rows, cols // 2), BF)
    return pl.pallas_call(
        prologue_body,
        out_shape=[
            half,
            half,
            jax.ShapeDtypeStruct((gate.shape[0], 2 * gate.shape[1]), BF),
        ],
        in_specs=[IN_SMEM] + [IN_VMEM] * 3,
        out_specs=[IN_VMEM] * 3,
        name="prologue",
    )(place, tokens, gate, up)


def join_body(s_ref, mine_ref, other_ref, out_ref):
    x_lo, y, core = s_ref[0], s_ref[1], s_ref[2]
    n = mine_ref.shape[1] // 8

    def plain(ref):
        x = ref[...].astype(F32)
        near = roll_blocks([x[:, i * n : (i + 1) * n] for i in range(4)], y, -1)
        far = roll_blocks([x[:, (i + 4) * n : (i + 5) * n] for i in range(4)], y, -1)
        low = [jnp.where(x_lo == 0, near[i], far[i]) for i in range(4)]
        high = [jnp.where(x_lo == 0, far[i], near[i]) for i in range(4)]
        return low + high

    mine, other = plain(mine_ref), plain(other_ref)
    for j in range(8):
        out_ref[:, 2 * j * n : (2 * j + 1) * n] = jnp.where(core == 0, mine[j], other[j]).astype(BF)
        out_ref[:, (2 * j + 1) * n : (2 * j + 2) * n] = jnp.where(
            core == 0, other[j], mine[j]
        ).astype(BF)


def join_columns(place, mine, other):
    rows, cols = mine.shape
    return pl.pallas_call(
        join_body,
        out_shape=jax.ShapeDtypeStruct((rows, 2 * cols), BF),
        in_specs=[IN_SMEM, IN_VMEM, IN_VMEM],
        out_specs=IN_VMEM,
        name="join_columns",
    )(place, mine, other)


def first_body(scale, lead, xm_ref, xo_ref, dm_ref, do_ref, out_ref, xt_ref):
    rows = xm_ref.shape[0]

    @pl.when(pl.program_id(0) == 0)
    def _():
        xt_ref[:, :rows] = xm_ref[...].T
        xt_ref[:, rows:] = xo_ref[...].T

    acc = jnp.dot(xt_ref[:lead, :rows], dm_ref[...], preferred_element_type=F32)
    acc += jnp.dot(xt_ref[:lead, rows:], do_ref[...], preferred_element_type=F32)
    out_ref[...] = (acc * scale).astype(BF)


def first_product(xm, xo, dm, do, scale, lead, tile=256):
    rows, d = xm.shape
    cols = dm.shape[1]
    whole = pl.BlockSpec((rows, d), lambda i: (0, 0))
    part = pl.BlockSpec((rows, tile), lambda i: (0, i))
    return pl.pallas_call(
        functools.partial(first_body, scale, lead),
        out_shape=[
            jax.ShapeDtypeStruct((lead, cols), BF),
            jax.ShapeDtypeStruct((d, 2 * rows), BF),
        ],
        grid=(cols // tile,),
        in_specs=[whole, whole, part, part],
        out_specs=[
            pl.BlockSpec((lead, tile), lambda i: (0, i)),
            pl.BlockSpec((d, 2 * rows), lambda i: (0, 0)),
        ],
        compiler_params=pltpu.CompilerParams(vmem_limit_bytes=VMEM_LIMIT),
        cost_estimate=pl.CostEstimate(
            flops=4 * rows * lead * cols + 4 * rows * d,
            bytes_accessed=4 * rows * (2 * d + cols) + 2 * lead * cols,
            transcendentals=0,
        ),
        name="first_product",
    )(xm, xo, dm, do)


def rest_body(scale, lead, xt_ref, dm_ref, do_ref, out_ref):
    rows = dm_ref.shape[0]
    acc = jnp.dot(xt_ref[lead:, :rows], dm_ref[...], preferred_element_type=F32)
    acc += jnp.dot(xt_ref[lead:, rows:], do_ref[...], preferred_element_type=F32)
    out_ref[...] = (acc * scale).astype(BF)


def rest_product(xt, dm, do, scale, lead, tile=256):
    d = xt.shape[0]
    rows, cols = dm.shape
    part = pl.BlockSpec((rows, tile), lambda i: (0, i))
    return pl.pallas_call(
        functools.partial(rest_body, scale, lead),
        out_shape=jax.ShapeDtypeStruct((d - lead, cols), BF),
        grid=(cols // tile,),
        in_specs=[pl.BlockSpec(xt.shape, lambda i: (0, 0)), part, part],
        out_specs=pl.BlockSpec((d - lead, tile), lambda i: (0, i)),
        compiler_params=pltpu.CompilerParams(vmem_limit_bytes=VMEM_LIMIT),
        cost_estimate=pl.CostEstimate(
            flops=4 * rows * (d - lead) * cols,
            bytes_accessed=4 * rows * (d + cols) + 2 * (d - lead) * cols,
            transcendentals=0,
        ),
        name="rest_product",
    )(xt, dm, do)


def input_product(delta, w):
    return lax.dot_general(
        delta, w, (((1,), (1,)), ((), ())), preferred_element_type=F32
    ).astype(BF)


def gather_weights(w):
    far = shift(w, "x_lo", 1)
    below, above = shift(w, "y", 1), shift(w, "y", -1)
    far_below, far_above = shift(far, "y", 1), shift(far, "y", -1)
    across, far_across = shift(below, "y", 1), shift(far_above, "y", -1)
    return jnp.concatenate(
        [w, above, across, below, far, far_above, far_across, far_below], 0
    )


def scatter_grads(first, rest, n):
    rest = [rest[i * n : (i + 1) * n] for i in range(6)]
    far_up, far_down, up, down, far_own, own = rest
    far_right = shift(first[:n], "y", 1)
    left = shift(first[n:], "y", -1)
    far_left = shift(far_down, "y", -1)
    far_right = shift(add(far_up, far_right), "y", 1)
    right = shift(up, "y", 1)
    left = shift(add(down, left), "y", -1)
    far_own = shift(add(far_own, far_left, far_right), "x_lo", 1)
    return add(own, right, left, far_own)


def per_device(tokens, gate_pre, up_pre, cotangent, gate_weight, up_weight):
    x_hi = lax.axis_index("x_hi")
    place = jnp.stack([lax.axis_index(a).astype(jnp.int32) for a in ("x_lo", "y", "core")])
    total_tokens = gate_pre.shape[0] * 16
    scale = 1.0 / math.sqrt(total_tokens)
    rows = tokens.shape[0]
    owned = gate_weight.shape[0]

    keep, give, w = prologue(place, tokens, gate_weight, up_weight)
    pair = jnp.stack([keep, shift(give, "core", 1)])
    far = shift(pair, "x_hi", 1)
    block = jnp.where(
        x_hi == 0, jnp.concatenate([pair, far], 1), jnp.concatenate([far, pair], 1)
    )
    x_mine = lax.all_gather(block[0], "z", axis=0, tiled=True)
    x_other = lax.all_gather(block[1], "z", axis=0, tiled=True)

    weights = gather_weights(w)
    deltas_mine = make_deltas(gate_pre, up_pre, cotangent)
    deltas_other = shift(deltas_mine, "core", 1)

    part_mine = input_product(deltas_mine, weights)
    part_other = input_product(deltas_other, weights)
    sums = [
        lax.psum_scatter(p, "z", scatter_dimension=0, tiled=True)
        for p in (part_mine, part_other)
    ]

    first, x_t = first_product(
        x_mine, x_other, deltas_mine, deltas_other, scale, 2 * owned
    )
    rest = rest_product(x_t, deltas_mine, deltas_other, scale, 2 * owned)
    grads = scatter_grads(first, rest, owned)

    sums = jnp.stack(sums)
    low, high = sums[:, :rows], sums[:, rows:]
    sent = shift(jnp.where(x_hi == 0, high, low), "x_hi", 1)
    sums = add(jnp.where(x_hi == 0, low, high), sent)
    input_grad = join_columns(place, sums[0], shift(sums[1], "core", 1))
    hidden = gate_weight.shape[1]
    return input_grad, grads[:, :hidden], grads[:, hidden:]


def solution(mesh):
    fine = Mesh(mesh.devices.reshape(8, 2, 2, 4, 2), ("z", "x_hi", "x_lo", "y", "core"))
    fsdp, fsdpt = ("z", "x_hi"), ("x_lo", "y", "core")
    both = P(fsdpt, fsdp)
    return jax.shard_map(
        per_device,
        mesh=fine,
        in_specs=(P(fsdpt + fsdp, None), both, both, both, both, both),
        out_specs=(P(fsdpt + fsdp, None), both, both),
        check_vma=False,
    )
```

time: 358 us -> 216 us (0.60)
  blocking collectives: 98.4 us -> 0 us
  waiting for transfers between devices: 175 us -> 80.9 us
  Pallas kernels: 0 us -> 39.4 us
  starting transfers between devices: 7.62 us -> 33 us
  matrix products: 30.8 us -> 17 us
  other arithmetic: 5.67 us -> 9.47 us
    all_gather x3 -> x2, waiting for transfers between devices: 140 us -> 22.7 us  [the longest x1 22.7 us: per_device(): x_other = lax.all_gather(block[1], 'z', axis=0, tiled=True)]
    unnamed x1 -> x0, blocking collectives: 98.4 us -> none
    pallas_call x0 -> x5, Pallas kernels: none -> 39.4 us  [the longest x1 12.9 us: rest_product(): pl.pallas_call(functools.partial(rest_body, scale, lead), out_shape=jax.S...]
    ppermute x0 -> x19, waiting for transfers between devices: none -> 34.2 us  [shift(): return lax.ppermute(x, axis, [(i, (i + k) % n) for i in range(n)])]
    ppermute x0 -> x19, starting transfers between devices: none -> 32.7 us  [shift(): return lax.ppermute(x, axis, [(i, (i + k) % n) for i in range(n)])]
    dot_general x3 -> x2, matrix products: 30.8 us -> 17 us  [input_product(): lax.dot_general(delta, w, (((1,), (1,)), ((), ())), preferred_element_typ...]
    unnamed x7 -> x6, waiting for transfers between devices: 35 us -> 24 us
    unnamed x3 -> x2, starting transfers between devices: 7.51 us -> 0.26 us
  transfers between devices with their start and end apart: 6 -> 23, of which waited for: 6 -> 11; matrix products, arithmetic and copies ran while one was open for 44% -> 19% of each run, Pallas kernels for 0% -> 16%
where the time goes in v2:
time: 216 us; the launch traced here: 215 us
  waiting for transfers between devices  80.9 us (37%)
  Pallas kernels  39.4 us (18%)
  starting transfers between devices  33 us (15%)
  local copies, waits for them, and re-layouts  21.2 us (10%)
  matrix products  17 us (8%)
  between operations  13.9 us (6%)
  other arithmetic  9.47 us (4%)
    ppermute x19, waiting for transfers between devices, shift(): return lax.ppermute(x, axis, [(i, (i + k) % n) for i in range(n)])  34.2 us
    ppermute x19, starting transfers between devices, shift(): return lax.ppermute(x, axis, [(i, (i + k) % n) for i in range(n)])  32.7 us
    unnamed x6, waiting for transfers between devices  24 us
    all_gather x1, waiting for transfers between devices, per_device(): x_other = lax.all_gather(block[1], 'z', axis=0, tiled=True)  22.7 us
    dot_general x2, matrix products, input_product(): lax.dot_general(delta, w, (((1,), (1,)), ((), ())), preferred_element_typ...  17 us
    unnamed x17, local copies, waits for them, and re-layouts  15.2 us
    pallas_call x1, Pallas kernels, rest_product(): pl.pallas_call(functools.partial(rest_body, scale, lead), out_shape=jax.S...  12.9 us
    pallas_call x1, Pallas kernels, first_product(): pl.pallas_call(functools.partial(first_body, scale, lead), out_shape=[jax...  12 us
  transfers between devices with their start and end apart: 23, of which 11 were waited for; matrix products, arithmetic and copies ran while one was open for 19% of the time, Pallas kernels for 16%

profile of v2, /device:TPU:1, one launch (start us, length us, event | category | flops | bytes accessed | tf_op | source)
XLA Modules:
  0.0 214.9 jit_solution(1385975658632451020)
XLA Ops:
  7.8 2.8 %prologue.1 = (bf16[44,1152]{1,0:T(8,128)(2,1)}, bf16[44,1152]{1,0:T(8,128)(2,1)}, bf16[144,2304]{1,0:T(8,128)(2,1)}) custom-call(s32[3]{0:T(128)} %pad_add_fusion.s_ref, bf16[44,2304]{1,0:T(8,128)(2,1)} %x_ref.1, bf16[144,1152]{1,0:T(8,128)(2,1)} %g_ref.3, bf16[144,1152]{1,0:T(8,128)(2,1)} %u_ref.3), custom_call_target="tpu_custom_call" | custom-call | tf_op jit(solution)/shard_map/prologue/pallas_call | solution.py:99
  10.6 3.2 %collective-permute-start.10 = (bf16[44,1152]{1,0:T(8,128)(2,1)}, bf16[44,1152]{1,0:T(8,128)(2,1)S(1)}, u32[]{:S(2)}, u32[]{:S(2)}) collective-permute-start(bf16[44,1152]{1,0:T(8,128)(2,1)} %get-tuple-element.10), channel_id=1, source_target_pairs={{0,1},{1,0},{2,3},{3,2},{4,5},{5,4},{6,7},{7,6},{8,9},{9,8},{10,11... | collective-permute-start | bytes 304136 | tf_op jit(solution)/shard_map/ppermute | solution.py:20
  17.1 7.1 %collective-permute-done.11 = bf16[2,44,1152]{2,1,0:T(8,128)(2,1)S(1)} collective-permute-done((bf16[2,44,1152]{2,1,0:T(8,128)(2,1)S(1)}, bf16[2,44,1152]{2,1,0:T(8,128)(2,1)S(1)}, u32[]{:S(2)}, u32[]{:S(2)}) %collective-permute-start.11) | collective-permute-done | bytes 202784 | tf_op jit(solution)/shard_map/ppermute | solution.py:20
  29.0 9.3 %deltas.1.dm_ref = bf16[704,2304]{1,0:T(8,128)(2,1)} custom-call(bf16[704,1152]{1,0:T(8,128)(2,1)} %g_ref.2, bf16[704,1152]{1,0:T(8,128)(2,1)} %u_ref.2, bf16[704,1152]{1,0:T(8,128)(2,1)} %c_ref.1), custom_call_target="tpu_custom_call" | custom-call | flops 20275200 | bytes 8110080 | tf_op jit(solution)/shard_map/deltas/pallas_call | solution.py:48
  40.0 3.0 %collective-permute-done.1 = bf16[144,2304]{1,0:T(8,128)(2,1)} collective-permute-done((bf16[144,2304]{1,0:T(8,128)(2,1)}, bf16[144,2304]{1,0:T(8,128)(2,1)}, u32[]{:S(2)}, u32[]{:S(2)}) %collective-permute-start.1) | collective-permute-done | bytes 663584 | tf_op jit(solution)/shard_map/ppermute | solution.py:20
  43.0 2.7 %collective-permute-start.4 = (bf16[144,2304]{1,0:T(8,128)(2,1)}, bf16[144,2304]{1,0:T(8,128)(2,1)}, u32[]{:S(2)}, u32[]{:S(2)}) collective-permute-start(bf16[144,2304]{1,0:T(8,128)(2,1)} %collective-permute-done.3), channel_id=1, source_target_pairs={{0,6},{2,0},{4,2},{6,4},{1,7},{3,1},{5,3},{7,5},{8,14},{10,8},{12,... | collective-permute-start | bytes 1990664 | tf_op jit(solution)/shard_map/ppermute | solution.py:20
  49.9 7.9 %collective-permute-done.4 = bf16[144,2304]{1,0:T(8,128)(2,1)} collective-permute-done((bf16[144,2304]{1,0:T(8,128)(2,1)}, bf16[144,2304]{1,0:T(8,128)(2,1)}, u32[]{:S(2)}, u32[]{:S(2)}) %collective-permute-start.4) | collective-permute-done | bytes 663584 | tf_op jit(solution)/shard_map/ppermute | solution.py:20
  57.8 3.4 %collective-permute-start.5 = (bf16[144,2304]{1,0:T(8,128)(2,1)}, bf16[144,2304]{1,0:T(8,128)(2,1)S(1)}, u32[]{:S(2)}, u32[]{:S(2)}) collective-permute-start(bf16[144,2304]{1,0:T(8,128)(2,1)} %collective-permute-done.4), channel_id=1, source_target_pairs={{0,6},{2,0},{4,2},{6,4},{1,7},{3,1},{5,3},{7,5},{8,14},{10,8},{12,... | collective-permute-start | bytes 1990664 | tf_op jit(solution)/shard_map/ppermute | solution.py:20
  69.3 3.2 %collective-permute-done.5 = bf16[144,2304]{1,0:T(8,128)(2,1)S(1)} collective-permute-done((bf16[144,2304]{1,0:T(8,128)(2,1)}, bf16[144,2304]{1,0:T(8,128)(2,1)S(1)}, u32[]{:S(2)}, u32[]{:S(2)}) %collective-permute-start.5) | collective-permute-done | bytes 663584 | tf_op jit(solution)/shard_map/ppermute | solution.py:20
  74.3 8.0 %convolution_convert_fusion.1 = bf16[704,1152]{1,0:T(8,128)(2,1)} fusion(bf16[704,2304]{1,0:T(8,128)(2,1)S(1)} %copy-done, bf16[1152,2304]{1,0:T(8,128)(2,1)} %constant_dynamic-update-slice_fusion), kind=kOutput, calls=%fused_computation.1 | convolution fusion | flops 3737935872 | bytes 10174464 | tf_op jit(solution)/shard_map/dot_general | solution.py:211
  82.5 22.7 %all-gather.7.cloned.1.call-done = bf16[1,704,1152]{2,1,0:T(8,128)(2,1)} async-done(((bf16[1,88,1152]{2,1,0:T(8,128)(2,1)}), bf16[1,704,1152]{2,1,0:T(8,128)(2,1)}) %all-gather.7.cloned.1.call-update) | async-done | bytes 1622032 | tf_op jit(solution)/shard_map/all_gather | solution.py:254
  106.9 12.0 %first_product.1 = (bf16[288,2304]{1,0:T(8,128)(2,1)}, bf16[1152,1408]{1,0:T(8,128)(2,1)}) custom-call(bf16[704,1152]{1,0:T(8,128)(2,1)} %bitcast.18, bf16[704,1152]{1,0:T(8,128)(2,1)} %bitcast.19, bf16[704,2304]{1,0:T(8,128)(2,1)} %deltas.1.dm_ref, bf16[704,2304]{1,0:T(8,128)(2,1)} %copy-done.1), custom_call_target="tpu_custom_call" | custom-call | flops 1871806464 | bytes 14303232 | tf_op jit(solution)/shard_map/first_product/pallas_call | solution.py:161
  120.2 2.6 %collective-permute-start.13 = (bf16[144,2304]{1,0:T(8,128)(2,1)S(1)}, bf16[144,2304]{1,0:T(8,128)(2,1)S(1)}, u32[]{:S(2)}, u32[]{:S(2)}) collective-permute-start(bf16[144,2304]{1,0:T(8,128)(2,1)S(1)} %get-tuple-element.17), channel_id=1, source_target_pairs={{0,6},{2,0},{4,2},{6,4},{1,7},{3,1},{5,3},{7,5},{8,14},{10,8},{12,... | collective-permute-start | bytes 1990664 | tf_op jit(solution)/shard_map/ppermute | solution.py:20
  122.8 9.0 %convolution_convert_fusion = bf16[704,1152]{1,0:T(8,128)(2,1)} fusion(bf16[704,2304]{1,0:T(8,128)(2,1)} %copy-done.1, bf16[1152,2304]{1,0:T(8,128)(2,1)} %constant_dynamic-update-slice_fusion), kind=kOutput, calls=%fused_computation | convolution fusion | flops 3737935872 | bytes 10174464 | tf_op jit(solution)/shard_map/dot_general | solution.py:211
  131.8 12.9 %rest_product.1 = bf16[864,2304]{1,0:T(8,128)(2,1)} custom-call(bf16[1152,1408]{1,0:T(8,128)(2,1)} %get-tuple-element.11.xt_ref, bf16[704,2304]{1,0:T(8,128)(2,1)} %deltas.1.dm_ref, bf16[704,2304]{1,0:T(8,128)(2,1)} %copy-done.1), custom_call_target="tpu_custom_call" | custom-call | flops 5605687296 | bytes 13713408 | tf_op jit(solution)/shard_map/rest_product/pallas_call | solution.py:194
  146.2 2.8 %collective-permute-start.15 = (bf16[144,2304]{1,0:T(8,128)(2,1)S(1)}, bf16[144,2304]{1,0:T(8,128)(2,1)S(1)}, u32[]{:S(2)}, u32[]{:S(2)}) collective-permute-start(bf16[144,2304]{1,0:T(8,128)(2,1)S(1)} %get-tuple-element.14), channel_id=1, source_target_pairs={{0,6},{2,0},{4,2},{6,4},{1,7},{3,1},{5,3},{7,5},{8,14},{10,8},{12,... | collective-permute-start | bytes 1990664 | tf_op jit(solution)/shard_map/ppermute | solution.py:20
  148.9 2.7 %add_convert_fusion.3 = (bf16[144,2304]{1,0:T(8,128)(2,1)}, bf16[144,2304]{1,0:T(8,128)(2,1)S(1)}) fusion(bf16[144,2304]{1,0:T(8,128)(2,1)S(1)} %collective-permute-done.13, bf16[864,2304]{1,0:T(8,128)(2,1)} %rest_product.1, bf16[144,2304]{1,0:T(8,128)(2,1)} %collective-permute-done.16), kind=kLoop, calls=%fused_computation.5 | loop fusion | flops 2654208 | bytes 3981312 | tf_op jit(solution)/shard_map/convert_element_type | solution.py:27
  151.6 2.7 %collective-permute-start.14 = (bf16[144,2304]{1,0:T(8,128)(2,1)}, bf16[144,2304]{1,0:T(8,128)(2,1)S(1)}, u32[]{:S(2)}, u32[]{:S(2)}) collective-permute-start(bf16[144,2304]{1,0:T(8,128)(2,1)} %get-tuple-element.15), channel_id=1, source_target_pairs={{0,6},{2,0},{4,2},{6,4},{1,7},{3,1},{5,3},{7,5},{8,14},{10,8},{12,... | collective-permute-start | bytes 1990664 | tf_op jit(solution)/shard_map/ppermute | solution.py:20
  154.3 3.3 %collective-permute-done.15 = bf16[144,2304]{1,0:T(8,128)(2,1)S(1)} collective-permute-done((bf16[144,2304]{1,0:T(8,128)(2,1)S(1)}, bf16[144,2304]{1,0:T(8,128)(2,1)S(1)}, u32[]{:S(2)}, u32[]{:S(2)}) %collective-permute-start.15) | collective-permute-done | bytes 663584 | tf_op jit(solution)/shard_map/ppermute | solution.py:20
  157.7 5.8 %collective-permute-done.17 = bf16[144,2304]{1,0:T(8,128)(2,1)S(1)} collective-permute-done((bf16[144,2304]{1,0:T(8,128)(2,1)S(1)}, bf16[144,2304]{1,0:T(8,128)(2,1)S(1)}, u32[]{:S(2)}, u32[]{:S(2)}) %collective-permute-start.17) | collective-permute-done | bytes 663584 | tf_op jit(solution)/shard_map/ppermute | solution.py:20
  166.1 24.0 %reduce-scatter.9.cloned.1.call-done = bf16[88,1152]{1,0:T(8,128)(2,1)} async-done(((bf16[704,1152]{1,0:T(8,128)(2,1)}), bf16[88,1152]{1,0:T(8,128)(2,1)}) %reduce-scatter.9.cloned.1.call-update) | async-done | bytes 202768
  191.3 2.4 %collective-permute-start.8 = (bf16[2,44,1152]{2,1,0:T(8,128)(2,1)S(1)}, bf16[2,44,1152]{2,1,0:T(8,128)(2,1)S(1)}, u32[]{:S(2)}, u32[]{:S(2)}) collective-permute-start(bf16[2,44,1152]{2,1,0:T(8,128)(2,1)S(1)} %broadcast_select_fusion), channel_id=1, source_target_pairs={{0,16},{16,0},{1,17},{17,1},{2,18},{18,2},{3,19},{19,3},{4,20},{20... | collective-permute-start | bytes 608264 | tf_op jit(solution)/shard_map/ppermute | solution.py:20
  195.2 2.5 %collective-permute-done.8 = bf16[2,44,1152]{2,1,0:T(8,128)(2,1)S(1)} collective-permute-done((bf16[2,44,1152]{2,1,0:T(8,128)(2,1)S(1)}, bf16[2,44,1152]{2,1,0:T(8,128)(2,1)S(1)}, u32[]{:S(2)}, u32[]{:S(2)}) %collective-permute-start.8) | collective-permute-done | bytes 202784 | tf_op jit(solution)/shard_map/ppermute | solution.py:20
  198.5 5.9 %collective-permute-start.9 = (bf16[44,1152]{1,0:T(8,128)(2,1)S(1)}, bf16[44,1152]{1,0:T(8,128)(2,1)S(1)}, u32[]{:S(2)}, u32[]{:S(2)}) collective-permute-start(bf16[44,1152]{1,0:T(8,128)(2,1)S(1)} %get-tuple-element.23), channel_id=1, source_target_pairs={{0,1},{1,0},{2,3},{3,2},{4,5},{5,4},{6,7},{7,6},{8,9},{9,8},{10,11... | collective-permute-start | bytes 304136 | tf_op jit(solution)/shard_map/ppermute | solution.py:20
  (64 shorter events, 39.0 us)
Async XLA Ops:
  7.2 75.4 %all-gather.5.cloned.1.call-start = ((), (), s32[]{:S(2)}) async-start(), calls=%async_computation.2 | async-start | bytes 1824768 | tf_op jit(solution)/shard_map/all_gather | solution.py:253
  10.6 4.4 %collective-permute-start.10 = (bf16[44,1152]{1,0:T(8,128)(2,1)}, bf16[44,1152]{1,0:T(8,128)(2,1)S(1)}, u32[]{:S(2)}, u32[]{:S(2)}) collective-permute-start(bf16[44,1152]{1,0:T(8,128)(2,1)} %get-tuple-element.10), channel_id=1, source_target_pairs={{0,1},{1,0},{2,3},{3,2},{4,5},{5,4},{6,7},{7,6},{8,9},{9,8},{10,11... | collective-permute-start | bytes 304136 | tf_op jit(solution)/shard_map/ppermute | solution.py:20
  16.0 8.2 %collective-permute-start.11 = (bf16[2,44,1152]{2,1,0:T(8,128)(2,1)S(1)}, bf16[2,44,1152]{2,1,0:T(8,128)(2,1)S(1)}, u32[]{:S(2)}, u32[]{:S(2)}) collective-permute-start(bf16[2,44,1152]{2,1,0:T(8,128)(2,1)S(1)} %pad_maximum_fusion.1), channel_id=1, source_target_pairs={{0,16},{16,0},{1,17},{17,1},{2,18},{18,2},{3,19},{19,3},{4,20},{20... | collective-permute-start | bytes 608264 | tf_op jit(solution)/shard_map/ppermute | solution.py:20
  26.2 79.0 %all-gather.7.cloned.1.call-start = ((), (), s32[]{:S(2)}) async-start(), calls=%async_computation.3 | async-start | bytes 1824768 | tf_op jit(solution)/shard_map/all_gather | solution.py:254
  26.2 16.8 %collective-permute-start.1 = (bf16[144,2304]{1,0:T(8,128)(2,1)}, bf16[144,2304]{1,0:T(8,128)(2,1)}, u32[]{:S(2)}, u32[]{:S(2)}) collective-permute-start(bf16[144,2304]{1,0:T(8,128)(2,1)} %get-tuple-element.8), channel_id=1, source_target_pairs={{0,2},{2,4},{4,6},{6,0},{1,3},{3,5},{5,7},{7,1},{8,10},{10,12},{12... | collective-permute-start | bytes 1990664 | tf_op jit(solution)/shard_map/ppermute | solution.py:20
  26.3 16.7 %collective-permute-start.3 = (bf16[144,2304]{1,0:T(8,128)(2,1)}, bf16[144,2304]{1,0:T(8,128)(2,1)}, u32[]{:S(2)}, u32[]{:S(2)}) collective-permute-start(bf16[144,2304]{1,0:T(8,128)(2,1)} %get-tuple-element.8), channel_id=1, source_target_pairs={{0,8},{8,0},{1,9},{9,1},{2,10},{10,2},{3,11},{11,3},{4,12},{12,4},... | collective-permute-start | bytes 1990664 | tf_op jit(solution)/shard_map/ppermute | solution.py:20
  27.1 20.8 %collective-permute-start = (bf16[144,2304]{1,0:T(8,128)(2,1)}, bf16[144,2304]{1,0:T(8,128)(2,1)}, u32[]{:S(2)}, u32[]{:S(2)}) collective-permute-start(bf16[144,2304]{1,0:T(8,128)(2,1)} %get-tuple-element.8), channel_id=1, source_target_pairs={{0,6},{2,0},{4,2},{6,4},{1,7},{3,1},{5,3},{7,5},{8,14},{10,8},{12,... | collective-permute-start | bytes 1990664 | tf_op jit(solution)/shard_map/ppermute | solution.py:20
  38.3 66.9 %collective-permute-start.7 = (bf16[704,2304]{1,0:T(8,128)(2,1)}, bf16[704,2304]{1,0:T(8,128)(2,1)S(1)}, u32[]{:S(2)}, u32[]{:S(2)}) collective-permute-start(bf16[704,2304]{1,0:T(8,128)(2,1)} %deltas.1.dm_ref), channel_id=1, source_target_pairs={{0,1},{1,0},{2,3},{3,2},{4,5},{5,4},{6,7},{7,6},{8,9},{9,8},{10,11... | collective-permute-start | bytes 9732104 | tf_op jit(solution)/shard_map/ppermute | solution.py:20
  43.0 18.2 %collective-permute-start.2 = (bf16[144,2304]{1,0:T(8,128)(2,1)}, bf16[144,2304]{1,0:T(8,128)(2,1)}, u32[]{:S(2)}, u32[]{:S(2)}) collective-permute-start(bf16[144,2304]{1,0:T(8,128)(2,1)} %collective-permute-done.1), channel_id=1, source_target_pairs={{0,2},{2,4},{4,6},{6,0},{1,3},{3,5},{5,7},{7,1},{8,10},{10,12},{12... | collective-permute-start | bytes 1990664 | tf_op jit(solution)/shard_map/ppermute | solution.py:20
  43.0 14.8 %collective-permute-start.4 = (bf16[144,2304]{1,0:T(8,128)(2,1)}, bf16[144,2304]{1,0:T(8,128)(2,1)}, u32[]{:S(2)}, u32[]{:S(2)}) collective-permute-start(bf16[144,2304]{1,0:T(8,128)(2,1)} %collective-permute-done.3), channel_id=1, source_target_pairs={{0,6},{2,0},{4,2},{6,4},{1,7},{3,1},{5,3},{7,5},{8,14},{10,8},{12,... | collective-permute-start | bytes 1990664 | tf_op jit(solution)/shard_map/ppermute | solution.py:20
  47.7 118.4 %reduce-scatter.7.cloned.1.call-start = ((), (), s32[]{:S(2)}) async-start(), calls=%async_computation.4 | async-start | bytes 1824768
  47.8 25.6 %collective-permute-start.6 = (bf16[144,2304]{1,0:T(8,128)(2,1)}, bf16[144,2304]{1,0:T(8,128)(2,1)S(1)}, u32[]{:S(2)}, u32[]{:S(2)}) collective-permute-start(bf16[144,2304]{1,0:T(8,128)(2,1)} %collective-permute-done.3), channel_id=1, source_target_pairs={{0,2},{2,4},{4,6},{6,0},{1,3},{3,5},{5,7},{7,1},{8,10},{10,12},{12... | collective-permute-start | bytes 1990664 | tf_op jit(solution)/shard_map/ppermute | solution.py:20
  57.8 14.6 %collective-permute-start.5 = (bf16[144,2304]{1,0:T(8,128)(2,1)}, bf16[144,2304]{1,0:T(8,128)(2,1)S(1)}, u32[]{:S(2)}, u32[]{:S(2)}) collective-permute-start(bf16[144,2304]{1,0:T(8,128)(2,1)} %collective-permute-done.4), channel_id=1, source_target_pairs={{0,6},{2,0},{4,2},{6,4},{1,7},{3,1},{5,3},{7,5},{8,14},{10,8},{12,... | collective-permute-start | bytes 1990664 | tf_op jit(solution)/shard_map/ppermute | solution.py:20
  82.3 107.8 %reduce-scatter.9.cloned.1.call-start = ((), (), s32[]{:S(2)}) async-start(), calls=%async_computation.5 | async-start | bytes 1824768
  120.2 28.7 %collective-permute-start.13 = (bf16[144,2304]{1,0:T(8,128)(2,1)S(1)}, bf16[144,2304]{1,0:T(8,128)(2,1)S(1)}, u32[]{:S(2)}, u32[]{:S(2)}) collective-permute-start(bf16[144,2304]{1,0:T(8,128)(2,1)S(1)} %get-tuple-element.17), channel_id=1, source_target_pairs={{0,6},{2,0},{4,2},{6,4},{1,7},{3,1},{5,3},{7,5},{8,14},{10,8},{12,... | collective-permute-start | bytes 1990664 | tf_op jit(solution)/shard_map/ppermute | solution.py:20
  122.8 26.1 %collective-permute-start.16 = (bf16[144,2304]{1,0:T(8,128)(2,1)S(1)}, bf16[144,2304]{1,0:T(8,128)(2,1)}, u32[]{:S(2)}, u32[]{:S(2)}) collective-permute-start(bf16[144,2304]{1,0:T(8,128)(2,1)S(1)} %get-tuple-element.18), channel_id=1, source_target_pairs={{0,2},{2,4},{4,6},{6,0},{1,3},{3,5},{5,7},{7,1},{8,10},{10,12},{12... | collective-permute-start | bytes 1990664 | tf_op jit(solution)/shard_map/ppermute | solution.py:20
  146.2 11.5 %collective-permute-start.15 = (bf16[144,2304]{1,0:T(8,128)(2,1)S(1)}, bf16[144,2304]{1,0:T(8,128)(2,1)S(1)}, u32[]{:S(2)}, u32[]{:S(2)}) collective-permute-start(bf16[144,2304]{1,0:T(8,128)(2,1)S(1)} %get-tuple-element.14), channel_id=1, source_target_pairs={{0,6},{2,0},{4,2},{6,4},{1,7},{3,1},{5,3},{7,5},{8,14},{10,8},{12,... | collective-permute-start | bytes 1990664 | tf_op jit(solution)/shard_map/ppermute | solution.py:20
  151.6 11.9 %collective-permute-start.17 = (bf16[144,2304]{1,0:T(8,128)(2,1)S(1)}, bf16[144,2304]{1,0:T(8,128)(2,1)S(1)}, u32[]{:S(2)}, u32[]{:S(2)}) collective-permute-start(bf16[144,2304]{1,0:T(8,128)(2,1)S(1)} %get-tuple-element.16), channel_id=1, source_target_pairs={{0,2},{2,4},{4,6},{6,0},{1,3},{3,5},{5,7},{7,1},{8,10},{10,12},{12... | collective-permute-start | bytes 1990664 | tf_op jit(solution)/shard_map/ppermute | solution.py:20
  151.6 42.1 %collective-permute-start.12 = (bf16[144,2304]{1,0:T(8,128)(2,1)S(1)}, bf16[144,2304]{1,0:T(8,128)(2,1)S(1)}, u32[]{:S(2)}, u32[]{:S(2)}) collective-permute-start(bf16[144,2304]{1,0:T(8,128)(2,1)S(1)} %get-tuple-element.13), channel_id=1, source_target_pairs={{0,2},{2,4},{4,6},{6,0},{1,3},{3,5},{5,7},{7,1},{8,10},{10,12},{12... | collective-permute-start | bytes 1990664 | tf_op jit(solution)/shard_map/ppermute | solution.py:20
  151.6 42.1 %collective-permute-start.14 = (bf16[144,2304]{1,0:T(8,128)(2,1)}, bf16[144,2304]{1,0:T(8,128)(2,1)S(1)}, u32[]{:S(2)}, u32[]{:S(2)}) collective-permute-start(bf16[144,2304]{1,0:T(8,128)(2,1)} %get-tuple-element.15), channel_id=1, source_target_pairs={{0,6},{2,0},{4,2},{6,4},{1,7},{3,1},{5,3},{7,5},{8,14},{10,8},{12,... | collective-permute-start | bytes 1990664 | tf_op jit(solution)/shard_map/ppermute | solution.py:20
  164.9 28.9 %collective-permute-start.18 = (bf16[144,2304]{1,0:T(8,128)(2,1)S(1)}, bf16[144,2304]{1,0:T(8,128)(2,1)S(1)}, u32[]{:S(2)}, u32[]{:S(2)}) collective-permute-start(bf16[144,2304]{1,0:T(8,128)(2,1)S(1)} %add_convert_fusion.1), channel_id=1, source_target_pairs={{0,8},{8,0},{1,9},{9,1},{2,10},{10,2},{3,11},{11,3},{4,12},{12,4},... | collective-permute-start | bytes 1990664 | tf_op jit(solution)/shard_map/ppermute | solution.py:20
  166.1 31.5 %copy-start.2 = (bf16[88,1152]{1,0:T(8,128)(2,1)S(1)}, bf16[88,1152]{1,0:T(8,128)(2,1)}, u32[]{:S(2)}) copy-start(bf16[88,1152]{1,0:T(8,128)(2,1)} %reduce-scatter.7.cloned.1.call-done) | copy-start | bytes 608260
  191.3 6.4 %collective-permute-start.8 = (bf16[2,44,1152]{2,1,0:T(8,128)(2,1)S(1)}, bf16[2,44,1152]{2,1,0:T(8,128)(2,1)S(1)}, u32[]{:S(2)}, u32[]{:S(2)}) collective-permute-start(bf16[2,44,1152]{2,1,0:T(8,128)(2,1)S(1)} %broadcast_select_fusion), channel_id=1, source_target_pairs={{0,16},{16,0},{1,17},{17,1},{2,18},{18,2},{3,19},{19,3},{4,20},{20... | collective-permute-start | bytes 608264 | tf_op jit(solution)/shard_map/ppermute | solution.py:20
  198.5 6.9 %collective-permute-start.9 = (bf16[44,1152]{1,0:T(8,128)(2,1)S(1)}, bf16[44,1152]{1,0:T(8,128)(2,1)S(1)}, u32[]{:S(2)}, u32[]{:S(2)}) collective-permute-start(bf16[44,1152]{1,0:T(8,128)(2,1)S(1)} %get-tuple-element.23), channel_id=1, source_target_pairs={{0,1},{1,0},{2,3},{3,2},{4,5},{5,4},{6,7},{7,6},{8,9},{9,8},{10,11... | collective-permute-start | bytes 304136 | tf_op jit(solution)/shard_map/ppermute | solution.py:20
  (4 other events, 20.9 us)
Sparse Core Ops, SparseCore 0:
  26.3 38.1 all-gather.4
  66.8 38.3 all-gather.6
  107.8 40.1 reduce-scatter.6
  150.4 39.6 reduce-scatter.8

commit v3 on v2

v3 whole, which is shorter than its diff:
```python
import functools
import math

import jax
import jax.numpy as jnp
from jax import lax
from jax.experimental import pallas as pl
from jax.experimental.pallas import tpu as pltpu
from jax.sharding import Mesh, PartitionSpec as P

BF = jnp.bfloat16
F32 = jnp.float32
VMEM_LIMIT = 56 * 1024 * 1024
IN_VMEM = pl.BlockSpec(memory_space=pltpu.VMEM)
SMALL = pl.CostEstimate(flops=1000, bytes_accessed=1000, transcendentals=0)
INPUT_FLOPS = 1e3
DELTA_FLOPS = 1e11
REST_FLOPS = 1e11
IN_SMEM = pl.BlockSpec(memory_space=pltpu.SMEM)


def shift(x, axis, k):
    n = lax.axis_size(axis)
    return lax.ppermute(x, axis, [(i, (i + k) % n) for i in range(n)])


def add(*xs):
    total = xs[0].astype(F32)
    for x in xs[1:]:
        total = total + x.astype(F32)
    return total.astype(BF)


def delta_body(g_ref, u_ref, c_ref, out_ref):
    g = g_ref[...].astype(F32)
    u = u_ref[...].astype(F32)
    c = c_ref[...].astype(F32)
    kappa = math.sqrt(2.0 / math.pi)
    g2 = g * g
    tangent = jnp.tanh(kappa * (g + 0.044715 * g2 * g))
    half = 0.5 * (1.0 + tangent)
    act = g * half
    slope = half + 0.5 * g * (1.0 - tangent * tangent) * kappa * (1.0 + 3.0 * 0.044715 * g2)
    n = g.shape[1]
    out_ref[:, :n] = (c * u * slope).astype(BF)
    out_ref[:, n:] = (c * act).astype(BF)


def make_deltas(g, u, c, tile=176):
    rows, cols = g.shape
    spec = pl.BlockSpec((tile, cols), lambda i: (i, 0))
    return pl.pallas_call(
        delta_body,
        out_shape=jax.ShapeDtypeStruct((rows, 2 * cols), BF),
        grid=(rows // tile,),
        in_specs=[spec] * 3,
        out_specs=pl.BlockSpec((tile, 2 * cols), lambda i: (i, 0)),
        compiler_params=pltpu.CompilerParams(vmem_limit_bytes=VMEM_LIMIT),
        cost_estimate=pl.CostEstimate(flops=int(DELTA_FLOPS), bytes_accessed=1000, transcendentals=0),
        name="deltas",
    )(g, u, c)


TOKEN_ORDER = ((1, 2), (0, 2), (1, 1), (1, 3), (0, 1), (0, 3), (1, 0), (0, 0))


def roll_blocks(blocks, y, sign):
    one = [jnp.where(y % 2 == 1, blocks[(i + sign) % 4], blocks[i]) for i in range(4)]
    return [jnp.where(y >= 2, one[(i + 2) % 4], one[i]) for i in range(4)]


def pack_body(g_ref, u_ref, w_ref):
    hidden = g_ref.shape[1]
    w_ref[:, :hidden] = g_ref[...]
    w_ref[:, hidden:] = u_ref[...]


def pack_weights(gate, up):
    return pl.pallas_call(
        pack_body,
        out_shape=jax.ShapeDtypeStruct((gate.shape[0], 2 * gate.shape[1]), BF),
        in_specs=[IN_VMEM] * 2,
        out_specs=IN_VMEM,
        cost_estimate=SMALL,
        name="pack_weights",
    )(gate, up)


def split_body(s_ref, near_ref, far_ref, mine_ref, other_ref, scratch):
    x_lo, y, core, x_hi = s_ref[0], s_ref[1], s_ref[2], s_ref[3]
    rows, cols = near_ref.shape
    n = cols // 16
    near, far = near_ref[...].astype(F32), far_ref[...].astype(F32)
    for h, x in enumerate(
        (jnp.where(x_hi == 0, near, far), jnp.where(x_hi == 0, far, near))
    ):
        for parity in range(2):
            raw = [
                jnp.where(
                    core == 0,
                    x[:, (2 * j + parity) * n : (2 * j + parity + 1) * n],
                    x[:, (2 * j + 1 - parity) * n : (2 * j + 2 - parity) * n],
                )
                for j in range(8)
            ]
            close = [jnp.where(x_lo == 0, raw[i], raw[i + 4]) for i in range(4)]
            away = [jnp.where(x_lo == 0, raw[i + 4], raw[i]) for i in range(4)]
            by_a = roll_blocks(close, y, 1), roll_blocks(away, y, 1)
            for j, (a, dy) in enumerate(TOKEN_ORDER):
                scratch[parity, h * rows : (h + 1) * rows, j * n : (j + 1) * n] = by_a[a][dy]
    mine_ref[...] = scratch[0].astype(BF)
    other_ref[...] = scratch[1].astype(BF)


def split_tokens(place, near, far):
    rows, cols = near.shape
    half = jax.ShapeDtypeStruct((2 * rows, cols // 2), BF)
    return pl.pallas_call(
        split_body,
        out_shape=[half, half],
        in_specs=[IN_SMEM] + [IN_VMEM] * 2,
        out_specs=[IN_VMEM] * 2,
        scratch_shapes=[pltpu.VMEM((2, 2 * rows, cols // 2), F32)],
        cost_estimate=SMALL,
        name="split_tokens",
    )(place, near, far)


def join_body(s_ref, mine_ref, other_ref, out_ref):
    x_lo, y, core = s_ref[0], s_ref[1], s_ref[2]
    n = mine_ref.shape[1] // 8

    def plain(ref):
        x = ref[...].astype(F32)
        near = roll_blocks([x[:, i * n : (i + 1) * n] for i in range(4)], y, -1)
        far = roll_blocks([x[:, (i + 4) * n : (i + 5) * n] for i in range(4)], y, -1)
        low = [jnp.where(x_lo == 0, near[i], far[i]) for i in range(4)]
        high = [jnp.where(x_lo == 0, far[i], near[i]) for i in range(4)]
        return low + high

    mine, other = plain(mine_ref), plain(other_ref)
    for j in range(8):
        out_ref[:, 2 * j * n : (2 * j + 1) * n] = jnp.where(core == 0, mine[j], other[j]).astype(BF)
        out_ref[:, (2 * j + 1) * n : (2 * j + 2) * n] = jnp.where(
            core == 0, other[j], mine[j]
        ).astype(BF)


def join_columns(place, mine, other):
    rows, cols = mine.shape
    return pl.pallas_call(
        join_body,
        out_shape=jax.ShapeDtypeStruct((rows, 2 * cols), BF),
        in_specs=[IN_SMEM, IN_VMEM, IN_VMEM],
        out_specs=IN_VMEM,
        cost_estimate=SMALL,
        name="join_columns",
    )(place, mine, other)


def weight_body(scale, start, skip, x_ref, d_ref, *out_refs):
    n = out_refs[0].shape[0]
    acc = lax.dot_general(
        x_ref[:, start : start + skip + n * len(out_refs)],
        d_ref[...],
        (((0,), (0,)), ((), ())),
        preferred_element_type=F32,
    )
    for i, out_ref in enumerate(out_refs):
        out_ref[...] = (acc[skip + i * n : skip + (i + 1) * n] * scale).astype(BF)


def weight_product(x, delta, scale, first, count, n, cost, tile=768):
    rows, d = x.shape
    cols = delta.shape[1]
    start = first // 128 * 128
    need = -(-(first + count) // 128) * 128 if first == 0 else d
    return pl.pallas_call(
        functools.partial(weight_body, scale, start, first - start),
        out_shape=[jax.ShapeDtypeStruct((n, cols), BF)] * (count // n),
        grid=(cols // tile,),
        in_specs=[
            pl.BlockSpec((rows, need), lambda i: (0, 0)),
            pl.BlockSpec((rows, tile), lambda i: (0, i)),
        ],
        out_specs=[pl.BlockSpec((n, tile), lambda i: (0, i))] * (count // n),
        compiler_params=pltpu.CompilerParams(vmem_limit_bytes=VMEM_LIMIT),
        cost_estimate=pl.CostEstimate(
            flops=int(cost), bytes_accessed=1000, transcendentals=0
        ),
        name=f"weight_product_{first}",
    )(x, delta)


def input_body(n, *refs):
    blocks, (d_ref, out_ref, w, sems) = refs[:n], refs[n:]
    size = blocks[0].shape[0]

    @pl.when(pl.program_id(0) == 0)
    def _():
        copies = [
            pltpu.make_async_copy(b, w.at[pl.ds(i * size, size)], sems.at[i])
            for i, b in enumerate(blocks)
        ]
        for c in copies:
            c.start()
        for c in copies:
            c.wait()

    out_ref[...] = lax.dot_general(
        d_ref[...], w[...], (((1,), (1,)), ((), ())), preferred_element_type=F32
    ).astype(BF)


def input_product(delta, blocks, tile=352):
    rows, cols = delta.shape
    n = len(blocks)
    d = n * blocks[0].shape[0]
    return pl.pallas_call(
        functools.partial(input_body, n),
        out_shape=jax.ShapeDtypeStruct((rows, d), BF),
        grid=(rows // tile,),
        in_specs=[pl.BlockSpec(memory_space=pl.ANY)] * n
        + [pl.BlockSpec((tile, cols), lambda i: (i, 0))],
        out_specs=pl.BlockSpec((tile, d), lambda i: (i, 0)),
        scratch_shapes=[pltpu.VMEM((d, cols), BF), pltpu.SemaphoreType.DMA((n,))],
        compiler_params=pltpu.CompilerParams(vmem_limit_bytes=40 * 1024 * 1024),
        cost_estimate=pl.CostEstimate(flops=int(INPUT_FLOPS), bytes_accessed=1000, transcendentals=0),
        name="input_product",
    )(*blocks, delta)


def gather_weights(w, after):
    far = shift(w, "x_lo", 1)
    below, above = shift(w, "y", 1), shift(w, "y", -1)
    far, below, above, after = lax.optimization_barrier((far, below, above, after))
    far_below, far_above = shift(far, "y", 1), shift(far, "y", -1)
    across, far_across = shift(below, "y", 1), shift(far_above, "y", -1)
    return [w, above, across, below, far, far_above, far_across, far_below], after


def scatter_grads(first, rest):
    far_up, far_down, up, down, far_own, own = rest
    far_right = shift(first[0], "y", 1)
    left = shift(first[1], "y", -1)
    far_left = shift(far_down, "y", -1)
    far_right = shift(add(far_up, far_right), "y", 1)
    right = shift(up, "y", 1)
    left = shift(add(down, left), "y", -1)
    far_own = shift(add(far_own, far_left, far_right), "x_lo", 1)
    return add(own, right, left, far_own)


def per_device(tokens, gate_pre, up_pre, cotangent, gate_weight, up_weight):
    x_hi = lax.axis_index("x_hi")
    place = jnp.stack(
        [lax.axis_index(a).astype(jnp.int32) for a in ("x_lo", "y", "core", "x_hi")]
    )
    scale = 1.0 / math.sqrt(gate_pre.shape[0] * 16)
    rows, hidden = tokens.shape[0], gate_weight.shape[1]
    owned = gate_weight.shape[0]

    far_tokens = shift(tokens, "x_hi", 1)
    keep, give = split_tokens(place, tokens, far_tokens)
    block = jnp.stack([keep, shift(give, "core", 1)])
    gate_pre, block = lax.optimization_barrier((gate_pre, block))
    x = lax.all_gather(block, "z", axis=0, tiled=True).reshape(-1, keep.shape[1])
    mine = make_deltas(gate_pre, up_pre, cotangent)
    blocks, mine = gather_weights(pack_weights(gate_weight, up_weight), mine)
    other = shift(mine, "core", 1)
    delta = jnp.stack([a.reshape(8, 2 * rows, -1) for a in (mine, other)], 1)
    delta = delta.reshape(-1, 2 * hidden)

    sums = lax.psum_scatter(
        input_product(delta, blocks), "z", scatter_dimension=0, tiled=True
    )

    first = weight_product(x, delta, scale, 0, 2 * owned, owned, 1e3)
    x, first = lax.optimization_barrier((x, first))
    rest = weight_product(x, delta, scale, 2 * owned, 6 * owned, owned, REST_FLOPS)
    grads = scatter_grads(first, rest)

    sums = sums.reshape(2, 2 * rows, -1)
    low, high = sums[:, :rows], sums[:, rows:]
    sent = shift(jnp.where(x_hi == 0, high, low), "x_hi", 1)
    sums = add(jnp.where(x_hi == 0, low, high), sent)
    input_grad = join_columns(place, sums[0], shift(sums[1], "core", 1))
    return input_grad, grads[:, :hidden], grads[:, hidden:]


def solution(mesh):
    fine = Mesh(mesh.devices.reshape(8, 2, 2, 4, 2), ("z", "x_hi", "x_lo", "y", "core"))
    fsdp, fsdpt = ("z", "x_hi"), ("x_lo", "y", "core")
    both = P(fsdpt, fsdp)
    return jax.shard_map(
        per_device,
        mesh=fine,
        in_specs=(P(fsdpt + fsdp, None), both, both, both, both, both),
        out_specs=(P(fsdpt + fsdp, None), both, both),
        check_vma=False,
    )
```

time: 216 us -> 180 us (0.83)
  local copies, waits for them, and re-layouts: 21.2 us -> 2.88 us
  matrix products: 17 us -> 0 us
  waiting for transfers between devices: 80.9 us -> 74 us
  Pallas kernels: 39.4 us -> 44.2 us
    ppermute x19, waiting for transfers between devices: 34.2 us -> 74 us  [shift(): return lax.ppermute(x, axis, [(i, (i + k) % n) for i in range(n)])]
    unnamed x6 -> x2, waiting for transfers between devices: 24 us -> 0.03 us
    all_gather x2 -> x1, waiting for transfers between devices: 22.7 us -> 0.02 us  [per_device(): lax.all_gather(block, 'z', axis=0, tiled=True).reshape(-1, keep.shape[1])]
    dot_general x2 -> x0, matrix products: 17 us -> none  [input_product(): lax.dot_general(delta, w, (((1,), (1,)), ((), ())), preferred_element_typ...]
    unnamed x17 -> x18, local copies, waits for them, and re-layouts: 15.2 us -> 1.34 us
    pallas_call x3 -> x5, Pallas kernels: 27.7 us -> 35.9 us  [the longest x2 17.2 us: weight_product(): pl.pallas_call(functools.partial(weight_body, scale, start, first - start...]
    another operation x1 -> x2, other arithmetic: 0.93 us -> 6.1 us  [the longest x1 5.31 us: per_device(): delta = jnp.stack([a.reshape(8, 2 * rows, -1) for a in (mine, other)], 1)]
    slice x3 -> x0, local copies, waits for them, and re-layouts: 3.55 us -> none  [the longest x1 1.4 us: scatter_grads(): rest = [rest[i * n:(i + 1) * n] for i in range(6)]]
  transfers between devices with their start and end apart: 23 -> 21, of which waited for: 11 -> 13; matrix products, arithmetic and copies ran while one was open for 19% -> 6% of each run, Pallas kernels for 16% -> 21%
where the time goes in v3:
time: 180 us; the launch traced here: 179 us
  waiting for transfers between devices  74 us (41%)
  Pallas kernels  44.2 us (25%)
  starting transfers between devices  33.4 us (19%)
  between operations  14.1 us (8%)
  other arithmetic  10.9 us (6%)
  local copies, waits for them, and re-layouts  2.88 us (2%)
    ppermute x19, waiting for transfers between devices, shift(): return lax.ppermute(x, axis, [(i, (i + k) % n) for i in range(n)])  74 us
    ppermute x19, starting transfers between devices, shift(): return lax.ppermute(x, axis, [(i, (i + k) % n) for i in range(n)])  33.3 us
    pallas_call x2, Pallas kernels, weight_product(): pl.pallas_call(functools.partial(weight_body, scale, start, first - start...  17.2 us
    pallas_call x1, Pallas kernels, input_product(): pl.pallas_call(functools.partial(input_body, n), out_shape=jax.ShapeDtype...  13.4 us
    pallas_call x1, Pallas kernels, make_deltas(): pl.pallas_call(delta_body, out_shape=jax.ShapeDtypeStruct((rows, 2 * cols...  5.91 us
    another operation x1, other arithmetic, per_device(): delta = jnp.stack([a.reshape(8, 2 * rows, -1) for a in (mine, other)], 1)  5.31 us
  transfers between devices with their start and end apart: 21, of which 13 were waited for; matrix products, arithmetic and copies ran while one was open for 6% of the time, Pallas kernels for 21%

profile of v3, /device:TPU:1, one launch (start us, length us, event | category | flops | bytes accessed | tf_op | source)
XLA Modules:
  0.0 179.5 jit_solution(1907846243094301751)
XLA Ops:
  7.2 3.7 %collective-permute-start.3 = (bf16[44,2304]{1,0:T(8,128)(2,1)}, bf16[44,2304]{1,0:T(8,128)(2,1)S(1)}, u32[]{:S(2)}, u32[]{:S(2)}) collective-permute-start(bf16[44,2304]{1,0:T(8,128)(2,1)} %near_ref.1), channel_id=1, source_target_pairs={{0,16},{16,0},{1,17},{17,1},{2,18},{18,2},{3,19},{19,3},{4,20},{20... | collective-permute-start | bytes 608264 | tf_op jit(solution)/shard_map/ppermute | solution.py:24
  11.5 3.8 %collective-permute-done.3.far_ref = bf16[44,2304]{1,0:T(8,128)(2,1)S(1)} collective-permute-done((bf16[44,2304]{1,0:T(8,128)(2,1)}, bf16[44,2304]{1,0:T(8,128)(2,1)S(1)}, u32[]{:S(2)}, u32[]{:S(2)}) %collective-permute-start.3) | collective-permute-done | bytes 202784 | tf_op jit(solution)/shard_map/ppermute | solution.py:24
  16.0 3.4 %split_tokens.1 = (bf16[88,1152]{1,0:T(8,128)(2,1)}, bf16[88,1152]{1,0:T(8,128)(2,1)}) custom-call(s32[4]{0:T(128)} %pad_add_fusion.s_ref, bf16[44,2304]{1,0:T(8,128)(2,1)} %near_ref.1, bf16[44,2304]{1,0:T(8,128)(2,1)} %copy-done.5), custom_call_target="tpu_custom_call" | custom-call | flops 1000 | bytes 1000 | tf_op jit(solution)/shard_map/split_tokens/pallas_call | solution.py:118
  19.3 2.9 %collective-permute-start.4 = (bf16[88,1152]{1,0:T(8,128)(2,1)}, bf16[88,1152]{1,0:T(8,128)(2,1)S(1)}, u32[]{:S(2)}, u32[]{:S(2)}) collective-permute-start(bf16[88,1152]{1,0:T(8,128)(2,1)} %get-tuple-element.23), channel_id=1, source_target_pairs={{0,1},{1,0},{2,3},{3,2},{4,5},{5,4},{6,7},{7,6},{8,9},{9,8},{10,11... | collective-permute-start | bytes 608264 | tf_op jit(solution)/shard_map/ppermute | solution.py:24
  28.5 5.9 %deltas.1 = bf16[704,2304]{1,0:T(8,128)(2,1)} custom-call(bf16[704,1152]{1,0:T(8,128)(2,1)} %g_ref.2, bf16[704,1152]{1,0:T(8,128)(2,1)} %u_ref.3, bf16[704,1152]{1,0:T(8,128)(2,1)} %c_ref.1), custom_call_target="tpu_custom_call" | custom-call | flops 99999997952 | bytes 1000 | tf_op jit(solution)/shard_map/deltas/pallas_call | solution.py:52
  34.4 6.5 %collective-permute-done.refs_4_ = bf16[144,2304]{1,0:T(8,128)(2,1)S(1)} collective-permute-done((bf16[144,2304]{1,0:T(8,128)(2,1)}, bf16[144,2304]{1,0:T(8,128)(2,1)S(1)}, u32[]{:S(2)}, u32[]{:S(2)}) %collective-permute-start) | collective-permute-done | bytes 663584 | tf_op jit(solution)/shard_map/ppermute | solution.py:24
  43.7 2.6 %collective-permute-start.6 = (bf16[144,2304]{1,0:T(8,128)(2,1)S(1)}, bf16[144,2304]{1,0:T(8,128)(2,1)S(1)}, u32[]{:S(2)}, u32[]{:S(2)}) collective-permute-start(bf16[144,2304]{1,0:T(8,128)(2,1)S(1)} %collective-permute-done.refs_4_), channel_id=1, source_target_pairs={{0,6},{2,0},{4,2},{6,4},{1,7},{3,1},{5,3},{7,5},{8,14},{10,8},{12,... | collective-permute-start | bytes 1990664 | tf_op jit(solution)/shard_map/ppermute | solution.py:24
  46.5 14.2 %collective-permute-done.6.refs_5_ = bf16[144,2304]{1,0:T(8,128)(2,1)S(1)} collective-permute-done((bf16[144,2304]{1,0:T(8,128)(2,1)S(1)}, bf16[144,2304]{1,0:T(8,128)(2,1)S(1)}, u32[]{:S(2)}, u32[]{:S(2)}) %collective-permute-start.6) | collective-permute-done | bytes 663584 | tf_op jit(solution)/shard_map/ppermute | solution.py:24
  60.7 3.5 %collective-permute-start.7 = (bf16[144,2304]{1,0:T(8,128)(2,1)S(1)}, bf16[144,2304]{1,0:T(8,128)(2,1)S(1)}, u32[]{:S(2)}, u32[]{:S(2)}) collective-permute-start(bf16[144,2304]{1,0:T(8,128)(2,1)S(1)} %collective-permute-done.6.refs_5_), channel_id=1, source_target_pairs={{0,6},{2,0},{4,2},{6,4},{1,7},{3,1},{5,3},{7,5},{8,14},{10,8},{12,... | collective-permute-start | bytes 1990664 | tf_op jit(solution)/shard_map/ppermute | solution.py:24
  64.2 5.3 %pad_maximum_fusion = bf16[8,2,88,2304]{3,2,1,0:T(8,128)(2,1)} fusion(bf16[8,1,88,2304]{3,2,1,0:T(8,128)(2,1)S(1)} %bitcast.25, bf16[8,1,88,2304]{3,2,1,0:T(8,128)(2,1)} %bitcast.24), kind=kLoop, calls=%fused_computation | loop fusion | flops 3244032 | bytes 12976128 | tf_op jit(solution)/shard_map/stack | solution.py:271
  69.6 8.5 %collective-permute-done.5.refs_2_ = bf16[144,2304]{1,0:T(8,128)(2,1)S(1)} collective-permute-done((bf16[144,2304]{1,0:T(8,128)(2,1)S(1)}, bf16[144,2304]{1,0:T(8,128)(2,1)S(1)}, u32[]{:S(2)}, u32[]{:S(2)}) %collective-permute-start.5) | collective-permute-done | bytes 663584 | tf_op jit(solution)/shard_map/ppermute | solution.py:24
  78.0 13.4 %input_product.1 = bf16[1408,1152]{1,0:T(8,128)(2,1)} custom-call(bf16[144,2304]{1,0:T(8,128)(2,1)S(1)} %copy-done, bf16[144,2304]{1,0:T(8,128)(2,1)S(1)} %collective-permute-done.2.refs_1_, bf16[144,2304]{1,0:T(8,128)(2,1)S(1)} %collective-permute-done.5.refs_2_, bf16[144,2304]{1,0:T(8,128)(2,1)S(1)} %collective-permute-done.1.refs_3_, ...), custom_call_target="tpu_custom_call" | custom-call | flops 1000 | bytes 1000 | tf_op jit(solution)/shard_map/input_product/pallas_call | solution.py:219
  91.5 6.4 %weight_product_0.1 = (bf16[144,2304]{1,0:T(8,128)(2,1)}, bf16[144,2304]{1,0:T(8,128)(2,1)}) custom-call(bf16[1408,1152]{1,0:T(8,128)(2,1)} %bitcast.22, bf16[1408,2304]{1,0:T(8,128)(2,1)} %bitcast.20), custom_call_target="tpu_custom_call" | custom-call | flops 1000 | bytes 1000 | tf_op jit(solution)/shard_map/weight_product_0/pallas_call | solution.py:178
  98.0 10.8 %weight_product_288.1 = (bf16[144,2304]{1,0:T(8,128)(2,1)}, bf16[144,2304]{1,0:T(8,128)(2,1)}, bf16[144,2304]{1,0:T(8,128)(2,1)}, bf16[144,2304]{1,0:T(8,128)(2,...) custom-call(bf16[1408,1152]{1,0:T(8,128)(2,1)} %bitcast.23, bf16[1408,2304]{1,0:T(8,128)(2,1)} %bitcast.21), custom_call_target="tpu_custom_call" | custom-call | flops 99999997952 | bytes 1000 | tf_op jit(solution)/shard_map/weight_product_288/pallas_call | solution.py:178
  108.7 3.3 %collective-permute-start.13 = (bf16[144,2304]{1,0:T(8,128)(2,1)S(1)}, bf16[144,2304]{1,0:T(8,128)(2,1)S(1)}, u32[]{:S(2)}, u32[]{:S(2)}) collective-permute-start(bf16[144,2304]{1,0:T(8,128)(2,1)S(1)} %copy-done.8), channel_id=1, source_target_pairs={{0,6},{2,0},{4,2},{6,4},{1,7},{3,1},{5,3},{7,5},{8,14},{10,8},{12,... | collective-permute-start | bytes 1990664 | tf_op jit(solution)/shard_map/ppermute | solution.py:24
  116.5 8.2 %collective-permute-done.13 = bf16[144,2304]{1,0:T(8,128)(2,1)S(1)} collective-permute-done((bf16[144,2304]{1,0:T(8,128)(2,1)S(1)}, bf16[144,2304]{1,0:T(8,128)(2,1)S(1)}, u32[]{:S(2)}, u32[]{:S(2)}) %collective-permute-start.13) | collective-permute-done | bytes 663584 | tf_op jit(solution)/shard_map/ppermute | solution.py:24
  124.8 3.6 %collective-permute-start.14 = (bf16[144,2304]{1,0:T(8,128)(2,1)S(1)}, bf16[144,2304]{1,0:T(8,128)(2,1)S(1)}, u32[]{:S(2)}, u32[]{:S(2)}) collective-permute-start(bf16[144,2304]{1,0:T(8,128)(2,1)S(1)} %add_convert_fusion.3), channel_id=1, source_target_pairs={{0,6},{2,0},{4,2},{6,4},{1,7},{3,1},{5,3},{7,5},{8,14},{10,8},{12,... | collective-permute-start | bytes 1990664 | tf_op jit(solution)/shard_map/ppermute | solution.py:24
  128.4 10.6 %collective-permute-done.15 = bf16[144,2304]{1,0:T(8,128)(2,1)S(1)} collective-permute-done((bf16[144,2304]{1,0:T(8,128)(2,1)}, bf16[144,2304]{1,0:T(8,128)(2,1)S(1)}, u32[]{:S(2)}, u32[]{:S(2)}) %collective-permute-start.15) | collective-permute-done | bytes 663584 | tf_op jit(solution)/shard_map/ppermute | solution.py:24
  139.0 4.1 %collective-permute-done.17 = bf16[144,2304]{1,0:T(8,128)(2,1)S(1)} collective-permute-done((bf16[144,2304]{1,0:T(8,128)(2,1)S(1)}, bf16[144,2304]{1,0:T(8,128)(2,1)S(1)}, u32[]{:S(2)}, u32[]{:S(2)}) %collective-permute-start.17) | collective-permute-done | bytes 663584 | tf_op jit(solution)/shard_map/ppermute | solution.py:24
  146.0 2.4 %collective-permute-start.10 = (bf16[2,44,1152]{2,1,0:T(8,128)(2,1)S(1)}, bf16[2,44,1152]{2,1,0:T(8,128)(2,1)S(1)}, u32[]{:S(2)}, u32[]{:S(2)}) collective-permute-start(bf16[2,44,1152]{2,1,0:T(8,128)(2,1)S(1)} %broadcast_select_fusion), channel_id=1, source_target_pairs={{0,16},{16,0},{1,17},{17,1},{2,18},{18,2},{3,19},{19,3},{4,20},{20... | collective-permute-start | bytes 608264 | tf_op jit(solution)/shard_map/ppermute | solution.py:24
  148.3 4.7 %collective-permute-done.14 = bf16[144,2304]{1,0:T(8,128)(2,1)S(1)} collective-permute-done((bf16[144,2304]{1,0:T(8,128)(2,1)S(1)}, bf16[144,2304]{1,0:T(8,128)(2,1)S(1)}, u32[]{:S(2)}, u32[]{:S(2)}) %collective-permute-start.14) | collective-permute-done | bytes 663584 | tf_op jit(solution)/shard_map/ppermute | solution.py:24
  153.1 4.4 %collective-permute-done.18 = bf16[144,2304]{1,0:T(8,128)(2,1)S(1)} collective-permute-done((bf16[144,2304]{1,0:T(8,128)(2,1)}, bf16[144,2304]{1,0:T(8,128)(2,1)S(1)}, u32[]{:S(2)}, u32[]{:S(2)}) %collective-permute-start.18) | collective-permute-done | bytes 663584 | tf_op jit(solution)/shard_map/ppermute | solution.py:24
  157.8 5.6 %collective-permute-done.10 = bf16[2,44,1152]{2,1,0:T(8,128)(2,1)S(1)} collective-permute-done((bf16[2,44,1152]{2,1,0:T(8,128)(2,1)S(1)}, bf16[2,44,1152]{2,1,0:T(8,128)(2,1)S(1)}, u32[]{:S(2)}, u32[]{:S(2)}) %collective-permute-start.10) | collective-permute-done | bytes 202784 | tf_op jit(solution)/shard_map/ppermute | solution.py:24
  164.2 4.5 %collective-permute-start.11 = (bf16[44,1152]{1,0:T(8,128)(2,1)S(1)}, bf16[44,1152]{1,0:T(8,128)(2,1)S(1)}, u32[]{:S(2)}, u32[]{:S(2)}) collective-permute-start(bf16[44,1152]{1,0:T(8,128)(2,1)S(1)} %get-tuple-element.43), channel_id=1, source_target_pairs={{0,1},{1,0},{2,3},{3,2},{4,5},{5,4},{6,7},{7,6},{8,9},{9,8},{10,11... | collective-permute-start | bytes 304136 | tf_op jit(solution)/shard_map/ppermute | solution.py:24
  (56 shorter events, 23.2 us)
Async XLA Ops:
  7.2 84.3 %all-gather.2.cloned.1.call-start = ((), (), s32[]{:S(2)}) async-start(), calls=%async_computation.2 | async-start | bytes 3649536 | tf_op jit(solution)/shard_map/all_gather | solution.py:267
  7.2 8.1 %collective-permute-start.3 = (bf16[44,2304]{1,0:T(8,128)(2,1)}, bf16[44,2304]{1,0:T(8,128)(2,1)S(1)}, u32[]{:S(2)}, u32[]{:S(2)}) collective-permute-start(bf16[44,2304]{1,0:T(8,128)(2,1)} %near_ref.1), channel_id=1, source_target_pairs={{0,16},{16,0},{1,17},{17,1},{2,18},{18,2},{3,19},{19,3},{4,20},{20... | collective-permute-start | bytes 608264 | tf_op jit(solution)/shard_map/ppermute | solution.py:24
  19.3 8.3 %collective-permute-start.4 = (bf16[88,1152]{1,0:T(8,128)(2,1)}, bf16[88,1152]{1,0:T(8,128)(2,1)S(1)}, u32[]{:S(2)}, u32[]{:S(2)}) collective-permute-start(bf16[88,1152]{1,0:T(8,128)(2,1)} %get-tuple-element.23), channel_id=1, source_target_pairs={{0,1},{1,0},{2,3},{3,2},{4,5},{5,4},{6,7},{7,6},{8,9},{9,8},{10,11... | collective-permute-start | bytes 608264 | tf_op jit(solution)/shard_map/ppermute | solution.py:24
  24.2 16.7 %collective-permute-start = (bf16[144,2304]{1,0:T(8,128)(2,1)}, bf16[144,2304]{1,0:T(8,128)(2,1)S(1)}, u32[]{:S(2)}, u32[]{:S(2)}) collective-permute-start(bf16[144,2304]{1,0:T(8,128)(2,1)} %pack_weights.1.refs_0_), channel_id=1, source_target_pairs={{0,8},{8,0},{1,9},{9,1},{2,10},{10,2},{3,11},{11,3},{4,12},{12,4},... | collective-permute-start | bytes 1990664 | tf_op jit(solution)/shard_map/ppermute | solution.py:24
  24.9 17.8 %collective-permute-start.1 = (bf16[144,2304]{1,0:T(8,128)(2,1)}, bf16[144,2304]{1,0:T(8,128)(2,1)S(1)}, u32[]{:S(2)}, u32[]{:S(2)}) collective-permute-start(bf16[144,2304]{1,0:T(8,128)(2,1)} %pack_weights.1.refs_0_), channel_id=1, source_target_pairs={{0,2},{2,4},{4,6},{6,0},{1,3},{3,5},{5,7},{7,1},{8,10},{10,12},{12... | collective-permute-start | bytes 1990664 | tf_op jit(solution)/shard_map/ppermute | solution.py:24
  26.2 16.5 %collective-permute-start.2 = (bf16[144,2304]{1,0:T(8,128)(2,1)}, bf16[144,2304]{1,0:T(8,128)(2,1)S(1)}, u32[]{:S(2)}, u32[]{:S(2)}) collective-permute-start(bf16[144,2304]{1,0:T(8,128)(2,1)} %pack_weights.1.refs_0_), channel_id=1, source_target_pairs={{0,6},{2,0},{4,2},{6,4},{1,7},{3,1},{5,3},{7,5},{8,14},{10,8},{12,... | collective-permute-start | bytes 1990664 | tf_op jit(solution)/shard_map/ppermute | solution.py:24
  28.5 116.4 %reduce-scatter.2.cloned.1.call-start = ((), (), s32[]{:S(2)}) async-start(), calls=%async_computation.1 | async-start | bytes 3649536 | tf_op jit(solution)/shard_map/reduce_scatter | solution.py:274
  42.7 21.5 %collective-permute-start.9 = (bf16[704,2304]{1,0:T(8,128)(2,1)}, bf16[704,2304]{1,0:T(8,128)(2,1)S(1)}, u32[]{:S(2)}, u32[]{:S(2)}) collective-permute-start(bf16[704,2304]{1,0:T(8,128)(2,1)} %deltas.1), channel_id=1, source_target_pairs={{0,1},{1,0},{2,3},{3,2},{4,5},{5,4},{6,7},{7,6},{8,9},{9,8},{10,11... | collective-permute-start | bytes 9732104 | tf_op jit(solution)/shard_map/ppermute | solution.py:24
  43.7 17.0 %collective-permute-start.6 = (bf16[144,2304]{1,0:T(8,128)(2,1)S(1)}, bf16[144,2304]{1,0:T(8,128)(2,1)S(1)}, u32[]{:S(2)}, u32[]{:S(2)}) collective-permute-start(bf16[144,2304]{1,0:T(8,128)(2,1)S(1)} %collective-permute-done.refs_4_), channel_id=1, source_target_pairs={{0,6},{2,0},{4,2},{6,4},{1,7},{3,1},{5,3},{7,5},{8,14},{10,8},{12,... | collective-permute-start | bytes 1990664 | tf_op jit(solution)/shard_map/ppermute | solution.py:24
  46.4 23.2 %collective-permute-start.8 = (bf16[144,2304]{1,0:T(8,128)(2,1)S(1)}, bf16[144,2304]{1,0:T(8,128)(2,1)S(1)}, u32[]{:S(2)}, u32[]{:S(2)}) collective-permute-start(bf16[144,2304]{1,0:T(8,128)(2,1)S(1)} %collective-permute-done.refs_4_), channel_id=1, source_target_pairs={{0,2},{2,4},{4,6},{6,0},{1,3},{3,5},{5,7},{7,1},{8,10},{10,12},{12... | collective-permute-start | bytes 1990664 | tf_op jit(solution)/shard_map/ppermute | solution.py:24
  46.4 31.6 %collective-permute-start.5 = (bf16[144,2304]{1,0:T(8,128)(2,1)S(1)}, bf16[144,2304]{1,0:T(8,128)(2,1)S(1)}, u32[]{:S(2)}, u32[]{:S(2)}) collective-permute-start(bf16[144,2304]{1,0:T(8,128)(2,1)S(1)} %collective-permute-done.1.refs_3_), channel_id=1, source_target_pairs={{0,2},{2,4},{4,6},{6,0},{1,3},{3,5},{5,7},{7,1},{8,10},{10,12},{12... | collective-permute-start | bytes 1990664 | tf_op jit(solution)/shard_map/ppermute | solution.py:24
  60.7 17.3 %collective-permute-start.7 = (bf16[144,2304]{1,0:T(8,128)(2,1)S(1)}, bf16[144,2304]{1,0:T(8,128)(2,1)S(1)}, u32[]{:S(2)}, u32[]{:S(2)}) collective-permute-start(bf16[144,2304]{1,0:T(8,128)(2,1)S(1)} %collective-permute-done.6.refs_5_), channel_id=1, source_target_pairs={{0,6},{2,0},{4,2},{6,4},{1,7},{3,1},{5,3},{7,5},{8,14},{10,8},{12,... | collective-permute-start | bytes 1990664 | tf_op jit(solution)/shard_map/ppermute | solution.py:24
  97.9 17.2 %collective-permute-start.16 = (bf16[144,2304]{1,0:T(8,128)(2,1)}, bf16[144,2304]{1,0:T(8,128)(2,1)S(1)}, u32[]{:S(2)}, u32[]{:S(2)}) collective-permute-start(bf16[144,2304]{1,0:T(8,128)(2,1)} %get-tuple-element.40), channel_id=1, source_target_pairs={{0,2},{2,4},{4,6},{6,0},{1,3},{3,5},{5,7},{7,1},{8,10},{10,12},{12... | collective-permute-start | bytes 1990664 | tf_op jit(solution)/shard_map/ppermute | solution.py:24
  108.7 15.9 %copy-start.4 = (bf16[144,2304]{1,0:T(8,128)(2,1)S(1)}, bf16[144,2304]{1,0:T(8,128)(2,1)}, u32[]{:S(2)}) copy-start(bf16[144,2304]{1,0:T(8,128)(2,1)} %get-tuple-element.35) | copy-start | bytes 1990660
  108.7 15.9 %collective-permute-start.13 = (bf16[144,2304]{1,0:T(8,128)(2,1)S(1)}, bf16[144,2304]{1,0:T(8,128)(2,1)S(1)}, u32[]{:S(2)}, u32[]{:S(2)}) collective-permute-start(bf16[144,2304]{1,0:T(8,128)(2,1)S(1)} %copy-done.8), channel_id=1, source_target_pairs={{0,6},{2,0},{4,2},{6,4},{1,7},{3,1},{5,3},{7,5},{8,14},{10,8},{12,... | collective-permute-start | bytes 1990664 | tf_op jit(solution)/shard_map/ppermute | solution.py:24
  112.0 27.0 %collective-permute-start.15 = (bf16[144,2304]{1,0:T(8,128)(2,1)}, bf16[144,2304]{1,0:T(8,128)(2,1)S(1)}, u32[]{:S(2)}, u32[]{:S(2)}) collective-permute-start(bf16[144,2304]{1,0:T(8,128)(2,1)} %get-tuple-element.38), channel_id=1, source_target_pairs={{0,6},{2,0},{4,2},{6,4},{1,7},{3,1},{5,3},{7,5},{8,14},{10,8},{12,... | collective-permute-start | bytes 1990664 | tf_op jit(solution)/shard_map/ppermute | solution.py:24
  113.4 35.0 %collective-permute-start.12 = (bf16[144,2304]{1,0:T(8,128)(2,1)}, bf16[144,2304]{1,0:T(8,128)(2,1)S(1)}, u32[]{:S(2)}, u32[]{:S(2)}) collective-permute-start(bf16[144,2304]{1,0:T(8,128)(2,1)} %get-tuple-element.34), channel_id=1, source_target_pairs={{0,2},{2,4},{4,6},{6,0},{1,3},{3,5},{5,7},{7,1},{8,10},{10,12},{12... | collective-permute-start | bytes 1990664 | tf_op jit(solution)/shard_map/ppermute | solution.py:24
  116.4 26.7 %copy-start.3 = (bf16[144,2304]{1,0:T(8,128)(2,1)S(1)}, bf16[144,2304]{1,0:T(8,128)(2,1)}, u32[]{:S(2)}) copy-start(bf16[144,2304]{1,0:T(8,128)(2,1)} %get-tuple-element.37) | copy-start | bytes 1990660
  116.4 26.6 %collective-permute-start.17 = (bf16[144,2304]{1,0:T(8,128)(2,1)S(1)}, bf16[144,2304]{1,0:T(8,128)(2,1)S(1)}, u32[]{:S(2)}, u32[]{:S(2)}) collective-permute-start(bf16[144,2304]{1,0:T(8,128)(2,1)S(1)} %add_convert_fusion.2), channel_id=1, source_target_pairs={{0,2},{2,4},{4,6},{6,0},{1,3},{3,5},{5,7},{7,1},{8,10},{10,12},{12... | collective-permute-start | bytes 1990664 | tf_op jit(solution)/shard_map/ppermute | solution.py:24
  124.8 28.3 %collective-permute-start.14 = (bf16[144,2304]{1,0:T(8,128)(2,1)S(1)}, bf16[144,2304]{1,0:T(8,128)(2,1)S(1)}, u32[]{:S(2)}, u32[]{:S(2)}) collective-permute-start(bf16[144,2304]{1,0:T(8,128)(2,1)S(1)} %add_convert_fusion.3), channel_id=1, source_target_pairs={{0,6},{2,0},{4,2},{6,4},{1,7},{3,1},{5,3},{7,5},{8,14},{10,8},{12,... | collective-permute-start | bytes 1990664 | tf_op jit(solution)/shard_map/ppermute | solution.py:24
  143.0 14.4 %copy-start.2 = (bf16[144,2304]{1,0:T(8,128)(2,1)S(1)}, bf16[144,2304]{1,0:T(8,128)(2,1)}, u32[]{:S(2)}) copy-start(bf16[144,2304]{1,0:T(8,128)(2,1)} %get-tuple-element.33) | copy-start | bytes 1990660
  144.2 13.3 %collective-permute-start.18 = (bf16[144,2304]{1,0:T(8,128)(2,1)}, bf16[144,2304]{1,0:T(8,128)(2,1)S(1)}, u32[]{:S(2)}, u32[]{:S(2)}) collective-permute-start(bf16[144,2304]{1,0:T(8,128)(2,1)} %add_convert_fusion.1), channel_id=1, source_target_pairs={{0,8},{8,0},{1,9},{9,1},{2,10},{10,2},{3,11},{11,3},{4,12},{12,4},... | collective-permute-start | bytes 1990664 | tf_op jit(solution)/shard_map/ppermute | solution.py:24
  146.0 17.4 %collective-permute-start.10 = (bf16[2,44,1152]{2,1,0:T(8,128)(2,1)S(1)}, bf16[2,44,1152]{2,1,0:T(8,128)(2,1)S(1)}, u32[]{:S(2)}, u32[]{:S(2)}) collective-permute-start(bf16[2,44,1152]{2,1,0:T(8,128)(2,1)S(1)} %broadcast_select_fusion), channel_id=1, source_target_pairs={{0,16},{16,0},{1,17},{17,1},{2,18},{18,2},{3,19},{19,3},{4,20},{20... | collective-permute-start | bytes 608264 | tf_op jit(solution)/shard_map/ppermute | solution.py:24
  164.2 5.5 %collective-permute-start.11 = (bf16[44,1152]{1,0:T(8,128)(2,1)S(1)}, bf16[44,1152]{1,0:T(8,128)(2,1)S(1)}, u32[]{:S(2)}, u32[]{:S(2)}) collective-permute-start(bf16[44,1152]{1,0:T(8,128)(2,1)S(1)} %get-tuple-element.43), channel_id=1, source_target_pairs={{0,1},{1,0},{2,3},{3,2},{4,5},{5,4},{6,7},{7,6},{8,9},{9,8},{10,11... | collective-permute-start | bytes 304136 | tf_op jit(solution)/shard_map/ppermute | solution.py:24
  (6 other events, 40.2 us)
Sparse Core Ops, SparseCore 0:
  28.6 47.5 all-gather.1
  91.6 49.5 reduce-scatter.1

commit v4 on v3

--- a/solution.py
+++ b/solution.py
@@ -14,6 +14,7 @@
 IN_VMEM = pl.BlockSpec(memory_space=pltpu.VMEM)
 SMALL = pl.CostEstimate(flops=1000, bytes_accessed=1000, transcendentals=0)
 INPUT_FLOPS = 1e3
+MARK_FLOPS = 1e12
 DELTA_FLOPS = 1e11
 REST_FLOPS = 1e11
 IN_SMEM = pl.BlockSpec(memory_space=pltpu.SMEM)
@@ -61,6 +62,24 @@
     )(g, u, c)
 
 
+def mark_body(*refs):
+    refs[-1][...] = jnp.zeros_like(refs[-1])
+
+
+def mark(name, *after):
+    return pl.pallas_call(
+        mark_body,
+        out_shape=jax.ShapeDtypeStruct((8, 128), F32),
+        in_specs=[pl.BlockSpec(memory_space=pl.ANY)] * len(after),
+        out_specs=IN_VMEM,
+        cost_estimate=pl.CostEstimate(
+            flops=int(MARK_FLOPS), bytes_accessed=1000, transcendentals=0
+        ),
+        name=name,
+    )(*after)
+
+
+INPUT_ORDER = ((0, 0), (0, 1), (0, 3), (1, 0), (1, 1), (1, 3), (0, 2), (1, 2))
 TOKEN_ORDER = ((1, 2), (0, 2), (1, 1), (1, 3), (0, 1), (0, 3), (1, 0), (0, 0))
 
 
@@ -69,61 +88,44 @@
     return [jnp.where(y >= 2, one[(i + 2) % 4], one[i]) for i in range(4)]
 
 
-def pack_body(g_ref, u_ref, w_ref):
+def prologue_body(s_ref, x_ref, g_ref, u_ref, mine_ref, other_ref, w_ref):
     hidden = g_ref.shape[1]
     w_ref[:, :hidden] = g_ref[...]
     w_ref[:, hidden:] = u_ref[...]
-
-
-def pack_weights(gate, up):
-    return pl.pallas_call(
-        pack_body,
-        out_shape=jax.ShapeDtypeStruct((gate.shape[0], 2 * gate.shape[1]), BF),
-        in_specs=[IN_VMEM] * 2,
-        out_specs=IN_VMEM,
+    x_lo, y, core = s_ref[0], s_ref[1], s_ref[2]
+    n = x_ref.shape[1] // 16
+    x = x_ref[...].astype(F32)
+    for parity, ref in ((0, mine_ref), (1, other_ref)):
+        raw = [
+            jnp.where(
+                core == 0,
+                x[:, (2 * j + parity) * n : (2 * j + parity + 1) * n],
+                x[:, (2 * j + 1 - parity) * n : (2 * j + 2 - parity) * n],
+            )
+            for j in range(8)
+        ]
+        close = [jnp.where(x_lo == 0, raw[i], raw[i + 4]) for i in range(4)]
+        away = [jnp.where(x_lo == 0, raw[i + 4], raw[i]) for i in range(4)]
+        by_a = roll_blocks(close, y, 1), roll_blocks(away, y, 1)
+        for j, (a, dy) in enumerate(TOKEN_ORDER):
+            ref[:, j * n : (j + 1) * n] = by_a[a][dy].astype(BF)
+
+
+def prologue(place, tokens, gate, up):
+    rows, cols = tokens.shape
+    half = jax.ShapeDtypeStruct((rows, cols // 2), BF)
+    return pl.pallas_call(
+        prologue_body,
+        out_shape=[
+            half,
+            half,
+            jax.ShapeDtypeStruct((gate.shape[0], 2 * gate.shape[1]), BF),
+        ],
+        in_specs=[IN_SMEM] + [IN_VMEM] * 3,
+        out_specs=[IN_VMEM] * 3,
         cost_estimate=SMALL,
-        name="pack_weights",
-    )(gate, up)
-
-
-def split_body(s_ref, near_ref, far_ref, mine_ref, other_ref, scratch):
-    x_lo, y, core, x_hi = s_ref[0], s_ref[1], s_ref[2], s_ref[3]
-    rows, cols = near_ref.shape
-    n = cols // 16
-    near, far = near_ref[...].astype(F32), far_ref[...].astype(F32)
-    for h, x in enumerate(
-        (jnp.where(x_hi == 0, near, far), jnp.where(x_hi == 0, far, near))
-    ):
-        for parity in range(2):
-            raw = [
-                jnp.where(
-                    core == 0,
-                    x[:, (2 * j + parity) * n : (2 * j + parity + 1) * n],
-                    x[:, (2 * j + 1 - parity) * n : (2 * j + 2 - parity) * n],
-                )
-                for j in range(8)
-            ]
-            close = [jnp.where(x_lo == 0, raw[i], raw[i + 4]) for i in range(4)]
-            away = [jnp.where(x_lo == 0, raw[i + 4], raw[i]) for i in range(4)]
-            by_a = roll_blocks(close, y, 1), roll_blocks(away, y, 1)
-            for j, (a, dy) in enumerate(TOKEN_ORDER):
-                scratch[parity, h * rows : (h + 1) * rows, j * n : (j + 1) * n] = by_a[a][dy]
-    mine_ref[...] = scratch[0].astype(BF)
-    other_ref[...] = scratch[1].astype(BF)
-
-
-def split_tokens(place, near, far):
-    rows, cols = near.shape
-    half = jax.ShapeDtypeStruct((2 * rows, cols // 2), BF)
-    return pl.pallas_call(
-        split_body,
-        out_shape=[half, half],
-        in_specs=[IN_SMEM] + [IN_VMEM] * 2,
-        out_specs=[IN_VMEM] * 2,
-        scratch_shapes=[pltpu.VMEM((2, 2 * rows, cols // 2), F32)],
-        cost_estimate=SMALL,
-        name="split_tokens",
-    )(place, near, far)
+        name="prologue",
+    )(place, tokens, gate, up)
 
 
 def join_body(s_ref, mine_ref, other_ref, out_ref):
@@ -132,8 +134,9 @@
 
     def plain(ref):
         x = ref[...].astype(F32)
-        near = roll_blocks([x[:, i * n : (i + 1) * n] for i in range(4)], y, -1)
-        far = roll_blocks([x[:, (i + 4) * n : (i + 5) * n] for i in range(4)], y, -1)
+        at = {owner: x[:, j * n : (j + 1) * n] for j, owner in enumerate(INPUT_ORDER)}
+        near = roll_blocks([at[0, dy] for dy in range(4)], y, -1)
+        far = roll_blocks([at[1, dy] for dy in range(4)], y, -1)
         low = [jnp.where(x_lo == 0, near[i], far[i]) for i in range(4)]
         high = [jnp.where(x_lo == 0, far[i], near[i]) for i in range(4)]
         return low + high
@@ -158,7 +161,8 @@
     )(place, mine, other)
 
 
-def weight_body(scale, start, skip, x_ref, d_ref, *out_refs):
+def weight_body(scale, start, skip, extra, x_ref, d_ref, *refs):
+    out_refs = refs[extra:]
     n = out_refs[0].shape[0]
     acc = lax.dot_general(
         x_ref[:, start : start + skip + n * len(out_refs)],
@@ -170,30 +174,33 @@
         out_ref[...] = (acc[skip + i * n : skip + (i + 1) * n] * scale).astype(BF)
 
 
-def weight_product(x, delta, scale, first, count, n, cost, tile=768):
+def weight_product(x, delta, scale, first, count, n, cost, after=None, tile=768):
     rows, d = x.shape
     cols = delta.shape[1]
     start = first // 128 * 128
     need = -(-(first + count) // 128) * 128 if first == 0 else d
-    return pl.pallas_call(
-        functools.partial(weight_body, scale, start, first - start),
+    after = [] if after is None else [after]
+    return pl.pallas_call(
+        functools.partial(weight_body, scale, start, first - start, len(after)),
         out_shape=[jax.ShapeDtypeStruct((n, cols), BF)] * (count // n),
         grid=(cols // tile,),
         in_specs=[
             pl.BlockSpec((rows, need), lambda i: (0, 0)),
             pl.BlockSpec((rows, tile), lambda i: (0, i)),
-        ],
+        ]
+        + [pl.BlockSpec(memory_space=pl.ANY)] * len(after),
         out_specs=[pl.BlockSpec((n, tile), lambda i: (0, i))] * (count // n),
         compiler_params=pltpu.CompilerParams(vmem_limit_bytes=VMEM_LIMIT),
         cost_estimate=pl.CostEstimate(
             flops=int(cost), bytes_accessed=1000, transcendentals=0
         ),
         name=f"weight_product_{first}",
-    )(x, delta)
-
-
-def input_body(n, *refs):
-    blocks, (d_ref, out_ref, w, sems) = refs[:n], refs[n:]
+    )(x, delta, *after)
+
+
+def input_body(n, done, *refs):
+    blocks, refs = refs[:n], refs[n:]
+    (d_ref, out_ref, w, sems), extra = refs[-4:], refs[:-4]
     size = blocks[0].shape[0]
 
     @pl.when(pl.program_id(0) == 0)
@@ -207,27 +214,37 @@
         for c in copies:
             c.wait()
 
-    out_ref[...] = lax.dot_general(
+    if done:
+        out_ref[:, :done] = extra[0][...]
+    out_ref[:, done:] = lax.dot_general(
         d_ref[...], w[...], (((1,), (1,)), ((), ())), preferred_element_type=F32
     ).astype(BF)
 
 
-def input_product(delta, blocks, tile=352):
+def input_product(delta, blocks, after, cost, tile=352):
     rows, cols = delta.shape
     n = len(blocks)
-    d = n * blocks[0].shape[0]
-    return pl.pallas_call(
-        functools.partial(input_body, n),
+    done = after.shape[1] if after.shape[0] == rows else 0
+    size = n * blocks[0].shape[0]
+    d = done + size
+    if done:
+        extra = pl.BlockSpec((tile, done), lambda i: (i, 0))
+    else:
+        extra = pl.BlockSpec(memory_space=pl.ANY)
+    return pl.pallas_call(
+        functools.partial(input_body, n, done),
         out_shape=jax.ShapeDtypeStruct((rows, d), BF),
         grid=(rows // tile,),
         in_specs=[pl.BlockSpec(memory_space=pl.ANY)] * n
-        + [pl.BlockSpec((tile, cols), lambda i: (i, 0))],
+        + [extra, pl.BlockSpec((tile, cols), lambda i: (i, 0))],
         out_specs=pl.BlockSpec((tile, d), lambda i: (i, 0)),
-        scratch_shapes=[pltpu.VMEM((d, cols), BF), pltpu.SemaphoreType.DMA((n,))],
+        scratch_shapes=[pltpu.VMEM((size, cols), BF), pltpu.SemaphoreType.DMA((n,))],
         compiler_params=pltpu.CompilerParams(vmem_limit_bytes=40 * 1024 * 1024),
-        cost_estimate=pl.CostEstimate(flops=int(INPUT_FLOPS), bytes_accessed=1000, transcendentals=0),
-        name="input_product",
-    )(*blocks, delta)
+        cost_estimate=pl.CostEstimate(
+            flops=int(cost), bytes_accessed=1000, transcendentals=0
+        ),
+        name=f"input_product_{done}",
+    )(*blocks, after, delta)
 
 
 def gather_weights(w, after):
@@ -236,7 +253,7 @@
     far, below, above, after = lax.optimization_barrier((far, below, above, after))
     far_below, far_above = shift(far, "y", 1), shift(far, "y", -1)
     across, far_across = shift(below, "y", 1), shift(far_above, "y", -1)
-    return [w, above, across, below, far, far_above, far_across, far_below], after
+    return [w, above, below, far, far_above, far_below], [across, far_across], after
 
 
 def scatter_grads(first, rest):
@@ -260,24 +277,28 @@
     rows, hidden = tokens.shape[0], gate_weight.shape[1]
     owned = gate_weight.shape[0]
 
-    far_tokens = shift(tokens, "x_hi", 1)
-    keep, give = split_tokens(place, tokens, far_tokens)
-    block = jnp.stack([keep, shift(give, "core", 1)])
+    keep, give, w = prologue(place, tokens, gate_weight, up_weight)
+    pair = jnp.stack([keep, shift(give, "core", 1)])
+    far = shift(pair, "x_hi", 1)
+    block = jnp.where(
+        x_hi == 0, jnp.concatenate([pair, far], 1), jnp.concatenate([far, pair], 1)
+    )
     gate_pre, block = lax.optimization_barrier((gate_pre, block))
     x = lax.all_gather(block, "z", axis=0, tiled=True).reshape(-1, keep.shape[1])
     mine = make_deltas(gate_pre, up_pre, cotangent)
-    blocks, mine = gather_weights(pack_weights(gate_weight, up_weight), mine)
+    early, late, mine = gather_weights(w, mine)
     other = shift(mine, "core", 1)
     delta = jnp.stack([a.reshape(8, 2 * rows, -1) for a in (mine, other)], 1)
     delta = delta.reshape(-1, 2 * hidden)
 
-    sums = lax.psum_scatter(
-        input_product(delta, blocks), "z", scatter_dimension=0, tiled=True
-    )
+    part = input_product(delta, early, place.reshape(1, -1), INPUT_FLOPS)
+    part = input_product(delta, late, part, 1e3)
+    sums = lax.psum_scatter(part, "z", scatter_dimension=0, tiled=True)
 
     first = weight_product(x, delta, scale, 0, 2 * owned, owned, 1e3)
-    x, first = lax.optimization_barrier((x, first))
-    rest = weight_product(x, delta, scale, 2 * owned, 6 * owned, owned, REST_FLOPS)
+    rest = weight_product(
+        x, delta, scale, 2 * owned, 6 * owned, owned, REST_FLOPS, mark("sent", *first)
+    )
     grads = scatter_grads(first, rest)
 
     sums = sums.reshape(2, 2 * rows, -1)

time: 180 us -> 169 us (0.939)
  waiting for transfers between devices: 74 us -> 67.7 us
  starting transfers between devices: 33.4 us -> 29.1 us
    ppermute x19, waiting for transfers between devices: 74 us -> 67.6 us  [shift(): return lax.ppermute(x, axis, [(i, (i + k) % n) for i in range(n)])]
    ppermute x19, starting transfers between devices: 33.3 us -> 29 us  [shift(): return lax.ppermute(x, axis, [(i, (i + k) % n) for i in range(n)])]
    another operation x1, other arithmetic: 5.31 us -> 2.58 us  [per_device(): delta = jnp.stack([a.reshape(8, 2 * rows, -1) for a in (mine, other)], 1)]
    select_n x0 -> x1, other arithmetic: none -> 1.88 us  [per_device(): jnp.where(x_hi == 0, jnp.concatenate([pair, far], 1), jnp.concatenate([fa...]
    pallas_call x3 -> x4, Pallas kernels: 18.7 us -> 18.1 us  [the longest x2 14.6 us: input_product(): pl.pallas_call(functools.partial(input_body, n, done), out_shape=jax.Shap...]
  transfers between devices with their start and end apart: 21 -> 21, of which waited for: 13 -> 11; matrix products, arithmetic and copies ran while one was open for 6% -> 6% of each run, Pallas kernels for 21% -> 23%
where the time goes in v4:
time: 169 us; the launch traced here: 168 us
  waiting for transfers between devices  67.7 us (40%)
  Pallas kernels  43.5 us (26%)
  starting transfers between devices  29.1 us (17%)
  between operations  14.2 us (8%)
  other arithmetic  11.3 us (7%)
  local copies, waits for them, and re-layouts  2.71 us (2%)
    ppermute x19, waiting for transfers between devices, shift(): return lax.ppermute(x, axis, [(i, (i + k) % n) for i in range(n)])  67.6 us
    ppermute x19, starting transfers between devices, shift(): return lax.ppermute(x, axis, [(i, (i + k) % n) for i in range(n)])  29 us
    pallas_call x2, Pallas kernels, weight_product(): pl.pallas_call(functools.partial(weight_body, scale, start, first - start...  17.1 us
    pallas_call x2, Pallas kernels, input_product(): pl.pallas_call(functools.partial(input_body, n, done), out_shape=jax.Shap...  14.6 us
    pallas_call x1, Pallas kernels, make_deltas(): pl.pallas_call(delta_body, out_shape=jax.ShapeDtypeStruct((rows, 2 * cols...  5.92 us
    convert_element_type x5, other arithmetic, add(): return total.astype(BF)  4.12 us
  transfers between devices with their start and end apart: 21, of which 11 were waited for; matrix products, arithmetic and copies ran while one was open for 6% of the time, Pallas kernels for 23%

profile of v4, /device:TPU:1, one launch (start us, length us, event | category | flops | bytes accessed | tf_op | source)
XLA Modules:
  0.0 168.4 jit_solution(1673054070243477615)
XLA Ops:
  7.8 2.8 %prologue.1 = (bf16[44,1152]{1,0:T(8,128)(2,1)}, bf16[44,1152]{1,0:T(8,128)(2,1)}, bf16[144,2304]{1,0:T(8,128)(2,1)}) custom-call(s32[4]{0:T(128)} %pad_add_fusion.s_ref, bf16[44,2304]{1,0:T(8,128)(2,1)} %x_ref.1, bf16[144,1152]{1,0:T(8,128)(2,1)} %g_ref.1, bf16[144,1152]{1,0:T(8,128)(2,1)} %u_ref.2), custom_call_target="tpu_custom_call" | custom-call | flops 1000 | bytes 1000 | tf_op jit(solution)/shard_map/prologue/pallas_call | solution.py:117
  10.7 3.2 %collective-permute-start.3 = (bf16[44,1152]{1,0:T(8,128)(2,1)}, bf16[44,1152]{1,0:T(8,128)(2,1)S(1)}, u32[]{:S(2)}, u32[]{:S(2)}) collective-permute-start(bf16[44,1152]{1,0:T(8,128)(2,1)} %get-tuple-element.22), channel_id=1, source_target_pairs={{0,1},{1,0},{2,3},{3,2},{4,5},{5,4},{6,7},{7,6},{8,9},{9,8},{10,11... | collective-permute-start | bytes 304136 | tf_op jit(solution)/shard_map/ppermute | solution.py:25
  20.2 4.1 %collective-permute-done.4 = bf16[2,44,1152]{2,1,0:T(8,128)(2,1)S(1)} collective-permute-done((bf16[2,44,1152]{2,1,0:T(8,128)(2,1)S(1)}, bf16[2,44,1152]{2,1,0:T(8,128)(2,1)S(1)}, u32[]{:S(2)}, u32[]{:S(2)}) %collective-permute-start.4) | collective-permute-done | bytes 202784 | tf_op jit(solution)/shard_map/ppermute | solution.py:25
  26.2 5.9 %deltas.1 = bf16[704,2304]{1,0:T(8,128)(2,1)} custom-call(bf16[704,1152]{1,0:T(8,128)(2,1)} %g_ref.2, bf16[704,1152]{1,0:T(8,128)(2,1)} %u_ref.3, bf16[704,1152]{1,0:T(8,128)(2,1)} %c_ref.1), custom_call_target="tpu_custom_call" | custom-call | flops 99999997952 | bytes 1000 | tf_op jit(solution)/shard_map/deltas/pallas_call | solution.py:53
  32.1 4.7 %collective-permute-done.refs_3_ = bf16[144,2304]{1,0:T(8,128)(2,1)S(1)} collective-permute-done((bf16[144,2304]{1,0:T(8,128)(2,1)}, bf16[144,2304]{1,0:T(8,128)(2,1)S(1)}, u32[]{:S(2)}, u32[]{:S(2)}) %collective-permute-start) | collective-permute-done | bytes 663584 | tf_op jit(solution)/shard_map/ppermute | solution.py:25
  38.0 2.7 %collective-permute-start.6 = (bf16[144,2304]{1,0:T(8,128)(2,1)S(1)}, bf16[144,2304]{1,0:T(8,128)(2,1)S(1)}, u32[]{:S(2)}, u32[]{:S(2)}) collective-permute-start(bf16[144,2304]{1,0:T(8,128)(2,1)S(1)} %collective-permute-done.refs_3_), channel_id=1, source_target_pairs={{0,6},{2,0},{4,2},{6,4},{1,7},{3,1},{5,3},{7,5},{8,14},{10,8},{12,... | collective-permute-start | bytes 1990664 | tf_op jit(solution)/shard_map/ppermute | solution.py:25
  40.8 14.2 %collective-permute-done.6.refs_4_ = bf16[144,2304]{1,0:T(8,128)(2,1)S(1)} collective-permute-done((bf16[144,2304]{1,0:T(8,128)(2,1)S(1)}, bf16[144,2304]{1,0:T(8,128)(2,1)S(1)}, u32[]{:S(2)}, u32[]{:S(2)}) %collective-permute-start.6) | collective-permute-done | bytes 663584 | tf_op jit(solution)/shard_map/ppermute | solution.py:25
  55.0 3.5 %collective-permute-start.7 = (bf16[144,2304]{1,0:T(8,128)(2,1)S(1)}, bf16[144,2304]{1,0:T(8,128)(2,1)S(1)}, u32[]{:S(2)}, u32[]{:S(2)}) collective-permute-start(bf16[144,2304]{1,0:T(8,128)(2,1)S(1)} %collective-permute-done.6.refs_4_), channel_id=1, source_target_pairs={{0,6},{2,0},{4,2},{6,4},{1,7},{3,1},{5,3},{7,5},{8,14},{10,8},{12,... | collective-permute-start | bytes 1990664 | tf_op jit(solution)/shard_map/ppermute | solution.py:25
  58.6 2.6 %pad_maximum_fusion = bf16[8,2,88,2304]{3,2,1,0:T(8,128)(2,1)S(1)} fusion(bf16[8,1,88,2304]{3,2,1,0:T(8,128)(2,1)S(1)} %bitcast.28, bf16[8,1,88,2304]{3,2,1,0:T(8,128)(2,1)} %bitcast.27), kind=kLoop, calls=%fused_computation | loop fusion | flops 3244032 | bytes 12976128 | tf_op jit(solution)/shard_map/stack | solution.py:291
  61.2 8.9 %input_product_0.1.refs_2_ = bf16[1408,864]{1,0:T(8,128)(2,1)S(1)} custom-call(bf16[144,2304]{1,0:T(8,128)(2,1)S(1)} %copy-done.1, bf16[144,2304]{1,0:T(8,128)(2,1)S(1)} %collective-permute-done.2.refs_1_, bf16[144,2304]{1,0:T(8,128)(2,1)S(1)} %collective-permute-done.1.refs_2_, bf16[144,2304]{1,0:T(8,128)(2,1)S(1)} %collective-permute-done.refs_3_, ...), custom_call_target="tpu_custom_call" | custom-call | flops 1000 | bytes 1000 | tf_op jit(solution)/shard_map/input_product_0/pallas_call | solution.py:234
  70.1 2.3 %collective-permute-done.5.refs_0_ = bf16[144,2304]{1,0:T(8,128)(2,1)S(1)} collective-permute-done((bf16[144,2304]{1,0:T(8,128)(2,1)S(1)}, bf16[144,2304]{1,0:T(8,128)(2,1)S(1)}, u32[]{:S(2)}, u32[]{:S(2)}) %collective-permute-start.5) | collective-permute-done | bytes 663584 | tf_op jit(solution)/shard_map/ppermute | solution.py:25
  72.5 5.8 %input_product_864.1 = bf16[1408,1152]{1,0:T(8,128)(2,1)} custom-call(bf16[144,2304]{1,0:T(8,128)(2,1)S(1)} %collective-permute-done.5.refs_0_, bf16[144,2304]{1,0:T(8,128)(2,1)S(1)} %collective-permute-done.7.refs_1_, bf16[1408,864]{1,0:T(8,128)(2,1)S(1)} %input_product_0.1.refs_2_, bf16[1408,2304]{1,0:T(8,128)(2,1)S(1)} %bitcast.22), custom_call_target="tpu_custom_call" | custom-call | flops 1000 | bytes 1000 | tf_op jit(solution)/shard_map/input_product_864/pallas_call | solution.py:234
  78.3 6.4 %weight_product_0.1 = (bf16[144,2304]{1,0:T(8,128)(2,1)}, bf16[144,2304]{1,0:T(8,128)(2,1)}) custom-call(bf16[1408,1152]{1,0:T(8,128)(2,1)} %bitcast.25, bf16[1408,2304]{1,0:T(8,128)(2,1)} %bitcast.23), custom_call_target="tpu_custom_call" | custom-call | flops 1000 | bytes 1000 | tf_op jit(solution)/shard_map/weight_product_0/pallas_call | solution.py:183
  84.7 3.1 %collective-permute-start.13 = (bf16[144,2304]{1,0:T(8,128)(2,1)}, bf16[144,2304]{1,0:T(8,128)(2,1)}, u32[]{:S(2)}, u32[]{:S(2)}) collective-permute-start(bf16[144,2304]{1,0:T(8,128)(2,1)} %get-tuple-element.30.refs_1_), channel_id=1, source_target_pairs={{0,6},{2,0},{4,2},{6,4},{1,7},{3,1},{5,3},{7,5},{8,14},{10,8},{12,... | collective-permute-start | bytes 1990664 | tf_op jit(solution)/shard_map/ppermute | solution.py:25
  88.9 10.7 %weight_product_288.1 = (bf16[144,2304]{1,0:T(8,128)(2,1)}, bf16[144,2304]{1,0:T(8,128)(2,1)}, bf16[144,2304]{1,0:T(8,128)(2,1)}, bf16[144,2304]{1,0:T(8,128)(2,...) custom-call(bf16[1408,1152]{1,0:T(8,128)(2,1)} %bitcast.26, bf16[1408,2304]{1,0:T(8,128)(2,1)} %bitcast.24, ...), custom_call_target="tpu_custom_call" | custom-call | flops 99999997952 | bytes 1000 | tf_op jit(solution)/shard_map/weight_product_288/pallas_call | solution.py:183
  99.6 2.7 %collective-permute-start.15 = (bf16[144,2304]{1,0:T(8,128)(2,1)}, bf16[144,2304]{1,0:T(8,128)(2,1)S(1)}, u32[]{:S(2)}, u32[]{:S(2)}) collective-permute-start(bf16[144,2304]{1,0:T(8,128)(2,1)} %get-tuple-element.35), channel_id=1, source_target_pairs={{0,6},{2,0},{4,2},{6,4},{1,7},{3,1},{5,3},{7,5},{8,14},{10,8},{12,... | collective-permute-start | bytes 1990664 | tf_op jit(solution)/shard_map/ppermute | solution.py:25
  102.3 2.5 %collective-permute-done.16 = bf16[144,2304]{1,0:T(8,128)(2,1)S(1)} collective-permute-done((bf16[144,2304]{1,0:T(8,128)(2,1)S(1)}, bf16[144,2304]{1,0:T(8,128)(2,1)S(1)}, u32[]{:S(2)}, u32[]{:S(2)}) %collective-permute-start.16) | collective-permute-done | bytes 663584 | tf_op jit(solution)/shard_map/ppermute | solution.py:25
  107.5 2.7 %collective-permute-start.14 = (bf16[144,2304]{1,0:T(8,128)(2,1)S(1)}, bf16[144,2304]{1,0:T(8,128)(2,1)S(1)}, u32[]{:S(2)}, u32[]{:S(2)}) collective-permute-start(bf16[144,2304]{1,0:T(8,128)(2,1)S(1)} %add_convert_fusion.3), channel_id=1, source_target_pairs={{0,6},{2,0},{4,2},{6,4},{1,7},{3,1},{5,3},{7,5},{8,14},{10,8},{12,... | collective-permute-start | bytes 1990664 | tf_op jit(solution)/shard_map/ppermute | solution.py:25
  110.1 4.4 %collective-permute-done.15 = bf16[144,2304]{1,0:T(8,128)(2,1)S(1)} collective-permute-done((bf16[144,2304]{1,0:T(8,128)(2,1)}, bf16[144,2304]{1,0:T(8,128)(2,1)S(1)}, u32[]{:S(2)}, u32[]{:S(2)}) %collective-permute-start.15) | collective-permute-done | bytes 663584 | tf_op jit(solution)/shard_map/ppermute | solution.py:25
  114.5 18.5 %collective-permute-done.17 = bf16[144,2304]{1,0:T(8,128)(2,1)S(1)} collective-permute-done((bf16[144,2304]{1,0:T(8,128)(2,1)S(1)}, bf16[144,2304]{1,0:T(8,128)(2,1)S(1)}, u32[]{:S(2)}, u32[]{:S(2)}) %collective-permute-start.17) | collective-permute-done | bytes 663584 | tf_op jit(solution)/shard_map/ppermute | solution.py:25
  137.2 10.6 %collective-permute-done.18 = bf16[144,2304]{1,0:T(8,128)(2,1)S(1)} collective-permute-done((bf16[144,2304]{1,0:T(8,128)(2,1)}, bf16[144,2304]{1,0:T(8,128)(2,1)S(1)}, u32[]{:S(2)}, u32[]{:S(2)}) %collective-permute-start.18) | collective-permute-done | bytes 663584 | tf_op jit(solution)/shard_map/ppermute | solution.py:25
  148.2 5.0 %collective-permute-done.10 = bf16[2,44,1152]{2,1,0:T(8,128)(2,1)S(1)} collective-permute-done((bf16[2,44,1152]{2,1,0:T(8,128)(2,1)S(1)}, bf16[2,44,1152]{2,1,0:T(8,128)(2,1)S(1)}, u32[]{:S(2)}, u32[]{:S(2)}) %collective-permute-start.10) | collective-permute-done | bytes 202784 | tf_op jit(solution)/shard_map/ppermute | solution.py:25
  154.0 3.6 %collective-permute-start.11 = (bf16[44,1152]{1,0:T(8,128)(2,1)S(1)}, bf16[44,1152]{1,0:T(8,128)(2,1)S(1)}, u32[]{:S(2)}, u32[]{:S(2)}) collective-permute-start(bf16[44,1152]{1,0:T(8,128)(2,1)S(1)} %get-tuple-element.39), channel_id=1, source_target_pairs={{0,1},{1,0},{2,3},{3,2},{4,5},{5,4},{6,7},{7,6},{8,9},{9,8},{10,11... | collective-permute-start | bytes 304136 | tf_op jit(solution)/shard_map/ppermute | solution.py:25
  159.2 2.4 %join_columns.1 = bf16[44,2304]{1,0:T(8,128)(2,1)} custom-call(s32[4]{0:T(128)} %pad_add_fusion.s_ref, bf16[44,1152]{1,0:T(8,128)(2,1)} %get-tuple-element.40.mine_ref, bf16[44,1152]{1,0:T(8,128)(2,1)} %copy-done.6), custom_call_target="tpu_custom_call" | custom-call | flops 1000 | bytes 1000 | tf_op jit(solution)/shard_map/join_columns/pallas_call | solution.py:154
  (57 shorter events, 20.9 us)
Async XLA Ops:
  7.2 71.1 %all-gather.2.cloned.1.call-start = ((), (), s32[]{:S(2)}) async-start(), calls=%async_computation.2 | async-start | bytes 3649536 | tf_op jit(solution)/shard_map/all_gather | solution.py:287
  10.7 4.4 %collective-permute-start.3 = (bf16[44,1152]{1,0:T(8,128)(2,1)}, bf16[44,1152]{1,0:T(8,128)(2,1)S(1)}, u32[]{:S(2)}, u32[]{:S(2)}) collective-permute-start(bf16[44,1152]{1,0:T(8,128)(2,1)} %get-tuple-element.22), channel_id=1, source_target_pairs={{0,1},{1,0},{2,3},{3,2},{4,5},{5,4},{6,7},{7,6},{8,9},{9,8},{10,11... | collective-permute-start | bytes 304136 | tf_op jit(solution)/shard_map/ppermute | solution.py:25
  16.0 8.2 %collective-permute-start.4 = (bf16[2,44,1152]{2,1,0:T(8,128)(2,1)S(1)}, bf16[2,44,1152]{2,1,0:T(8,128)(2,1)S(1)}, u32[]{:S(2)}, u32[]{:S(2)}) collective-permute-start(bf16[2,44,1152]{2,1,0:T(8,128)(2,1)S(1)} %pad_maximum_fusion.1), channel_id=1, source_target_pairs={{0,16},{16,0},{1,17},{17,1},{2,18},{18,2},{3,19},{19,3},{4,20},{20... | collective-permute-start | bytes 608264 | tf_op jit(solution)/shard_map/ppermute | solution.py:25
  17.1 19.7 %collective-permute-start = (bf16[144,2304]{1,0:T(8,128)(2,1)}, bf16[144,2304]{1,0:T(8,128)(2,1)S(1)}, u32[]{:S(2)}, u32[]{:S(2)}) collective-permute-start(bf16[144,2304]{1,0:T(8,128)(2,1)} %get-tuple-element.20.refs_0_), channel_id=1, source_target_pairs={{0,8},{8,0},{1,9},{9,1},{2,10},{10,2},{3,11},{11,3},{4,12},{12,4},... | collective-permute-start | bytes 1990664 | tf_op jit(solution)/shard_map/ppermute | solution.py:25
  17.4 19.4 %collective-permute-start.1 = (bf16[144,2304]{1,0:T(8,128)(2,1)}, bf16[144,2304]{1,0:T(8,128)(2,1)S(1)}, u32[]{:S(2)}, u32[]{:S(2)}) collective-permute-start(bf16[144,2304]{1,0:T(8,128)(2,1)} %get-tuple-element.20.refs_0_), channel_id=1, source_target_pairs={{0,2},{2,4},{4,6},{6,0},{1,3},{3,5},{5,7},{7,1},{8,10},{10,12},{12... | collective-permute-start | bytes 1990664 | tf_op jit(solution)/shard_map/ppermute | solution.py:25
  18.7 18.1 %collective-permute-start.2 = (bf16[144,2304]{1,0:T(8,128)(2,1)}, bf16[144,2304]{1,0:T(8,128)(2,1)S(1)}, u32[]{:S(2)}, u32[]{:S(2)}) collective-permute-start(bf16[144,2304]{1,0:T(8,128)(2,1)} %get-tuple-element.20.refs_0_), channel_id=1, source_target_pairs={{0,6},{2,0},{4,2},{6,4},{1,7},{3,1},{5,3},{7,5},{8,14},{10,8},{12,... | collective-permute-start | bytes 1990664 | tf_op jit(solution)/shard_map/ppermute | solution.py:25
  26.2 109.1 %reduce-scatter.2.cloned.1.call-start = ((), (), s32[]{:S(2)}) async-start(), calls=%async_computation.1 | async-start | bytes 3649536 | tf_op jit(solution)/shard_map/reduce_scatter | solution.py:296
  36.8 21.8 %collective-permute-start.9 = (bf16[704,2304]{1,0:T(8,128)(2,1)}, bf16[704,2304]{1,0:T(8,128)(2,1)S(1)}, u32[]{:S(2)}, u32[]{:S(2)}) collective-permute-start(bf16[704,2304]{1,0:T(8,128)(2,1)} %deltas.1), channel_id=1, source_target_pairs={{0,1},{1,0},{2,3},{3,2},{4,5},{5,4},{6,7},{7,6},{8,9},{9,8},{10,11... | collective-permute-start | bytes 9732104 | tf_op jit(solution)/shard_map/ppermute | solution.py:25
  38.0 17.0 %collective-permute-start.6 = (bf16[144,2304]{1,0:T(8,128)(2,1)S(1)}, bf16[144,2304]{1,0:T(8,128)(2,1)S(1)}, u32[]{:S(2)}, u32[]{:S(2)}) collective-permute-start(bf16[144,2304]{1,0:T(8,128)(2,1)S(1)} %collective-permute-done.refs_3_), channel_id=1, source_target_pairs={{0,6},{2,0},{4,2},{6,4},{1,7},{3,1},{5,3},{7,5},{8,14},{10,8},{12,... | collective-permute-start | bytes 1990664 | tf_op jit(solution)/shard_map/ppermute | solution.py:25
  40.8 20.5 %collective-permute-start.8 = (bf16[144,2304]{1,0:T(8,128)(2,1)S(1)}, bf16[144,2304]{1,0:T(8,128)(2,1)S(1)}, u32[]{:S(2)}, u32[]{:S(2)}) collective-permute-start(bf16[144,2304]{1,0:T(8,128)(2,1)S(1)} %collective-permute-done.refs_3_), channel_id=1, source_target_pairs={{0,2},{2,4},{4,6},{6,0},{1,3},{3,5},{5,7},{7,1},{8,10},{10,12},{12... | collective-permute-start | bytes 1990664 | tf_op jit(solution)/shard_map/ppermute | solution.py:25
  40.8 31.7 %collective-permute-start.5 = (bf16[144,2304]{1,0:T(8,128)(2,1)S(1)}, bf16[144,2304]{1,0:T(8,128)(2,1)S(1)}, u32[]{:S(2)}, u32[]{:S(2)}) collective-permute-start(bf16[144,2304]{1,0:T(8,128)(2,1)S(1)} %collective-permute-done.1.refs_2_), channel_id=1, source_target_pairs={{0,2},{2,4},{4,6},{6,0},{1,3},{3,5},{5,7},{7,1},{8,10},{10,12},{12... | collective-permute-start | bytes 1990664 | tf_op jit(solution)/shard_map/ppermute | solution.py:25
  55.0 17.4 %collective-permute-start.7 = (bf16[144,2304]{1,0:T(8,128)(2,1)S(1)}, bf16[144,2304]{1,0:T(8,128)(2,1)S(1)}, u32[]{:S(2)}, u32[]{:S(2)}) collective-permute-start(bf16[144,2304]{1,0:T(8,128)(2,1)S(1)} %collective-permute-done.6.refs_4_), channel_id=1, source_target_pairs={{0,6},{2,0},{4,2},{6,4},{1,7},{3,1},{5,3},{7,5},{8,14},{10,8},{12,... | collective-permute-start | bytes 1990664 | tf_op jit(solution)/shard_map/ppermute | solution.py:25
  61.2 11.2 %copy-start = (bf16[8,2,88,2304]{3,2,1,0:T(8,128)(2,1)}, bf16[8,2,88,2304]{3,2,1,0:T(8,128)(2,1)S(1)}, u32[]{:S(2)}) copy-start(bf16[8,2,88,2304]{3,2,1,0:T(8,128)(2,1)S(1)} %pad_maximum_fusion) | copy-start | bytes 19464196
  84.7 21.4 %collective-permute-start.13 = (bf16[144,2304]{1,0:T(8,128)(2,1)}, bf16[144,2304]{1,0:T(8,128)(2,1)}, u32[]{:S(2)}, u32[]{:S(2)}) collective-permute-start(bf16[144,2304]{1,0:T(8,128)(2,1)} %get-tuple-element.30.refs_1_), channel_id=1, source_target_pairs={{0,6},{2,0},{4,2},{6,4},{1,7},{3,1},{5,3},{7,5},{8,14},{10,8},{12,... | collective-permute-start | bytes 1990664 | tf_op jit(solution)/shard_map/ppermute | solution.py:25
  88.9 15.9 %collective-permute-start.16 = (bf16[144,2304]{1,0:T(8,128)(2,1)S(1)}, bf16[144,2304]{1,0:T(8,128)(2,1)S(1)}, u32[]{:S(2)}, u32[]{:S(2)}) collective-permute-start(bf16[144,2304]{1,0:T(8,128)(2,1)S(1)} %copy-done.7), channel_id=1, source_target_pairs={{0,2},{2,4},{4,6},{6,0},{1,3},{3,5},{5,7},{7,1},{8,10},{10,12},{12... | collective-permute-start | bytes 1990664 | tf_op jit(solution)/shard_map/ppermute | solution.py:25
  99.6 14.9 %collective-permute-start.15 = (bf16[144,2304]{1,0:T(8,128)(2,1)}, bf16[144,2304]{1,0:T(8,128)(2,1)S(1)}, u32[]{:S(2)}, u32[]{:S(2)}) collective-permute-start(bf16[144,2304]{1,0:T(8,128)(2,1)} %get-tuple-element.35), channel_id=1, source_target_pairs={{0,6},{2,0},{4,2},{6,4},{1,7},{3,1},{5,3},{7,5},{8,14},{10,8},{12,... | collective-permute-start | bytes 1990664 | tf_op jit(solution)/shard_map/ppermute | solution.py:25
  102.3 34.9 %collective-permute-start.12 = (bf16[144,2304]{1,0:T(8,128)(2,1)}, bf16[144,2304]{1,0:T(8,128)(2,1)S(1)}, u32[]{:S(2)}, u32[]{:S(2)}) collective-permute-start(bf16[144,2304]{1,0:T(8,128)(2,1)} %get-tuple-element.32), channel_id=1, source_target_pairs={{0,2},{2,4},{4,6},{6,0},{1,3},{3,5},{5,7},{7,1},{8,10},{10,12},{12... | collective-permute-start | bytes 1990664 | tf_op jit(solution)/shard_map/ppermute | solution.py:25
  106.0 27.0 %copy-start.4 = (bf16[144,2304]{1,0:T(8,128)(2,1)S(1)}, bf16[144,2304]{1,0:T(8,128)(2,1)}, u32[]{:S(2)}) copy-start(bf16[144,2304]{1,0:T(8,128)(2,1)} %get-tuple-element.34) | copy-start | bytes 1990660
  106.0 27.0 %collective-permute-start.17 = (bf16[144,2304]{1,0:T(8,128)(2,1)S(1)}, bf16[144,2304]{1,0:T(8,128)(2,1)S(1)}, u32[]{:S(2)}, u32[]{:S(2)}) collective-permute-start(bf16[144,2304]{1,0:T(8,128)(2,1)S(1)} %add_convert_fusion.2), channel_id=1, source_target_pairs={{0,2},{2,4},{4,6},{6,0},{1,3},{3,5},{5,7},{7,1},{8,10},{10,12},{12... | collective-permute-start | bytes 1990664 | tf_op jit(solution)/shard_map/ppermute | solution.py:25
  107.5 29.7 %collective-permute-start.14 = (bf16[144,2304]{1,0:T(8,128)(2,1)S(1)}, bf16[144,2304]{1,0:T(8,128)(2,1)S(1)}, u32[]{:S(2)}, u32[]{:S(2)}) collective-permute-start(bf16[144,2304]{1,0:T(8,128)(2,1)S(1)} %add_convert_fusion.3), channel_id=1, source_target_pairs={{0,6},{2,0},{4,2},{6,4},{1,7},{3,1},{5,3},{7,5},{8,14},{10,8},{12,... | collective-permute-start | bytes 1990664 | tf_op jit(solution)/shard_map/ppermute | solution.py:25
  133.0 14.8 %copy-start.3 = (bf16[144,2304]{1,0:T(8,128)(2,1)S(1)}, bf16[144,2304]{1,0:T(8,128)(2,1)}, u32[]{:S(2)}) copy-start(bf16[144,2304]{1,0:T(8,128)(2,1)} %get-tuple-element.31) | copy-start | bytes 1990660
  134.1 13.8 %collective-permute-start.18 = (bf16[144,2304]{1,0:T(8,128)(2,1)}, bf16[144,2304]{1,0:T(8,128)(2,1)S(1)}, u32[]{:S(2)}, u32[]{:S(2)}) collective-permute-start(bf16[144,2304]{1,0:T(8,128)(2,1)} %add_convert_fusion.1), channel_id=1, source_target_pairs={{0,8},{8,0},{1,9},{9,1},{2,10},{10,2},{3,11},{11,3},{4,12},{12,4},... | collective-permute-start | bytes 1990664 | tf_op jit(solution)/shard_map/ppermute | solution.py:25
  136.4 16.8 %collective-permute-start.10 = (bf16[2,44,1152]{2,1,0:T(8,128)(2,1)S(1)}, bf16[2,44,1152]{2,1,0:T(8,128)(2,1)S(1)}, u32[]{:S(2)}, u32[]{:S(2)}) collective-permute-start(bf16[2,44,1152]{2,1,0:T(8,128)(2,1)S(1)} %broadcast_select_fusion), channel_id=1, source_target_pairs={{0,16},{16,0},{1,17},{17,1},{2,18},{18,2},{3,19},{19,3},{4,20},{20... | collective-permute-start | bytes 608264 | tf_op jit(solution)/shard_map/ppermute | solution.py:25
  154.0 4.6 %collective-permute-start.11 = (bf16[44,1152]{1,0:T(8,128)(2,1)S(1)}, bf16[44,1152]{1,0:T(8,128)(2,1)S(1)}, u32[]{:S(2)}, u32[]{:S(2)}) collective-permute-start(bf16[44,1152]{1,0:T(8,128)(2,1)S(1)} %get-tuple-element.39), channel_id=1, source_target_pairs={{0,1},{1,0},{2,3},{3,2},{4,5},{5,4},{6,7},{7,6},{8,9},{9,8},{10,11... | collective-permute-start | bytes 304136 | tf_op jit(solution)/shard_map/ppermute | solution.py:25
  (5 other events, 16.3 us)
Sparse Core Ops, SparseCore 0:
  26.3 48.4 all-gather.1
  78.4 48.4 reduce-scatter.1

commit v5 on v4

--- a/solution.py
+++ b/solution.py
@@ -79,7 +79,7 @@
     )(*after)
 
 
-INPUT_ORDER = ((0, 0), (0, 1), (0, 3), (1, 0), (1, 1), (1, 3), (0, 2), (1, 2))
+INPUT_ORDER = ((0, 0), (0, 1), (0, 3), (0, 2), (1, 0), (1, 1), (1, 3), (1, 2))
 TOKEN_ORDER = ((1, 2), (0, 2), (1, 1), (1, 3), (0, 1), (0, 3), (1, 0), (0, 0))
 
 
@@ -128,12 +128,12 @@
     )(place, tokens, gate, up)
 
 
-def join_body(s_ref, mine_ref, other_ref, out_ref):
+def join_body(s_ref, m0_ref, m1_ref, o0_ref, o1_ref, out_ref):
     x_lo, y, core = s_ref[0], s_ref[1], s_ref[2]
-    n = mine_ref.shape[1] // 8
-
-    def plain(ref):
-        x = ref[...].astype(F32)
+    n = m0_ref.shape[1] // 8
+
+    def plain(first, second):
+        x = first[...].astype(F32) + second[...].astype(F32)
         at = {owner: x[:, j * n : (j + 1) * n] for j, owner in enumerate(INPUT_ORDER)}
         near = roll_blocks([at[0, dy] for dy in range(4)], y, -1)
         far = roll_blocks([at[1, dy] for dy in range(4)], y, -1)
@@ -141,7 +141,7 @@
         high = [jnp.where(x_lo == 0, far[i], near[i]) for i in range(4)]
         return low + high
 
-    mine, other = plain(mine_ref), plain(other_ref)
+    mine, other = plain(m0_ref, m1_ref), plain(o0_ref, o1_ref)
     for j in range(8):
         out_ref[:, 2 * j * n : (2 * j + 1) * n] = jnp.where(core == 0, mine[j], other[j]).astype(BF)
         out_ref[:, (2 * j + 1) * n : (2 * j + 2) * n] = jnp.where(
@@ -149,16 +149,16 @@
         ).astype(BF)
 
 
-def join_columns(place, mine, other):
-    rows, cols = mine.shape
+def join_columns(place, *parts):
+    rows, cols = parts[0].shape
     return pl.pallas_call(
         join_body,
         out_shape=jax.ShapeDtypeStruct((rows, 2 * cols), BF),
-        in_specs=[IN_SMEM, IN_VMEM, IN_VMEM],
+        in_specs=[IN_SMEM] + [IN_VMEM] * 4,
         out_specs=IN_VMEM,
         cost_estimate=SMALL,
         name="join_columns",
-    )(place, mine, other)
+    )(place, *parts)
 
 
 def weight_body(scale, start, skip, extra, x_ref, d_ref, *refs):
@@ -172,6 +172,59 @@
     )
     for i, out_ref in enumerate(out_refs):
         out_ref[...] = (acc[skip + i * n : skip + (i + 1) * n] * scale).astype(BF)
+
+
+def first_body(scale, x_ref, d_ref, *out_refs):
+    n = out_refs[0].shape[0]
+    acc = lax.dot_general(
+        x_ref[:, : n * len(out_refs) // 2],
+        d_ref[...],
+        (((0,), (0,)), ((), ())),
+        preferred_element_type=F32,
+    )
+    for half in range(2):
+
+        @pl.when(pl.program_id(0) == half)
+        def _():
+            for i, out_ref in enumerate(out_refs[half::2]):
+                out_ref[...] = (acc[i * n : (i + 1) * n] * scale).astype(BF)
+
+
+def first_product(x, delta, scale, n):
+    rows = x.shape[0]
+    half = delta.shape[1] // 2
+    return pl.pallas_call(
+        functools.partial(first_body, scale),
+        out_shape=[jax.ShapeDtypeStruct((n, half), BF)] * 4,
+        grid=(2,),
+        in_specs=[
+            pl.BlockSpec((rows, -(-2 * n // 128) * 128), lambda i: (0, 0)),
+            pl.BlockSpec((rows, half), lambda i: (0, i)),
+        ],
+        out_specs=[pl.BlockSpec((n, half), lambda i: (0, 0))] * 4,
+        compiler_params=pltpu.CompilerParams(vmem_limit_bytes=VMEM_LIMIT),
+        cost_estimate=SMALL,
+        name="first_product",
+    )(x, delta)
+
+
+def merge_body(up_ref, right_ref, down_ref, left_ref, up_out, down_out):
+    half = right_ref.shape[1]
+    up_out[:, :half] = (up_ref[:, :half].astype(F32) + right_ref[...].astype(F32)).astype(BF)
+    up_out[:, half:] = up_ref[:, half:]
+    down_out[:, :half] = down_ref[:, :half]
+    down_out[:, half:] = (down_ref[:, half:].astype(F32) + left_ref[...].astype(F32)).astype(BF)
+
+
+def merge(up, right, down, left):
+    return pl.pallas_call(
+        merge_body,
+        out_shape=[jax.ShapeDtypeStruct(up.shape, BF)] * 2,
+        in_specs=[IN_VMEM] * 4,
+        out_specs=[IN_VMEM] * 2,
+        cost_estimate=SMALL,
+        name="merge",
+    )(up, right, down, left)
 
 
 def weight_product(x, delta, scale, first, count, n, cost, after=None, tile=768):
@@ -201,12 +254,17 @@
 def input_body(n, done, *refs):
     blocks, refs = refs[:n], refs[n:]
     (d_ref, out_ref, w, sems), extra = refs[-4:], refs[:-4]
-    size = blocks[0].shape[0]
+    size, width = blocks[0].shape
+    across = w.shape[1] // width
 
     @pl.when(pl.program_id(0) == 0)
     def _():
         copies = [
-            pltpu.make_async_copy(b, w.at[pl.ds(i * size, size)], sems.at[i])
+            pltpu.make_async_copy(
+                b,
+                w.at[pl.ds(i // across * size, size), pl.ds(i % across * width, width)],
+                sems.at[i],
+            )
             for i, b in enumerate(blocks)
         ]
         for c in copies:
@@ -225,7 +283,7 @@
     rows, cols = delta.shape
     n = len(blocks)
     done = after.shape[1] if after.shape[0] == rows else 0
-    size = n * blocks[0].shape[0]
+    size = n * blocks[0].size // cols
     d = done + size
     if done:
         extra = pl.BlockSpec((tile, done), lambda i: (i, 0))
@@ -248,24 +306,26 @@
 
 
 def gather_weights(w, after):
-    far = shift(w, "x_lo", 1)
-    below, above = shift(w, "y", 1), shift(w, "y", -1)
+    half = w.shape[1] // 2
+    far, below, above = shift(w, "x_lo", 1), shift(w, "y", 1), shift(w, "y", -1)
     far, below, above, after = lax.optimization_barrier((far, below, above, after))
-    far_below, far_above = shift(far, "y", 1), shift(far, "y", -1)
-    across, far_across = shift(below, "y", 1), shift(far_above, "y", -1)
-    return [w, above, below, far, far_above, far_below], [across, far_across], after
+    far_below, far_above = shift(below, "x_lo", 1), shift(far, "y", -1)
+    across = shift(below, "y", 1)
+    last = [shift(far_below[:, :half], "y", 1), shift(far_above[:, half:], "y", -1)]
+    return [w, above, below, across, far, far_above, far_below], last, after
 
 
 def scatter_grads(first, rest):
     far_up, far_down, up, down, far_own, own = rest
-    far_right = shift(first[0], "y", 1)
-    left = shift(first[1], "y", -1)
-    far_left = shift(far_down, "y", -1)
-    far_right = shift(add(far_up, far_right), "y", 1)
-    right = shift(up, "y", 1)
-    left = shift(add(down, left), "y", -1)
+    far_right, far_left = shift(first[0], "y", 1), shift(first[1], "y", -1)
+    right, left = shift(first[2], "y", 1), shift(first[3], "y", -1)
+    far_up, far_down = merge(far_up, far_right, far_down, far_left)
+    far_right, far_left = shift(far_up, "y", 1), shift(far_down, "y", -1)
+    up, down = merge(up, right, down, left)
+    up, down, far_right, far_left = lax.optimization_barrier((up, down, far_right, far_left))
     far_own = shift(add(far_own, far_left, far_right), "x_lo", 1)
-    return add(own, right, left, far_own)
+    right, left = shift(up, "y", 1), shift(down, "y", -1)
+    return own, right, left, far_own
 
 
 def per_device(tokens, gate_pre, up_pre, cotangent, gate_weight, up_weight):
@@ -295,17 +355,24 @@
     part = input_product(delta, late, part, 1e3)
     sums = lax.psum_scatter(part, "z", scatter_dimension=0, tiled=True)
 
-    first = weight_product(x, delta, scale, 0, 2 * owned, owned, 1e3)
+    first = first_product(x, delta, scale, owned)
     rest = weight_product(
         x, delta, scale, 2 * owned, 6 * owned, owned, REST_FLOPS, mark("sent", *first)
     )
-    grads = scatter_grads(first, rest)
-
-    sums = sums.reshape(2, 2 * rows, -1)
-    low, high = sums[:, :rows], sums[:, rows:]
-    sent = shift(jnp.where(x_hi == 0, high, low), "x_hi", 1)
-    sums = add(jnp.where(x_hi == 0, low, high), sent)
-    input_grad = join_columns(place, sums[0], shift(sums[1], "core", 1))
+    own, *terms = scatter_grads(first, rest)
+
+    sums = sums.reshape(2, 2, rows, -1)
+    here = jnp.where(x_hi == 0, sums[:, 0], sums[:, 1])
+    there = jnp.where(x_hi == 0, sums[:, 1], sums[:, 0])
+    input_grad = join_columns(
+        place,
+        here[0],
+        shift(there[0], "x_hi", 1),
+        shift(here[1], "core", 1),
+        lax.ppermute(there[1], ("x_hi", "core"), [(i, 3 - i) for i in range(4)]),
+    )
+    input_grad, own = lax.optimization_barrier((input_grad, own))
+    grads = add(own, *terms)
     return input_grad, grads[:, :hidden], grads[:, hidden:]
 
 

time: 169 us -> 164 us (0.970)
  waiting for transfers between devices: 67.7 us -> 49.9 us
  starting transfers between devices: 29.1 us -> 38.3 us
  Pallas kernels: 43.5 us -> 47.5 us
  other arithmetic: 11.3 us -> 7.56 us
    ppermute x19 -> x22, waiting for transfers between devices: 67.6 us -> 47.3 us  [shift(): return lax.ppermute(x, axis, [(i, (i + k) % n) for i in range(n)])]
    pallas_call x0 -> x3, Pallas kernels: none -> 11.8 us  [the longest x1 6.29 us: first_product(): pl.pallas_call(functools.partial(first_body, scale), out_shape=[jax.Shape...]
    pallas_call x2 -> x1, Pallas kernels: 17.1 us -> 10.8 us  [weight_product(): pl.pallas_call(functools.partial(weight_body, scale, start, first - start...]
    ppermute x19 -> x22, starting transfers between devices: 29 us -> 35.2 us  [shift(): return lax.ppermute(x, axis, [(i, (i + k) % n) for i in range(n)])]
    ppermute x0 -> x1, starting transfers between devices: none -> 3.09 us  [per_device(): lax.ppermute(there[1], ('x_hi', 'core'), [(i, 3 - i) for i in range(4)])]
    convert_element_type x5 -> x2, other arithmetic: 4.12 us -> 1.46 us  [add(): return total.astype(BF)]
    ppermute x0 -> x1, waiting for transfers between devices: none -> 2.58 us  [per_device(): lax.ppermute(there[1], ('x_hi', 'core'), [(i, 3 - i) for i in range(4)])]
  transfers between devices with their start and end apart: 21 -> 25, of which waited for: 11 -> 7; matrix products, arithmetic and copies ran while one was open for 6% -> 5% of each run, Pallas kernels for 23% -> 28%
where the time goes in v5:
time: 164 us; the launch traced here: 162 us
  waiting for transfers between devices  49.9 us (30%)
  Pallas kernels  47.5 us (29%)
  starting transfers between devices  38.3 us (23%)
  between operations  14.2 us (9%)
  other arithmetic  7.56 us (5%)
  local copies, waits for them, and re-layouts  4.2 us (3%)
    ppermute x22, waiting for transfers between devices, shift(): return lax.ppermute(x, axis, [(i, (i + k) % n) for i in range(n)])  47.3 us
    ppermute x22, starting transfers between devices, shift(): return lax.ppermute(x, axis, [(i, (i + k) % n) for i in range(n)])  35.2 us
    pallas_call x2, Pallas kernels, input_product(): pl.pallas_call(functools.partial(input_body, n, done), out_shape=jax.Shap...  13.1 us
    pallas_call x1, Pallas kernels, weight_product(): pl.pallas_call(functools.partial(weight_body, scale, start, first - start...  10.8 us
    pallas_call x1, Pallas kernels, first_product(): pl.pallas_call(functools.partial(first_body, scale), out_shape=[jax.Shape...  6.29 us
    pallas_call x1, Pallas kernels, make_deltas(): pl.pallas_call(delta_body, out_shape=jax.ShapeDtypeStruct((rows, 2 * cols...  5.9 us
    pallas_call x2, Pallas kernels, merge(): pl.pallas_call(merge_body, out_shape=[jax.ShapeDtypeStruct(up.shape, BF)]...  5.49 us
  transfers between devices with their start and end apart: 25, of which 7 were waited for; matrix products, arithmetic and copies ran while one was open for 5% of the time, Pallas kernels for 28%

profile of v5, /device:TPU:1, one launch (start us, length us, event | category | flops | bytes accessed | tf_op | source)
XLA Modules:
  0.0 161.7 jit_solution(17462664008599400666)
XLA Ops:
  7.8 2.8 %prologue.1 = (bf16[44,1152]{1,0:T(8,128)(2,1)}, bf16[44,1152]{1,0:T(8,128)(2,1)}, bf16[144,2304]{1,0:T(8,128)(2,1)}) custom-call(s32[4]{0:T(128)} %pad_add_fusion.s_ref, bf16[44,2304]{1,0:T(8,128)(2,1)} %x_ref.1, bf16[144,1152]{1,0:T(8,128)(2,1)} %g_ref.1, bf16[144,1152]{1,0:T(8,128)(2,1)} %u_ref.2), custom_call_target="tpu_custom_call" | custom-call | flops 1000 | bytes 1000 | tf_op jit(solution)/shard_map/prologue/pallas_call | solution.py:117
  10.7 3.2 %collective-permute-start.3 = (bf16[44,1152]{1,0:T(8,128)(2,1)}, bf16[44,1152]{1,0:T(8,128)(2,1)S(1)}, u32[]{:S(2)}, u32[]{:S(2)}) collective-permute-start(bf16[44,1152]{1,0:T(8,128)(2,1)} %get-tuple-element.34), channel_id=1, source_target_pairs={{0,1},{1,0},{2,3},{3,2},{4,5},{5,4},{6,7},{7,6},{8,9},{9,8},{10,11... | collective-permute-start | bytes 304136 | tf_op jit(solution)/shard_map/ppermute | solution.py:25
  20.1 4.1 %collective-permute-done.4 = bf16[2,44,1152]{2,1,0:T(8,128)(2,1)S(1)} collective-permute-done((bf16[2,44,1152]{2,1,0:T(8,128)(2,1)S(1)}, bf16[2,44,1152]{2,1,0:T(8,128)(2,1)S(1)}, u32[]{:S(2)}, u32[]{:S(2)}) %collective-permute-start.4) | collective-permute-done | bytes 202784 | tf_op jit(solution)/shard_map/ppermute | solution.py:25
  26.2 5.9 %deltas.1 = bf16[704,2304]{1,0:T(8,128)(2,1)} custom-call(bf16[704,1152]{1,0:T(8,128)(2,1)} %g_ref.2, bf16[704,1152]{1,0:T(8,128)(2,1)} %u_ref.3, bf16[704,1152]{1,0:T(8,128)(2,1)} %c_ref.1), custom_call_target="tpu_custom_call" | custom-call | flops 99999997952 | bytes 1000 | tf_op jit(solution)/shard_map/deltas/pallas_call | solution.py:53
  32.1 4.7 %collective-permute-done.refs_4_ = bf16[144,2304]{1,0:T(8,128)(2,1)S(1)} collective-permute-done((bf16[144,2304]{1,0:T(8,128)(2,1)}, bf16[144,2304]{1,0:T(8,128)(2,1)S(1)}, u32[]{:S(2)}, u32[]{:S(2)}) %collective-permute-start) | collective-permute-done | bytes 663584 | tf_op jit(solution)/shard_map/ppermute | solution.py:25
  39.2 2.7 %collective-permute-start.7 = (bf16[144,2304]{1,0:T(8,128)(2,1)S(1)}, bf16[144,2304]{1,0:T(8,128)(2,1)S(1)}, u32[]{:S(2)}, u32[]{:S(2)}) collective-permute-start(bf16[144,2304]{1,0:T(8,128)(2,1)S(1)} %collective-permute-done.refs_4_), channel_id=1, source_target_pairs={{0,6},{2,0},{4,2},{6,4},{1,7},{3,1},{5,3},{7,5},{8,14},{10,8},{12,... | collective-permute-start | bytes 1990664 | tf_op jit(solution)/shard_map/ppermute | solution.py:25
  42.0 12.6 %collective-permute-done.5.refs_6_ = bf16[144,2304]{1,0:T(8,128)(2,1)S(1)} collective-permute-done((bf16[144,2304]{1,0:T(8,128)(2,1)S(1)}, bf16[144,2304]{1,0:T(8,128)(2,1)S(1)}, u32[]{:S(2)}, u32[]{:S(2)}) %collective-permute-start.5) | collective-permute-done | bytes 663584 | tf_op jit(solution)/shard_map/ppermute | solution.py:25
  56.0 3.6 %collective-permute-start.8 = (bf16[144,1152]{1,0:T(8,128)(2,1)S(1)}, bf16[144,1152]{1,0:T(8,128)(2,1)S(1)}, u32[]{:S(2)}, u32[]{:S(2)}) collective-permute-start(bf16[144,1152]{1,0:T(8,128)(2,1)S(1)} %slice.47), channel_id=1, source_target_pairs={{0,6},{2,0},{4,2},{6,4},{1,7},{3,1},{5,3},{7,5},{8,14},{10,8},{12,... | collective-permute-start | bytes 995336 | tf_op jit(solution)/shard_map/ppermute | solution.py:25
  59.7 2.6 %pad_maximum_fusion = bf16[8,2,88,2304]{3,2,1,0:T(8,128)(2,1)S(1)} fusion(bf16[8,1,88,2304]{3,2,1,0:T(8,128)(2,1)S(1)} %bitcast.31, bf16[8,1,88,2304]{3,2,1,0:T(8,128)(2,1)} %bitcast.30), kind=kLoop, calls=%fused_computation | loop fusion | flops 3244032 | bytes 12976128 | tf_op jit(solution)/shard_map/stack | solution.py:351
  62.3 9.1 %input_product_0.1.refs_2_ = bf16[1408,1008]{1,0:T(8,128)(2,1)S(1)} custom-call(bf16[144,2304]{1,0:T(8,128)(2,1)S(1)} %copy-done.1, bf16[144,2304]{1,0:T(8,128)(2,1)S(1)} %collective-permute-done.2.refs_1_, bf16[144,2304]{1,0:T(8,128)(2,1)S(1)} %collective-permute-done.1.refs_2_, bf16[144,2304]{1,0:T(8,128)(2,1)S(1)} %collective-permute-done.9.refs_3_, ...), custom_call_target="tpu_custom_call" | custom-call | flops 1000 | bytes 1000 | tf_op jit(solution)/shard_map/input_product_0/pallas_call | solution.py:292
  71.4 4.0 %input_product_1008.1 = bf16[1408,1152]{1,0:T(8,128)(2,1)} custom-call(bf16[144,1152]{1,0:T(8,128)(2,1)S(1)} %collective-permute-done.6.refs_0_, bf16[144,1152]{1,0:T(8,128)(2,1)S(1)} %collective-permute-done.8.refs_1_, bf16[1408,1008]{1,0:T(8,128)(2,1)S(1)} %input_product_0.1.refs_2_, bf16[1408,2304]{1,0:T(8,128)(2,1)S(1)} %bitcast.25), custom_call_target="tpu_custom_call" | custom-call | flops 1000 | bytes 1000 | tf_op jit(solution)/shard_map/input_product_1008/pallas_call | solution.py:292
  75.5 6.3 %first_product.1 = (bf16[144,1152]{1,0:T(8,128)(2,1)}, bf16[144,1152]{1,0:T(8,128)(2,1)}, bf16[144,1152]{1,0:T(8,128)(2,1)}, bf16[144,1152]{1,0:T(8,128)(2,1)}) custom-call(bf16[1408,1152]{1,0:T(8,128)(2,1)} %bitcast.28, bf16[1408,2304]{1,0:T(8,128)(2,1)} %bitcast.26), custom_call_target="tpu_custom_call" | custom-call | flops 1000 | bytes 1000 | tf_op jit(solution)/shard_map/first_product/pallas_call | solution.py:196
  85.0 10.8 %weight_product_288.1 = (bf16[144,2304]{1,0:T(8,128)(2,1)}, bf16[144,2304]{1,0:T(8,128)(2,1)}, bf16[144,2304]{1,0:T(8,128)(2,1)}, bf16[144,2304]{1,0:T(8,128)(2,...) custom-call(bf16[1408,1152]{1,0:T(8,128)(2,1)} %bitcast.29, bf16[1408,2304]{1,0:T(8,128)(2,1)} %bitcast.27, ...), custom_call_target="tpu_custom_call" | custom-call | flops 99999997952 | bytes 1000 | tf_op jit(solution)/shard_map/weight_product_288/pallas_call | solution.py:236
  95.8 2.8 %merge.3 = (bf16[144,2304]{1,0:T(8,128)(2,1)}, bf16[144,2304]{1,0:T(8,128)(2,1)}) custom-call(bf16[144,2304]{1,0:T(8,128)(2,1)} %get-tuple-element.52.up_ref, bf16[144,1152]{1,0:T(8,128)(2,1)} %collective-permute-done.16.right_ref, bf16[144,2304]{1,0:T(8,128)(2,1)} %get-tuple-element.53.down_ref, bf16[144,1152]{1,0:T(8,128)(2,1)} %collective-permute-done.17.left_ref), custom_call_target="tpu_custom_call" | custom-call | flops 1000 | bytes 1000 | tf_op jit(solution)/shard_map/merge/pallas_call | solution.py:220
  98.7 2.7 %collective-permute-start.19 = (bf16[144,2304]{1,0:T(8,128)(2,1)}, bf16[144,2304]{1,0:T(8,128)(2,1)S(1)}, u32[]{:S(2)}, u32[]{:S(2)}) collective-permute-start(bf16[144,2304]{1,0:T(8,128)(2,1)} %get-tuple-element.55), channel_id=1, source_target_pairs={{0,6},{2,0},{4,2},{6,4},{1,7},{3,1},{5,3},{7,5},{8,14},{10,8},{12,... | collective-permute-start | bytes 1990664 | tf_op jit(solution)/shard_map/ppermute | solution.py:25
  101.4 2.7 %collective-permute-start.15 = (bf16[144,1152]{1,0:T(8,128)(2,1)S(1)}, bf16[144,1152]{1,0:T(8,128)(2,1)S(1)}, u32[]{:S(2)}, u32[]{:S(2)}) collective-permute-start(bf16[144,1152]{1,0:T(8,128)(2,1)S(1)} %copy-done.9), channel_id=1, source_target_pairs={{0,6},{2,0},{4,2},{6,4},{1,7},{3,1},{5,3},{7,5},{8,14},{10,8},{12,... | collective-permute-start | bytes 995336 | tf_op jit(solution)/shard_map/ppermute | solution.py:25
  104.0 17.5 %collective-permute-done.14.right_ref = bf16[144,1152]{1,0:T(8,128)(2,1)S(1)} collective-permute-done((bf16[144,1152]{1,0:T(8,128)(2,1)S(1)}, bf16[144,1152]{1,0:T(8,128)(2,1)S(1)}, u32[]{:S(2)}, u32[]{:S(2)}) %collective-permute-start.14) | collective-permute-done | bytes 331808 | tf_op jit(solution)/shard_map/ppermute | solution.py:25
  122.4 2.7 %merge.2 = (bf16[144,2304]{1,0:T(8,128)(2,1)}, bf16[144,2304]{1,0:T(8,128)(2,1)}) custom-call(bf16[144,2304]{1,0:T(8,128)(2,1)} %get-tuple-element.48.up_ref, bf16[144,1152]{1,0:T(8,128)(2,1)} %copy-done.4, bf16[144,2304]{1,0:T(8,128)(2,1)} %get-tuple-element.49.down_ref, bf16[144,1152]{1,0:T(8,128)(2,1)} %copy-done.5), custom_call_target="tpu_custom_call" | custom-call | flops 1000 | bytes 1000 | tf_op jit(solution)/shard_map/merge/pallas_call | solution.py:220
  130.4 3.2 %collective-permute-start.11 = (bf16[44,1152]{1,0:T(8,128)(2,1)S(1)}, bf16[44,1152]{1,0:T(8,128)(2,1)S(1)}, u32[]{:S(2)}, u32[]{:S(2)}) collective-permute-start(bf16[44,1152]{1,0:T(8,128)(2,1)S(1)} %get-tuple-element.66), channel_id=1, source_target_pairs={{0,16},{16,0},{1,17},{17,1},{2,18},{18,2},{3,19},{19,3},{4,20},{20... | collective-permute-start | bytes 304136 | tf_op jit(solution)/shard_map/ppermute | solution.py:25
  134.3 3.3 %collective-permute-start.12 = (bf16[44,1152]{1,0:T(8,128)(2,1)S(1)}, bf16[44,1152]{1,0:T(8,128)(2,1)S(1)}, u32[]{:S(2)}, u32[]{:S(2)}) collective-permute-start(bf16[44,1152]{1,0:T(8,128)(2,1)S(1)} %get-tuple-element.67), channel_id=1, source_target_pairs={{0,1},{1,0},{2,3},{3,2},{4,5},{5,4},{6,7},{7,6},{8,9},{9,8},{10,11... | collective-permute-start | bytes 304136 | tf_op jit(solution)/shard_map/ppermute | solution.py:25
  137.6 7.2 %collective-permute-done.11.m1_ref = bf16[44,1152]{1,0:T(8,128)(2,1)S(1)} collective-permute-done((bf16[44,1152]{1,0:T(8,128)(2,1)S(1)}, bf16[44,1152]{1,0:T(8,128)(2,1)S(1)}, u32[]{:S(2)}, u32[]{:S(2)}) %collective-permute-start.11) | collective-permute-done | bytes 101408 | tf_op jit(solution)/shard_map/ppermute | solution.py:25
  144.8 3.1 %collective-permute-start.13 = (bf16[44,1152]{1,0:T(8,128)(2,1)S(1)}, bf16[44,1152]{1,0:T(8,128)(2,1)S(1)}, u32[]{:S(2)}, u32[]{:S(2)}) collective-permute-start(bf16[44,1152]{1,0:T(8,128)(2,1)S(1)} %get-tuple-element.65), channel_id=1, source_target_pairs={{0,17},{1,16},{16,1},{17,0},{2,19},{3,18},{18,3},{19,2},{4,21},{5,... | collective-permute-start | bytes 304136 | tf_op jit(solution)/shard_map/ppermute | solution.py:372
  147.9 2.6 %collective-permute-done.13.o1_ref = bf16[44,1152]{1,0:T(8,128)(2,1)S(1)} collective-permute-done((bf16[44,1152]{1,0:T(8,128)(2,1)S(1)}, bf16[44,1152]{1,0:T(8,128)(2,1)S(1)}, u32[]{:S(2)}, u32[]{:S(2)}) %collective-permute-start.13) | collective-permute-done | bytes 101408 | tf_op jit(solution)/shard_map/ppermute | solution.py:372
  151.1 2.5 %join_columns.1 = bf16[44,2304]{1,0:T(8,128)(2,1)} custom-call(s32[4]{0:T(128)} %pad_add_fusion.s_ref, bf16[44,1152]{1,0:T(8,128)(2,1)} %get-tuple-element.68.m0_ref, bf16[44,1152]{1,0:T(8,128)(2,1)} %copy-done.6, bf16[44,1152]{1,0:T(8,128)(2,1)} %copy-done.7, bf16[44,1152]{1,0:T(8,128)(2,1)} %copy-done.8), custom_call_target="tpu_custom_call" | custom-call | flops 1000 | bytes 1000 | tf_op jit(solution)/shard_map/join_columns/pallas_call | solution.py:154
  (74 shorter events, 24.8 us)
Async XLA Ops:
  7.2 68.3 %all-gather.2.cloned.1.call-start = ((), (), s32[]{:S(2)}) async-start(), calls=%async_computation.2 | async-start | bytes 3649536 | tf_op jit(solution)/shard_map/all_gather | solution.py:347
  16.0 8.2 %collective-permute-start.4 = (bf16[2,44,1152]{2,1,0:T(8,128)(2,1)S(1)}, bf16[2,44,1152]{2,1,0:T(8,128)(2,1)S(1)}, u32[]{:S(2)}, u32[]{:S(2)}) collective-permute-start(bf16[2,44,1152]{2,1,0:T(8,128)(2,1)S(1)} %pad_maximum_fusion.1), channel_id=1, source_target_pairs={{0,16},{16,0},{1,17},{17,1},{2,18},{18,2},{3,19},{19,3},{4,20},{20... | collective-permute-start | bytes 608264 | tf_op jit(solution)/shard_map/ppermute | solution.py:25
  17.1 19.7 %collective-permute-start = (bf16[144,2304]{1,0:T(8,128)(2,1)}, bf16[144,2304]{1,0:T(8,128)(2,1)S(1)}, u32[]{:S(2)}, u32[]{:S(2)}) collective-permute-start(bf16[144,2304]{1,0:T(8,128)(2,1)} %get-tuple-element.32.refs_0_), channel_id=1, source_target_pairs={{0,8},{8,0},{1,9},{9,1},{2,10},{10,2},{3,11},{11,3},{4,12},{12,4},... | collective-permute-start | bytes 1990664 | tf_op jit(solution)/shard_map/ppermute | solution.py:25
  17.4 19.4 %collective-permute-start.1 = (bf16[144,2304]{1,0:T(8,128)(2,1)}, bf16[144,2304]{1,0:T(8,128)(2,1)S(1)}, u32[]{:S(2)}, u32[]{:S(2)}) collective-permute-start(bf16[144,2304]{1,0:T(8,128)(2,1)} %get-tuple-element.32.refs_0_), channel_id=1, source_target_pairs={{0,2},{2,4},{4,6},{6,0},{1,3},{3,5},{5,7},{7,1},{8,10},{10,12},{12... | collective-permute-start | bytes 1990664 | tf_op jit(solution)/shard_map/ppermute | solution.py:25
  18.7 18.1 %collective-permute-start.2 = (bf16[144,2304]{1,0:T(8,128)(2,1)}, bf16[144,2304]{1,0:T(8,128)(2,1)S(1)}, u32[]{:S(2)}, u32[]{:S(2)}) collective-permute-start(bf16[144,2304]{1,0:T(8,128)(2,1)} %get-tuple-element.32.refs_0_), channel_id=1, source_target_pairs={{0,6},{2,0},{4,2},{6,4},{1,7},{3,1},{5,3},{7,5},{8,14},{10,8},{12,... | collective-permute-start | bytes 1990664 | tf_op jit(solution)/shard_map/ppermute | solution.py:25
  26.1 103.1 %reduce-scatter.2.cloned.1.call-start = ((), (), s32[]{:S(2)}) async-start(), calls=%async_computation.1 | async-start | bytes 3649536 | tf_op jit(solution)/shard_map/reduce_scatter | solution.py:356
  36.8 22.8 %collective-permute-start.10 = (bf16[704,2304]{1,0:T(8,128)(2,1)}, bf16[704,2304]{1,0:T(8,128)(2,1)S(1)}, u32[]{:S(2)}, u32[]{:S(2)}) collective-permute-start(bf16[704,2304]{1,0:T(8,128)(2,1)} %deltas.1), channel_id=1, source_target_pairs={{0,1},{1,0},{2,3},{3,2},{4,5},{5,4},{6,7},{7,6},{8,9},{9,8},{10,11... | collective-permute-start | bytes 9732104 | tf_op jit(solution)/shard_map/ppermute | solution.py:25
  38.0 16.6 %collective-permute-start.5 = (bf16[144,2304]{1,0:T(8,128)(2,1)S(1)}, bf16[144,2304]{1,0:T(8,128)(2,1)S(1)}, u32[]{:S(2)}, u32[]{:S(2)}) collective-permute-start(bf16[144,2304]{1,0:T(8,128)(2,1)S(1)} %collective-permute-done.1.refs_2_), channel_id=1, source_target_pairs={{0,8},{8,0},{1,9},{9,1},{2,10},{10,2},{3,11},{11,3},{4,12},{12,4},... | collective-permute-start | bytes 1990664 | tf_op jit(solution)/shard_map/ppermute | solution.py:25
  39.2 16.8 %collective-permute-start.7 = (bf16[144,2304]{1,0:T(8,128)(2,1)S(1)}, bf16[144,2304]{1,0:T(8,128)(2,1)S(1)}, u32[]{:S(2)}, u32[]{:S(2)}) collective-permute-start(bf16[144,2304]{1,0:T(8,128)(2,1)S(1)} %collective-permute-done.refs_4_), channel_id=1, source_target_pairs={{0,6},{2,0},{4,2},{6,4},{1,7},{3,1},{5,3},{7,5},{8,14},{10,8},{12,... | collective-permute-start | bytes 1990664 | tf_op jit(solution)/shard_map/ppermute | solution.py:25
  41.9 20.3 %collective-permute-start.9 = (bf16[144,2304]{1,0:T(8,128)(2,1)S(1)}, bf16[144,2304]{1,0:T(8,128)(2,1)S(1)}, u32[]{:S(2)}, u32[]{:S(2)}) collective-permute-start(bf16[144,2304]{1,0:T(8,128)(2,1)S(1)} %collective-permute-done.1.refs_2_), channel_id=1, source_target_pairs={{0,2},{2,4},{4,6},{6,0},{1,3},{3,5},{5,7},{7,1},{8,10},{10,12},{12... | collective-permute-start | bytes 1990664 | tf_op jit(solution)/shard_map/ppermute | solution.py:25
  54.6 16.8 %collective-permute-start.6 = (bf16[144,1152]{1,0:T(8,128)(2,1)S(1)}, bf16[144,1152]{1,0:T(8,128)(2,1)S(1)}, u32[]{:S(2)}, u32[]{:S(2)}) collective-permute-start(bf16[144,1152]{1,0:T(8,128)(2,1)S(1)} %slice.46), channel_id=1, source_target_pairs={{0,2},{2,4},{4,6},{6,0},{1,3},{3,5},{5,7},{7,1},{8,10},{10,12},{12... | collective-permute-start | bytes 995336 | tf_op jit(solution)/shard_map/ppermute | solution.py:25
  56.0 15.4 %collective-permute-start.8 = (bf16[144,1152]{1,0:T(8,128)(2,1)S(1)}, bf16[144,1152]{1,0:T(8,128)(2,1)S(1)}, u32[]{:S(2)}, u32[]{:S(2)}) collective-permute-start(bf16[144,1152]{1,0:T(8,128)(2,1)S(1)} %slice.47), channel_id=1, source_target_pairs={{0,6},{2,0},{4,2},{6,4},{1,7},{3,1},{5,3},{7,5},{8,14},{10,8},{12,... | collective-permute-start | bytes 995336 | tf_op jit(solution)/shard_map/ppermute | solution.py:25
  81.8 14.1 %collective-permute-start.16 = (bf16[144,1152]{1,0:T(8,128)(2,1)}, bf16[144,1152]{1,0:T(8,128)(2,1)}, u32[]{:S(2)}, u32[]{:S(2)}) collective-permute-start(bf16[144,1152]{1,0:T(8,128)(2,1)} %get-tuple-element.41.refs_0_), channel_id=1, source_target_pairs={{0,2},{2,4},{4,6},{6,0},{1,3},{3,5},{5,7},{7,1},{8,10},{10,12},{12... | collective-permute-start | bytes 995336 | tf_op jit(solution)/shard_map/ppermute | solution.py:25
  82.2 13.6 %collective-permute-start.17 = (bf16[144,1152]{1,0:T(8,128)(2,1)}, bf16[144,1152]{1,0:T(8,128)(2,1)}, u32[]{:S(2)}, u32[]{:S(2)}) collective-permute-start(bf16[144,1152]{1,0:T(8,128)(2,1)} %get-tuple-element.42.refs_1_), channel_id=1, source_target_pairs={{0,6},{2,0},{4,2},{6,4},{1,7},{3,1},{5,3},{7,5},{8,14},{10,8},{12,... | collective-permute-start | bytes 995336 | tf_op jit(solution)/shard_map/ppermute | solution.py:25
  98.7 26.4 %collective-permute-start.18 = (bf16[144,2304]{1,0:T(8,128)(2,1)}, bf16[144,2304]{1,0:T(8,128)(2,1)S(1)}, u32[]{:S(2)}, u32[]{:S(2)}) collective-permute-start(bf16[144,2304]{1,0:T(8,128)(2,1)} %get-tuple-element.54), channel_id=1, source_target_pairs={{0,2},{2,4},{4,6},{6,0},{1,3},{3,5},{5,7},{7,1},{8,10},{10,12},{12... | collective-permute-start | bytes 1990664 | tf_op jit(solution)/shard_map/ppermute | solution.py:25
  98.7 26.4 %collective-permute-start.19 = (bf16[144,2304]{1,0:T(8,128)(2,1)}, bf16[144,2304]{1,0:T(8,128)(2,1)S(1)}, u32[]{:S(2)}, u32[]{:S(2)}) collective-permute-start(bf16[144,2304]{1,0:T(8,128)(2,1)} %get-tuple-element.55), channel_id=1, source_target_pairs={{0,6},{2,0},{4,2},{6,4},{1,7},{3,1},{5,3},{7,5},{8,14},{10,8},{12,... | collective-permute-start | bytes 1990664 | tf_op jit(solution)/shard_map/ppermute | solution.py:25
  101.3 20.2 %collective-permute-start.14 = (bf16[144,1152]{1,0:T(8,128)(2,1)S(1)}, bf16[144,1152]{1,0:T(8,128)(2,1)S(1)}, u32[]{:S(2)}, u32[]{:S(2)}) collective-permute-start(bf16[144,1152]{1,0:T(8,128)(2,1)S(1)} %copy-done.10), channel_id=1, source_target_pairs={{0,2},{2,4},{4,6},{6,0},{1,3},{3,5},{5,7},{7,1},{8,10},{10,12},{12... | collective-permute-start | bytes 995336 | tf_op jit(solution)/shard_map/ppermute | solution.py:25
  101.4 20.2 %collective-permute-start.15 = (bf16[144,1152]{1,0:T(8,128)(2,1)S(1)}, bf16[144,1152]{1,0:T(8,128)(2,1)S(1)}, u32[]{:S(2)}, u32[]{:S(2)}) collective-permute-start(bf16[144,1152]{1,0:T(8,128)(2,1)S(1)} %copy-done.9), channel_id=1, source_target_pairs={{0,6},{2,0},{4,2},{6,4},{1,7},{3,1},{5,3},{7,5},{8,14},{10,8},{12,... | collective-permute-start | bytes 995336 | tf_op jit(solution)/shard_map/ppermute | solution.py:25
  126.2 27.5 %collective-permute-start.22 = (bf16[144,2304]{1,0:T(8,128)(2,1)}, bf16[144,2304]{1,0:T(8,128)(2,1)S(1)}, u32[]{:S(2)}, u32[]{:S(2)}) collective-permute-start(bf16[144,2304]{1,0:T(8,128)(2,1)} %add_convert_fusion.1), channel_id=1, source_target_pairs={{0,8},{8,0},{1,9},{9,1},{2,10},{10,2},{3,11},{11,3},{4,12},{12,4},... | collective-permute-start | bytes 1990664 | tf_op jit(solution)/shard_map/ppermute | solution.py:25
  126.6 27.0 %collective-permute-start.20 = (bf16[144,2304]{1,0:T(8,128)(2,1)}, bf16[144,2304]{1,0:T(8,128)(2,1)S(1)}, u32[]{:S(2)}, u32[]{:S(2)}) collective-permute-start(bf16[144,2304]{1,0:T(8,128)(2,1)} %get-tuple-element.56), channel_id=1, source_target_pairs={{0,2},{2,4},{4,6},{6,0},{1,3},{3,5},{5,7},{7,1},{8,10},{10,12},{12... | collective-permute-start | bytes 1990664 | tf_op jit(solution)/shard_map/ppermute | solution.py:25
  127.1 26.5 %collective-permute-start.21 = (bf16[144,2304]{1,0:T(8,128)(2,1)}, bf16[144,2304]{1,0:T(8,128)(2,1)S(1)}, u32[]{:S(2)}, u32[]{:S(2)}) collective-permute-start(bf16[144,2304]{1,0:T(8,128)(2,1)} %get-tuple-element.57), channel_id=1, source_target_pairs={{0,6},{2,0},{4,2},{6,4},{1,7},{3,1},{5,3},{7,5},{8,14},{10,8},{12,... | collective-permute-start | bytes 1990664 | tf_op jit(solution)/shard_map/ppermute | solution.py:25
  130.4 14.4 %collective-permute-start.11 = (bf16[44,1152]{1,0:T(8,128)(2,1)S(1)}, bf16[44,1152]{1,0:T(8,128)(2,1)S(1)}, u32[]{:S(2)}, u32[]{:S(2)}) collective-permute-start(bf16[44,1152]{1,0:T(8,128)(2,1)S(1)} %get-tuple-element.66), channel_id=1, source_target_pairs={{0,16},{16,0},{1,17},{17,1},{2,18},{18,2},{3,19},{19,3},{4,20},{20... | collective-permute-start | bytes 304136 | tf_op jit(solution)/shard_map/ppermute | solution.py:25
  134.3 13.5 %collective-permute-start.12 = (bf16[44,1152]{1,0:T(8,128)(2,1)S(1)}, bf16[44,1152]{1,0:T(8,128)(2,1)S(1)}, u32[]{:S(2)}, u32[]{:S(2)}) collective-permute-start(bf16[44,1152]{1,0:T(8,128)(2,1)S(1)} %get-tuple-element.67), channel_id=1, source_target_pairs={{0,1},{1,0},{2,3},{3,2},{4,5},{5,4},{6,7},{7,6},{8,9},{9,8},{10,11... | collective-permute-start | bytes 304136 | tf_op jit(solution)/shard_map/ppermute | solution.py:25
  144.8 5.7 %collective-permute-start.13 = (bf16[44,1152]{1,0:T(8,128)(2,1)S(1)}, bf16[44,1152]{1,0:T(8,128)(2,1)S(1)}, u32[]{:S(2)}, u32[]{:S(2)}) collective-permute-start(bf16[44,1152]{1,0:T(8,128)(2,1)S(1)} %get-tuple-element.65), channel_id=1, source_target_pairs={{0,17},{1,16},{16,1},{17,0},{2,19},{3,18},{18,3},{19,2},{4,21},{5,... | collective-permute-start | bytes 304136 | tf_op jit(solution)/shard_map/ppermute | solution.py:372
  (12 other events, 94.5 us)
Sparse Core Ops, SparseCore 0:
  26.3 48.4 all-gather.1
  77.3 44.1 reduce-scatter.1

commit v6 on v5

--- a/solution.py
+++ b/solution.py
@@ -80,7 +80,7 @@
 
 
 INPUT_ORDER = ((0, 0), (0, 1), (0, 3), (0, 2), (1, 0), (1, 1), (1, 3), (1, 2))
-TOKEN_ORDER = ((1, 2), (0, 2), (1, 1), (1, 3), (0, 1), (0, 3), (1, 0), (0, 0))
+TOKEN_ORDER = ((1, 2), (1, 1), (1, 3), (0, 2), (1, 0), (0, 1), (0, 3), (0, 0))
 
 
 def roll_blocks(blocks, y, sign):
@@ -174,38 +174,22 @@
         out_ref[...] = (acc[skip + i * n : skip + (i + 1) * n] * scale).astype(BF)
 
 
-def first_body(scale, x_ref, d_ref, *out_refs):
-    n = out_refs[0].shape[0]
-    acc = lax.dot_general(
-        x_ref[:, : n * len(out_refs) // 2],
-        d_ref[...],
-        (((0,), (0,)), ((), ())),
-        preferred_element_type=F32,
-    )
-    for half in range(2):
-
-        @pl.when(pl.program_id(0) == half)
-        def _():
-            for i, out_ref in enumerate(out_refs[half::2]):
-                out_ref[...] = (acc[i * n : (i + 1) * n] * scale).astype(BF)
-
-
-def first_product(x, delta, scale, n):
-    rows = x.shape[0]
-    half = delta.shape[1] // 2
-    return pl.pallas_call(
-        functools.partial(first_body, scale),
-        out_shape=[jax.ShapeDtypeStruct((n, half), BF)] * 4,
-        grid=(2,),
-        in_specs=[
-            pl.BlockSpec((rows, -(-2 * n // 128) * 128), lambda i: (0, 0)),
-            pl.BlockSpec((rows, half), lambda i: (0, i)),
-        ],
-        out_specs=[pl.BlockSpec((n, half), lambda i: (0, 0))] * 4,
-        compiler_params=pltpu.CompilerParams(vmem_limit_bytes=VMEM_LIMIT),
+def halves_body(a_ref, b_ref, gate_ref, up_ref):
+    half = gate_ref.shape[1]
+    gate_ref[...] = (a_ref[:, :half].astype(F32) + b_ref[:, :half].astype(F32)).astype(BF)
+    up_ref[...] = (a_ref[:, half:].astype(F32) + b_ref[:, half:].astype(F32)).astype(BF)
+
+
+def add_halves(a, b):
+    rows, cols = a.shape
+    return pl.pallas_call(
+        halves_body,
+        out_shape=[jax.ShapeDtypeStruct((rows, cols // 2), BF)] * 2,
+        in_specs=[IN_VMEM] * 2,
+        out_specs=[IN_VMEM] * 2,
         cost_estimate=SMALL,
-        name="first_product",
-    )(x, delta)
+        name="add_halves",
+    )(a, b)
 
 
 def merge_body(up_ref, right_ref, down_ref, left_ref, up_out, down_out):
@@ -305,27 +289,27 @@
     )(*blocks, after, delta)
 
 
-def gather_weights(w, after):
+def gather_weights(w, after, then):
     half = w.shape[1] // 2
     far, below, above = shift(w, "x_lo", 1), shift(w, "y", 1), shift(w, "y", -1)
     far, below, above, after = lax.optimization_barrier((far, below, above, after))
     far_below, far_above = shift(below, "x_lo", 1), shift(far, "y", -1)
     across = shift(below, "y", 1)
+    then = then(after)
+    far_below, far_above, then = lax.optimization_barrier((far_below, far_above, then))
     last = [shift(far_below[:, :half], "y", 1), shift(far_above[:, half:], "y", -1)]
-    return [w, above, below, across, far, far_above, far_below], last, after
+    return [w, above, below, across, far, far_above, far_below], last, then
 
 
 def scatter_grads(first, rest):
-    far_up, far_down, up, down, far_own, own = rest
-    far_right, far_left = shift(first[0], "y", 1), shift(first[1], "y", -1)
-    right, left = shift(first[2], "y", 1), shift(first[3], "y", -1)
-    far_up, far_down = merge(far_up, far_right, far_down, far_left)
-    far_right, far_left = shift(far_up, "y", 1), shift(far_down, "y", -1)
+    across = shift(first[0], "x_lo", 1)
+    far_right, far_left = shift(first[1], "y", 1), shift(first[2], "y", -1)
+    far, far_own, up, down, own = rest
+    right, left = add_halves(far, across)
+    right, left = shift(right, "y", 1), shift(left, "y", -1)
+    far_own = shift(add(far_own, far_left, far_right), "x_lo", 1)
     up, down = merge(up, right, down, left)
-    up, down, far_right, far_left = lax.optimization_barrier((up, down, far_right, far_left))
-    far_own = shift(add(far_own, far_left, far_right), "x_lo", 1)
-    right, left = shift(up, "y", 1), shift(down, "y", -1)
-    return own, right, left, far_own
+    return own, shift(up, "y", 1), shift(down, "y", -1), far_own
 
 
 def per_device(tokens, gate_pre, up_pre, cotangent, gate_weight, up_weight):
@@ -346,18 +330,21 @@
     gate_pre, block = lax.optimization_barrier((gate_pre, block))
     x = lax.all_gather(block, "z", axis=0, tiled=True).reshape(-1, keep.shape[1])
     mine = make_deltas(gate_pre, up_pre, cotangent)
-    early, late, mine = gather_weights(w, mine)
-    other = shift(mine, "core", 1)
-    delta = jnp.stack([a.reshape(8, 2 * rows, -1) for a in (mine, other)], 1)
-    delta = delta.reshape(-1, 2 * hidden)
+
+    def both_cores(mine):
+        other = shift(mine, "core", 1)
+        delta = jnp.stack([a.reshape(8, 2 * rows, -1) for a in (mine, other)], 1)
+        return delta.reshape(-1, 2 * hidden)
+
+    early, late, delta = gather_weights(w, mine, both_cores)
 
     part = input_product(delta, early, place.reshape(1, -1), INPUT_FLOPS)
     part = input_product(delta, late, part, 1e3)
     sums = lax.psum_scatter(part, "z", scatter_dimension=0, tiled=True)
 
-    first = first_product(x, delta, scale, owned)
+    first = weight_product(x, delta, scale, 0, 3 * owned, owned, 1e3)
     rest = weight_product(
-        x, delta, scale, 2 * owned, 6 * owned, owned, REST_FLOPS, mark("sent", *first)
+        x, delta, scale, 3 * owned, 5 * owned, owned, REST_FLOPS, mark("sent", *first)
     )
     own, *terms = scatter_grads(first, rest)
 

time: 164 us -> 149 us (0.909); the launches traced: 162 us -> 149 us
  waiting for transfers between devices: 49.9 us -> 36.8 us
  starting transfers between devices: 38.3 us -> 36.6 us
    ppermute x22 -> x21, waiting for transfers between devices: 47.3 us -> 28.6 us  [shift(): return lax.ppermute(x, axis, [(i, (i + k) % n) for i in range(n)])]
    pallas_call x1 -> x2, Pallas kernels: 10.8 us -> 17.1 us  [weight_product(): pl.pallas_call(functools.partial(weight_body, scale, start, first - start...]
    pallas_call x1, Pallas kernels: 6.29 us -> 2.22 us  [add_halves(): pl.pallas_call(halves_body, out_shape=[jax.ShapeDtypeStruct((rows, cols /...]
    ppermute x22 -> x21, starting transfers between devices: 35.2 us -> 31.8 us  [shift(): return lax.ppermute(x, axis, [(i, (i + k) % n) for i in range(n)])]
    reduce_scatter x1, waiting for transfers between devices: 0.01 us -> 2.94 us  [per_device(): sums = lax.psum_scatter(part, 'z', scatter_dimension=0, tiled=True)]
    pallas_call x2 -> x1, Pallas kernels: 5.49 us -> 2.68 us  [merge(): pl.pallas_call(merge_body, out_shape=[jax.ShapeDtypeStruct(up.shape, BF)]...]
    all_gather x1, waiting for transfers between devices: 0.02 us -> 1.72 us  [per_device(): lax.all_gather(block, 'z', axis=0, tiled=True).reshape(-1, keep.shape[1])]
    ppermute x1, starting transfers between devices: 3.09 us -> 4.76 us  [per_device(): lax.ppermute(there[1], ('x_hi', 'core'), [(i, 3 - i) for i in range(4)])]
  transfers between devices with their start and end apart: 25 -> 24, of which waited for: 7 -> 12; matrix products, arithmetic and copies ran while one was open for 5% -> 6% of each run, Pallas kernels for 28% -> 30%
where the time goes in v6:
time: 149 us
  Pallas kernels  46.9 us (31%)
  waiting for transfers between devices  36.8 us (25%)
  starting transfers between devices  36.6 us (25%)
  between operations  14.2 us (10%)
  other arithmetic  8.81 us (6%)
  local copies, waits for them, and re-layouts  5.55 us (4%)
    ppermute x21, starting transfers between devices, shift(): return lax.ppermute(x, axis, [(i, (i + k) % n) for i in range(n)])  31.8 us
    ppermute x21, waiting for transfers between devices, shift(): return lax.ppermute(x, axis, [(i, (i + k) % n) for i in range(n)])  28.6 us
    pallas_call x2, Pallas kernels, weight_product(): pl.pallas_call(functools.partial(weight_body, scale, start, first - start...  17.1 us
    pallas_call x2, Pallas kernels, input_product(): pl.pallas_call(functools.partial(input_body, n, done), out_shape=jax.Shap...  13.1 us
    pallas_call x1, Pallas kernels, make_deltas(): pl.pallas_call(delta_body, out_shape=jax.ShapeDtypeStruct((rows, 2 * cols...  5.91 us
    ppermute x1, starting transfers between devices, per_device(): lax.ppermute(there[1], ('x_hi', 'core'), [(i, 3 - i) for i in range(4)])  4.76 us
    ppermute x1, waiting for transfers between devices, per_device(): lax.ppermute(there[1], ('x_hi', 'core'), [(i, 3 - i) for i in range(4)])  3.55 us
  transfers between devices with their start and end apart: 24, of which 12 were waited for; matrix products, arithmetic and copies ran while one was open for 6% of the time, Pallas kernels for 30%

profile of v6, /device:TPU:1, one launch (start us, length us, event | category | flops | bytes accessed | tf_op | source)
XLA Modules:
  0.0 148.9 jit_solution(3111971709447420960)
XLA Ops:
  7.9 2.8 %prologue.1 = (bf16[44,1152]{1,0:T(8,128)(2,1)}, bf16[44,1152]{1,0:T(8,128)(2,1)}, bf16[144,2304]{1,0:T(8,128)(2,1)}) custom-call(s32[4]{0:T(128)} %pad_add_fusion.s_ref, bf16[44,2304]{1,0:T(8,128)(2,1)} %x_ref.1, bf16[144,1152]{1,0:T(8,128)(2,1)} %g_ref.1, bf16[144,1152]{1,0:T(8,128)(2,1)} %u_ref.2), custom_call_target="tpu_custom_call" | custom-call | flops 1000 | bytes 1000 | tf_op jit(solution)/shard_map/prologue/pallas_call | solution.py:117
  10.7 3.2 %collective-permute-start.3 = (bf16[44,1152]{1,0:T(8,128)(2,1)}, bf16[44,1152]{1,0:T(8,128)(2,1)S(1)}, u32[]{:S(2)}, u32[]{:S(2)}) collective-permute-start(bf16[44,1152]{1,0:T(8,128)(2,1)} %get-tuple-element.31), channel_id=1, source_target_pairs={{0,1},{1,0},{2,3},{3,2},{4,5},{5,4},{6,7},{7,6},{8,9},{9,8},{10,11... | collective-permute-start | bytes 304136 | tf_op jit(solution)/shard_map/ppermute | solution.py:25
  20.2 4.1 %collective-permute-done.4 = bf16[2,44,1152]{2,1,0:T(8,128)(2,1)S(1)} collective-permute-done((bf16[2,44,1152]{2,1,0:T(8,128)(2,1)S(1)}, bf16[2,44,1152]{2,1,0:T(8,128)(2,1)S(1)}, u32[]{:S(2)}, u32[]{:S(2)}) %collective-permute-start.4) | collective-permute-done | bytes 202784 | tf_op jit(solution)/shard_map/ppermute | solution.py:25
  26.3 5.9 %deltas.1 = bf16[704,2304]{1,0:T(8,128)(2,1)} custom-call(bf16[704,1152]{1,0:T(8,128)(2,1)} %g_ref.2, bf16[704,1152]{1,0:T(8,128)(2,1)} %u_ref.3, bf16[704,1152]{1,0:T(8,128)(2,1)} %c_ref.1), custom_call_target="tpu_custom_call" | custom-call | flops 99999997952 | bytes 1000 | tf_op jit(solution)/shard_map/deltas/pallas_call | solution.py:53
  32.2 4.7 %collective-permute-done.refs_4_ = bf16[144,2304]{1,0:T(8,128)(2,1)S(1)} collective-permute-done((bf16[144,2304]{1,0:T(8,128)(2,1)}, bf16[144,2304]{1,0:T(8,128)(2,1)S(1)}, u32[]{:S(2)}, u32[]{:S(2)}) %collective-permute-start) | collective-permute-done | bytes 663584 | tf_op jit(solution)/shard_map/ppermute | solution.py:25
  39.2 2.7 %collective-permute-start.6 = (bf16[144,2304]{1,0:T(8,128)(2,1)S(1)}, bf16[144,2304]{1,0:T(8,128)(2,1)S(1)}, u32[]{:S(2)}, u32[]{:S(2)}) collective-permute-start(bf16[144,2304]{1,0:T(8,128)(2,1)S(1)} %collective-permute-done.refs_4_), channel_id=1, source_target_pairs={{0,6},{2,0},{4,2},{6,4},{1,7},{3,1},{5,3},{7,5},{8,14},{10,8},{12,... | collective-permute-start | bytes 1990664 | tf_op jit(solution)/shard_map/ppermute | solution.py:25
  43.7 2.5 %pad_maximum_fusion = bf16[8,2,88,2304]{3,2,1,0:T(8,128)(2,1)S(1)} fusion(bf16[8,1,88,2304]{3,2,1,0:T(8,128)(2,1)S(1)} %bitcast.31, bf16[8,1,88,2304]{3,2,1,0:T(8,128)(2,1)} %bitcast.30), kind=kLoop, calls=%fused_computation | loop fusion | flops 3244032 | bytes 12976128 | tf_op jit(solution)/shard_map/stack | solution.py:336
  46.2 8.4 %collective-permute-done.5.refs_6_ = bf16[144,2304]{1,0:T(8,128)(2,1)S(1)} collective-permute-done((bf16[144,2304]{1,0:T(8,128)(2,1)S(1)}, bf16[144,2304]{1,0:T(8,128)(2,1)S(1)}, u32[]{:S(2)}, u32[]{:S(2)}) %collective-permute-start.5) | collective-permute-done | bytes 663584 | tf_op jit(solution)/shard_map/ppermute | solution.py:25
  56.9 2.9 %collective-permute-start.9 = (bf16[144,1152]{1,0:T(8,128)(2,1)S(1)}, bf16[144,1152]{1,0:T(8,128)(2,1)S(1)}, u32[]{:S(2)}, u32[]{:S(2)}) collective-permute-start(bf16[144,1152]{1,0:T(8,128)(2,1)S(1)} %slice.37), channel_id=1, source_target_pairs={{0,6},{2,0},{4,2},{6,4},{1,7},{3,1},{5,3},{7,5},{8,14},{10,8},{12,... | collective-permute-start | bytes 995336 | tf_op jit(solution)/shard_map/ppermute | solution.py:25
  59.9 9.1 %input_product_0.1.refs_2_ = bf16[1408,1008]{1,0:T(8,128)(2,1)S(1)} custom-call(bf16[144,2304]{1,0:T(8,128)(2,1)S(1)} %copy-done.1, bf16[144,2304]{1,0:T(8,128)(2,1)S(1)} %collective-permute-done.2.refs_1_, bf16[144,2304]{1,0:T(8,128)(2,1)S(1)} %collective-permute-done.1.refs_2_, bf16[144,2304]{1,0:T(8,128)(2,1)S(1)} %collective-permute-done.10.refs_3_, ...), custom_call_target="tpu_custom_call" | custom-call | flops 1000 | bytes 1000 | tf_op jit(solution)/shard_map/input_product_0/pallas_call | solution.py:276
  69.1 4.0 %input_product_1008.1 = bf16[1408,1152]{1,0:T(8,128)(2,1)} custom-call(bf16[144,1152]{1,0:T(8,128)(2,1)S(1)} %collective-permute-done.8.refs_0_, bf16[144,1152]{1,0:T(8,128)(2,1)S(1)} %collective-permute-done.9.refs_1_, bf16[1408,1008]{1,0:T(8,128)(2,1)S(1)} %input_product_0.1.refs_2_, bf16[1408,2304]{1,0:T(8,128)(2,1)S(1)} %bitcast.25), custom_call_target="tpu_custom_call" | custom-call | flops 1000 | bytes 1000 | tf_op jit(solution)/shard_map/input_product_1008/pallas_call | solution.py:276
  74.8 7.3 %weight_product_0.1 = (bf16[144,2304]{1,0:T(8,128)(2,1)}, bf16[144,2304]{1,0:T(8,128)(2,1)}, bf16[144,2304]{1,0:T(8,128)(2,1)}) custom-call(bf16[1408,1152]{1,0:T(8,128)(2,1)} %bitcast.28, bf16[1408,2304]{1,0:T(8,128)(2,1)} %bitcast.26), custom_call_target="tpu_custom_call" | custom-call | flops 1000 | bytes 1000 | tf_op jit(solution)/shard_map/weight_product_0/pallas_call | solution.py:220
  87.1 9.8 %weight_product_432.1 = (bf16[144,2304]{1,0:T(8,128)(2,1)}, bf16[144,2304]{1,0:T(8,128)(2,1)}, bf16[144,2304]{1,0:T(8,128)(2,1)}, bf16[144,2304]{1,0:T(8,128)(2,1)}, bf16[144,2304]{1,0:T(8,128)(2,1)}) custom-call(bf16[1408,1152]{1,0:T(8,128)(2,1)} %bitcast.29, bf16[1408,2304]{1,0:T(8,128)(2,1)} %bitcast.27, f32[8,128]{1,0:T(8,128)} %sent.1.refs_0_), custom_call_target="tpu_custom_call" | custom-call | flops 99999997952 | bytes 1000 | tf_op jit(solution)/shard_map/weight_product_432/pallas_call | solution.py:220
  96.9 4.2 %collective-permute-done.14.b_ref = bf16[144,2304]{1,0:T(8,128)(2,1)S(1)} collective-permute-done((bf16[144,2304]{1,0:T(8,128)(2,1)S(1)}, bf16[144,2304]{1,0:T(8,128)(2,1)S(1)}, u32[]{:S(2)}, u32[]{:S(2)}) %collective-permute-start.14) | collective-permute-done | bytes 663584 | tf_op jit(solution)/shard_map/ppermute | solution.py:25
  104.3 2.7 %collective-permute-start.16 = (bf16[144,1152]{1,0:T(8,128)(2,1)}, bf16[144,1152]{1,0:T(8,128)(2,1)S(1)}, u32[]{:S(2)}, u32[]{:S(2)}) collective-permute-start(bf16[144,1152]{1,0:T(8,128)(2,1)} %get-tuple-element.51), channel_id=1, source_target_pairs={{0,6},{2,0},{4,2},{6,4},{1,7},{3,1},{5,3},{7,5},{8,14},{10,8},{12,... | collective-permute-start | bytes 995336 | tf_op jit(solution)/shard_map/ppermute | solution.py:25
  106.9 2.4 %add_convert_fusion.1 = bf16[144,2304]{1,0:T(8,128)(2,1)} fusion(bf16[144,2304]{1,0:T(8,128)(2,1)} %collective-permute-done.20, bf16[144,2304]{1,0:T(8,128)(2,1)} %collective-permute-done.19, bf16[144,2304]{1,0:T(8,128)(2,1)S(1)} %copy-done.4), kind=kLoop, calls=%fused_computation.2 | loop fusion | flops 1990656 | bytes 2654208 | tf_op jit(solution)/shard_map/convert_element_type | solution.py:32
  110.6 2.5 %collective-permute-done.15.right_ref = bf16[144,1152]{1,0:T(8,128)(2,1)S(1)} collective-permute-done((bf16[144,1152]{1,0:T(8,128)(2,1)}, bf16[144,1152]{1,0:T(8,128)(2,1)S(1)}, u32[]{:S(2)}, u32[]{:S(2)}) %collective-permute-start.15) | collective-permute-done | bytes 331808 | tf_op jit(solution)/shard_map/ppermute | solution.py:25
  113.8 2.7 %merge.1 = (bf16[144,2304]{1,0:T(8,128)(2,1)}, bf16[144,2304]{1,0:T(8,128)(2,1)}) custom-call(bf16[144,2304]{1,0:T(8,128)(2,1)} %get-tuple-element.47.up_ref, bf16[144,1152]{1,0:T(8,128)(2,1)} %copy-done.5, bf16[144,2304]{1,0:T(8,128)(2,1)} %get-tuple-element.50.down_ref, bf16[144,1152]{1,0:T(8,128)(2,1)} %copy-done.6), custom_call_target="tpu_custom_call" | custom-call | flops 1000 | bytes 1000 | tf_op jit(solution)/shard_map/merge/pallas_call | solution.py:204
  118.8 2.9 %reduce-scatter.2.cloned.1.call-done = bf16[176,1152]{1,0:T(8,128)(2,1)} async-done(((bf16[1408,1152]{1,0:T(8,128)(2,1)}), bf16[176,1152]{1,0:T(8,128)(2,1)}) %reduce-scatter.2.cloned.1.call-update) | async-done | bytes 405520 | tf_op jit(solution)/shard_map/reduce_scatter | solution.py:343
  122.9 2.7 %collective-permute-start.11 = (bf16[44,1152]{1,0:T(8,128)(2,1)S(1)}, bf16[44,1152]{1,0:T(8,128)(2,1)S(1)}, u32[]{:S(2)}, u32[]{:S(2)}) collective-permute-start(bf16[44,1152]{1,0:T(8,128)(2,1)S(1)} %get-tuple-element.60), channel_id=1, source_target_pairs={{0,16},{16,0},{1,17},{17,1},{2,18},{18,2},{3,19},{19,3},{4,20},{20... | collective-permute-start | bytes 304136 | tf_op jit(solution)/shard_map/ppermute | solution.py:25
  126.3 2.7 %collective-permute-start.12 = (bf16[44,1152]{1,0:T(8,128)(2,1)S(1)}, bf16[44,1152]{1,0:T(8,128)(2,1)S(1)}, u32[]{:S(2)}, u32[]{:S(2)}) collective-permute-start(bf16[44,1152]{1,0:T(8,128)(2,1)S(1)} %get-tuple-element.61), channel_id=1, source_target_pairs={{0,1},{1,0},{2,3},{3,2},{4,5},{5,4},{6,7},{7,6},{8,9},{9,8},{10,11... | collective-permute-start | bytes 304136 | tf_op jit(solution)/shard_map/ppermute | solution.py:25
  129.4 4.8 %collective-permute-start.13 = (bf16[44,1152]{1,0:T(8,128)(2,1)S(1)}, bf16[44,1152]{1,0:T(8,128)(2,1)S(1)}, u32[]{:S(2)}, u32[]{:S(2)}) collective-permute-start(bf16[44,1152]{1,0:T(8,128)(2,1)S(1)} %get-tuple-element.59), channel_id=1, source_target_pairs={{0,17},{1,16},{16,1},{17,0},{2,19},{3,18},{18,3},{19,2},{4,21},{5,... | collective-permute-start | bytes 304136 | tf_op jit(solution)/shard_map/ppermute | solution.py:359
  134.1 3.5 %collective-permute-done.13.o1_ref = bf16[44,1152]{1,0:T(8,128)(2,1)S(1)} collective-permute-done((bf16[44,1152]{1,0:T(8,128)(2,1)S(1)}, bf16[44,1152]{1,0:T(8,128)(2,1)S(1)}, u32[]{:S(2)}, u32[]{:S(2)}) %collective-permute-start.13) | collective-permute-done | bytes 101408 | tf_op jit(solution)/shard_map/ppermute | solution.py:359
  138.3 2.5 %join_columns.1 = bf16[44,2304]{1,0:T(8,128)(2,1)} custom-call(s32[4]{0:T(128)} %pad_add_fusion.s_ref, bf16[44,1152]{1,0:T(8,128)(2,1)} %get-tuple-element.62.m0_ref, bf16[44,1152]{1,0:T(8,128)(2,1)} %copy-done.7, bf16[44,1152]{1,0:T(8,128)(2,1)} %copy-done.8, bf16[44,1152]{1,0:T(8,128)(2,1)} %copy-done.9), custom_call_target="tpu_custom_call" | custom-call | flops 1000 | bytes 1000 | tf_op jit(solution)/shard_map/join_columns/pallas_call | solution.py:154
  (72 shorter events, 33.6 us)
Async XLA Ops:
  7.2 67.6 %all-gather.2.cloned.1.call-start = ((), (), s32[]{:S(2)}) async-start(), calls=%async_computation.2 | async-start | bytes 3649536 | tf_op jit(solution)/shard_map/all_gather | solution.py:331
  10.7 4.4 %collective-permute-start.3 = (bf16[44,1152]{1,0:T(8,128)(2,1)}, bf16[44,1152]{1,0:T(8,128)(2,1)S(1)}, u32[]{:S(2)}, u32[]{:S(2)}) collective-permute-start(bf16[44,1152]{1,0:T(8,128)(2,1)} %get-tuple-element.31), channel_id=1, source_target_pairs={{0,1},{1,0},{2,3},{3,2},{4,5},{5,4},{6,7},{7,6},{8,9},{9,8},{10,11... | collective-permute-start | bytes 304136 | tf_op jit(solution)/shard_map/ppermute | solution.py:25
  16.1 8.2 %collective-permute-start.4 = (bf16[2,44,1152]{2,1,0:T(8,128)(2,1)S(1)}, bf16[2,44,1152]{2,1,0:T(8,128)(2,1)S(1)}, u32[]{:S(2)}, u32[]{:S(2)}) collective-permute-start(bf16[2,44,1152]{2,1,0:T(8,128)(2,1)S(1)} %pad_maximum_fusion.1), channel_id=1, source_target_pairs={{0,16},{16,0},{1,17},{17,1},{2,18},{18,2},{3,19},{19,3},{4,20},{20... | collective-permute-start | bytes 608264 | tf_op jit(solution)/shard_map/ppermute | solution.py:25
  17.2 19.7 %collective-permute-start = (bf16[144,2304]{1,0:T(8,128)(2,1)}, bf16[144,2304]{1,0:T(8,128)(2,1)S(1)}, u32[]{:S(2)}, u32[]{:S(2)}) collective-permute-start(bf16[144,2304]{1,0:T(8,128)(2,1)} %get-tuple-element.29.refs_0_), channel_id=1, source_target_pairs={{0,8},{8,0},{1,9},{9,1},{2,10},{10,2},{3,11},{11,3},{4,12},{12,4},... | collective-permute-start | bytes 1990664 | tf_op jit(solution)/shard_map/ppermute | solution.py:25
  17.5 19.4 %collective-permute-start.1 = (bf16[144,2304]{1,0:T(8,128)(2,1)}, bf16[144,2304]{1,0:T(8,128)(2,1)S(1)}, u32[]{:S(2)}, u32[]{:S(2)}) collective-permute-start(bf16[144,2304]{1,0:T(8,128)(2,1)} %get-tuple-element.29.refs_0_), channel_id=1, source_target_pairs={{0,2},{2,4},{4,6},{6,0},{1,3},{3,5},{5,7},{7,1},{8,10},{10,12},{12... | collective-permute-start | bytes 1990664 | tf_op jit(solution)/shard_map/ppermute | solution.py:25
  18.8 18.1 %collective-permute-start.2 = (bf16[144,2304]{1,0:T(8,128)(2,1)}, bf16[144,2304]{1,0:T(8,128)(2,1)S(1)}, u32[]{:S(2)}, u32[]{:S(2)}) collective-permute-start(bf16[144,2304]{1,0:T(8,128)(2,1)} %get-tuple-element.29.refs_0_), channel_id=1, source_target_pairs={{0,6},{2,0},{4,2},{6,4},{1,7},{3,1},{5,3},{7,5},{8,14},{10,8},{12,... | collective-permute-start | bytes 1990664 | tf_op jit(solution)/shard_map/ppermute | solution.py:25
  26.2 95.6 %reduce-scatter.2.cloned.1.call-start = ((), (), s32[]{:S(2)}) async-start(), calls=%async_computation.1 | async-start | bytes 3649536 | tf_op jit(solution)/shard_map/reduce_scatter | solution.py:343
  36.9 6.8 %collective-permute-start.7 = (bf16[704,2304]{1,0:T(8,128)(2,1)}, bf16[704,2304]{1,0:T(8,128)(2,1)S(1)}, u32[]{:S(2)}, u32[]{:S(2)}) collective-permute-start(bf16[704,2304]{1,0:T(8,128)(2,1)} %deltas.1), channel_id=1, source_target_pairs={{0,1},{1,0},{2,3},{3,2},{4,5},{5,4},{6,7},{7,6},{8,9},{9,8},{10,11... | collective-permute-start | bytes 9732104 | tf_op jit(solution)/shard_map/ppermute | solution.py:25
  38.1 16.6 %collective-permute-start.5 = (bf16[144,2304]{1,0:T(8,128)(2,1)S(1)}, bf16[144,2304]{1,0:T(8,128)(2,1)S(1)}, u32[]{:S(2)}, u32[]{:S(2)}) collective-permute-start(bf16[144,2304]{1,0:T(8,128)(2,1)S(1)} %collective-permute-done.1.refs_2_), channel_id=1, source_target_pairs={{0,8},{8,0},{1,9},{9,1},{2,10},{10,2},{3,11},{11,3},{4,12},{12,4},... | collective-permute-start | bytes 1990664 | tf_op jit(solution)/shard_map/ppermute | solution.py:25
  39.2 16.7 %collective-permute-start.6 = (bf16[144,2304]{1,0:T(8,128)(2,1)S(1)}, bf16[144,2304]{1,0:T(8,128)(2,1)S(1)}, u32[]{:S(2)}, u32[]{:S(2)}) collective-permute-start(bf16[144,2304]{1,0:T(8,128)(2,1)S(1)} %collective-permute-done.refs_4_), channel_id=1, source_target_pairs={{0,6},{2,0},{4,2},{6,4},{1,7},{3,1},{5,3},{7,5},{8,14},{10,8},{12,... | collective-permute-start | bytes 1990664 | tf_op jit(solution)/shard_map/ppermute | solution.py:25
  42.0 17.9 %collective-permute-start.10 = (bf16[144,2304]{1,0:T(8,128)(2,1)S(1)}, bf16[144,2304]{1,0:T(8,128)(2,1)S(1)}, u32[]{:S(2)}, u32[]{:S(2)}) collective-permute-start(bf16[144,2304]{1,0:T(8,128)(2,1)S(1)} %collective-permute-done.1.refs_2_), channel_id=1, source_target_pairs={{0,2},{2,4},{4,6},{6,0},{1,3},{3,5},{5,7},{7,1},{8,10},{10,12},{12... | collective-permute-start | bytes 1990664 | tf_op jit(solution)/shard_map/ppermute | solution.py:25
  55.9 13.1 %collective-permute-start.8 = (bf16[144,1152]{1,0:T(8,128)(2,1)S(1)}, bf16[144,1152]{1,0:T(8,128)(2,1)S(1)}, u32[]{:S(2)}, u32[]{:S(2)}) collective-permute-start(bf16[144,1152]{1,0:T(8,128)(2,1)S(1)} %slice.36), channel_id=1, source_target_pairs={{0,2},{2,4},{4,6},{6,0},{1,3},{3,5},{5,7},{7,1},{8,10},{10,12},{12... | collective-permute-start | bytes 995336 | tf_op jit(solution)/shard_map/ppermute | solution.py:25
  56.9 12.1 %collective-permute-start.9 = (bf16[144,1152]{1,0:T(8,128)(2,1)S(1)}, bf16[144,1152]{1,0:T(8,128)(2,1)S(1)}, u32[]{:S(2)}, u32[]{:S(2)}) collective-permute-start(bf16[144,1152]{1,0:T(8,128)(2,1)S(1)} %slice.37), channel_id=1, source_target_pairs={{0,6},{2,0},{4,2},{6,4},{1,7},{3,1},{5,3},{7,5},{8,14},{10,8},{12,... | collective-permute-start | bytes 995336 | tf_op jit(solution)/shard_map/ppermute | solution.py:25
  82.1 24.8 %collective-permute-start.20 = (bf16[144,2304]{1,0:T(8,128)(2,1)}, bf16[144,2304]{1,0:T(8,128)(2,1)}, u32[]{:S(2)}, u32[]{:S(2)}) collective-permute-start(bf16[144,2304]{1,0:T(8,128)(2,1)} %get-tuple-element.42.refs_1_), channel_id=1, source_target_pairs={{0,2},{2,4},{4,6},{6,0},{1,3},{3,5},{5,7},{7,1},{8,10},{10,12},{12... | collective-permute-start | bytes 1990664 | tf_op jit(solution)/shard_map/ppermute | solution.py:25
  83.3 23.6 %collective-permute-start.19 = (bf16[144,2304]{1,0:T(8,128)(2,1)}, bf16[144,2304]{1,0:T(8,128)(2,1)}, u32[]{:S(2)}, u32[]{:S(2)}) collective-permute-start(bf16[144,2304]{1,0:T(8,128)(2,1)} %get-tuple-element.43.refs_2_), channel_id=1, source_target_pairs={{0,6},{2,0},{4,2},{6,4},{1,7},{3,1},{5,3},{7,5},{8,14},{10,8},{12,... | collective-permute-start | bytes 1990664 | tf_op jit(solution)/shard_map/ppermute | solution.py:25
  85.9 15.3 %collective-permute-start.14 = (bf16[144,2304]{1,0:T(8,128)(2,1)S(1)}, bf16[144,2304]{1,0:T(8,128)(2,1)S(1)}, u32[]{:S(2)}, u32[]{:S(2)}) collective-permute-start(bf16[144,2304]{1,0:T(8,128)(2,1)S(1)} %copy-done.10), channel_id=1, source_target_pairs={{0,8},{8,0},{1,9},{9,1},{2,10},{10,2},{3,11},{11,3},{4,12},{12,4},... | collective-permute-start | bytes 1990664 | tf_op jit(solution)/shard_map/ppermute | solution.py:25
  104.2 8.8 %collective-permute-start.15 = (bf16[144,1152]{1,0:T(8,128)(2,1)}, bf16[144,1152]{1,0:T(8,128)(2,1)S(1)}, u32[]{:S(2)}, u32[]{:S(2)}) collective-permute-start(bf16[144,1152]{1,0:T(8,128)(2,1)} %get-tuple-element.49), channel_id=1, source_target_pairs={{0,2},{2,4},{4,6},{6,0},{1,3},{3,5},{5,7},{7,1},{8,10},{10,12},{12... | collective-permute-start | bytes 995336 | tf_op jit(solution)/shard_map/ppermute | solution.py:25
  104.3 8.8 %collective-permute-start.16 = (bf16[144,1152]{1,0:T(8,128)(2,1)}, bf16[144,1152]{1,0:T(8,128)(2,1)S(1)}, u32[]{:S(2)}, u32[]{:S(2)}) collective-permute-start(bf16[144,1152]{1,0:T(8,128)(2,1)} %get-tuple-element.51), channel_id=1, source_target_pairs={{0,6},{2,0},{4,2},{6,4},{1,7},{3,1},{5,3},{7,5},{8,14},{10,8},{12,... | collective-permute-start | bytes 995336 | tf_op jit(solution)/shard_map/ppermute | solution.py:25
  109.3 31.5 %collective-permute-start.21 = (bf16[144,2304]{1,0:T(8,128)(2,1)}, bf16[144,2304]{1,0:T(8,128)(2,1)S(1)}, u32[]{:S(2)}, u32[]{:S(2)}) collective-permute-start(bf16[144,2304]{1,0:T(8,128)(2,1)} %add_convert_fusion.1), channel_id=1, source_target_pairs={{0,8},{8,0},{1,9},{9,1},{2,10},{10,2},{3,11},{11,3},{4,12},{12,4},... | collective-permute-start | bytes 1990664 | tf_op jit(solution)/shard_map/ppermute | solution.py:25
  116.5 24.3 %collective-permute-start.18 = (bf16[144,2304]{1,0:T(8,128)(2,1)}, bf16[144,2304]{1,0:T(8,128)(2,1)S(1)}, u32[]{:S(2)}, u32[]{:S(2)}) collective-permute-start(bf16[144,2304]{1,0:T(8,128)(2,1)} %get-tuple-element.53), channel_id=1, source_target_pairs={{0,6},{2,0},{4,2},{6,4},{1,7},{3,1},{5,3},{7,5},{8,14},{10,8},{12,... | collective-permute-start | bytes 1990664 | tf_op jit(solution)/shard_map/ppermute | solution.py:25
  118.8 22.0 %collective-permute-start.17 = (bf16[144,2304]{1,0:T(8,128)(2,1)}, bf16[144,2304]{1,0:T(8,128)(2,1)S(1)}, u32[]{:S(2)}, u32[]{:S(2)}) collective-permute-start(bf16[144,2304]{1,0:T(8,128)(2,1)} %get-tuple-element.52), channel_id=1, source_target_pairs={{0,2},{2,4},{4,6},{6,0},{1,3},{3,5},{5,7},{7,1},{8,10},{10,12},{12... | collective-permute-start | bytes 1990664 | tf_op jit(solution)/shard_map/ppermute | solution.py:25
  122.9 6.4 %collective-permute-start.11 = (bf16[44,1152]{1,0:T(8,128)(2,1)S(1)}, bf16[44,1152]{1,0:T(8,128)(2,1)S(1)}, u32[]{:S(2)}, u32[]{:S(2)}) collective-permute-start(bf16[44,1152]{1,0:T(8,128)(2,1)S(1)} %get-tuple-element.60), channel_id=1, source_target_pairs={{0,16},{16,0},{1,17},{17,1},{2,18},{18,2},{3,19},{19,3},{4,20},{20... | collective-permute-start | bytes 304136 | tf_op jit(solution)/shard_map/ppermute | solution.py:25
  126.3 7.9 %collective-permute-start.12 = (bf16[44,1152]{1,0:T(8,128)(2,1)S(1)}, bf16[44,1152]{1,0:T(8,128)(2,1)S(1)}, u32[]{:S(2)}, u32[]{:S(2)}) collective-permute-start(bf16[44,1152]{1,0:T(8,128)(2,1)S(1)} %get-tuple-element.61), channel_id=1, source_target_pairs={{0,1},{1,0},{2,3},{3,2},{4,5},{5,4},{6,7},{7,6},{8,9},{9,8},{10,11... | collective-permute-start | bytes 304136 | tf_op jit(solution)/shard_map/ppermute | solution.py:25
  129.4 8.3 %collective-permute-start.13 = (bf16[44,1152]{1,0:T(8,128)(2,1)S(1)}, bf16[44,1152]{1,0:T(8,128)(2,1)S(1)}, u32[]{:S(2)}, u32[]{:S(2)}) collective-permute-start(bf16[44,1152]{1,0:T(8,128)(2,1)S(1)} %get-tuple-element.59), channel_id=1, source_target_pairs={{0,17},{1,16},{16,1},{17,0},{2,19},{3,18},{18,3},{19,2},{4,21},{5,... | collective-permute-start | bytes 304136 | tf_op jit(solution)/shard_map/ppermute | solution.py:359
  (11 other events, 84.7 us)
Sparse Core Ops, SparseCore 0:
  26.3 48.4 all-gather.1
  77.4 44.3 reduce-scatter.1

commit v7 on v6

--- a/solution.py
+++ b/solution.py
@@ -13,7 +13,6 @@
 VMEM_LIMIT = 56 * 1024 * 1024
 IN_VMEM = pl.BlockSpec(memory_space=pltpu.VMEM)
 SMALL = pl.CostEstimate(flops=1000, bytes_accessed=1000, transcendentals=0)
-INPUT_FLOPS = 1e3
 MARK_FLOPS = 1e12
 DELTA_FLOPS = 1e11
 REST_FLOPS = 1e11
@@ -23,6 +22,10 @@
 def shift(x, axis, k):
     n = lax.axis_size(axis)
     return lax.ppermute(x, axis, [(i, (i + k) % n) for i in range(n)])
+
+
+def both_flipped(x):
+    return lax.ppermute(x, ("x_hi", "core"), [(i, 3 - i) for i in range(4)])
 
 
 def add(*xs):
@@ -79,7 +82,7 @@
     )(*after)
 
 
-INPUT_ORDER = ((0, 0), (0, 1), (0, 3), (0, 2), (1, 0), (1, 1), (1, 3), (1, 2))
+INPUT_ORDER = ((0, 0), (0, 1), (0, 3), (1, 0), (0, 2), (1, 1), (1, 3), (1, 2))
 TOKEN_ORDER = ((1, 2), (1, 1), (1, 3), (0, 2), (1, 0), (0, 1), (0, 3), (0, 0))
 
 
@@ -128,6 +131,29 @@
     )(place, tokens, gate, up)
 
 
+def cut_body(s_ref, x_ref, m0_ref, m1_ref, o0_ref, o1_ref):
+    n = m0_ref.shape[0]
+    x = x_ref[...].astype(F32)
+    parts = [x[i * n : (i + 1) * n] for i in range(4)]
+    low = s_ref[3] == 0
+    m0_ref[...] = jnp.where(low, parts[0], parts[1]).astype(BF)
+    m1_ref[...] = jnp.where(low, parts[1], parts[0]).astype(BF)
+    o0_ref[...] = jnp.where(low, parts[2], parts[3]).astype(BF)
+    o1_ref[...] = jnp.where(low, parts[3], parts[2]).astype(BF)
+
+
+def cut_sums(place, sums):
+    rows, cols = sums.shape
+    return pl.pallas_call(
+        cut_body,
+        out_shape=[jax.ShapeDtypeStruct((rows // 4, cols), BF)] * 4,
+        in_specs=[IN_SMEM, IN_VMEM],
+        out_specs=[IN_VMEM] * 4,
+        cost_estimate=SMALL,
+        name="cut_sums",
+    )(place, sums)
+
+
 def join_body(s_ref, m0_ref, m1_ref, o0_ref, o1_ref, out_ref):
     x_lo, y, core = s_ref[0], s_ref[1], s_ref[2]
     n = m0_ref.shape[1] // 8
@@ -215,7 +241,7 @@
     rows, d = x.shape
     cols = delta.shape[1]
     start = first // 128 * 128
-    need = -(-(first + count) // 128) * 128 if first == 0 else d
+    need = min(d, -(-(first + count) // 128) * 128)
     after = [] if after is None else [after]
     return pl.pallas_call(
         functools.partial(weight_body, scale, start, first - start, len(after)),
@@ -256,37 +282,34 @@
         for c in copies:
             c.wait()
 
-    if done:
-        out_ref[:, :done] = extra[0][...]
+    at = 0
+    for ref in extra if done else ():
+        out_ref[:, at : at + ref.shape[1]] = ref[...]
+        at += ref.shape[1]
     out_ref[:, done:] = lax.dot_general(
         d_ref[...], w[...], (((1,), (1,)), ((), ())), preferred_element_type=F32
     ).astype(BF)
 
 
-def input_product(delta, blocks, after, cost, tile=352):
+def input_product(delta, blocks, before=(), tile=352):
     rows, cols = delta.shape
     n = len(blocks)
-    done = after.shape[1] if after.shape[0] == rows else 0
+    done = sum(b.shape[1] for b in before)
     size = n * blocks[0].size // cols
     d = done + size
-    if done:
-        extra = pl.BlockSpec((tile, done), lambda i: (i, 0))
-    else:
-        extra = pl.BlockSpec(memory_space=pl.ANY)
     return pl.pallas_call(
         functools.partial(input_body, n, done),
         out_shape=jax.ShapeDtypeStruct((rows, d), BF),
         grid=(rows // tile,),
         in_specs=[pl.BlockSpec(memory_space=pl.ANY)] * n
-        + [extra, pl.BlockSpec((tile, cols), lambda i: (i, 0))],
+        + [pl.BlockSpec((tile, b.shape[1]), lambda i: (i, 0)) for b in before]
+        + [pl.BlockSpec((tile, cols), lambda i: (i, 0))],
         out_specs=pl.BlockSpec((tile, d), lambda i: (i, 0)),
         scratch_shapes=[pltpu.VMEM((size, cols), BF), pltpu.SemaphoreType.DMA((n,))],
         compiler_params=pltpu.CompilerParams(vmem_limit_bytes=40 * 1024 * 1024),
-        cost_estimate=pl.CostEstimate(
-            flops=int(cost), bytes_accessed=1000, transcendentals=0
-        ),
-        name=f"input_product_{done}",
-    )(*blocks, after, delta)
+        cost_estimate=SMALL,
+        name=f"input_product_{n}",
+    )(*blocks, *before, delta)
 
 
 def gather_weights(w, after, then):
@@ -295,16 +318,16 @@
     far, below, above, after = lax.optimization_barrier((far, below, above, after))
     far_below, far_above = shift(below, "x_lo", 1), shift(far, "y", -1)
     across = shift(below, "y", 1)
-    then = then(after)
+    then = then(after, [w, above, below, far])
     far_below, far_above, then = lax.optimization_barrier((far_below, far_above, then))
     last = [shift(far_below[:, :half], "y", 1), shift(far_above[:, half:], "y", -1)]
-    return [w, above, below, across, far, far_above, far_below], last, then
-
-
-def scatter_grads(first, rest):
-    across = shift(first[0], "x_lo", 1)
-    far_right, far_left = shift(first[1], "y", 1), shift(first[2], "y", -1)
-    far, far_own, up, down, own = rest
+    return [across, far_above, far_below], last, then
+
+
+def scatter_grads(blocks):
+    across, far_up, far_down, far, far_own, up, down, own = blocks
+    across = shift(across, "x_lo", 1)
+    far_right, far_left = shift(far_up, "y", 1), shift(far_down, "y", -1)
     right, left = add_halves(far, across)
     right, left = shift(right, "y", 1), shift(left, "y", -1)
     far_own = shift(add(far_own, far_left, far_right), "x_lo", 1)
@@ -331,35 +354,32 @@
     x = lax.all_gather(block, "z", axis=0, tiled=True).reshape(-1, keep.shape[1])
     mine = make_deltas(gate_pre, up_pre, cotangent)
 
-    def both_cores(mine):
+    def first_part(mine, blocks):
         other = shift(mine, "core", 1)
         delta = jnp.stack([a.reshape(8, 2 * rows, -1) for a in (mine, other)], 1)
-        return delta.reshape(-1, 2 * hidden)
-
-    early, late, delta = gather_weights(w, mine, both_cores)
-
-    part = input_product(delta, early, place.reshape(1, -1), INPUT_FLOPS)
-    part = input_product(delta, late, part, 1e3)
+        delta = delta.reshape(-1, 2 * hidden)
+        return delta, input_product(delta, blocks)
+
+    middle, last, (delta, part) = gather_weights(w, mine, first_part)
+    part = [part, input_product(delta, middle)]
+    part = input_product(delta, last, part)
     sums = lax.psum_scatter(part, "z", scatter_dimension=0, tiled=True)
 
-    first = weight_product(x, delta, scale, 0, 3 * owned, owned, 1e3)
+    first = weight_product(x, delta, scale, 0, owned, owned, 1e3)
+    middle = weight_product(
+        x, delta, scale, owned, 3 * owned, owned, REST_FLOPS, mark("sent", *first)
+    )
     rest = weight_product(
-        x, delta, scale, 3 * owned, 5 * owned, owned, REST_FLOPS, mark("sent", *first)
-    )
-    own, *terms = scatter_grads(first, rest)
-
-    sums = sums.reshape(2, 2, rows, -1)
-    here = jnp.where(x_hi == 0, sums[:, 0], sums[:, 1])
-    there = jnp.where(x_hi == 0, sums[:, 1], sums[:, 0])
-    input_grad = join_columns(
-        place,
-        here[0],
-        shift(there[0], "x_hi", 1),
-        shift(here[1], "core", 1),
-        lax.ppermute(there[1], ("x_hi", "core"), [(i, 3 - i) for i in range(4)]),
-    )
-    input_grad, own = lax.optimization_barrier((input_grad, own))
-    grads = add(own, *terms)
+        x, delta, scale, 4 * owned, 4 * owned, owned, REST_FLOPS, mark("sent_too", *middle)
+    )
+    terms = scatter_grads(first + middle + rest)
+
+    here, there, here_other, there_other = cut_sums(place, sums)
+    parts = [here, shift(there, "x_hi", 1), both_flipped(there_other)]
+    parts.append(shift(here_other, "core", 1))
+    grads = add(*terms)
+    grads, *parts = lax.optimization_barrier((grads, *parts))
+    input_grad = join_columns(place, *parts)
     return input_grad, grads[:, :hidden], grads[:, hidden:]
 
 

time: 149 us -> 147 us (0.987); the launches traced: 149 us -> 144 us
  Pallas kernels: 46.9 us -> 56.6 us
  waiting for transfers between devices: 36.8 us -> 31.9 us
  starting transfers between devices: 36.6 us -> 32.1 us
  local copies, waits for them, and re-layouts: 5.55 us -> 1.7 us
    pallas_call x2 -> x3, Pallas kernels: 17.1 us -> 21.9 us  [weight_product(): pl.pallas_call(functools.partial(weight_body, scale, start, first - start...]
    ppermute x1, waiting for transfers between devices: 3.55 us -> 0.01 us  [both_flipped(): return lax.ppermute(x, ('x_hi', 'core'), [(i, 3 - i) for i in range(4)])]
    ppermute x21, starting transfers between devices: 31.8 us -> 28.6 us  [shift(): return lax.ppermute(x, axis, [(i, (i + k) % n) for i in range(n)])]
    reduce_scatter x1, waiting for transfers between devices: 2.94 us -> 0.35 us  [per_device(): sums = lax.psum_scatter(part, 'z', scatter_dimension=0, tiled=True)]
    pallas_call x2 -> x3, Pallas kernels: 13.1 us -> 15.5 us  [input_product(): pl.pallas_call(functools.partial(input_body, n, done), out_shape=jax.Shap...]
    all_gather x1, waiting for transfers between devices: 1.72 us -> 4.13 us  [per_device(): lax.all_gather(block, 'z', axis=0, tiled=True).reshape(-1, keep.shape[1])]
    unnamed x22 -> x18, local copies, waits for them, and re-layouts: 2.85 us -> 0.75 us
    pallas_call x0 -> x1, Pallas kernels: none -> 1.83 us  [cut_sums(): pl.pallas_call(cut_body, out_shape=[jax.ShapeDtypeStruct((rows // 4, cols...]
  transfers between devices with their start and end apart: 24 -> 24, of which waited for: 12 -> 13; matrix products, arithmetic and copies ran while one was open for 6% -> 4% of each run, Pallas kernels for 30% -> 36%
where the time goes in v7:
time: 147 us; the launch traced here: 144 us
  Pallas kernels  56.6 us (39%)
  starting transfers between devices  32.1 us (22%)
  waiting for transfers between devices  31.9 us (22%)
  between operations  14.2 us (10%)
  other arithmetic  7.84 us (5%)
  local copies, waits for them, and re-layouts  1.7 us (1%)
    ppermute x21, starting transfers between devices, shift(): return lax.ppermute(x, axis, [(i, (i + k) % n) for i in range(n)])  28.6 us
    ppermute x21, waiting for transfers between devices, shift(): return lax.ppermute(x, axis, [(i, (i + k) % n) for i in range(n)])  27.4 us
    pallas_call x3, Pallas kernels, weight_product(): pl.pallas_call(functools.partial(weight_body, scale, start, first - start...  21.9 us
    pallas_call x3, Pallas kernels, input_product(): pl.pallas_call(functools.partial(input_body, n, done), out_shape=jax.Shap...  15.5 us
    pallas_call x1, Pallas kernels, make_deltas(): pl.pallas_call(delta_body, out_shape=jax.ShapeDtypeStruct((rows, 2 * cols...  5.91 us
    all_gather x1, waiting for transfers between devices, per_device(): lax.all_gather(block, 'z', axis=0, tiled=True).reshape(-1, keep.shape[1])  4.13 us
    ppermute x1, starting transfers between devices, both_flipped(): return lax.ppermute(x, ('x_hi', 'core'), [(i, 3 - i) for i in range(4)])  3.43 us
  transfers between devices with their start and end apart: 24, of which 13 were waited for; matrix products, arithmetic and copies ran while one was open for 4% of the time, Pallas kernels for 36%

profile of v7, /device:TPU:1, one launch (start us, length us, event | category | flops | bytes accessed | tf_op | source)
XLA Modules:
  0.0 144.3 jit_solution(4967722595950204805)
XLA Ops:
  7.8 2.8 %prologue.1 = (bf16[44,1152]{1,0:T(8,128)(2,1)}, bf16[44,1152]{1,0:T(8,128)(2,1)}, bf16[144,2304]{1,0:T(8,128)(2,1)}) custom-call(s32[4]{0:T(128)} %pad_add_fusion.s_ref, bf16[44,2304]{1,0:T(8,128)(2,1)} %x_ref.1, bf16[144,1152]{1,0:T(8,128)(2,1)} %g_ref.1, bf16[144,1152]{1,0:T(8,128)(2,1)} %u_ref.2), custom_call_target="tpu_custom_call" | custom-call | flops 1000 | bytes 1000 | tf_op jit(solution)/shard_map/prologue/pallas_call | solution.py:120
  10.6 3.2 %collective-permute-start = (bf16[44,1152]{1,0:T(8,128)(2,1)}, bf16[44,1152]{1,0:T(8,128)(2,1)S(1)}, u32[]{:S(2)}, u32[]{:S(2)}) collective-permute-start(bf16[44,1152]{1,0:T(8,128)(2,1)} %get-tuple-element.37), channel_id=1, source_target_pairs={{0,1},{1,0},{2,3},{3,2},{4,5},{5,4},{6,7},{7,6},{8,9},{9,8},{10,11... | collective-permute-start | bytes 304136 | tf_op jit(solution)/shard_map/ppermute | solution.py:24
  20.1 4.1 %collective-permute-done.1 = bf16[2,44,1152]{2,1,0:T(8,128)(2,1)S(1)} collective-permute-done((bf16[2,44,1152]{2,1,0:T(8,128)(2,1)S(1)}, bf16[2,44,1152]{2,1,0:T(8,128)(2,1)S(1)}, u32[]{:S(2)}, u32[]{:S(2)}) %collective-permute-start.1) | collective-permute-done | bytes 202784 | tf_op jit(solution)/shard_map/ppermute | solution.py:24
  26.2 5.9 %deltas.1 = bf16[704,2304]{1,0:T(8,128)(2,1)} custom-call(bf16[704,1152]{1,0:T(8,128)(2,1)} %g_ref.2, bf16[704,1152]{1,0:T(8,128)(2,1)} %u_ref.3, bf16[704,1152]{1,0:T(8,128)(2,1)} %c_ref.1), custom_call_target="tpu_custom_call" | custom-call | flops 99999997952 | bytes 1000 | tf_op jit(solution)/shard_map/deltas/pallas_call | solution.py:56
  32.1 4.7 %collective-permute-done.2.refs_3_ = bf16[144,2304]{1,0:T(8,128)(2,1)S(1)} collective-permute-done((bf16[144,2304]{1,0:T(8,128)(2,1)}, bf16[144,2304]{1,0:T(8,128)(2,1)S(1)}, u32[]{:S(2)}, u32[]{:S(2)}) %collective-permute-start.2) | collective-permute-done | bytes 663584 | tf_op jit(solution)/shard_map/ppermute | solution.py:24
  39.2 2.7 %collective-permute-start.6 = (bf16[144,2304]{1,0:T(8,128)(2,1)S(1)}, bf16[144,2304]{1,0:T(8,128)(2,1)S(1)}, u32[]{:S(2)}, u32[]{:S(2)}) collective-permute-start(bf16[144,2304]{1,0:T(8,128)(2,1)S(1)} %collective-permute-done.2.refs_3_), channel_id=1, source_target_pairs={{0,6},{2,0},{4,2},{6,4},{1,7},{3,1},{5,3},{7,5},{8,14},{10,8},{12,... | collective-permute-start | bytes 1990664 | tf_op jit(solution)/shard_map/ppermute | solution.py:24
  43.6 2.5 %pad_maximum_fusion = bf16[8,2,88,2304]{3,2,1,0:T(8,128)(2,1)S(1)} fusion(bf16[8,1,88,2304]{3,2,1,0:T(8,128)(2,1)S(1)} %bitcast.24, bf16[8,1,88,2304]{3,2,1,0:T(8,128)(2,1)} %bitcast.23), kind=kLoop, calls=%fused_computation | loop fusion | flops 3244032 | bytes 12976128 | tf_op jit(solution)/shard_map/stack | solution.py:359
  46.2 6.8 %input_product_4.1.refs_2_ = bf16[1408,576]{1,0:T(8,128)(2,1)S(1)} custom-call(bf16[144,2304]{1,0:T(8,128)(2,1)S(1)} %copy-done.1, bf16[144,2304]{1,0:T(8,128)(2,1)S(1)} %collective-permute-done.4.refs_1_, bf16[144,2304]{1,0:T(8,128)(2,1)S(1)} %collective-permute-done.3.refs_2_, bf16[144,2304]{1,0:T(8,128)(2,1)S(1)} %collective-permute-done.2.refs_3_, ...), custom_call_target="tpu_custom_call" | custom-call | flops 1000 | bytes 1000 | tf_op jit(solution)/shard_map/input_product_4/pallas_call | solution.py:300
  56.8 2.9 %collective-permute-start.17 = (bf16[144,1152]{1,0:T(8,128)(2,1)S(1)}, bf16[144,1152]{1,0:T(8,128)(2,1)S(1)}, u32[]{:S(2)}, u32[]{:S(2)}) collective-permute-start(bf16[144,1152]{1,0:T(8,128)(2,1)S(1)} %slice.13), channel_id=1, source_target_pairs={{0,6},{2,0},{4,2},{6,4},{1,7},{3,1},{5,3},{7,5},{8,14},{10,8},{12,... | collective-permute-start | bytes 995336 | tf_op jit(solution)/shard_map/ppermute | solution.py:24
  59.8 4.8 %input_product_3.1.refs_3_ = bf16[1408,432]{1,0:T(8,128)(2,1)S(1)} custom-call(bf16[144,2304]{1,0:T(8,128)(2,1)S(1)} %collective-permute-done.18.refs_0_, bf16[144,2304]{1,0:T(8,128)(2,1)S(1)} %collective-permute-done.6.refs_1_, bf16[144,2304]{1,0:T(8,128)(2,1)S(1)} %collective-permute-done.5.refs_2_, bf16[1408,2304]{1,0:T(8,128)(2,1)S(1)} %bitcast.15), custom_call_target="tpu_custom_call" | custom-call | flops 1000 | bytes 1000 | tf_op jit(solution)/shard_map/input_product_3/pallas_call | solution.py:300
  66.6 3.9 %input_product_2.1 = bf16[1408,1152]{1,0:T(8,128)(2,1)} custom-call(bf16[144,1152]{1,0:T(8,128)(2,1)S(1)} %collective-permute-done.16.refs_0_, bf16[144,1152]{1,0:T(8,128)(2,1)S(1)} %collective-permute-done.17.refs_1_, bf16[1408,576]{1,0:T(8,128)(2,1)S(1)} %input_product_4.1.refs_2_, bf16[1408,432]{1,0:T(8,128)(2,1)S(1)} %input_product_3.1.refs_3_, ...), custom_call_target="tpu_custom_call" | custom-call | flops 1000 | bytes 1000 | tf_op jit(solution)/shard_map/input_product_2/pallas_call | solution.py:300
  70.6 4.1 %all-gather.2.cloned.1.call-done = bf16[16,88,1152]{2,1,0:T(8,128)(2,1)} async-done(((bf16[2,88,1152]{2,1,0:T(8,128)(2,1)}), bf16[16,88,1152]{2,1,0:T(8,128)(2,1)}) %all-gather.2.cloned.1.call-update) | async-done | bytes 3244048 | tf_op jit(solution)/shard_map/all_gather | solution.py:354
  74.7 5.5 %weight_product_0.1.refs_0_ = bf16[144,2304]{1,0:T(8,128)(2,1)} custom-call(bf16[1408,1152]{1,0:T(8,128)(2,1)} %bitcast.20, bf16[1408,2304]{1,0:T(8,128)(2,1)} %bitcast.17), custom_call_target="tpu_custom_call" | custom-call | flops 1000 | bytes 1000 | tf_op jit(solution)/shard_map/weight_product_0/pallas_call | solution.py:246
  82.0 7.5 %weight_product_144.1 = (bf16[144,2304]{1,0:T(8,128)(2,1)}, bf16[144,2304]{1,0:T(8,128)(2,1)}, bf16[144,2304]{1,0:T(8,128)(2,1)}) custom-call(bf16[1408,1152]{1,0:T(8,128)(2,1)} %bitcast.21, bf16[1408,2304]{1,0:T(8,128)(2,1)} %bitcast.18, f32[8,128]{1,0:T(8,128)} %sent.1.refs_0_), custom_call_target="tpu_custom_call" | custom-call | flops 99999997952 | bytes 1000 | tf_op jit(solution)/shard_map/weight_product_144/pallas_call | solution.py:246
  89.5 2.5 %collective-permute-start.13 = (bf16[144,2304]{1,0:T(8,128)(2,1)}, bf16[144,2304]{1,0:T(8,128)(2,1)}, u32[]{:S(2)}, u32[]{:S(2)}) collective-permute-start(bf16[144,2304]{1,0:T(8,128)(2,1)} %get-tuple-element.47.refs_1_), channel_id=1, source_target_pairs={{0,6},{2,0},{4,2},{6,4},{1,7},{3,1},{5,3},{7,5},{8,14},{10,8},{12,... | collective-permute-start | bytes 1990664 | tf_op jit(solution)/shard_map/ppermute | solution.py:24
  92.5 8.9 %weight_product_576.1 = (bf16[144,2304]{1,0:T(8,128)(2,1)}, bf16[144,2304]{1,0:T(8,128)(2,1)}, bf16[144,2304]{1,0:T(8,128)(2,1)}, bf16[144,2304]{1,0:T(8,128)(2,1)}) custom-call(bf16[1408,1152]{1,0:T(8,128)(2,1)} %bitcast.22, bf16[1408,2304]{1,0:T(8,128)(2,1)} %bitcast.19, f32[8,128]{1,0:T(8,128)} %sent_too.1.refs_0_), custom_call_target="tpu_custom_call" | custom-call | flops 99999997952 | bytes 1000 | tf_op jit(solution)/shard_map/weight_product_576/pallas_call | solution.py:246
  103.7 2.7 %collective-permute-start.10 = (bf16[144,1152]{1,0:T(8,128)(2,1)}, bf16[144,1152]{1,0:T(8,128)(2,1)S(1)}, u32[]{:S(2)}, u32[]{:S(2)}) collective-permute-start(bf16[144,1152]{1,0:T(8,128)(2,1)} %get-tuple-element.53), channel_id=1, source_target_pairs={{0,6},{2,0},{4,2},{6,4},{1,7},{3,1},{5,3},{7,5},{8,14},{10,8},{12,... | collective-permute-start | bytes 995336 | tf_op jit(solution)/shard_map/ppermute | solution.py:24
  112.1 3.1 %collective-permute-done.9.right_ref = bf16[144,1152]{1,0:T(8,128)(2,1)S(1)} collective-permute-done((bf16[144,1152]{1,0:T(8,128)(2,1)}, bf16[144,1152]{1,0:T(8,128)(2,1)S(1)}, u32[]{:S(2)}, u32[]{:S(2)}) %collective-permute-start.9) | collective-permute-done | bytes 331808 | tf_op jit(solution)/shard_map/ppermute | solution.py:24
  115.9 2.7 %merge.1 = (bf16[144,2304]{1,0:T(8,128)(2,1)}, bf16[144,2304]{1,0:T(8,128)(2,1)}) custom-call(bf16[144,2304]{1,0:T(8,128)(2,1)} %get-tuple-element.50.up_ref, bf16[144,1152]{1,0:T(8,128)(2,1)} %copy-done.5, bf16[144,2304]{1,0:T(8,128)(2,1)} %get-tuple-element.52.down_ref, bf16[144,1152]{1,0:T(8,128)(2,1)} %copy-done.4), custom_call_target="tpu_custom_call" | custom-call | flops 1000 | bytes 1000 | tf_op jit(solution)/shard_map/merge/pallas_call | solution.py:230
  118.6 2.7 %collective-permute-start.12 = (bf16[144,2304]{1,0:T(8,128)(2,1)}, bf16[144,2304]{1,0:T(8,128)(2,1)S(1)}, u32[]{:S(2)}, u32[]{:S(2)}) collective-permute-start(bf16[144,2304]{1,0:T(8,128)(2,1)} %get-tuple-element.55), channel_id=1, source_target_pairs={{0,6},{2,0},{4,2},{6,4},{1,7},{3,1},{5,3},{7,5},{8,14},{10,8},{12,... | collective-permute-start | bytes 1990664 | tf_op jit(solution)/shard_map/ppermute | solution.py:24
  123.5 2.7 %collective-permute-start.19 = (bf16[44,1152]{1,0:T(8,128)(2,1)}, bf16[44,1152]{1,0:T(8,128)(2,1)S(1)}, u32[]{:S(2)}, u32[]{:S(2)}) collective-permute-start(bf16[44,1152]{1,0:T(8,128)(2,1)} %get-tuple-element.61), channel_id=1, source_target_pairs={{0,16},{16,0},{1,17},{17,1},{2,18},{18,2},{3,19},{19,3},{4,20},{20... | collective-permute-start | bytes 304136 | tf_op jit(solution)/shard_map/ppermute | solution.py:24
  126.2 3.4 %collective-permute-start.20 = (bf16[44,1152]{1,0:T(8,128)(2,1)}, bf16[44,1152]{1,0:T(8,128)(2,1)S(1)}, u32[]{:S(2)}, u32[]{:S(2)}) collective-permute-start(bf16[44,1152]{1,0:T(8,128)(2,1)} %get-tuple-element.62), channel_id=1, source_target_pairs={{0,17},{1,16},{16,1},{17,0},{2,19},{3,18},{18,3},{19,2},{4,21},{5,... | collective-permute-start | bytes 304136 | tf_op jit(solution)/shard_map/ppermute | solution.py:28
  129.6 4.0 %collective-permute-done.11 = bf16[144,2304]{1,0:T(8,128)(2,1)S(1)} collective-permute-done((bf16[144,2304]{1,0:T(8,128)(2,1)}, bf16[144,2304]{1,0:T(8,128)(2,1)S(1)}, u32[]{:S(2)}, u32[]{:S(2)}) %collective-permute-start.11) | collective-permute-done | bytes 663584 | tf_op jit(solution)/shard_map/ppermute | solution.py:24
  135.0 2.5 %join_columns.1 = bf16[44,2304]{1,0:T(8,128)(2,1)} custom-call(s32[4]{0:T(128)} %pad_add_fusion.s_ref, bf16[44,1152]{1,0:T(8,128)(2,1)} %get-tuple-element.64.m0_ref, bf16[44,1152]{1,0:T(8,128)(2,1)} %copy-done.6, bf16[44,1152]{1,0:T(8,128)(2,1)} %copy-done.7, bf16[44,1152]{1,0:T(8,128)(2,1)} %copy-done.8), custom_call_target="tpu_custom_call" | custom-call | flops 1000 | bytes 1000 | tf_op jit(solution)/shard_map/join_columns/pallas_call | solution.py:180
  (67 shorter events, 33.4 us)
Async XLA Ops:
  7.2 67.6 %all-gather.2.cloned.1.call-start = ((), (), s32[]{:S(2)}) async-start(), calls=%async_computation.1 | async-start | bytes 3649536 | tf_op jit(solution)/shard_map/all_gather | solution.py:354
  10.6 4.4 %collective-permute-start = (bf16[44,1152]{1,0:T(8,128)(2,1)}, bf16[44,1152]{1,0:T(8,128)(2,1)S(1)}, u32[]{:S(2)}, u32[]{:S(2)}) collective-permute-start(bf16[44,1152]{1,0:T(8,128)(2,1)} %get-tuple-element.37), channel_id=1, source_target_pairs={{0,1},{1,0},{2,3},{3,2},{4,5},{5,4},{6,7},{7,6},{8,9},{9,8},{10,11... | collective-permute-start | bytes 304136 | tf_op jit(solution)/shard_map/ppermute | solution.py:24
  16.0 8.2 %collective-permute-start.1 = (bf16[2,44,1152]{2,1,0:T(8,128)(2,1)S(1)}, bf16[2,44,1152]{2,1,0:T(8,128)(2,1)S(1)}, u32[]{:S(2)}, u32[]{:S(2)}) collective-permute-start(bf16[2,44,1152]{2,1,0:T(8,128)(2,1)S(1)} %pad_maximum_fusion.1), channel_id=1, source_target_pairs={{0,16},{16,0},{1,17},{17,1},{2,18},{18,2},{3,19},{19,3},{4,20},{20... | collective-permute-start | bytes 608264 | tf_op jit(solution)/shard_map/ppermute | solution.py:24
  17.1 19.7 %collective-permute-start.2 = (bf16[144,2304]{1,0:T(8,128)(2,1)}, bf16[144,2304]{1,0:T(8,128)(2,1)S(1)}, u32[]{:S(2)}, u32[]{:S(2)}) collective-permute-start(bf16[144,2304]{1,0:T(8,128)(2,1)} %get-tuple-element.39.refs_0_), channel_id=1, source_target_pairs={{0,8},{8,0},{1,9},{9,1},{2,10},{10,2},{3,11},{11,3},{4,12},{12,4},... | collective-permute-start | bytes 1990664 | tf_op jit(solution)/shard_map/ppermute | solution.py:24
  17.4 19.4 %collective-permute-start.3 = (bf16[144,2304]{1,0:T(8,128)(2,1)}, bf16[144,2304]{1,0:T(8,128)(2,1)S(1)}, u32[]{:S(2)}, u32[]{:S(2)}) collective-permute-start(bf16[144,2304]{1,0:T(8,128)(2,1)} %get-tuple-element.39.refs_0_), channel_id=1, source_target_pairs={{0,2},{2,4},{4,6},{6,0},{1,3},{3,5},{5,7},{7,1},{8,10},{10,12},{12... | collective-permute-start | bytes 1990664 | tf_op jit(solution)/shard_map/ppermute | solution.py:24
  18.7 18.1 %collective-permute-start.4 = (bf16[144,2304]{1,0:T(8,128)(2,1)}, bf16[144,2304]{1,0:T(8,128)(2,1)S(1)}, u32[]{:S(2)}, u32[]{:S(2)}) collective-permute-start(bf16[144,2304]{1,0:T(8,128)(2,1)} %get-tuple-element.39.refs_0_), channel_id=1, source_target_pairs={{0,6},{2,0},{4,2},{6,4},{1,7},{3,1},{5,3},{7,5},{8,14},{10,8},{12,... | collective-permute-start | bytes 1990664 | tf_op jit(solution)/shard_map/ppermute | solution.py:24
  26.1 95.5 %reduce-scatter.2.cloned.1.call-start = ((), (), s32[]{:S(2)}) async-start(), calls=%async_computation.2 | async-start | bytes 3649536 | tf_op jit(solution)/shard_map/reduce_scatter | solution.py:366
  36.8 6.8 %collective-permute-start.7 = (bf16[704,2304]{1,0:T(8,128)(2,1)}, bf16[704,2304]{1,0:T(8,128)(2,1)S(1)}, u32[]{:S(2)}, u32[]{:S(2)}) collective-permute-start(bf16[704,2304]{1,0:T(8,128)(2,1)} %deltas.1), channel_id=1, source_target_pairs={{0,1},{1,0},{2,3},{3,2},{4,5},{5,4},{6,7},{7,6},{8,9},{9,8},{10,11... | collective-permute-start | bytes 9732104 | tf_op jit(solution)/shard_map/ppermute | solution.py:24
  38.0 16.6 %collective-permute-start.5 = (bf16[144,2304]{1,0:T(8,128)(2,1)S(1)}, bf16[144,2304]{1,0:T(8,128)(2,1)S(1)}, u32[]{:S(2)}, u32[]{:S(2)}) collective-permute-start(bf16[144,2304]{1,0:T(8,128)(2,1)S(1)} %collective-permute-done.3.refs_2_), channel_id=1, source_target_pairs={{0,8},{8,0},{1,9},{9,1},{2,10},{10,2},{3,11},{11,3},{4,12},{12,4},... | collective-permute-start | bytes 1990664 | tf_op jit(solution)/shard_map/ppermute | solution.py:24
  39.2 16.7 %collective-permute-start.6 = (bf16[144,2304]{1,0:T(8,128)(2,1)S(1)}, bf16[144,2304]{1,0:T(8,128)(2,1)S(1)}, u32[]{:S(2)}, u32[]{:S(2)}) collective-permute-start(bf16[144,2304]{1,0:T(8,128)(2,1)S(1)} %collective-permute-done.2.refs_3_), channel_id=1, source_target_pairs={{0,6},{2,0},{4,2},{6,4},{1,7},{3,1},{5,3},{7,5},{8,14},{10,8},{12,... | collective-permute-start | bytes 1990664 | tf_op jit(solution)/shard_map/ppermute | solution.py:24
  41.9 17.9 %collective-permute-start.18 = (bf16[144,2304]{1,0:T(8,128)(2,1)S(1)}, bf16[144,2304]{1,0:T(8,128)(2,1)S(1)}, u32[]{:S(2)}, u32[]{:S(2)}) collective-permute-start(bf16[144,2304]{1,0:T(8,128)(2,1)S(1)} %collective-permute-done.3.refs_2_), channel_id=1, source_target_pairs={{0,2},{2,4},{4,6},{6,0},{1,3},{3,5},{5,7},{7,1},{8,10},{10,12},{12... | collective-permute-start | bytes 1990664 | tf_op jit(solution)/shard_map/ppermute | solution.py:24
  55.9 10.8 %collective-permute-start.16 = (bf16[144,1152]{1,0:T(8,128)(2,1)S(1)}, bf16[144,1152]{1,0:T(8,128)(2,1)S(1)}, u32[]{:S(2)}, u32[]{:S(2)}) collective-permute-start(bf16[144,1152]{1,0:T(8,128)(2,1)S(1)} %slice.12), channel_id=1, source_target_pairs={{0,2},{2,4},{4,6},{6,0},{1,3},{3,5},{5,7},{7,1},{8,10},{10,12},{12... | collective-permute-start | bytes 995336 | tf_op jit(solution)/shard_map/ppermute | solution.py:24
  56.8 9.8 %collective-permute-start.17 = (bf16[144,1152]{1,0:T(8,128)(2,1)S(1)}, bf16[144,1152]{1,0:T(8,128)(2,1)S(1)}, u32[]{:S(2)}, u32[]{:S(2)}) collective-permute-start(bf16[144,1152]{1,0:T(8,128)(2,1)S(1)} %slice.13), channel_id=1, source_target_pairs={{0,6},{2,0},{4,2},{6,4},{1,7},{3,1},{5,3},{7,5},{8,14},{10,8},{12,... | collective-permute-start | bytes 995336 | tf_op jit(solution)/shard_map/ppermute | solution.py:24
  80.8 20.6 %collective-permute-start.8 = (bf16[144,2304]{1,0:T(8,128)(2,1)}, bf16[144,2304]{1,0:T(8,128)(2,1)}, u32[]{:S(2)}, u32[]{:S(2)}) collective-permute-start(bf16[144,2304]{1,0:T(8,128)(2,1)} %weight_product_0.1.refs_0_), channel_id=1, source_target_pairs={{0,8},{8,0},{1,9},{9,1},{2,10},{10,2},{3,11},{11,3},{4,12},{12,4},... | collective-permute-start | bytes 1990664 | tf_op jit(solution)/shard_map/ppermute | solution.py:24
  89.5 16.9 %collective-permute-start.13 = (bf16[144,2304]{1,0:T(8,128)(2,1)}, bf16[144,2304]{1,0:T(8,128)(2,1)}, u32[]{:S(2)}, u32[]{:S(2)}) collective-permute-start(bf16[144,2304]{1,0:T(8,128)(2,1)} %get-tuple-element.47.refs_1_), channel_id=1, source_target_pairs={{0,6},{2,0},{4,2},{6,4},{1,7},{3,1},{5,3},{7,5},{8,14},{10,8},{12,... | collective-permute-start | bytes 1990664 | tf_op jit(solution)/shard_map/ppermute | solution.py:24
  91.9 16.5 %collective-permute-start.14 = (bf16[144,2304]{1,0:T(8,128)(2,1)}, bf16[144,2304]{1,0:T(8,128)(2,1)}, u32[]{:S(2)}, u32[]{:S(2)}) collective-permute-start(bf16[144,2304]{1,0:T(8,128)(2,1)} %get-tuple-element.46.refs_0_), channel_id=1, source_target_pairs={{0,2},{2,4},{4,6},{6,0},{1,3},{3,5},{5,7},{7,1},{8,10},{10,12},{12... | collective-permute-start | bytes 1990664 | tf_op jit(solution)/shard_map/ppermute | solution.py:24
  103.7 8.3 %collective-permute-start.10 = (bf16[144,1152]{1,0:T(8,128)(2,1)}, bf16[144,1152]{1,0:T(8,128)(2,1)S(1)}, u32[]{:S(2)}, u32[]{:S(2)}) collective-permute-start(bf16[144,1152]{1,0:T(8,128)(2,1)} %get-tuple-element.53), channel_id=1, source_target_pairs={{0,6},{2,0},{4,2},{6,4},{1,7},{3,1},{5,3},{7,5},{8,14},{10,8},{12,... | collective-permute-start | bytes 995336 | tf_op jit(solution)/shard_map/ppermute | solution.py:24
  106.4 8.8 %collective-permute-start.9 = (bf16[144,1152]{1,0:T(8,128)(2,1)}, bf16[144,1152]{1,0:T(8,128)(2,1)S(1)}, u32[]{:S(2)}, u32[]{:S(2)}) collective-permute-start(bf16[144,1152]{1,0:T(8,128)(2,1)} %get-tuple-element.51), channel_id=1, source_target_pairs={{0,2},{2,4},{4,6},{6,0},{1,3},{3,5},{5,7},{7,1},{8,10},{10,12},{12... | collective-permute-start | bytes 995336 | tf_op jit(solution)/shard_map/ppermute | solution.py:24
  110.0 19.6 %collective-permute-start.15 = (bf16[144,2304]{1,0:T(8,128)(2,1)S(1)}, bf16[144,2304]{1,0:T(8,128)(2,1)S(1)}, u32[]{:S(2)}, u32[]{:S(2)}) collective-permute-start(bf16[144,2304]{1,0:T(8,128)(2,1)S(1)} %add_convert_fusion.1), channel_id=1, source_target_pairs={{0,8},{8,0},{1,9},{9,1},{2,10},{10,2},{3,11},{11,3},{4,12},{12,4},... | collective-permute-start | bytes 1990664 | tf_op jit(solution)/shard_map/ppermute | solution.py:24
  118.6 15.0 %collective-permute-start.11 = (bf16[144,2304]{1,0:T(8,128)(2,1)}, bf16[144,2304]{1,0:T(8,128)(2,1)S(1)}, u32[]{:S(2)}, u32[]{:S(2)}) collective-permute-start(bf16[144,2304]{1,0:T(8,128)(2,1)} %get-tuple-element.54), channel_id=1, source_target_pairs={{0,2},{2,4},{4,6},{6,0},{1,3},{3,5},{5,7},{7,1},{8,10},{10,12},{12... | collective-permute-start | bytes 1990664 | tf_op jit(solution)/shard_map/ppermute | solution.py:24
  118.6 15.0 %collective-permute-start.12 = (bf16[144,2304]{1,0:T(8,128)(2,1)}, bf16[144,2304]{1,0:T(8,128)(2,1)S(1)}, u32[]{:S(2)}, u32[]{:S(2)}) collective-permute-start(bf16[144,2304]{1,0:T(8,128)(2,1)} %get-tuple-element.55), channel_id=1, source_target_pairs={{0,6},{2,0},{4,2},{6,4},{1,7},{3,1},{5,3},{7,5},{8,14},{10,8},{12,... | collective-permute-start | bytes 1990664 | tf_op jit(solution)/shard_map/ppermute | solution.py:24
  123.5 10.5 %collective-permute-start.19 = (bf16[44,1152]{1,0:T(8,128)(2,1)}, bf16[44,1152]{1,0:T(8,128)(2,1)S(1)}, u32[]{:S(2)}, u32[]{:S(2)}) collective-permute-start(bf16[44,1152]{1,0:T(8,128)(2,1)} %get-tuple-element.61), channel_id=1, source_target_pairs={{0,16},{16,0},{1,17},{17,1},{2,18},{18,2},{3,19},{19,3},{4,20},{20... | collective-permute-start | bytes 304136 | tf_op jit(solution)/shard_map/ppermute | solution.py:24
  126.2 7.9 %collective-permute-start.20 = (bf16[44,1152]{1,0:T(8,128)(2,1)}, bf16[44,1152]{1,0:T(8,128)(2,1)S(1)}, u32[]{:S(2)}, u32[]{:S(2)}) collective-permute-start(bf16[44,1152]{1,0:T(8,128)(2,1)} %get-tuple-element.62), channel_id=1, source_target_pairs={{0,17},{1,16},{16,1},{17,0},{2,19},{3,18},{18,3},{19,2},{4,21},{5,... | collective-permute-start | bytes 304136 | tf_op jit(solution)/shard_map/ppermute | solution.py:28
  129.6 4.4 %collective-permute-start.21 = (bf16[44,1152]{1,0:T(8,128)(2,1)}, bf16[44,1152]{1,0:T(8,128)(2,1)S(1)}, u32[]{:S(2)}, u32[]{:S(2)}) collective-permute-start(bf16[44,1152]{1,0:T(8,128)(2,1)} %get-tuple-element.63), channel_id=1, source_target_pairs={{0,1},{1,0},{2,3},{3,2},{4,5},{5,4},{6,7},{7,6},{8,9},{9,8},{10,11... | collective-permute-start | bytes 304136 | tf_op jit(solution)/shard_map/ppermute | solution.py:24
  (9 other events, 60.3 us)
Sparse Core Ops, SparseCore 0:
  26.2 48.4 all-gather.1
  77.3 44.2 reduce-scatter.1

commit v8 on v7

--- a/solution.py
+++ b/solution.py
@@ -16,7 +16,6 @@
 MARK_FLOPS = 1e12
 DELTA_FLOPS = 1e11
 REST_FLOPS = 1e11
-IN_SMEM = pl.BlockSpec(memory_space=pltpu.SMEM)
 
 
 def shift(x, axis, k):
@@ -82,7 +81,7 @@
     )(*after)
 
 
-INPUT_ORDER = ((0, 0), (0, 1), (0, 3), (1, 0), (0, 2), (1, 1), (1, 3), (1, 2))
+INPUT_ORDER = ((0, 0), (1, 0), (0, 1), (0, 3), (0, 2), (1, 1), (1, 3), (1, 2))
 TOKEN_ORDER = ((1, 2), (1, 1), (1, 3), (0, 2), (1, 0), (0, 1), (0, 3), (0, 0))
 
 
@@ -91,11 +90,11 @@
     return [jnp.where(y >= 2, one[(i + 2) % 4], one[i]) for i in range(4)]
 
 
-def prologue_body(s_ref, x_ref, g_ref, u_ref, mine_ref, other_ref, w_ref):
+def prologue_body(x_ref, g_ref, u_ref, mine_ref, other_ref, w_ref):
     hidden = g_ref.shape[1]
     w_ref[:, :hidden] = g_ref[...]
     w_ref[:, hidden:] = u_ref[...]
-    x_lo, y, core = s_ref[0], s_ref[1], s_ref[2]
+    x_lo, y, core = (lax.axis_index(a) for a in ("x_lo", "y", "core"))
     n = x_ref.shape[1] // 16
     x = x_ref[...].astype(F32)
     for parity, ref in ((0, mine_ref), (1, other_ref)):
@@ -114,7 +113,7 @@
             ref[:, j * n : (j + 1) * n] = by_a[a][dy].astype(BF)
 
 
-def prologue(place, tokens, gate, up):
+def prologue(tokens, gate, up):
     rows, cols = tokens.shape
     half = jax.ShapeDtypeStruct((rows, cols // 2), BF)
     return pl.pallas_call(
@@ -124,38 +123,38 @@
             half,
             jax.ShapeDtypeStruct((gate.shape[0], 2 * gate.shape[1]), BF),
         ],
-        in_specs=[IN_SMEM] + [IN_VMEM] * 3,
+        in_specs=[IN_VMEM] * 3,
         out_specs=[IN_VMEM] * 3,
         cost_estimate=SMALL,
         name="prologue",
-    )(place, tokens, gate, up)
-
-
-def cut_body(s_ref, x_ref, m0_ref, m1_ref, o0_ref, o1_ref):
+    )(tokens, gate, up)
+
+
+def cut_body(x_ref, m0_ref, m1_ref, o0_ref, o1_ref):
     n = m0_ref.shape[0]
     x = x_ref[...].astype(F32)
     parts = [x[i * n : (i + 1) * n] for i in range(4)]
-    low = s_ref[3] == 0
+    low = lax.axis_index("x_hi") == 0
     m0_ref[...] = jnp.where(low, parts[0], parts[1]).astype(BF)
     m1_ref[...] = jnp.where(low, parts[1], parts[0]).astype(BF)
     o0_ref[...] = jnp.where(low, parts[2], parts[3]).astype(BF)
     o1_ref[...] = jnp.where(low, parts[3], parts[2]).astype(BF)
 
 
-def cut_sums(place, sums):
+def cut_sums(sums):
     rows, cols = sums.shape
     return pl.pallas_call(
         cut_body,
         out_shape=[jax.ShapeDtypeStruct((rows // 4, cols), BF)] * 4,
-        in_specs=[IN_SMEM, IN_VMEM],
+        in_specs=[IN_VMEM],
         out_specs=[IN_VMEM] * 4,
         cost_estimate=SMALL,
         name="cut_sums",
-    )(place, sums)
-
-
-def join_body(s_ref, m0_ref, m1_ref, o0_ref, o1_ref, out_ref):
-    x_lo, y, core = s_ref[0], s_ref[1], s_ref[2]
+    )(sums)
+
+
+def join_body(m0_ref, m1_ref, o0_ref, o1_ref, out_ref):
+    x_lo, y, core = (lax.axis_index(a) for a in ("x_lo", "y", "core"))
     n = m0_ref.shape[1] // 8
 
     def plain(first, second):
@@ -175,16 +174,16 @@
         ).astype(BF)
 
 
-def join_columns(place, *parts):
+def join_columns(*parts):
     rows, cols = parts[0].shape
     return pl.pallas_call(
         join_body,
         out_shape=jax.ShapeDtypeStruct((rows, 2 * cols), BF),
-        in_specs=[IN_SMEM] + [IN_VMEM] * 4,
+        in_specs=[IN_VMEM] * 4,
         out_specs=IN_VMEM,
         cost_estimate=SMALL,
         name="join_columns",
-    )(place, *parts)
+    )(*parts)
 
 
 def weight_body(scale, start, skip, extra, x_ref, d_ref, *refs):
@@ -314,22 +313,23 @@
 
 def gather_weights(w, after, then):
     half = w.shape[1] // 2
-    far, below, above = shift(w, "x_lo", 1), shift(w, "y", 1), shift(w, "y", -1)
-    far, below, above, after = lax.optimization_barrier((far, below, above, after))
+    below, above, far = shift(w, "y", 1), shift(w, "y", -1), shift(w, "x_lo", 1)
+    below, above, far, after = lax.optimization_barrier((below, above, far, after))
     far_below, far_above = shift(below, "x_lo", 1), shift(far, "y", -1)
     across = shift(below, "y", 1)
-    then = then(after, [w, above, below, far])
+    then = then(after, [w, far, above, below])
     far_below, far_above, then = lax.optimization_barrier((far_below, far_above, then))
     last = [shift(far_below[:, :half], "y", 1), shift(far_above[:, half:], "y", -1)]
     return [across, far_above, far_below], last, then
 
 
-def scatter_grads(blocks):
-    across, far_up, far_down, far, far_own, up, down, own = blocks
+def scatter_grads(blocks, others):
+    across, far_up, far_down, far, far_own = blocks
     across = shift(across, "x_lo", 1)
     far_right, far_left = shift(far_up, "y", 1), shift(far_down, "y", -1)
-    right, left = add_halves(far, across)
-    right, left = shift(right, "y", 1), shift(left, "y", -1)
+    halves = add_halves(far, across)
+    up, down, own = others(*halves)
+    right, left = shift(halves[0], "y", 1), shift(halves[1], "y", -1)
     far_own = shift(add(far_own, far_left, far_right), "x_lo", 1)
     up, down = merge(up, right, down, left)
     return own, shift(up, "y", 1), shift(down, "y", -1), far_own
@@ -337,14 +337,11 @@
 
 def per_device(tokens, gate_pre, up_pre, cotangent, gate_weight, up_weight):
     x_hi = lax.axis_index("x_hi")
-    place = jnp.stack(
-        [lax.axis_index(a).astype(jnp.int32) for a in ("x_lo", "y", "core", "x_hi")]
-    )
     scale = 1.0 / math.sqrt(gate_pre.shape[0] * 16)
     rows, hidden = tokens.shape[0], gate_weight.shape[1]
     owned = gate_weight.shape[0]
 
-    keep, give, w = prologue(place, tokens, gate_weight, up_weight)
+    keep, give, w = prologue(tokens, gate_weight, up_weight)
     pair = jnp.stack([keep, shift(give, "core", 1)])
     far = shift(pair, "x_hi", 1)
     block = jnp.where(
@@ -365,21 +362,24 @@
     part = input_product(delta, last, part)
     sums = lax.psum_scatter(part, "z", scatter_dimension=0, tiled=True)
 
-    first = weight_product(x, delta, scale, 0, owned, owned, 1e3)
+    first = weight_product(x, delta, scale, 0, owned, owned, 1e3, tile=hidden)
     middle = weight_product(
-        x, delta, scale, owned, 3 * owned, owned, REST_FLOPS, mark("sent", *first)
+        x, delta, scale, owned, 4 * owned, owned, REST_FLOPS, mark("sent", *first)
     )
-    rest = weight_product(
-        x, delta, scale, 4 * owned, 4 * owned, owned, REST_FLOPS, mark("sent_too", *middle)
-    )
-    terms = scatter_grads(first + middle + rest)
-
-    here, there, here_other, there_other = cut_sums(place, sums)
+
+    def last_products(*after):
+        return weight_product(
+            x, delta, scale, 5 * owned, 3 * owned, owned, REST_FLOPS, mark("sent_too", *after)
+        )
+
+    terms = scatter_grads(first + middle, last_products)
+
+    here, there, here_other, there_other = cut_sums(sums)
     parts = [here, shift(there, "x_hi", 1), both_flipped(there_other)]
     parts.append(shift(here_other, "core", 1))
     grads = add(*terms)
     grads, *parts = lax.optimization_barrier((grads, *parts))
-    input_grad = join_columns(place, *parts)
+    input_grad = join_columns(*parts)
     return input_grad, grads[:, :hidden], grads[:, hidden:]
 
 

time: 147 us -> 147 us (level); the launches traced: 144 us -> 146 us
  starting transfers between devices: 32.1 us -> 34 us
  local copies, waits for them, and re-layouts: 1.7 us -> 3.45 us
    ppermute x21, starting transfers between devices: 28.6 us -> 30.5 us  [shift(): return lax.ppermute(x, axis, [(i, (i + k) % n) for i in range(n)])]
    unnamed x18 -> x22, local copies, waits for them, and re-layouts: 0.75 us -> 2.5 us
  transfers between devices with their start and end apart: 24 -> 24, of which waited for: 13 -> 13; matrix products, arithmetic and copies ran while one was open for 4% -> 4% of each run, Pallas kernels for 36% -> 35%
where the time goes in v8:
time: 147 us; the launch traced here: 146 us
  Pallas kernels  55.9 us (38%)
  starting transfers between devices  34 us (23%)
  waiting for transfers between devices  31.2 us (21%)
  between operations  14.2 us (10%)
  other arithmetic  7.25 us (5%)
  local copies, waits for them, and re-layouts  3.45 us (2%)
    ppermute x21, starting transfers between devices, shift(): return lax.ppermute(x, axis, [(i, (i + k) % n) for i in range(n)])  30.5 us
    ppermute x21, waiting for transfers between devices, shift(): return lax.ppermute(x, axis, [(i, (i + k) % n) for i in range(n)])  26.3 us
    pallas_call x3, Pallas kernels, weight_product(): pl.pallas_call(functools.partial(weight_body, scale, start, first - start...  21.3 us
    pallas_call x3, Pallas kernels, input_product(): pl.pallas_call(functools.partial(input_body, n, done), out_shape=jax.Shap...  15.5 us
    pallas_call x1, Pallas kernels, make_deltas(): pl.pallas_call(delta_body, out_shape=jax.ShapeDtypeStruct((rows, 2 * cols...  5.91 us
    all_gather x1, waiting for transfers between devices, per_device(): lax.all_gather(block, 'z', axis=0, tiled=True).reshape(-1, keep.shape[1])  3.94 us
    ppermute x1, starting transfers between devices, both_flipped(): return lax.ppermute(x, ('x_hi', 'core'), [(i, 3 - i) for i in range(4)])  3.41 us
  transfers between devices with their start and end apart: 24, of which 13 were waited for; matrix products, arithmetic and copies ran while one was open for 4% of the time, Pallas kernels for 35%

profile of v8, /device:TPU:1, one launch (start us, length us, event | category | flops | bytes accessed | tf_op | source)
XLA Modules:
  0.0 145.9 jit_solution(12448155601701012803)
XLA Ops:
  7.2 2.8 %prologue.1 = (bf16[44,1152]{1,0:T(8,128)(2,1)}, bf16[44,1152]{1,0:T(8,128)(2,1)}, bf16[144,2304]{1,0:T(8,128)(2,1)}) custom-call(bf16[44,2304]{1,0:T(8,128)(2,1)} %x_ref.1, bf16[144,1152]{1,0:T(8,128)(2,1)} %g_ref.1, bf16[144,1152]{1,0:T(8,128)(2,1)} %u_ref.2), custom_call_target="tpu_custom_call" | custom-call | flops 1000 | bytes 1000 | tf_op jit(solution)/shard_map/prologue/pallas_call | solution.py:119
  10.0 3.2 %collective-permute-start = (bf16[44,1152]{1,0:T(8,128)(2,1)}, bf16[44,1152]{1,0:T(8,128)(2,1)S(1)}, u32[]{:S(2)}, u32[]{:S(2)}) collective-permute-start(bf16[44,1152]{1,0:T(8,128)(2,1)} %get-tuple-element.37), channel_id=1, source_target_pairs={{0,1},{1,0},{2,3},{3,2},{4,5},{5,4},{6,7},{7,6},{8,9},{9,8},{10,11... | collective-permute-start | bytes 304136 | tf_op jit(solution)/shard_map/ppermute | solution.py:23
  19.5 4.1 %collective-permute-done.1 = bf16[2,44,1152]{2,1,0:T(8,128)(2,1)S(1)} collective-permute-done((bf16[2,44,1152]{2,1,0:T(8,128)(2,1)S(1)}, bf16[2,44,1152]{2,1,0:T(8,128)(2,1)S(1)}, u32[]{:S(2)}, u32[]{:S(2)}) %collective-permute-start.1) | collective-permute-done | bytes 202784 | tf_op jit(solution)/shard_map/ppermute | solution.py:23
  25.6 5.9 %deltas.1 = bf16[704,2304]{1,0:T(8,128)(2,1)} custom-call(bf16[704,1152]{1,0:T(8,128)(2,1)} %g_ref.2, bf16[704,1152]{1,0:T(8,128)(2,1)} %u_ref.3, bf16[704,1152]{1,0:T(8,128)(2,1)} %c_ref.1), custom_call_target="tpu_custom_call" | custom-call | flops 99999997952 | bytes 1000 | tf_op jit(solution)/shard_map/deltas/pallas_call | solution.py:55
  31.5 2.4 %collective-permute-done.2.refs_3_ = bf16[144,2304]{1,0:T(8,128)(2,1)S(1)} collective-permute-done((bf16[144,2304]{1,0:T(8,128)(2,1)}, bf16[144,2304]{1,0:T(8,128)(2,1)S(1)}, u32[]{:S(2)}, u32[]{:S(2)}) %collective-permute-start.2) | collective-permute-done | bytes 663584 | tf_op jit(solution)/shard_map/ppermute | solution.py:23
  38.5 2.7 %collective-permute-start.6 = (bf16[144,2304]{1,0:T(8,128)(2,1)S(1)}, bf16[144,2304]{1,0:T(8,128)(2,1)S(1)}, u32[]{:S(2)}, u32[]{:S(2)}) collective-permute-start(bf16[144,2304]{1,0:T(8,128)(2,1)S(1)} %collective-permute-done.4.refs_1_), channel_id=1, source_target_pairs={{0,6},{2,0},{4,2},{6,4},{1,7},{3,1},{5,3},{7,5},{8,14},{10,8},{12,... | collective-permute-start | bytes 1990664 | tf_op jit(solution)/shard_map/ppermute | solution.py:23
  43.0 2.5 %pad_maximum_fusion = bf16[8,2,88,2304]{3,2,1,0:T(8,128)(2,1)S(1)} fusion(bf16[8,1,88,2304]{3,2,1,0:T(8,128)(2,1)S(1)} %bitcast.20, bf16[8,1,88,2304]{3,2,1,0:T(8,128)(2,1)} %bitcast.19), kind=kLoop, calls=%fused_computation | loop fusion | flops 3244032 | bytes 12976128 | tf_op jit(solution)/shard_map/stack | solution.py:356
  45.6 6.8 %input_product_4.1.refs_2_ = bf16[1408,576]{1,0:T(8,128)(2,1)S(1)} custom-call(bf16[144,2304]{1,0:T(8,128)(2,1)S(1)} %copy-done.1, bf16[144,2304]{1,0:T(8,128)(2,1)S(1)} %collective-permute-done.4.refs_1_, bf16[144,2304]{1,0:T(8,128)(2,1)S(1)} %collective-permute-done.3.refs_2_, bf16[144,2304]{1,0:T(8,128)(2,1)S(1)} %collective-permute-done.2.refs_3_, ...), custom_call_target="tpu_custom_call" | custom-call | flops 1000 | bytes 1000 | tf_op jit(solution)/shard_map/input_product_4/pallas_call | solution.py:299
  56.3 2.9 %collective-permute-start.17 = (bf16[144,1152]{1,0:T(8,128)(2,1)S(1)}, bf16[144,1152]{1,0:T(8,128)(2,1)S(1)}, u32[]{:S(2)}, u32[]{:S(2)}) collective-permute-start(bf16[144,1152]{1,0:T(8,128)(2,1)S(1)} %slice.13), channel_id=1, source_target_pairs={{0,6},{2,0},{4,2},{6,4},{1,7},{3,1},{5,3},{7,5},{8,14},{10,8},{12,... | collective-permute-start | bytes 995336 | tf_op jit(solution)/shard_map/ppermute | solution.py:23
  59.2 4.8 %input_product_3.1.refs_3_ = bf16[1408,432]{1,0:T(8,128)(2,1)S(1)} custom-call(bf16[144,2304]{1,0:T(8,128)(2,1)S(1)} %collective-permute-done.18.refs_0_, bf16[144,2304]{1,0:T(8,128)(2,1)S(1)} %collective-permute-done.6.refs_1_, bf16[144,2304]{1,0:T(8,128)(2,1)S(1)} %collective-permute-done.5.refs_2_, bf16[1408,2304]{1,0:T(8,128)(2,1)S(1)} %bitcast.11), custom_call_target="tpu_custom_call" | custom-call | flops 1000 | bytes 1000 | tf_op jit(solution)/shard_map/input_product_3/pallas_call | solution.py:299
  66.2 4.0 %input_product_2.1 = bf16[1408,1152]{1,0:T(8,128)(2,1)} custom-call(bf16[144,1152]{1,0:T(8,128)(2,1)S(1)} %collective-permute-done.16.refs_0_, bf16[144,1152]{1,0:T(8,128)(2,1)S(1)} %collective-permute-done.17.refs_1_, bf16[1408,576]{1,0:T(8,128)(2,1)S(1)} %input_product_4.1.refs_2_, bf16[1408,432]{1,0:T(8,128)(2,1)S(1)} %input_product_3.1.refs_3_, ...), custom_call_target="tpu_custom_call" | custom-call | flops 1000 | bytes 1000 | tf_op jit(solution)/shard_map/input_product_2/pallas_call | solution.py:299
  70.2 3.9 %all-gather.2.cloned.1.call-done = bf16[16,88,1152]{2,1,0:T(8,128)(2,1)} async-done(((bf16[2,88,1152]{2,1,0:T(8,128)(2,1)}), bf16[16,88,1152]{2,1,0:T(8,128)(2,1)}) %all-gather.2.cloned.1.call-update) | async-done | bytes 3244048 | tf_op jit(solution)/shard_map/all_gather | solution.py:351
  74.1 4.7 %weight_product_0.1.refs_0_ = bf16[144,2304]{1,0:T(8,128)(2,1)} custom-call(bf16[1408,1152]{1,0:T(8,128)(2,1)} %bitcast.16, bf16[1408,2304]{1,0:T(8,128)(2,1)} %bitcast.13), custom_call_target="tpu_custom_call" | custom-call | flops 1000 | bytes 1000 | tf_op jit(solution)/shard_map/weight_product_0/pallas_call | solution.py:245
  81.1 8.4 %weight_product_144.1 = (bf16[144,2304]{1,0:T(8,128)(2,1)}, bf16[144,2304]{1,0:T(8,128)(2,1)}, bf16[144,2304]{1,0:T(8,128)(2,1)}, bf16[144,2304]{1,0:T(8,128)(2,1)}) custom-call(bf16[1408,1152]{1,0:T(8,128)(2,1)} %bitcast.17, bf16[1408,2304]{1,0:T(8,128)(2,1)} %bitcast.14, f32[8,128]{1,0:T(8,128)} %sent.1.refs_0_), custom_call_target="tpu_custom_call" | custom-call | flops 99999997952 | bytes 1000 | tf_op jit(solution)/shard_map/weight_product_144/pallas_call | solution.py:245
  89.4 2.4 %collective-permute-start.13 = (bf16[144,2304]{1,0:T(8,128)(2,1)}, bf16[144,2304]{1,0:T(8,128)(2,1)}, u32[]{:S(2)}, u32[]{:S(2)}) collective-permute-start(bf16[144,2304]{1,0:T(8,128)(2,1)} %get-tuple-element.55), channel_id=1, source_target_pairs={{0,6},{2,0},{4,2},{6,4},{1,7},{3,1},{5,3},{7,5},{8,14},{10,8},{12,... | collective-permute-start | bytes 1990664 | tf_op jit(solution)/shard_map/ppermute | solution.py:23
  91.9 3.9 %collective-permute-done.8.b_ref = bf16[144,2304]{1,0:T(8,128)(2,1)S(1)} collective-permute-done((bf16[144,2304]{1,0:T(8,128)(2,1)S(1)}, bf16[144,2304]{1,0:T(8,128)(2,1)S(1)}, u32[]{:S(2)}, u32[]{:S(2)}) %collective-permute-start.8) | collective-permute-done | bytes 663584 | tf_op jit(solution)/shard_map/ppermute | solution.py:23
  98.9 2.4 %collective-permute-start.10 = (bf16[144,1152]{1,0:T(8,128)(2,1)}, bf16[144,1152]{1,0:T(8,128)(2,1)}, u32[]{:S(2)}, u32[]{:S(2)}) collective-permute-start(bf16[144,1152]{1,0:T(8,128)(2,1)} %get-tuple-element.48.refs_1_), channel_id=1, source_target_pairs={{0,6},{2,0},{4,2},{6,4},{1,7},{3,1},{5,3},{7,5},{8,14},{10,8},{12,... | collective-permute-start | bytes 995336 | tf_op jit(solution)/shard_map/ppermute | solution.py:23
  102.3 8.2 %weight_product_720.1 = (bf16[144,2304]{1,0:T(8,128)(2,1)}, bf16[144,2304]{1,0:T(8,128)(2,1)}, bf16[144,2304]{1,0:T(8,128)(2,1)}) custom-call(bf16[1408,1152]{1,0:T(8,128)(2,1)} %bitcast.18, bf16[1408,2304]{1,0:T(8,128)(2,1)} %bitcast.15, f32[8,128]{1,0:T(8,128)} %sent_too.1.refs_0_), custom_call_target="tpu_custom_call" | custom-call | flops 99999997952 | bytes 1000 | tf_op jit(solution)/shard_map/weight_product_720/pallas_call | solution.py:245
  116.2 2.7 %merge.1 = (bf16[144,2304]{1,0:T(8,128)(2,1)}, bf16[144,2304]{1,0:T(8,128)(2,1)}) custom-call(bf16[144,2304]{1,0:T(8,128)(2,1)} %get-tuple-element.50.up_ref, bf16[144,1152]{1,0:T(8,128)(2,1)} %copy-done.6, bf16[144,2304]{1,0:T(8,128)(2,1)} %get-tuple-element.51.down_ref, bf16[144,1152]{1,0:T(8,128)(2,1)} %collective-permute-done.10.left_ref), custom_call_target="tpu_custom_call" | custom-call | flops 1000 | bytes 1000 | tf_op jit(solution)/shard_map/merge/pallas_call | solution.py:229
  118.8 2.7 %collective-permute-start.12 = (bf16[144,2304]{1,0:T(8,128)(2,1)}, bf16[144,2304]{1,0:T(8,128)(2,1)S(1)}, u32[]{:S(2)}, u32[]{:S(2)}) collective-permute-start(bf16[144,2304]{1,0:T(8,128)(2,1)} %get-tuple-element.53), channel_id=1, source_target_pairs={{0,6},{2,0},{4,2},{6,4},{1,7},{3,1},{5,3},{7,5},{8,14},{10,8},{12,... | collective-permute-start | bytes 1990664 | tf_op jit(solution)/shard_map/ppermute | solution.py:23
  123.3 2.6 %collective-permute-start.19 = (bf16[44,1152]{1,0:T(8,128)(2,1)}, bf16[44,1152]{1,0:T(8,128)(2,1)S(1)}, u32[]{:S(2)}, u32[]{:S(2)}) collective-permute-start(bf16[44,1152]{1,0:T(8,128)(2,1)} %get-tuple-element.61), channel_id=1, source_target_pairs={{0,16},{16,0},{1,17},{17,1},{2,18},{18,2},{3,19},{19,3},{4,20},{20... | collective-permute-start | bytes 304136 | tf_op jit(solution)/shard_map/ppermute | solution.py:23
  125.9 3.4 %collective-permute-start.20 = (bf16[44,1152]{1,0:T(8,128)(2,1)}, bf16[44,1152]{1,0:T(8,128)(2,1)S(1)}, u32[]{:S(2)}, u32[]{:S(2)}) collective-permute-start(bf16[44,1152]{1,0:T(8,128)(2,1)} %get-tuple-element.62), channel_id=1, source_target_pairs={{0,17},{1,16},{16,1},{17,0},{2,19},{3,18},{18,3},{19,2},{4,21},{5,... | collective-permute-start | bytes 304136 | tf_op jit(solution)/shard_map/ppermute | solution.py:27
  130.7 3.7 %collective-permute-done.11 = bf16[144,2304]{1,0:T(8,128)(2,1)S(1)} collective-permute-done((bf16[144,2304]{1,0:T(8,128)(2,1)}, bf16[144,2304]{1,0:T(8,128)(2,1)S(1)}, u32[]{:S(2)}, u32[]{:S(2)}) %collective-permute-start.11) | collective-permute-done | bytes 663584 | tf_op jit(solution)/shard_map/ppermute | solution.py:23
  136.6 2.4 %join_columns.1 = bf16[44,2304]{1,0:T(8,128)(2,1)} custom-call(bf16[44,1152]{1,0:T(8,128)(2,1)} %get-tuple-element.64.m0_ref, bf16[44,1152]{1,0:T(8,128)(2,1)} %copy-done.7, bf16[44,1152]{1,0:T(8,128)(2,1)} %copy-done.8, bf16[44,1152]{1,0:T(8,128)(2,1)} %copy-done.9), custom_call_target="tpu_custom_call" | custom-call | flops 1000 | bytes 1000 | tf_op jit(solution)/shard_map/join_columns/pallas_call | solution.py:179
  (70 shorter events, 38.1 us)
Async XLA Ops:
  7.2 67.0 %all-gather.2.cloned.1.call-start = ((), (), s32[]{:S(2)}) async-start(), calls=%async_computation.1 | async-start | bytes 3649536 | tf_op jit(solution)/shard_map/all_gather | solution.py:351
  10.0 4.4 %collective-permute-start = (bf16[44,1152]{1,0:T(8,128)(2,1)}, bf16[44,1152]{1,0:T(8,128)(2,1)S(1)}, u32[]{:S(2)}, u32[]{:S(2)}) collective-permute-start(bf16[44,1152]{1,0:T(8,128)(2,1)} %get-tuple-element.37), channel_id=1, source_target_pairs={{0,1},{1,0},{2,3},{3,2},{4,5},{5,4},{6,7},{7,6},{8,9},{9,8},{10,11... | collective-permute-start | bytes 304136 | tf_op jit(solution)/shard_map/ppermute | solution.py:23
  15.4 8.2 %collective-permute-start.1 = (bf16[2,44,1152]{2,1,0:T(8,128)(2,1)S(1)}, bf16[2,44,1152]{2,1,0:T(8,128)(2,1)S(1)}, u32[]{:S(2)}, u32[]{:S(2)}) collective-permute-start(bf16[2,44,1152]{2,1,0:T(8,128)(2,1)S(1)} %pad_maximum_fusion.1), channel_id=1, source_target_pairs={{0,16},{16,0},{1,17},{17,1},{2,18},{18,2},{3,19},{19,3},{4,20},{20... | collective-permute-start | bytes 608264 | tf_op jit(solution)/shard_map/ppermute | solution.py:23
  16.5 17.4 %collective-permute-start.2 = (bf16[144,2304]{1,0:T(8,128)(2,1)}, bf16[144,2304]{1,0:T(8,128)(2,1)S(1)}, u32[]{:S(2)}, u32[]{:S(2)}) collective-permute-start(bf16[144,2304]{1,0:T(8,128)(2,1)} %get-tuple-element.39.refs_0_), channel_id=1, source_target_pairs={{0,2},{2,4},{4,6},{6,0},{1,3},{3,5},{5,7},{7,1},{8,10},{10,12},{12... | collective-permute-start | bytes 1990664 | tf_op jit(solution)/shard_map/ppermute | solution.py:23
  17.8 16.1 %collective-permute-start.3 = (bf16[144,2304]{1,0:T(8,128)(2,1)}, bf16[144,2304]{1,0:T(8,128)(2,1)S(1)}, u32[]{:S(2)}, u32[]{:S(2)}) collective-permute-start(bf16[144,2304]{1,0:T(8,128)(2,1)} %get-tuple-element.39.refs_0_), channel_id=1, source_target_pairs={{0,6},{2,0},{4,2},{6,4},{1,7},{3,1},{5,3},{7,5},{8,14},{10,8},{12,... | collective-permute-start | bytes 1990664 | tf_op jit(solution)/shard_map/ppermute | solution.py:23
  19.2 16.7 %collective-permute-start.4 = (bf16[144,2304]{1,0:T(8,128)(2,1)}, bf16[144,2304]{1,0:T(8,128)(2,1)S(1)}, u32[]{:S(2)}, u32[]{:S(2)}) collective-permute-start(bf16[144,2304]{1,0:T(8,128)(2,1)} %get-tuple-element.39.refs_0_), channel_id=1, source_target_pairs={{0,8},{8,0},{1,9},{9,1},{2,10},{10,2},{3,11},{11,3},{4,12},{12,4},... | collective-permute-start | bytes 1990664 | tf_op jit(solution)/shard_map/ppermute | solution.py:23
  25.5 96.0 %reduce-scatter.2.cloned.1.call-start = ((), (), s32[]{:S(2)}) async-start(), calls=%async_computation.2 | async-start | bytes 3649536 | tf_op jit(solution)/shard_map/reduce_scatter | solution.py:363
  36.0 7.1 %collective-permute-start.7 = (bf16[704,2304]{1,0:T(8,128)(2,1)}, bf16[704,2304]{1,0:T(8,128)(2,1)S(1)}, u32[]{:S(2)}, u32[]{:S(2)}) collective-permute-start(bf16[704,2304]{1,0:T(8,128)(2,1)} %deltas.1), channel_id=1, source_target_pairs={{0,1},{1,0},{2,3},{3,2},{4,5},{5,4},{6,7},{7,6},{8,9},{9,8},{10,11... | collective-permute-start | bytes 9732104 | tf_op jit(solution)/shard_map/ppermute | solution.py:23
  37.4 16.6 %collective-permute-start.5 = (bf16[144,2304]{1,0:T(8,128)(2,1)S(1)}, bf16[144,2304]{1,0:T(8,128)(2,1)S(1)}, u32[]{:S(2)}, u32[]{:S(2)}) collective-permute-start(bf16[144,2304]{1,0:T(8,128)(2,1)S(1)} %collective-permute-done.2.refs_3_), channel_id=1, source_target_pairs={{0,8},{8,0},{1,9},{9,1},{2,10},{10,2},{3,11},{11,3},{4,12},{12,4},... | collective-permute-start | bytes 1990664 | tf_op jit(solution)/shard_map/ppermute | solution.py:23
  38.5 16.8 %collective-permute-start.6 = (bf16[144,2304]{1,0:T(8,128)(2,1)S(1)}, bf16[144,2304]{1,0:T(8,128)(2,1)S(1)}, u32[]{:S(2)}, u32[]{:S(2)}) collective-permute-start(bf16[144,2304]{1,0:T(8,128)(2,1)S(1)} %collective-permute-done.4.refs_1_), channel_id=1, source_target_pairs={{0,6},{2,0},{4,2},{6,4},{1,7},{3,1},{5,3},{7,5},{8,14},{10,8},{12,... | collective-permute-start | bytes 1990664 | tf_op jit(solution)/shard_map/ppermute | solution.py:23
  41.3 18.0 %collective-permute-start.18 = (bf16[144,2304]{1,0:T(8,128)(2,1)S(1)}, bf16[144,2304]{1,0:T(8,128)(2,1)S(1)}, u32[]{:S(2)}, u32[]{:S(2)}) collective-permute-start(bf16[144,2304]{1,0:T(8,128)(2,1)S(1)} %collective-permute-done.2.refs_3_), channel_id=1, source_target_pairs={{0,2},{2,4},{4,6},{6,0},{1,3},{3,5},{5,7},{7,1},{8,10},{10,12},{12... | collective-permute-start | bytes 1990664 | tf_op jit(solution)/shard_map/ppermute | solution.py:23
  55.3 10.9 %collective-permute-start.16 = (bf16[144,1152]{1,0:T(8,128)(2,1)S(1)}, bf16[144,1152]{1,0:T(8,128)(2,1)S(1)}, u32[]{:S(2)}, u32[]{:S(2)}) collective-permute-start(bf16[144,1152]{1,0:T(8,128)(2,1)S(1)} %slice.12), channel_id=1, source_target_pairs={{0,2},{2,4},{4,6},{6,0},{1,3},{3,5},{5,7},{7,1},{8,10},{10,12},{12... | collective-permute-start | bytes 995336 | tf_op jit(solution)/shard_map/ppermute | solution.py:23
  56.3 9.9 %collective-permute-start.17 = (bf16[144,1152]{1,0:T(8,128)(2,1)S(1)}, bf16[144,1152]{1,0:T(8,128)(2,1)S(1)}, u32[]{:S(2)}, u32[]{:S(2)}) collective-permute-start(bf16[144,1152]{1,0:T(8,128)(2,1)S(1)} %slice.13), channel_id=1, source_target_pairs={{0,6},{2,0},{4,2},{6,4},{1,7},{3,1},{5,3},{7,5},{8,14},{10,8},{12,... | collective-permute-start | bytes 995336 | tf_op jit(solution)/shard_map/ppermute | solution.py:23
  79.9 15.9 %collective-permute-start.8 = (bf16[144,2304]{1,0:T(8,128)(2,1)S(1)}, bf16[144,2304]{1,0:T(8,128)(2,1)S(1)}, u32[]{:S(2)}, u32[]{:S(2)}) collective-permute-start(bf16[144,2304]{1,0:T(8,128)(2,1)S(1)} %copy-done.5), channel_id=1, source_target_pairs={{0,8},{8,0},{1,9},{9,1},{2,10},{10,2},{3,11},{11,3},{4,12},{12,4},... | collective-permute-start | bytes 1990664 | tf_op jit(solution)/shard_map/ppermute | solution.py:23
  89.4 21.1 %collective-permute-start.13 = (bf16[144,2304]{1,0:T(8,128)(2,1)}, bf16[144,2304]{1,0:T(8,128)(2,1)}, u32[]{:S(2)}, u32[]{:S(2)}) collective-permute-start(bf16[144,2304]{1,0:T(8,128)(2,1)} %get-tuple-element.55), channel_id=1, source_target_pairs={{0,6},{2,0},{4,2},{6,4},{1,7},{3,1},{5,3},{7,5},{8,14},{10,8},{12,... | collective-permute-start | bytes 1990664 | tf_op jit(solution)/shard_map/ppermute | solution.py:23
  91.9 18.6 %collective-permute-start.14 = (bf16[144,2304]{1,0:T(8,128)(2,1)}, bf16[144,2304]{1,0:T(8,128)(2,1)}, u32[]{:S(2)}, u32[]{:S(2)}) collective-permute-start(bf16[144,2304]{1,0:T(8,128)(2,1)} %get-tuple-element.56), channel_id=1, source_target_pairs={{0,2},{2,4},{4,6},{6,0},{1,3},{3,5},{5,7},{7,1},{8,10},{10,12},{12... | collective-permute-start | bytes 1990664 | tf_op jit(solution)/shard_map/ppermute | solution.py:23
  98.9 14.5 %collective-permute-start.10 = (bf16[144,1152]{1,0:T(8,128)(2,1)}, bf16[144,1152]{1,0:T(8,128)(2,1)}, u32[]{:S(2)}, u32[]{:S(2)}) collective-permute-start(bf16[144,1152]{1,0:T(8,128)(2,1)} %get-tuple-element.48.refs_1_), channel_id=1, source_target_pairs={{0,6},{2,0},{4,2},{6,4},{1,7},{3,1},{5,3},{7,5},{8,14},{10,8},{12,... | collective-permute-start | bytes 995336 | tf_op jit(solution)/shard_map/ppermute | solution.py:23
  102.3 13.2 %collective-permute-start.9 = (bf16[144,1152]{1,0:T(8,128)(2,1)S(1)}, bf16[144,1152]{1,0:T(8,128)(2,1)S(1)}, u32[]{:S(2)}, u32[]{:S(2)}) collective-permute-start(bf16[144,1152]{1,0:T(8,128)(2,1)S(1)} %copy-done.10), channel_id=1, source_target_pairs={{0,2},{2,4},{4,6},{6,0},{1,3},{3,5},{5,7},{7,1},{8,10},{10,12},{12... | collective-permute-start | bytes 995336 | tf_op jit(solution)/shard_map/ppermute | solution.py:23
  112.1 17.2 %collective-permute-start.15 = (bf16[144,2304]{1,0:T(8,128)(2,1)S(1)}, bf16[144,2304]{1,0:T(8,128)(2,1)S(1)}, u32[]{:S(2)}, u32[]{:S(2)}) collective-permute-start(bf16[144,2304]{1,0:T(8,128)(2,1)S(1)} %add_convert_fusion.1), channel_id=1, source_target_pairs={{0,8},{8,0},{1,9},{9,1},{2,10},{10,2},{3,11},{11,3},{4,12},{12,4},... | collective-permute-start | bytes 1990664 | tf_op jit(solution)/shard_map/ppermute | solution.py:23
  118.8 15.5 %collective-permute-start.11 = (bf16[144,2304]{1,0:T(8,128)(2,1)}, bf16[144,2304]{1,0:T(8,128)(2,1)S(1)}, u32[]{:S(2)}, u32[]{:S(2)}) collective-permute-start(bf16[144,2304]{1,0:T(8,128)(2,1)} %get-tuple-element.52), channel_id=1, source_target_pairs={{0,2},{2,4},{4,6},{6,0},{1,3},{3,5},{5,7},{7,1},{8,10},{10,12},{12... | collective-permute-start | bytes 1990664 | tf_op jit(solution)/shard_map/ppermute | solution.py:23
  118.8 15.5 %collective-permute-start.12 = (bf16[144,2304]{1,0:T(8,128)(2,1)}, bf16[144,2304]{1,0:T(8,128)(2,1)S(1)}, u32[]{:S(2)}, u32[]{:S(2)}) collective-permute-start(bf16[144,2304]{1,0:T(8,128)(2,1)} %get-tuple-element.53), channel_id=1, source_target_pairs={{0,6},{2,0},{4,2},{6,4},{1,7},{3,1},{5,3},{7,5},{8,14},{10,8},{12,... | collective-permute-start | bytes 1990664 | tf_op jit(solution)/shard_map/ppermute | solution.py:23
  123.3 11.4 %collective-permute-start.19 = (bf16[44,1152]{1,0:T(8,128)(2,1)}, bf16[44,1152]{1,0:T(8,128)(2,1)S(1)}, u32[]{:S(2)}, u32[]{:S(2)}) collective-permute-start(bf16[44,1152]{1,0:T(8,128)(2,1)} %get-tuple-element.61), channel_id=1, source_target_pairs={{0,16},{16,0},{1,17},{17,1},{2,18},{18,2},{3,19},{19,3},{4,20},{20... | collective-permute-start | bytes 304136 | tf_op jit(solution)/shard_map/ppermute | solution.py:23
  125.9 9.8 %collective-permute-start.20 = (bf16[44,1152]{1,0:T(8,128)(2,1)}, bf16[44,1152]{1,0:T(8,128)(2,1)S(1)}, u32[]{:S(2)}, u32[]{:S(2)}) collective-permute-start(bf16[44,1152]{1,0:T(8,128)(2,1)} %get-tuple-element.62), channel_id=1, source_target_pairs={{0,17},{1,16},{16,1},{17,0},{2,19},{3,18},{18,3},{19,2},{4,21},{5,... | collective-permute-start | bytes 304136 | tf_op jit(solution)/shard_map/ppermute | solution.py:27
  129.3 6.4 %collective-permute-start.21 = (bf16[44,1152]{1,0:T(8,128)(2,1)}, bf16[44,1152]{1,0:T(8,128)(2,1)S(1)}, u32[]{:S(2)}, u32[]{:S(2)}) collective-permute-start(bf16[44,1152]{1,0:T(8,128)(2,1)} %get-tuple-element.63), channel_id=1, source_target_pairs={{0,1},{1,0},{2,3},{3,2},{4,5},{5,4},{6,7},{7,6},{8,9},{9,8},{10,11... | collective-permute-start | bytes 304136 | tf_op jit(solution)/shard_map/ppermute | solution.py:23
  (11 other events, 61.0 us)
Sparse Core Ops, SparseCore 0:
  25.7 48.4 all-gather.1
  76.7 44.3 reduce-scatter.1

commit v9 on v8

--- a/solution.py
+++ b/solution.py
@@ -323,13 +323,13 @@
     return [across, far_above, far_below], last, then
 
 
-def scatter_grads(blocks, others):
-    across, far_up, far_down, far, far_own = blocks
+def scatter_grads(blocks):
+    across, far_up, far_down, far, far_own, up, down, own = blocks
     across = shift(across, "x_lo", 1)
     far_right, far_left = shift(far_up, "y", 1), shift(far_down, "y", -1)
-    halves = add_halves(far, across)
-    up, down, own = others(*halves)
-    right, left = shift(halves[0], "y", 1), shift(halves[1], "y", -1)
+    across, far_right, far_left = lax.optimization_barrier((across, far_right, far_left))
+    right, left = add_halves(far, across)
+    right, left = shift(right, "y", 1), shift(left, "y", -1)
     far_own = shift(add(far_own, far_left, far_right), "x_lo", 1)
     up, down = merge(up, right, down, left)
     return own, shift(up, "y", 1), shift(down, "y", -1), far_own
@@ -362,17 +362,11 @@
     part = input_product(delta, last, part)
     sums = lax.psum_scatter(part, "z", scatter_dimension=0, tiled=True)
 
-    first = weight_product(x, delta, scale, 0, owned, owned, 1e3, tile=hidden)
-    middle = weight_product(
-        x, delta, scale, owned, 4 * owned, owned, REST_FLOPS, mark("sent", *first)
+    first = weight_product(x, delta, scale, 0, 3 * owned, owned, 1e3, tile=hidden)
+    rest = weight_product(
+        x, delta, scale, 3 * owned, 5 * owned, owned, REST_FLOPS, mark("sent", *first)
     )
-
-    def last_products(*after):
-        return weight_product(
-            x, delta, scale, 5 * owned, 3 * owned, owned, REST_FLOPS, mark("sent_too", *after)
-        )
-
-    terms = scatter_grads(first + middle, last_products)
+    terms = scatter_grads(first + rest)
 
     here, there, here_other, there_other = cut_sums(sums)
     parts = [here, shift(there, "x_hi", 1), both_flipped(there_other)]

time: 147 us -> 145 us (0.986)
  waiting for transfers between devices: 31.2 us -> 36.2 us
  Pallas kernels: 55.9 us -> 51.3 us
  starting transfers between devices: 34 us -> 31.7 us
    ppermute x21, waiting for transfers between devices: 26.3 us -> 31.2 us  [shift(): return lax.ppermute(x, axis, [(i, (i + k) % n) for i in range(n)])]
    pallas_call x3 -> x2, Pallas kernels: 21.3 us -> 17.3 us  [weight_product(): pl.pallas_call(functools.partial(weight_body, scale, start, first - start...]
    ppermute x21, starting transfers between devices: 30.5 us -> 28.9 us  [shift(): return lax.ppermute(x, axis, [(i, (i + k) % n) for i in range(n)])]
  transfers between devices with their start and end apart: 24 -> 24, of which waited for: 13 -> 15; matrix products, arithmetic and copies ran while one was open for 4% -> 4% of each run, Pallas kernels for 35% -> 32%
where the time goes in v9:
time: 145 us; the launch traced here: 143 us
  Pallas kernels  51.3 us (35%)
  waiting for transfers between devices  36.2 us (25%)
  starting transfers between devices  31.7 us (22%)
  between operations  14.2 us (10%)
  other arithmetic  7.06 us (5%)
  local copies, waits for them, and re-layouts  2.3 us (2%)
    ppermute x21, waiting for transfers between devices, shift(): return lax.ppermute(x, axis, [(i, (i + k) % n) for i in range(n)])  31.2 us
    ppermute x21, starting transfers between devices, shift(): return lax.ppermute(x, axis, [(i, (i + k) % n) for i in range(n)])  28.9 us
    pallas_call x2, Pallas kernels, weight_product(): pl.pallas_call(functools.partial(weight_body, scale, start, first - start...  17.3 us
    pallas_call x3, Pallas kernels, input_product(): pl.pallas_call(functools.partial(input_body, n, done), out_shape=jax.Shap...  15.5 us
    pallas_call x1, Pallas kernels, make_deltas(): pl.pallas_call(delta_body, out_shape=jax.ShapeDtypeStruct((rows, 2 * cols...  5.91 us
    all_gather x1, waiting for transfers between devices, per_device(): lax.all_gather(block, 'z', axis=0, tiled=True).reshape(-1, keep.shape[1])  4.01 us
  transfers between devices with their start and end apart: 24, of which 15 were waited for; matrix products, arithmetic and copies ran while one was open for 4% of the time, Pallas kernels for 32%

profile of v9, /device:TPU:1, one launch (start us, length us, event | category | flops | bytes accessed | tf_op | source)
XLA Modules:
  0.0 142.7 jit_solution(5307054587902743395)
XLA Ops:
  7.2 2.8 %prologue.1 = (bf16[44,1152]{1,0:T(8,128)(2,1)}, bf16[44,1152]{1,0:T(8,128)(2,1)}, bf16[144,2304]{1,0:T(8,128)(2,1)}) custom-call(bf16[44,2304]{1,0:T(8,128)(2,1)} %x_ref.1, bf16[144,1152]{1,0:T(8,128)(2,1)} %g_ref.1, bf16[144,1152]{1,0:T(8,128)(2,1)} %u_ref.2), custom_call_target="tpu_custom_call" | custom-call | flops 1000 | bytes 1000 | tf_op jit(solution)/shard_map/prologue/pallas_call | solution.py:119
  10.1 3.2 %collective-permute-start = (bf16[44,1152]{1,0:T(8,128)(2,1)}, bf16[44,1152]{1,0:T(8,128)(2,1)S(1)}, u32[]{:S(2)}, u32[]{:S(2)}) collective-permute-start(bf16[44,1152]{1,0:T(8,128)(2,1)} %get-tuple-element.41), channel_id=1, source_target_pairs={{0,1},{1,0},{2,3},{3,2},{4,5},{5,4},{6,7},{7,6},{8,9},{9,8},{10,11... | collective-permute-start | bytes 304136 | tf_op jit(solution)/shard_map/ppermute | solution.py:23
  19.5 4.1 %collective-permute-done.1 = bf16[2,44,1152]{2,1,0:T(8,128)(2,1)S(1)} collective-permute-done((bf16[2,44,1152]{2,1,0:T(8,128)(2,1)S(1)}, bf16[2,44,1152]{2,1,0:T(8,128)(2,1)S(1)}, u32[]{:S(2)}, u32[]{:S(2)}) %collective-permute-start.1) | collective-permute-done | bytes 202784 | tf_op jit(solution)/shard_map/ppermute | solution.py:23
  25.6 5.9 %deltas.1 = bf16[704,2304]{1,0:T(8,128)(2,1)} custom-call(bf16[704,1152]{1,0:T(8,128)(2,1)} %g_ref.2, bf16[704,1152]{1,0:T(8,128)(2,1)} %u_ref.3, bf16[704,1152]{1,0:T(8,128)(2,1)} %c_ref.1), custom_call_target="tpu_custom_call" | custom-call | flops 99999997952 | bytes 1000 | tf_op jit(solution)/shard_map/deltas/pallas_call | solution.py:55
  31.5 2.3 %collective-permute-done.2.refs_3_ = bf16[144,2304]{1,0:T(8,128)(2,1)S(1)} collective-permute-done((bf16[144,2304]{1,0:T(8,128)(2,1)}, bf16[144,2304]{1,0:T(8,128)(2,1)S(1)}, u32[]{:S(2)}, u32[]{:S(2)}) %collective-permute-start.2) | collective-permute-done | bytes 663584 | tf_op jit(solution)/shard_map/ppermute | solution.py:23
  38.6 2.7 %collective-permute-start.6 = (bf16[144,2304]{1,0:T(8,128)(2,1)S(1)}, bf16[144,2304]{1,0:T(8,128)(2,1)S(1)}, u32[]{:S(2)}, u32[]{:S(2)}) collective-permute-start(bf16[144,2304]{1,0:T(8,128)(2,1)S(1)} %collective-permute-done.4.refs_1_), channel_id=1, source_target_pairs={{0,6},{2,0},{4,2},{6,4},{1,7},{3,1},{5,3},{7,5},{8,14},{10,8},{12,... | collective-permute-start | bytes 1990664 | tf_op jit(solution)/shard_map/ppermute | solution.py:23
  43.0 2.5 %pad_maximum_fusion = bf16[8,2,88,2304]{3,2,1,0:T(8,128)(2,1)S(1)} fusion(bf16[8,1,88,2304]{3,2,1,0:T(8,128)(2,1)S(1)} %bitcast.18, bf16[8,1,88,2304]{3,2,1,0:T(8,128)(2,1)} %bitcast.17), kind=kLoop, calls=%fused_computation | loop fusion | flops 3244032 | bytes 12976128 | tf_op jit(solution)/shard_map/stack | solution.py:356
  45.6 6.8 %input_product_4.1.refs_2_ = bf16[1408,576]{1,0:T(8,128)(2,1)S(1)} custom-call(bf16[144,2304]{1,0:T(8,128)(2,1)S(1)} %copy-done.1, bf16[144,2304]{1,0:T(8,128)(2,1)S(1)} %collective-permute-done.4.refs_1_, bf16[144,2304]{1,0:T(8,128)(2,1)S(1)} %collective-permute-done.3.refs_2_, bf16[144,2304]{1,0:T(8,128)(2,1)S(1)} %collective-permute-done.2.refs_3_, ...), custom_call_target="tpu_custom_call" | custom-call | flops 1000 | bytes 1000 | tf_op jit(solution)/shard_map/input_product_4/pallas_call | solution.py:299
  56.3 2.9 %collective-permute-start.17 = (bf16[144,1152]{1,0:T(8,128)(2,1)S(1)}, bf16[144,1152]{1,0:T(8,128)(2,1)S(1)}, u32[]{:S(2)}, u32[]{:S(2)}) collective-permute-start(bf16[144,1152]{1,0:T(8,128)(2,1)S(1)} %slice.13), channel_id=1, source_target_pairs={{0,6},{2,0},{4,2},{6,4},{1,7},{3,1},{5,3},{7,5},{8,14},{10,8},{12,... | collective-permute-start | bytes 995336 | tf_op jit(solution)/shard_map/ppermute | solution.py:23
  59.2 4.8 %input_product_3.1.refs_3_ = bf16[1408,432]{1,0:T(8,128)(2,1)S(1)} custom-call(bf16[144,2304]{1,0:T(8,128)(2,1)S(1)} %collective-permute-done.18.refs_0_, bf16[144,2304]{1,0:T(8,128)(2,1)S(1)} %collective-permute-done.6.refs_1_, bf16[144,2304]{1,0:T(8,128)(2,1)S(1)} %collective-permute-done.5.refs_2_, bf16[1408,2304]{1,0:T(8,128)(2,1)S(1)} %bitcast.11), custom_call_target="tpu_custom_call" | custom-call | flops 1000 | bytes 1000 | tf_op jit(solution)/shard_map/input_product_3/pallas_call | solution.py:299
  66.2 3.9 %input_product_2.1 = bf16[1408,1152]{1,0:T(8,128)(2,1)} custom-call(bf16[144,1152]{1,0:T(8,128)(2,1)S(1)} %collective-permute-done.16.refs_0_, bf16[144,1152]{1,0:T(8,128)(2,1)S(1)} %collective-permute-done.17.refs_1_, bf16[1408,576]{1,0:T(8,128)(2,1)S(1)} %input_product_4.1.refs_2_, bf16[1408,432]{1,0:T(8,128)(2,1)S(1)} %input_product_3.1.refs_3_, ...), custom_call_target="tpu_custom_call" | custom-call | flops 1000 | bytes 1000 | tf_op jit(solution)/shard_map/input_product_2/pallas_call | solution.py:299
  70.1 4.0 %all-gather.2.cloned.1.call-done = bf16[16,88,1152]{2,1,0:T(8,128)(2,1)} async-done(((bf16[2,88,1152]{2,1,0:T(8,128)(2,1)}), bf16[16,88,1152]{2,1,0:T(8,128)(2,1)}) %all-gather.2.cloned.1.call-update) | async-done | bytes 3244048 | tf_op jit(solution)/shard_map/all_gather | solution.py:351
  74.2 7.3 %weight_product_0.1 = (bf16[144,2304]{1,0:T(8,128)(2,1)}, bf16[144,2304]{1,0:T(8,128)(2,1)}, bf16[144,2304]{1,0:T(8,128)(2,1)}) custom-call(bf16[1408,1152]{1,0:T(8,128)(2,1)} %bitcast.15, bf16[1408,2304]{1,0:T(8,128)(2,1)} %bitcast.13), custom_call_target="tpu_custom_call" | custom-call | flops 1000 | bytes 1000 | tf_op jit(solution)/shard_map/weight_product_0/pallas_call | solution.py:245
  81.4 2.5 %collective-permute-start.10 = (bf16[144,2304]{1,0:T(8,128)(2,1)}, bf16[144,2304]{1,0:T(8,128)(2,1)}, u32[]{:S(2)}, u32[]{:S(2)}) collective-permute-start(bf16[144,2304]{1,0:T(8,128)(2,1)} %get-tuple-element.52.refs_2_), channel_id=1, source_target_pairs={{0,6},{2,0},{4,2},{6,4},{1,7},{3,1},{5,3},{7,5},{8,14},{10,8},{12,... | collective-permute-start | bytes 1990664 | tf_op jit(solution)/shard_map/ppermute | solution.py:23
  86.2 10.0 %weight_product_432.1 = (bf16[144,2304]{1,0:T(8,128)(2,1)}, bf16[144,2304]{1,0:T(8,128)(2,1)}, bf16[144,2304]{1,0:T(8,128)(2,1)}, bf16[144,2304]{1,0:T(8,128)(2,1)}, bf16[144,2304]{1,0:T(8,128)(2,1)}) custom-call(bf16[1408,1152]{1,0:T(8,128)(2,1)} %bitcast.16, bf16[1408,2304]{1,0:T(8,128)(2,1)} %bitcast.14, f32[8,128]{1,0:T(8,128)} %sent.1.refs_0_), custom_call_target="tpu_custom_call" | custom-call | flops 99999997952 | bytes 1000 | tf_op jit(solution)/shard_map/weight_product_432/pallas_call | solution.py:245
  99.7 3.0 %collective-permute-done.9 = bf16[144,2304]{1,0:T(8,128)(2,1)S(1)} collective-permute-done((bf16[144,2304]{1,0:T(8,128)(2,1)S(1)}, bf16[144,2304]{1,0:T(8,128)(2,1)S(1)}, u32[]{:S(2)}, u32[]{:S(2)}) %collective-permute-start.9) | collective-permute-done | bytes 663584 | tf_op jit(solution)/shard_map/ppermute | solution.py:23
  104.9 2.7 %collective-permute-start.12 = (bf16[144,1152]{1,0:T(8,128)(2,1)}, bf16[144,1152]{1,0:T(8,128)(2,1)S(1)}, u32[]{:S(2)}, u32[]{:S(2)}) collective-permute-start(bf16[144,1152]{1,0:T(8,128)(2,1)} %get-tuple-element.59), channel_id=1, source_target_pairs={{0,6},{2,0},{4,2},{6,4},{1,7},{3,1},{5,3},{7,5},{8,14},{10,8},{12,... | collective-permute-start | bytes 995336 | tf_op jit(solution)/shard_map/ppermute | solution.py:23
  109.3 4.3 %collective-permute-done.11.right_ref = bf16[144,1152]{1,0:T(8,128)(2,1)S(1)} collective-permute-done((bf16[144,1152]{1,0:T(8,128)(2,1)}, bf16[144,1152]{1,0:T(8,128)(2,1)S(1)}, u32[]{:S(2)}, u32[]{:S(2)}) %collective-permute-start.11) | collective-permute-done | bytes 331808 | tf_op jit(solution)/shard_map/ppermute | solution.py:23
  114.5 2.7 %merge.1 = (bf16[144,2304]{1,0:T(8,128)(2,1)}, bf16[144,2304]{1,0:T(8,128)(2,1)}) custom-call(bf16[144,2304]{1,0:T(8,128)(2,1)} %get-tuple-element.54.up_ref, bf16[144,1152]{1,0:T(8,128)(2,1)} %copy-done.4, bf16[144,2304]{1,0:T(8,128)(2,1)} %get-tuple-element.58.down_ref, bf16[144,1152]{1,0:T(8,128)(2,1)} %copy-done.5), custom_call_target="tpu_custom_call" | custom-call | flops 1000 | bytes 1000 | tf_op jit(solution)/shard_map/merge/pallas_call | solution.py:229
  117.2 2.7 %collective-permute-start.14 = (bf16[144,2304]{1,0:T(8,128)(2,1)}, bf16[144,2304]{1,0:T(8,128)(2,1)S(1)}, u32[]{:S(2)}, u32[]{:S(2)}) collective-permute-start(bf16[144,2304]{1,0:T(8,128)(2,1)} %get-tuple-element.61), channel_id=1, source_target_pairs={{0,6},{2,0},{4,2},{6,4},{1,7},{3,1},{5,3},{7,5},{8,14},{10,8},{12,... | collective-permute-start | bytes 1990664 | tf_op jit(solution)/shard_map/ppermute | solution.py:23
  122.7 3.0 %collective-permute-start.19 = (bf16[44,1152]{1,0:T(8,128)(2,1)}, bf16[44,1152]{1,0:T(8,128)(2,1)S(1)}, u32[]{:S(2)}, u32[]{:S(2)}) collective-permute-start(bf16[44,1152]{1,0:T(8,128)(2,1)} %get-tuple-element.69), channel_id=1, source_target_pairs={{0,16},{16,0},{1,17},{17,1},{2,18},{18,2},{3,19},{19,3},{4,20},{20... | collective-permute-start | bytes 304136 | tf_op jit(solution)/shard_map/ppermute | solution.py:23
  125.6 2.7 %collective-permute-start.20 = (bf16[44,1152]{1,0:T(8,128)(2,1)}, bf16[44,1152]{1,0:T(8,128)(2,1)S(1)}, u32[]{:S(2)}, u32[]{:S(2)}) collective-permute-start(bf16[44,1152]{1,0:T(8,128)(2,1)} %get-tuple-element.70), channel_id=1, source_target_pairs={{0,17},{1,16},{16,1},{17,0},{2,19},{3,18},{18,3},{19,2},{4,21},{5,... | collective-permute-start | bytes 304136 | tf_op jit(solution)/shard_map/ppermute | solution.py:27
  128.3 3.8 %collective-permute-done.13 = bf16[144,2304]{1,0:T(8,128)(2,1)S(1)} collective-permute-done((bf16[144,2304]{1,0:T(8,128)(2,1)}, bf16[144,2304]{1,0:T(8,128)(2,1)S(1)}, u32[]{:S(2)}, u32[]{:S(2)}) %collective-permute-start.13) | collective-permute-done | bytes 663584 | tf_op jit(solution)/shard_map/ppermute | solution.py:23
  133.5 2.4 %join_columns.1 = bf16[44,2304]{1,0:T(8,128)(2,1)} custom-call(bf16[44,1152]{1,0:T(8,128)(2,1)} %get-tuple-element.72.m0_ref, bf16[44,1152]{1,0:T(8,128)(2,1)} %copy-done.6, bf16[44,1152]{1,0:T(8,128)(2,1)} %copy-done.7, bf16[44,1152]{1,0:T(8,128)(2,1)} %copy-done.8), custom_call_target="tpu_custom_call" | custom-call | flops 1000 | bytes 1000 | tf_op jit(solution)/shard_map/join_columns/pallas_call | solution.py:179
  (66 shorter events, 35.5 us)
Async XLA Ops:
  7.2 67.0 %all-gather.2.cloned.1.call-start = ((), (), s32[]{:S(2)}) async-start(), calls=%async_computation.1 | async-start | bytes 3649536 | tf_op jit(solution)/shard_map/all_gather | solution.py:351
  10.1 4.4 %collective-permute-start = (bf16[44,1152]{1,0:T(8,128)(2,1)}, bf16[44,1152]{1,0:T(8,128)(2,1)S(1)}, u32[]{:S(2)}, u32[]{:S(2)}) collective-permute-start(bf16[44,1152]{1,0:T(8,128)(2,1)} %get-tuple-element.41), channel_id=1, source_target_pairs={{0,1},{1,0},{2,3},{3,2},{4,5},{5,4},{6,7},{7,6},{8,9},{9,8},{10,11... | collective-permute-start | bytes 304136 | tf_op jit(solution)/shard_map/ppermute | solution.py:23
  15.4 8.2 %collective-permute-start.1 = (bf16[2,44,1152]{2,1,0:T(8,128)(2,1)S(1)}, bf16[2,44,1152]{2,1,0:T(8,128)(2,1)S(1)}, u32[]{:S(2)}, u32[]{:S(2)}) collective-permute-start(bf16[2,44,1152]{2,1,0:T(8,128)(2,1)S(1)} %pad_maximum_fusion.1), channel_id=1, source_target_pairs={{0,16},{16,0},{1,17},{17,1},{2,18},{18,2},{3,19},{19,3},{4,20},{20... | collective-permute-start | bytes 608264 | tf_op jit(solution)/shard_map/ppermute | solution.py:23
  16.5 17.4 %collective-permute-start.2 = (bf16[144,2304]{1,0:T(8,128)(2,1)}, bf16[144,2304]{1,0:T(8,128)(2,1)S(1)}, u32[]{:S(2)}, u32[]{:S(2)}) collective-permute-start(bf16[144,2304]{1,0:T(8,128)(2,1)} %get-tuple-element.43.refs_0_), channel_id=1, source_target_pairs={{0,2},{2,4},{4,6},{6,0},{1,3},{3,5},{5,7},{7,1},{8,10},{10,12},{12... | collective-permute-start | bytes 1990664 | tf_op jit(solution)/shard_map/ppermute | solution.py:23
  17.8 16.1 %collective-permute-start.3 = (bf16[144,2304]{1,0:T(8,128)(2,1)}, bf16[144,2304]{1,0:T(8,128)(2,1)S(1)}, u32[]{:S(2)}, u32[]{:S(2)}) collective-permute-start(bf16[144,2304]{1,0:T(8,128)(2,1)} %get-tuple-element.43.refs_0_), channel_id=1, source_target_pairs={{0,6},{2,0},{4,2},{6,4},{1,7},{3,1},{5,3},{7,5},{8,14},{10,8},{12,... | collective-permute-start | bytes 1990664 | tf_op jit(solution)/shard_map/ppermute | solution.py:23
  19.2 16.7 %collective-permute-start.4 = (bf16[144,2304]{1,0:T(8,128)(2,1)}, bf16[144,2304]{1,0:T(8,128)(2,1)S(1)}, u32[]{:S(2)}, u32[]{:S(2)}) collective-permute-start(bf16[144,2304]{1,0:T(8,128)(2,1)} %get-tuple-element.43.refs_0_), channel_id=1, source_target_pairs={{0,8},{8,0},{1,9},{9,1},{2,10},{10,2},{3,11},{11,3},{4,12},{12,4},... | collective-permute-start | bytes 1990664 | tf_op jit(solution)/shard_map/ppermute | solution.py:23
  25.5 95.3 %reduce-scatter.2.cloned.1.call-start = ((), (), s32[]{:S(2)}) async-start(), calls=%async_computation.2 | async-start | bytes 3649536 | tf_op jit(solution)/shard_map/reduce_scatter | solution.py:363
  36.0 7.1 %collective-permute-start.7 = (bf16[704,2304]{1,0:T(8,128)(2,1)}, bf16[704,2304]{1,0:T(8,128)(2,1)S(1)}, u32[]{:S(2)}, u32[]{:S(2)}) collective-permute-start(bf16[704,2304]{1,0:T(8,128)(2,1)} %deltas.1), channel_id=1, source_target_pairs={{0,1},{1,0},{2,3},{3,2},{4,5},{5,4},{6,7},{7,6},{8,9},{9,8},{10,11... | collective-permute-start | bytes 9732104 | tf_op jit(solution)/shard_map/ppermute | solution.py:23
  37.4 16.6 %collective-permute-start.5 = (bf16[144,2304]{1,0:T(8,128)(2,1)S(1)}, bf16[144,2304]{1,0:T(8,128)(2,1)S(1)}, u32[]{:S(2)}, u32[]{:S(2)}) collective-permute-start(bf16[144,2304]{1,0:T(8,128)(2,1)S(1)} %collective-permute-done.2.refs_3_), channel_id=1, source_target_pairs={{0,8},{8,0},{1,9},{9,1},{2,10},{10,2},{3,11},{11,3},{4,12},{12,4},... | collective-permute-start | bytes 1990664 | tf_op jit(solution)/shard_map/ppermute | solution.py:23
  38.6 16.8 %collective-permute-start.6 = (bf16[144,2304]{1,0:T(8,128)(2,1)S(1)}, bf16[144,2304]{1,0:T(8,128)(2,1)S(1)}, u32[]{:S(2)}, u32[]{:S(2)}) collective-permute-start(bf16[144,2304]{1,0:T(8,128)(2,1)S(1)} %collective-permute-done.4.refs_1_), channel_id=1, source_target_pairs={{0,6},{2,0},{4,2},{6,4},{1,7},{3,1},{5,3},{7,5},{8,14},{10,8},{12,... | collective-permute-start | bytes 1990664 | tf_op jit(solution)/shard_map/ppermute | solution.py:23
  41.3 18.0 %collective-permute-start.18 = (bf16[144,2304]{1,0:T(8,128)(2,1)S(1)}, bf16[144,2304]{1,0:T(8,128)(2,1)S(1)}, u32[]{:S(2)}, u32[]{:S(2)}) collective-permute-start(bf16[144,2304]{1,0:T(8,128)(2,1)S(1)} %collective-permute-done.2.refs_3_), channel_id=1, source_target_pairs={{0,2},{2,4},{4,6},{6,0},{1,3},{3,5},{5,7},{7,1},{8,10},{10,12},{12... | collective-permute-start | bytes 1990664 | tf_op jit(solution)/shard_map/ppermute | solution.py:23
  55.3 10.9 %collective-permute-start.16 = (bf16[144,1152]{1,0:T(8,128)(2,1)S(1)}, bf16[144,1152]{1,0:T(8,128)(2,1)S(1)}, u32[]{:S(2)}, u32[]{:S(2)}) collective-permute-start(bf16[144,1152]{1,0:T(8,128)(2,1)S(1)} %slice.12), channel_id=1, source_target_pairs={{0,2},{2,4},{4,6},{6,0},{1,3},{3,5},{5,7},{7,1},{8,10},{10,12},{12... | collective-permute-start | bytes 995336 | tf_op jit(solution)/shard_map/ppermute | solution.py:23
  56.3 9.9 %collective-permute-start.17 = (bf16[144,1152]{1,0:T(8,128)(2,1)S(1)}, bf16[144,1152]{1,0:T(8,128)(2,1)S(1)}, u32[]{:S(2)}, u32[]{:S(2)}) collective-permute-start(bf16[144,1152]{1,0:T(8,128)(2,1)S(1)} %slice.13), channel_id=1, source_target_pairs={{0,6},{2,0},{4,2},{6,4},{1,7},{3,1},{5,3},{7,5},{8,14},{10,8},{12,... | collective-permute-start | bytes 995336 | tf_op jit(solution)/shard_map/ppermute | solution.py:23
  81.4 16.4 %collective-permute-start.10 = (bf16[144,2304]{1,0:T(8,128)(2,1)}, bf16[144,2304]{1,0:T(8,128)(2,1)}, u32[]{:S(2)}, u32[]{:S(2)}) collective-permute-start(bf16[144,2304]{1,0:T(8,128)(2,1)} %get-tuple-element.52.refs_2_), channel_id=1, source_target_pairs={{0,6},{2,0},{4,2},{6,4},{1,7},{3,1},{5,3},{7,5},{8,14},{10,8},{12,... | collective-permute-start | bytes 1990664 | tf_op jit(solution)/shard_map/ppermute | solution.py:23
  83.9 15.8 %collective-permute-start.8 = (bf16[144,2304]{1,0:T(8,128)(2,1)}, bf16[144,2304]{1,0:T(8,128)(2,1)}, u32[]{:S(2)}, u32[]{:S(2)}) collective-permute-start(bf16[144,2304]{1,0:T(8,128)(2,1)} %get-tuple-element.50.refs_0_), channel_id=1, source_target_pairs={{0,8},{8,0},{1,9},{9,1},{2,10},{10,2},{3,11},{11,3},{4,12},{12,4},... | collective-permute-start | bytes 1990664 | tf_op jit(solution)/shard_map/ppermute | solution.py:23
  86.2 16.5 %collective-permute-start.9 = (bf16[144,2304]{1,0:T(8,128)(2,1)S(1)}, bf16[144,2304]{1,0:T(8,128)(2,1)S(1)}, u32[]{:S(2)}, u32[]{:S(2)}) collective-permute-start(bf16[144,2304]{1,0:T(8,128)(2,1)S(1)} %copy-done.9), channel_id=1, source_target_pairs={{0,2},{2,4},{4,6},{6,0},{1,3},{3,5},{5,7},{7,1},{8,10},{10,12},{12... | collective-permute-start | bytes 1990664 | tf_op jit(solution)/shard_map/ppermute | solution.py:23
  104.9 8.8 %collective-permute-start.11 = (bf16[144,1152]{1,0:T(8,128)(2,1)}, bf16[144,1152]{1,0:T(8,128)(2,1)S(1)}, u32[]{:S(2)}, u32[]{:S(2)}) collective-permute-start(bf16[144,1152]{1,0:T(8,128)(2,1)} %get-tuple-element.57), channel_id=1, source_target_pairs={{0,2},{2,4},{4,6},{6,0},{1,3},{3,5},{5,7},{7,1},{8,10},{10,12},{12... | collective-permute-start | bytes 995336 | tf_op jit(solution)/shard_map/ppermute | solution.py:23
  104.9 8.8 %collective-permute-start.12 = (bf16[144,1152]{1,0:T(8,128)(2,1)}, bf16[144,1152]{1,0:T(8,128)(2,1)S(1)}, u32[]{:S(2)}, u32[]{:S(2)}) collective-permute-start(bf16[144,1152]{1,0:T(8,128)(2,1)} %get-tuple-element.59), channel_id=1, source_target_pairs={{0,6},{2,0},{4,2},{6,4},{1,7},{3,1},{5,3},{7,5},{8,14},{10,8},{12,... | collective-permute-start | bytes 995336 | tf_op jit(solution)/shard_map/ppermute | solution.py:23
  108.9 19.4 %collective-permute-start.15 = (bf16[144,2304]{1,0:T(8,128)(2,1)S(1)}, bf16[144,2304]{1,0:T(8,128)(2,1)S(1)}, u32[]{:S(2)}, u32[]{:S(2)}) collective-permute-start(bf16[144,2304]{1,0:T(8,128)(2,1)S(1)} %add_convert_fusion.1), channel_id=1, source_target_pairs={{0,8},{8,0},{1,9},{9,1},{2,10},{10,2},{3,11},{11,3},{4,12},{12,4},... | collective-permute-start | bytes 1990664 | tf_op jit(solution)/shard_map/ppermute | solution.py:23
  117.2 15.0 %collective-permute-start.13 = (bf16[144,2304]{1,0:T(8,128)(2,1)}, bf16[144,2304]{1,0:T(8,128)(2,1)S(1)}, u32[]{:S(2)}, u32[]{:S(2)}) collective-permute-start(bf16[144,2304]{1,0:T(8,128)(2,1)} %get-tuple-element.60), channel_id=1, source_target_pairs={{0,2},{2,4},{4,6},{6,0},{1,3},{3,5},{5,7},{7,1},{8,10},{10,12},{12... | collective-permute-start | bytes 1990664 | tf_op jit(solution)/shard_map/ppermute | solution.py:23
  117.2 15.0 %collective-permute-start.14 = (bf16[144,2304]{1,0:T(8,128)(2,1)}, bf16[144,2304]{1,0:T(8,128)(2,1)S(1)}, u32[]{:S(2)}, u32[]{:S(2)}) collective-permute-start(bf16[144,2304]{1,0:T(8,128)(2,1)} %get-tuple-element.61), channel_id=1, source_target_pairs={{0,6},{2,0},{4,2},{6,4},{1,7},{3,1},{5,3},{7,5},{8,14},{10,8},{12,... | collective-permute-start | bytes 1990664 | tf_op jit(solution)/shard_map/ppermute | solution.py:23
  122.7 9.8 %collective-permute-start.19 = (bf16[44,1152]{1,0:T(8,128)(2,1)}, bf16[44,1152]{1,0:T(8,128)(2,1)S(1)}, u32[]{:S(2)}, u32[]{:S(2)}) collective-permute-start(bf16[44,1152]{1,0:T(8,128)(2,1)} %get-tuple-element.69), channel_id=1, source_target_pairs={{0,16},{16,0},{1,17},{17,1},{2,18},{18,2},{3,19},{19,3},{4,20},{20... | collective-permute-start | bytes 304136 | tf_op jit(solution)/shard_map/ppermute | solution.py:23
  125.6 6.9 %collective-permute-start.20 = (bf16[44,1152]{1,0:T(8,128)(2,1)}, bf16[44,1152]{1,0:T(8,128)(2,1)S(1)}, u32[]{:S(2)}, u32[]{:S(2)}) collective-permute-start(bf16[44,1152]{1,0:T(8,128)(2,1)} %get-tuple-element.70), channel_id=1, source_target_pairs={{0,17},{1,16},{16,1},{17,0},{2,19},{3,18},{18,3},{19,2},{4,21},{5,... | collective-permute-start | bytes 304136 | tf_op jit(solution)/shard_map/ppermute | solution.py:27
  128.3 4.2 %collective-permute-start.21 = (bf16[44,1152]{1,0:T(8,128)(2,1)}, bf16[44,1152]{1,0:T(8,128)(2,1)S(1)}, u32[]{:S(2)}, u32[]{:S(2)}) collective-permute-start(bf16[44,1152]{1,0:T(8,128)(2,1)} %get-tuple-element.71), channel_id=1, source_target_pairs={{0,1},{1,0},{2,3},{3,2},{4,5},{5,4},{6,7},{7,6},{8,9},{9,8},{10,11... | collective-permute-start | bytes 304136 | tf_op jit(solution)/shard_map/ppermute | solution.py:23
  (10 other events, 63.2 us)
Sparse Core Ops, SparseCore 0:
  25.7 48.4 all-gather.1
  76.7 44.1 reduce-scatter.1

commit v10 on v9

--- a/solution.py
+++ b/solution.py
@@ -327,7 +327,6 @@
     across, far_up, far_down, far, far_own, up, down, own = blocks
     across = shift(across, "x_lo", 1)
     far_right, far_left = shift(far_up, "y", 1), shift(far_down, "y", -1)
-    across, far_right, far_left = lax.optimization_barrier((across, far_right, far_left))
     right, left = add_halves(far, across)
     right, left = shift(right, "y", 1), shift(left, "y", -1)
     far_own = shift(add(far_own, far_left, far_right), "x_lo", 1)
@@ -371,10 +370,11 @@
     here, there, here_other, there_other = cut_sums(sums)
     parts = [here, shift(there, "x_hi", 1), both_flipped(there_other)]
     parts.append(shift(here_other, "core", 1))
-    grads = add(*terms)
-    grads, *parts = lax.optimization_barrier((grads, *parts))
     input_grad = join_columns(*parts)
-    return input_grad, grads[:, :hidden], grads[:, hidden:]
+    input_grad, *terms = lax.optimization_barrier((input_grad, *terms))
+    gate_grad = add(*(t[:, :hidden] for t in terms))
+    up_grad = add(*(t[:, hidden:] for t in terms))
+    return input_grad, gate_grad, up_grad
 
 
 def solution(mesh):

time: 145 us -> 144 us (level); the launches traced: 143 us -> 144 us
  starting transfers between devices: 31.7 us -> 35.8 us
  waiting for transfers between devices: 36.2 us -> 32.8 us
    ppermute x21, waiting for transfers between devices: 31.2 us -> 22.7 us  [shift(): return lax.ppermute(x, axis, [(i, (i + k) % n) for i in range(n)])]
    reduce_scatter x1, waiting for transfers between devices: 1.02 us -> 5.81 us  [per_device(): sums = lax.psum_scatter(part, 'z', scatter_dimension=0, tiled=True)]
    ppermute x21, starting transfers between devices: 28.9 us -> 33.1 us  [shift(): return lax.ppermute(x, axis, [(i, (i + k) % n) for i in range(n)])]
  transfers between devices with their start and end apart: 24 -> 24, of which waited for: 15 -> 15; matrix products, arithmetic and copies ran while one was open for 4% -> 4% of each run, Pallas kernels for 32% -> 34%
where the time goes in v10:
time: 144 us
  Pallas kernels  51.2 us (36%)
  starting transfers between devices  35.8 us (25%)
  waiting for transfers between devices  32.8 us (23%)
  between operations  14.1 us (10%)
  other arithmetic  8.11 us (6%)
    ppermute x21, starting transfers between devices, shift(): return lax.ppermute(x, axis, [(i, (i + k) % n) for i in range(n)])  33.1 us
    ppermute x21, waiting for transfers between devices, shift(): return lax.ppermute(x, axis, [(i, (i + k) % n) for i in range(n)])  22.7 us
    pallas_call x2, Pallas kernels, weight_product(): pl.pallas_call(functools.partial(weight_body, scale, start, first - start...  17.1 us
    pallas_call x3, Pallas kernels, input_product(): pl.pallas_call(functools.partial(input_body, n, done), out_shape=jax.Shap...  15.5 us
    pallas_call x1, Pallas kernels, make_deltas(): pl.pallas_call(delta_body, out_shape=jax.ShapeDtypeStruct((rows, 2 * cols...  5.91 us
    reduce_scatter x1, waiting for transfers between devices, per_device(): sums = lax.psum_scatter(part, 'z', scatter_dimension=0, tiled=True)  5.81 us
    all_gather x1, waiting for transfers between devices, per_device(): lax.all_gather(block, 'z', axis=0, tiled=True).reshape(-1, keep.shape[1])  4.02 us
  transfers between devices with their start and end apart: 24, of which 15 were waited for; matrix products, arithmetic and copies ran while one was open for 4% of the time, Pallas kernels for 34%

profile of v10, /device:TPU:1, one launch (start us, length us, event | category | flops | bytes accessed | tf_op | source)
XLA Modules:
  0.0 143.5 jit_solution(6013984634367648253)
XLA Ops:
  7.2 2.9 %prologue.1 = (bf16[44,1152]{1,0:T(8,128)(2,1)}, bf16[44,1152]{1,0:T(8,128)(2,1)}, bf16[144,2304]{1,0:T(8,128)(2,1)}) custom-call(bf16[44,2304]{1,0:T(8,128)(2,1)} %x_ref.1, bf16[144,1152]{1,0:T(8,128)(2,1)} %g_ref.1, bf16[144,1152]{1,0:T(8,128)(2,1)} %u_ref.2), custom_call_target="tpu_custom_call" | custom-call | flops 1000 | bytes 1000 | tf_op jit(solution)/shard_map/prologue/pallas_call | solution.py:119
  10.1 3.2 %collective-permute-start.3 = (bf16[44,1152]{1,0:T(8,128)(2,1)}, bf16[44,1152]{1,0:T(8,128)(2,1)S(1)}, u32[]{:S(2)}, u32[]{:S(2)}) collective-permute-start(bf16[44,1152]{1,0:T(8,128)(2,1)} %get-tuple-element.39), channel_id=1, source_target_pairs={{0,1},{1,0},{2,3},{3,2},{4,5},{5,4},{6,7},{7,6},{8,9},{9,8},{10,11... | collective-permute-start | bytes 304136 | tf_op jit(solution)/shard_map/ppermute | solution.py:23
  19.6 4.1 %collective-permute-done.4 = bf16[2,44,1152]{2,1,0:T(8,128)(2,1)S(1)} collective-permute-done((bf16[2,44,1152]{2,1,0:T(8,128)(2,1)S(1)}, bf16[2,44,1152]{2,1,0:T(8,128)(2,1)S(1)}, u32[]{:S(2)}, u32[]{:S(2)}) %collective-permute-start.4) | collective-permute-done | bytes 202784 | tf_op jit(solution)/shard_map/ppermute | solution.py:23
  25.6 5.9 %deltas.1 = bf16[704,2304]{1,0:T(8,128)(2,1)} custom-call(bf16[704,1152]{1,0:T(8,128)(2,1)} %g_ref.2, bf16[704,1152]{1,0:T(8,128)(2,1)} %u_ref.3, bf16[704,1152]{1,0:T(8,128)(2,1)} %c_ref.1), custom_call_target="tpu_custom_call" | custom-call | flops 99999997952 | bytes 1000 | tf_op jit(solution)/shard_map/deltas/pallas_call | solution.py:55
  31.5 2.3 %collective-permute-done.refs_3_ = bf16[144,2304]{1,0:T(8,128)(2,1)S(1)} collective-permute-done((bf16[144,2304]{1,0:T(8,128)(2,1)}, bf16[144,2304]{1,0:T(8,128)(2,1)S(1)}, u32[]{:S(2)}, u32[]{:S(2)}) %collective-permute-start) | collective-permute-done | bytes 663584 | tf_op jit(solution)/shard_map/ppermute | solution.py:23
  33.9 2.1 %collective-permute-done.2.refs_1_ = bf16[144,2304]{1,0:T(8,128)(2,1)S(1)} collective-permute-done((bf16[144,2304]{1,0:T(8,128)(2,1)}, bf16[144,2304]{1,0:T(8,128)(2,1)S(1)}, u32[]{:S(2)}, u32[]{:S(2)}) %collective-permute-start.2) | collective-permute-done | bytes 663584 | tf_op jit(solution)/shard_map/ppermute | solution.py:23
  38.6 2.7 %collective-permute-start.6 = (bf16[144,2304]{1,0:T(8,128)(2,1)S(1)}, bf16[144,2304]{1,0:T(8,128)(2,1)S(1)}, u32[]{:S(2)}, u32[]{:S(2)}) collective-permute-start(bf16[144,2304]{1,0:T(8,128)(2,1)S(1)} %collective-permute-done.2.refs_1_), channel_id=1, source_target_pairs={{0,6},{2,0},{4,2},{6,4},{1,7},{3,1},{5,3},{7,5},{8,14},{10,8},{12,... | collective-permute-start | bytes 1990664 | tf_op jit(solution)/shard_map/ppermute | solution.py:23
  43.1 2.5 %pad_maximum_fusion = bf16[8,2,88,2304]{3,2,1,0:T(8,128)(2,1)S(1)} fusion(bf16[8,1,88,2304]{3,2,1,0:T(8,128)(2,1)S(1)} %bitcast.18, bf16[8,1,88,2304]{3,2,1,0:T(8,128)(2,1)} %bitcast.17), kind=kLoop, calls=%fused_computation | loop fusion | flops 3244032 | bytes 12976128 | tf_op jit(solution)/shard_map/stack | solution.py:355
  45.6 6.8 %input_product_4.1.refs_2_ = bf16[1408,576]{1,0:T(8,128)(2,1)S(1)} custom-call(bf16[144,2304]{1,0:T(8,128)(2,1)S(1)} %copy-done.1, bf16[144,2304]{1,0:T(8,128)(2,1)S(1)} %collective-permute-done.2.refs_1_, bf16[144,2304]{1,0:T(8,128)(2,1)S(1)} %collective-permute-done.1.refs_2_, bf16[144,2304]{1,0:T(8,128)(2,1)S(1)} %collective-permute-done.refs_3_, ...), custom_call_target="tpu_custom_call" | custom-call | flops 1000 | bytes 1000 | tf_op jit(solution)/shard_map/input_product_4/pallas_call | solution.py:299
  56.3 2.9 %collective-permute-start.9 = (bf16[144,1152]{1,0:T(8,128)(2,1)S(1)}, bf16[144,1152]{1,0:T(8,128)(2,1)S(1)}, u32[]{:S(2)}, u32[]{:S(2)}) collective-permute-start(bf16[144,1152]{1,0:T(8,128)(2,1)S(1)} %slice.31), channel_id=1, source_target_pairs={{0,6},{2,0},{4,2},{6,4},{1,7},{3,1},{5,3},{7,5},{8,14},{10,8},{12,... | collective-permute-start | bytes 995336 | tf_op jit(solution)/shard_map/ppermute | solution.py:23
  59.3 4.8 %input_product_3.1.refs_3_ = bf16[1408,432]{1,0:T(8,128)(2,1)S(1)} custom-call(bf16[144,2304]{1,0:T(8,128)(2,1)S(1)} %collective-permute-done.10.refs_0_, bf16[144,2304]{1,0:T(8,128)(2,1)S(1)} %collective-permute-done.6.refs_1_, bf16[144,2304]{1,0:T(8,128)(2,1)S(1)} %collective-permute-done.5.refs_2_, bf16[1408,2304]{1,0:T(8,128)(2,1)S(1)} %bitcast.11), custom_call_target="tpu_custom_call" | custom-call | flops 1000 | bytes 1000 | tf_op jit(solution)/shard_map/input_product_3/pallas_call | solution.py:299
  64.1 2.2 %collective-permute-done.8.refs_0_ = bf16[144,1152]{1,0:T(8,128)(2,1)S(1)} collective-permute-done((bf16[144,1152]{1,0:T(8,128)(2,1)S(1)}, bf16[144,1152]{1,0:T(8,128)(2,1)S(1)}, u32[]{:S(2)}, u32[]{:S(2)}) %collective-permute-start.8) | collective-permute-done | bytes 331808 | tf_op jit(solution)/shard_map/ppermute | solution.py:23
  66.2 3.9 %input_product_2.1 = bf16[1408,1152]{1,0:T(8,128)(2,1)} custom-call(bf16[144,1152]{1,0:T(8,128)(2,1)S(1)} %collective-permute-done.8.refs_0_, bf16[144,1152]{1,0:T(8,128)(2,1)S(1)} %collective-permute-done.9.refs_1_, bf16[1408,576]{1,0:T(8,128)(2,1)S(1)} %input_product_4.1.refs_2_, bf16[1408,432]{1,0:T(8,128)(2,1)S(1)} %input_product_3.1.refs_3_, ...), custom_call_target="tpu_custom_call" | custom-call | flops 1000 | bytes 1000 | tf_op jit(solution)/shard_map/input_product_2/pallas_call | solution.py:299
  70.2 4.0 %all-gather.2.cloned.1.call-done = bf16[16,88,1152]{2,1,0:T(8,128)(2,1)} async-done(((bf16[2,88,1152]{2,1,0:T(8,128)(2,1)}), bf16[16,88,1152]{2,1,0:T(8,128)(2,1)}) %all-gather.2.cloned.1.call-update) | async-done | bytes 3244048 | tf_op jit(solution)/shard_map/all_gather | solution.py:350
  74.2 7.2 %weight_product_0.1 = (bf16[144,2304]{1,0:T(8,128)(2,1)}, bf16[144,2304]{1,0:T(8,128)(2,1)}, bf16[144,2304]{1,0:T(8,128)(2,1)}) custom-call(bf16[1408,1152]{1,0:T(8,128)(2,1)} %bitcast.15, bf16[1408,2304]{1,0:T(8,128)(2,1)} %bitcast.13), custom_call_target="tpu_custom_call" | custom-call | flops 1000 | bytes 1000 | tf_op jit(solution)/shard_map/weight_product_0/pallas_call | solution.py:245
  86.4 9.9 %weight_product_432.1 = (bf16[144,2304]{1,0:T(8,128)(2,1)}, bf16[144,2304]{1,0:T(8,128)(2,1)}, bf16[144,2304]{1,0:T(8,128)(2,1)}, bf16[144,2304]{1,0:T(8,128)(2,1)}, bf16[144,2304]{1,0:T(8,128)(2,1)}) custom-call(bf16[1408,1152]{1,0:T(8,128)(2,1)} %bitcast.16, bf16[1408,2304]{1,0:T(8,128)(2,1)} %bitcast.14, f32[8,128]{1,0:T(8,128)} %sent.1.refs_0_), custom_call_target="tpu_custom_call" | custom-call | flops 99999997952 | bytes 1000 | tf_op jit(solution)/shard_map/weight_product_432/pallas_call | solution.py:245
  97.5 2.3 %add_halves.1 = (bf16[144,1152]{1,0:T(8,128)(2,1)}, bf16[144,1152]{1,0:T(8,128)(2,1)}) custom-call(bf16[144,2304]{1,0:T(8,128)(2,1)} %get-tuple-element.59.a_ref, bf16[144,2304]{1,0:T(8,128)(2,1)} %collective-permute-done.14.b_ref), custom_call_target="tpu_custom_call" | custom-call | flops 1000 | bytes 1000 | tf_op jit(solution)/shard_map/add_halves/pallas_call | solution.py:210
  105.4 3.7 %collective-permute-done.15.right_ref = bf16[144,1152]{1,0:T(8,128)(2,1)S(1)} collective-permute-done((bf16[144,1152]{1,0:T(8,128)(2,1)}, bf16[144,1152]{1,0:T(8,128)(2,1)S(1)}, u32[]{:S(2)}, u32[]{:S(2)}) %collective-permute-start.15) | collective-permute-done | bytes 331808 | tf_op jit(solution)/shard_map/ppermute | solution.py:23
  109.9 2.7 %merge.1 = (bf16[144,2304]{1,0:T(8,128)(2,1)}, bf16[144,2304]{1,0:T(8,128)(2,1)}) custom-call(bf16[144,2304]{1,0:T(8,128)(2,1)} %get-tuple-element.58.up_ref, bf16[144,1152]{1,0:T(8,128)(2,1)} %copy-done.3, bf16[144,2304]{1,0:T(8,128)(2,1)} %get-tuple-element.61.down_ref, bf16[144,1152]{1,0:T(8,128)(2,1)} %copy-done.4), custom_call_target="tpu_custom_call" | custom-call | flops 1000 | bytes 1000 | tf_op jit(solution)/shard_map/merge/pallas_call | solution.py:229
  115.3 5.8 %reduce-scatter.2.cloned.1.call-done.x_ref = bf16[176,1152]{1,0:T(8,128)(2,1)} async-done(((bf16[1408,1152]{1,0:T(8,128)(2,1)}), bf16[176,1152]{1,0:T(8,128)(2,1)}) %reduce-scatter.2.cloned.1.call-update) | async-done | bytes 405520 | tf_op jit(solution)/shard_map/reduce_scatter | solution.py:362
  122.9 2.5 %collective-permute-start.11 = (bf16[44,1152]{1,0:T(8,128)(2,1)}, bf16[44,1152]{1,0:T(8,128)(2,1)S(1)}, u32[]{:S(2)}, u32[]{:S(2)}) collective-permute-start(bf16[44,1152]{1,0:T(8,128)(2,1)} %get-tuple-element.50), channel_id=1, source_target_pairs={{0,16},{16,0},{1,17},{17,1},{2,18},{18,2},{3,19},{19,3},{4,20},{20... | collective-permute-start | bytes 304136 | tf_op jit(solution)/shard_map/ppermute | solution.py:23
  125.5 2.7 %collective-permute-start.12 = (bf16[44,1152]{1,0:T(8,128)(2,1)}, bf16[44,1152]{1,0:T(8,128)(2,1)S(1)}, u32[]{:S(2)}, u32[]{:S(2)}) collective-permute-start(bf16[44,1152]{1,0:T(8,128)(2,1)} %get-tuple-element.51), channel_id=1, source_target_pairs={{0,17},{1,16},{16,1},{17,0},{2,19},{3,18},{18,3},{19,2},{4,21},{5,... | collective-permute-start | bytes 304136 | tf_op jit(solution)/shard_map/ppermute | solution.py:27
  128.2 3.5 %collective-permute-start.13 = (bf16[44,1152]{1,0:T(8,128)(2,1)}, bf16[44,1152]{1,0:T(8,128)(2,1)}, u32[]{:S(2)}, u32[]{:S(2)}) collective-permute-start(bf16[44,1152]{1,0:T(8,128)(2,1)} %get-tuple-element.52), channel_id=1, source_target_pairs={{0,1},{1,0},{2,3},{3,2},{4,5},{5,4},{6,7},{7,6},{8,9},{9,8},{10,11... | collective-permute-start | bytes 304136 | tf_op jit(solution)/shard_map/ppermute | solution.py:23
  133.0 2.4 %join_columns.1 = bf16[44,2304]{1,0:T(8,128)(2,1)} custom-call(bf16[44,1152]{1,0:T(8,128)(2,1)} %get-tuple-element.49.m0_ref, bf16[44,1152]{1,0:T(8,128)(2,1)} %copy-done.5, bf16[44,1152]{1,0:T(8,128)(2,1)} %copy-done.6, bf16[44,1152]{1,0:T(8,128)(2,1)} %collective-permute-done.13.o1_ref), custom_call_target="tpu_custom_call" | custom-call | flops 1000 | bytes 1000 | tf_op jit(solution)/shard_map/join_columns/pallas_call | solution.py:179
  (61 shorter events, 36.1 us)
Async XLA Ops:
  7.2 67.0 %all-gather.2.cloned.1.call-start = ((), (), s32[]{:S(2)}) async-start(), calls=%async_computation.2 | async-start | bytes 3649536 | tf_op jit(solution)/shard_map/all_gather | solution.py:350
  10.1 4.4 %collective-permute-start.3 = (bf16[44,1152]{1,0:T(8,128)(2,1)}, bf16[44,1152]{1,0:T(8,128)(2,1)S(1)}, u32[]{:S(2)}, u32[]{:S(2)}) collective-permute-start(bf16[44,1152]{1,0:T(8,128)(2,1)} %get-tuple-element.39), channel_id=1, source_target_pairs={{0,1},{1,0},{2,3},{3,2},{4,5},{5,4},{6,7},{7,6},{8,9},{9,8},{10,11... | collective-permute-start | bytes 304136 | tf_op jit(solution)/shard_map/ppermute | solution.py:23
  15.4 8.2 %collective-permute-start.4 = (bf16[2,44,1152]{2,1,0:T(8,128)(2,1)S(1)}, bf16[2,44,1152]{2,1,0:T(8,128)(2,1)S(1)}, u32[]{:S(2)}, u32[]{:S(2)}) collective-permute-start(bf16[2,44,1152]{2,1,0:T(8,128)(2,1)S(1)} %pad_maximum_fusion.1), channel_id=1, source_target_pairs={{0,16},{16,0},{1,17},{17,1},{2,18},{18,2},{3,19},{19,3},{4,20},{20... | collective-permute-start | bytes 608264 | tf_op jit(solution)/shard_map/ppermute | solution.py:23
  16.5 17.4 %collective-permute-start = (bf16[144,2304]{1,0:T(8,128)(2,1)}, bf16[144,2304]{1,0:T(8,128)(2,1)S(1)}, u32[]{:S(2)}, u32[]{:S(2)}) collective-permute-start(bf16[144,2304]{1,0:T(8,128)(2,1)} %get-tuple-element.37.refs_0_), channel_id=1, source_target_pairs={{0,2},{2,4},{4,6},{6,0},{1,3},{3,5},{5,7},{7,1},{8,10},{10,12},{12... | collective-permute-start | bytes 1990664 | tf_op jit(solution)/shard_map/ppermute | solution.py:23
  17.8 16.1 %collective-permute-start.1 = (bf16[144,2304]{1,0:T(8,128)(2,1)}, bf16[144,2304]{1,0:T(8,128)(2,1)S(1)}, u32[]{:S(2)}, u32[]{:S(2)}) collective-permute-start(bf16[144,2304]{1,0:T(8,128)(2,1)} %get-tuple-element.37.refs_0_), channel_id=1, source_target_pairs={{0,6},{2,0},{4,2},{6,4},{1,7},{3,1},{5,3},{7,5},{8,14},{10,8},{12,... | collective-permute-start | bytes 1990664 | tf_op jit(solution)/shard_map/ppermute | solution.py:23
  19.3 16.7 %collective-permute-start.2 = (bf16[144,2304]{1,0:T(8,128)(2,1)}, bf16[144,2304]{1,0:T(8,128)(2,1)S(1)}, u32[]{:S(2)}, u32[]{:S(2)}) collective-permute-start(bf16[144,2304]{1,0:T(8,128)(2,1)} %get-tuple-element.37.refs_0_), channel_id=1, source_target_pairs={{0,8},{8,0},{1,9},{9,1},{2,10},{10,2},{3,11},{11,3},{4,12},{12,4},... | collective-permute-start | bytes 1990664 | tf_op jit(solution)/shard_map/ppermute | solution.py:23
  25.6 95.5 %reduce-scatter.2.cloned.1.call-start = ((), (), s32[]{:S(2)}) async-start(), calls=%async_computation.1 | async-start | bytes 3649536 | tf_op jit(solution)/shard_map/reduce_scatter | solution.py:362
  36.0 7.1 %collective-permute-start.7 = (bf16[704,2304]{1,0:T(8,128)(2,1)}, bf16[704,2304]{1,0:T(8,128)(2,1)S(1)}, u32[]{:S(2)}, u32[]{:S(2)}) collective-permute-start(bf16[704,2304]{1,0:T(8,128)(2,1)} %deltas.1), channel_id=1, source_target_pairs={{0,1},{1,0},{2,3},{3,2},{4,5},{5,4},{6,7},{7,6},{8,9},{9,8},{10,11... | collective-permute-start | bytes 9732104 | tf_op jit(solution)/shard_map/ppermute | solution.py:23
  37.4 16.6 %collective-permute-start.5 = (bf16[144,2304]{1,0:T(8,128)(2,1)S(1)}, bf16[144,2304]{1,0:T(8,128)(2,1)S(1)}, u32[]{:S(2)}, u32[]{:S(2)}) collective-permute-start(bf16[144,2304]{1,0:T(8,128)(2,1)S(1)} %collective-permute-done.refs_3_), channel_id=1, source_target_pairs={{0,8},{8,0},{1,9},{9,1},{2,10},{10,2},{3,11},{11,3},{4,12},{12,4},... | collective-permute-start | bytes 1990664 | tf_op jit(solution)/shard_map/ppermute | solution.py:23
  38.6 16.8 %collective-permute-start.6 = (bf16[144,2304]{1,0:T(8,128)(2,1)S(1)}, bf16[144,2304]{1,0:T(8,128)(2,1)S(1)}, u32[]{:S(2)}, u32[]{:S(2)}) collective-permute-start(bf16[144,2304]{1,0:T(8,128)(2,1)S(1)} %collective-permute-done.2.refs_1_), channel_id=1, source_target_pairs={{0,6},{2,0},{4,2},{6,4},{1,7},{3,1},{5,3},{7,5},{8,14},{10,8},{12,... | collective-permute-start | bytes 1990664 | tf_op jit(solution)/shard_map/ppermute | solution.py:23
  41.3 18.0 %collective-permute-start.10 = (bf16[144,2304]{1,0:T(8,128)(2,1)S(1)}, bf16[144,2304]{1,0:T(8,128)(2,1)S(1)}, u32[]{:S(2)}, u32[]{:S(2)}) collective-permute-start(bf16[144,2304]{1,0:T(8,128)(2,1)S(1)} %collective-permute-done.refs_3_), channel_id=1, source_target_pairs={{0,2},{2,4},{4,6},{6,0},{1,3},{3,5},{5,7},{7,1},{8,10},{10,12},{12... | collective-permute-start | bytes 1990664 | tf_op jit(solution)/shard_map/ppermute | solution.py:23
  55.4 10.9 %collective-permute-start.8 = (bf16[144,1152]{1,0:T(8,128)(2,1)S(1)}, bf16[144,1152]{1,0:T(8,128)(2,1)S(1)}, u32[]{:S(2)}, u32[]{:S(2)}) collective-permute-start(bf16[144,1152]{1,0:T(8,128)(2,1)S(1)} %slice.30), channel_id=1, source_target_pairs={{0,2},{2,4},{4,6},{6,0},{1,3},{3,5},{5,7},{7,1},{8,10},{10,12},{12... | collective-permute-start | bytes 995336 | tf_op jit(solution)/shard_map/ppermute | solution.py:23
  56.3 9.9 %collective-permute-start.9 = (bf16[144,1152]{1,0:T(8,128)(2,1)S(1)}, bf16[144,1152]{1,0:T(8,128)(2,1)S(1)}, u32[]{:S(2)}, u32[]{:S(2)}) collective-permute-start(bf16[144,1152]{1,0:T(8,128)(2,1)S(1)} %slice.31), channel_id=1, source_target_pairs={{0,6},{2,0},{4,2},{6,4},{1,7},{3,1},{5,3},{7,5},{8,14},{10,8},{12,... | collective-permute-start | bytes 995336 | tf_op jit(solution)/shard_map/ppermute | solution.py:23
  81.4 16.1 %collective-permute-start.14 = (bf16[144,2304]{1,0:T(8,128)(2,1)}, bf16[144,2304]{1,0:T(8,128)(2,1)}, u32[]{:S(2)}, u32[]{:S(2)}) collective-permute-start(bf16[144,2304]{1,0:T(8,128)(2,1)} %get-tuple-element.54.refs_0_), channel_id=1, source_target_pairs={{0,8},{8,0},{1,9},{9,1},{2,10},{10,2},{3,11},{11,3},{4,12},{12,4},... | collective-permute-start | bytes 1990664 | tf_op jit(solution)/shard_map/ppermute | solution.py:23
  82.6 19.9 %collective-permute-start.20 = (bf16[144,2304]{1,0:T(8,128)(2,1)}, bf16[144,2304]{1,0:T(8,128)(2,1)}, u32[]{:S(2)}, u32[]{:S(2)}) collective-permute-start(bf16[144,2304]{1,0:T(8,128)(2,1)} %get-tuple-element.55.refs_1_), channel_id=1, source_target_pairs={{0,2},{2,4},{4,6},{6,0},{1,3},{3,5},{5,7},{7,1},{8,10},{10,12},{12... | collective-permute-start | bytes 1990664 | tf_op jit(solution)/shard_map/ppermute | solution.py:23
  84.9 17.6 %collective-permute-start.19 = (bf16[144,2304]{1,0:T(8,128)(2,1)S(1)}, bf16[144,2304]{1,0:T(8,128)(2,1)S(1)}, u32[]{:S(2)}, u32[]{:S(2)}) collective-permute-start(bf16[144,2304]{1,0:T(8,128)(2,1)S(1)} %copy-done.7), channel_id=1, source_target_pairs={{0,6},{2,0},{4,2},{6,4},{1,7},{3,1},{5,3},{7,5},{8,14},{10,8},{12,... | collective-permute-start | bytes 1990664 | tf_op jit(solution)/shard_map/ppermute | solution.py:23
  99.8 9.3 %collective-permute-start.15 = (bf16[144,1152]{1,0:T(8,128)(2,1)}, bf16[144,1152]{1,0:T(8,128)(2,1)S(1)}, u32[]{:S(2)}, u32[]{:S(2)}) collective-permute-start(bf16[144,1152]{1,0:T(8,128)(2,1)} %get-tuple-element.60), channel_id=1, source_target_pairs={{0,2},{2,4},{4,6},{6,0},{1,3},{3,5},{5,7},{7,1},{8,10},{10,12},{12... | collective-permute-start | bytes 995336 | tf_op jit(solution)/shard_map/ppermute | solution.py:23
  101.0 8.1 %collective-permute-start.16 = (bf16[144,1152]{1,0:T(8,128)(2,1)}, bf16[144,1152]{1,0:T(8,128)(2,1)S(1)}, u32[]{:S(2)}, u32[]{:S(2)}) collective-permute-start(bf16[144,1152]{1,0:T(8,128)(2,1)} %get-tuple-element.62), channel_id=1, source_target_pairs={{0,6},{2,0},{4,2},{6,4},{1,7},{3,1},{5,3},{7,5},{8,14},{10,8},{12,... | collective-permute-start | bytes 995336 | tf_op jit(solution)/shard_map/ppermute | solution.py:23
  104.1 31.4 %collective-permute-start.21 = (bf16[144,2304]{1,0:T(8,128)(2,1)S(1)}, bf16[144,2304]{1,0:T(8,128)(2,1)S(1)}, u32[]{:S(2)}, u32[]{:S(2)}) collective-permute-start(bf16[144,2304]{1,0:T(8,128)(2,1)S(1)} %add_convert_fusion), channel_id=1, source_target_pairs={{0,8},{8,0},{1,9},{9,1},{2,10},{10,2},{3,11},{11,3},{4,12},{12,4},... | collective-permute-start | bytes 1990664 | tf_op jit(solution)/shard_map/ppermute | solution.py:23
  112.6 22.9 %collective-permute-start.17 = (bf16[144,2304]{1,0:T(8,128)(2,1)}, bf16[144,2304]{1,0:T(8,128)(2,1)S(1)}, u32[]{:S(2)}, u32[]{:S(2)}) collective-permute-start(bf16[144,2304]{1,0:T(8,128)(2,1)} %get-tuple-element.63), channel_id=1, source_target_pairs={{0,2},{2,4},{4,6},{6,0},{1,3},{3,5},{5,7},{7,1},{8,10},{10,12},{12... | collective-permute-start | bytes 1990664 | tf_op jit(solution)/shard_map/ppermute | solution.py:23
  113.4 22.1 %collective-permute-start.18 = (bf16[144,2304]{1,0:T(8,128)(2,1)}, bf16[144,2304]{1,0:T(8,128)(2,1)S(1)}, u32[]{:S(2)}, u32[]{:S(2)}) collective-permute-start(bf16[144,2304]{1,0:T(8,128)(2,1)} %get-tuple-element.64), channel_id=1, source_target_pairs={{0,6},{2,0},{4,2},{6,4},{1,7},{3,1},{5,3},{7,5},{8,14},{10,8},{12,... | collective-permute-start | bytes 1990664 | tf_op jit(solution)/shard_map/ppermute | solution.py:23
  122.9 5.3 %collective-permute-start.11 = (bf16[44,1152]{1,0:T(8,128)(2,1)}, bf16[44,1152]{1,0:T(8,128)(2,1)S(1)}, u32[]{:S(2)}, u32[]{:S(2)}) collective-permute-start(bf16[44,1152]{1,0:T(8,128)(2,1)} %get-tuple-element.50), channel_id=1, source_target_pairs={{0,16},{16,0},{1,17},{17,1},{2,18},{18,2},{3,19},{19,3},{4,20},{20... | collective-permute-start | bytes 304136 | tf_op jit(solution)/shard_map/ppermute | solution.py:23
  125.5 6.5 %collective-permute-start.12 = (bf16[44,1152]{1,0:T(8,128)(2,1)}, bf16[44,1152]{1,0:T(8,128)(2,1)S(1)}, u32[]{:S(2)}, u32[]{:S(2)}) collective-permute-start(bf16[44,1152]{1,0:T(8,128)(2,1)} %get-tuple-element.51), channel_id=1, source_target_pairs={{0,17},{1,16},{16,1},{17,0},{2,19},{3,18},{18,3},{19,2},{4,21},{5,... | collective-permute-start | bytes 304136 | tf_op jit(solution)/shard_map/ppermute | solution.py:27
  128.2 4.8 %collective-permute-start.13 = (bf16[44,1152]{1,0:T(8,128)(2,1)}, bf16[44,1152]{1,0:T(8,128)(2,1)}, u32[]{:S(2)}, u32[]{:S(2)}) collective-permute-start(bf16[44,1152]{1,0:T(8,128)(2,1)} %get-tuple-element.52), channel_id=1, source_target_pairs={{0,1},{1,0},{2,3},{3,2},{4,5},{5,4},{6,7},{7,6},{8,9},{9,8},{10,11... | collective-permute-start | bytes 304136 | tf_op jit(solution)/shard_map/ppermute | solution.py:23
  (8 other events, 69.7 us)
Sparse Core Ops, SparseCore 0:
  25.7 48.4 all-gather.1
  76.7 44.3 reduce-scatter.1

commit v11 on v10

--- a/solution.py
+++ b/solution.py
@@ -370,11 +370,10 @@
     here, there, here_other, there_other = cut_sums(sums)
     parts = [here, shift(there, "x_hi", 1), both_flipped(there_other)]
     parts.append(shift(here_other, "core", 1))
-    input_grad = join_columns(*parts)
-    input_grad, *terms = lax.optimization_barrier((input_grad, *terms))
     gate_grad = add(*(t[:, :hidden] for t in terms))
     up_grad = add(*(t[:, hidden:] for t in terms))
-    return input_grad, gate_grad, up_grad
+    gate_grad, up_grad, *parts = lax.optimization_barrier((gate_grad, up_grad, *parts))
+    return join_columns(*parts), gate_grad, up_grad
 
 
 def solution(mesh):

time: 144 us -> 143 us (level)
  starting transfers between devices: 35.8 us -> 31.7 us
  waiting for transfers between devices: 32.8 us -> 35.4 us
    ppermute x21, starting transfers between devices: 33.1 us -> 28.7 us  [shift(): return lax.ppermute(x, axis, [(i, (i + k) % n) for i in range(n)])]
    ppermute x21, waiting for transfers between devices: 22.7 us -> 26 us  [shift(): return lax.ppermute(x, axis, [(i, (i + k) % n) for i in range(n)])]
    reduce_scatter x1, waiting for transfers between devices: 5.81 us -> 3.8 us  [per_device(): sums = lax.psum_scatter(part, 'z', scatter_dimension=0, tiled=True)]
  transfers between devices with their start and end apart: 24 -> 24, of which waited for: 15 -> 16; matrix products, arithmetic and copies ran while one was open for 4% -> 5% of each run, Pallas kernels for 34% -> 32%
where the time goes in v11:
time: 143 us; the launch traced here: 142 us
  Pallas kernels  51.2 us (36%)
  waiting for transfers between devices  35.4 us (25%)
  starting transfers between devices  31.7 us (22%)
  between operations  14.1 us (10%)
  other arithmetic  8.09 us (6%)
  local copies, waits for them, and re-layouts  1.97 us (1%)
    ppermute x21, starting transfers between devices, shift(): return lax.ppermute(x, axis, [(i, (i + k) % n) for i in range(n)])  28.7 us
    ppermute x21, waiting for transfers between devices, shift(): return lax.ppermute(x, axis, [(i, (i + k) % n) for i in range(n)])  26 us
    pallas_call x2, Pallas kernels, weight_product(): pl.pallas_call(functools.partial(weight_body, scale, start, first - start...  17.2 us
    pallas_call x3, Pallas kernels, input_product(): pl.pallas_call(functools.partial(input_body, n, done), out_shape=jax.Shap...  15.4 us
    pallas_call x1, Pallas kernels, make_deltas(): pl.pallas_call(delta_body, out_shape=jax.ShapeDtypeStruct((rows, 2 * cols...  5.93 us
    all_gather x1, waiting for transfers between devices, per_device(): lax.all_gather(block, 'z', axis=0, tiled=True).reshape(-1, keep.shape[1])  4.02 us
    reduce_scatter x1, waiting for transfers between devices, per_device(): sums = lax.psum_scatter(part, 'z', scatter_dimension=0, tiled=True)  3.8 us
    ppermute x1, starting transfers between devices, both_flipped(): return lax.ppermute(x, ('x_hi', 'core'), [(i, 3 - i) for i in range(4)])  2.88 us
  transfers between devices with their start and end apart: 24, of which 16 were waited for; matrix products, arithmetic and copies ran while one was open for 5% of the time, Pallas kernels for 32%

profile of v11, /device:TPU:1, one launch (start us, length us, event | category | flops | bytes accessed | tf_op | source)
XLA Modules:
  0.0 142.5 jit_solution(9261444819722043531)
XLA Ops:
  7.2 2.8 %prologue.1 = (bf16[44,1152]{1,0:T(8,128)(2,1)}, bf16[44,1152]{1,0:T(8,128)(2,1)}, bf16[144,2304]{1,0:T(8,128)(2,1)}) custom-call(bf16[44,2304]{1,0:T(8,128)(2,1)} %x_ref.1, bf16[144,1152]{1,0:T(8,128)(2,1)} %g_ref.1, bf16[144,1152]{1,0:T(8,128)(2,1)} %u_ref.2), custom_call_target="tpu_custom_call" | custom-call | flops 1000 | bytes 1000 | tf_op jit(solution)/shard_map/prologue/pallas_call | solution.py:119
  10.1 3.2 %collective-permute-start = (bf16[44,1152]{1,0:T(8,128)(2,1)}, bf16[44,1152]{1,0:T(8,128)(2,1)S(1)}, u32[]{:S(2)}, u32[]{:S(2)}) collective-permute-start(bf16[44,1152]{1,0:T(8,128)(2,1)} %get-tuple-element.39), channel_id=1, source_target_pairs={{0,1},{1,0},{2,3},{3,2},{4,5},{5,4},{6,7},{7,6},{8,9},{9,8},{10,11... | collective-permute-start | bytes 304136 | tf_op jit(solution)/shard_map/ppermute | solution.py:23
  19.5 4.1 %collective-permute-done.1 = bf16[2,44,1152]{2,1,0:T(8,128)(2,1)S(1)} collective-permute-done((bf16[2,44,1152]{2,1,0:T(8,128)(2,1)S(1)}, bf16[2,44,1152]{2,1,0:T(8,128)(2,1)S(1)}, u32[]{:S(2)}, u32[]{:S(2)}) %collective-permute-start.1) | collective-permute-done | bytes 202784 | tf_op jit(solution)/shard_map/ppermute | solution.py:23
  25.6 5.9 %deltas.1 = bf16[704,2304]{1,0:T(8,128)(2,1)} custom-call(bf16[704,1152]{1,0:T(8,128)(2,1)} %g_ref.2, bf16[704,1152]{1,0:T(8,128)(2,1)} %u_ref.3, bf16[704,1152]{1,0:T(8,128)(2,1)} %c_ref.1), custom_call_target="tpu_custom_call" | custom-call | flops 99999997952 | bytes 1000 | tf_op jit(solution)/shard_map/deltas/pallas_call | solution.py:55
  31.5 2.3 %collective-permute-done.2.refs_3_ = bf16[144,2304]{1,0:T(8,128)(2,1)S(1)} collective-permute-done((bf16[144,2304]{1,0:T(8,128)(2,1)}, bf16[144,2304]{1,0:T(8,128)(2,1)S(1)}, u32[]{:S(2)}, u32[]{:S(2)}) %collective-permute-start.2) | collective-permute-done | bytes 663584 | tf_op jit(solution)/shard_map/ppermute | solution.py:23
  38.6 2.7 %collective-permute-start.6 = (bf16[144,2304]{1,0:T(8,128)(2,1)S(1)}, bf16[144,2304]{1,0:T(8,128)(2,1)S(1)}, u32[]{:S(2)}, u32[]{:S(2)}) collective-permute-start(bf16[144,2304]{1,0:T(8,128)(2,1)S(1)} %collective-permute-done.4.refs_1_), channel_id=1, source_target_pairs={{0,6},{2,0},{4,2},{6,4},{1,7},{3,1},{5,3},{7,5},{8,14},{10,8},{12,... | collective-permute-start | bytes 1990664 | tf_op jit(solution)/shard_map/ppermute | solution.py:23
  43.0 2.5 %pad_maximum_fusion = bf16[8,2,88,2304]{3,2,1,0:T(8,128)(2,1)S(1)} fusion(bf16[8,1,88,2304]{3,2,1,0:T(8,128)(2,1)S(1)} %bitcast.18, bf16[8,1,88,2304]{3,2,1,0:T(8,128)(2,1)} %bitcast.17), kind=kLoop, calls=%fused_computation | loop fusion | flops 3244032 | bytes 12976128 | tf_op jit(solution)/shard_map/stack | solution.py:355
  45.6 6.8 %input_product_4.1.refs_2_ = bf16[1408,576]{1,0:T(8,128)(2,1)S(1)} custom-call(bf16[144,2304]{1,0:T(8,128)(2,1)S(1)} %copy-done.1, bf16[144,2304]{1,0:T(8,128)(2,1)S(1)} %collective-permute-done.4.refs_1_, bf16[144,2304]{1,0:T(8,128)(2,1)S(1)} %collective-permute-done.3.refs_2_, bf16[144,2304]{1,0:T(8,128)(2,1)S(1)} %collective-permute-done.2.refs_3_, ...), custom_call_target="tpu_custom_call" | custom-call | flops 1000 | bytes 1000 | tf_op jit(solution)/shard_map/input_product_4/pallas_call | solution.py:299
  56.3 2.9 %collective-permute-start.17 = (bf16[144,1152]{1,0:T(8,128)(2,1)S(1)}, bf16[144,1152]{1,0:T(8,128)(2,1)S(1)}, u32[]{:S(2)}, u32[]{:S(2)}) collective-permute-start(bf16[144,1152]{1,0:T(8,128)(2,1)S(1)} %slice.39), channel_id=1, source_target_pairs={{0,6},{2,0},{4,2},{6,4},{1,7},{3,1},{5,3},{7,5},{8,14},{10,8},{12,... | collective-permute-start | bytes 995336 | tf_op jit(solution)/shard_map/ppermute | solution.py:23
  59.2 4.8 %input_product_3.1.refs_3_ = bf16[1408,432]{1,0:T(8,128)(2,1)S(1)} custom-call(bf16[144,2304]{1,0:T(8,128)(2,1)S(1)} %collective-permute-done.18.refs_0_, bf16[144,2304]{1,0:T(8,128)(2,1)S(1)} %collective-permute-done.6.refs_1_, bf16[144,2304]{1,0:T(8,128)(2,1)S(1)} %collective-permute-done.5.refs_2_, bf16[1408,2304]{1,0:T(8,128)(2,1)S(1)} %bitcast.11), custom_call_target="tpu_custom_call" | custom-call | flops 1000 | bytes 1000 | tf_op jit(solution)/shard_map/input_product_3/pallas_call | solution.py:299
  66.2 3.9 %input_product_2.1 = bf16[1408,1152]{1,0:T(8,128)(2,1)} custom-call(bf16[144,1152]{1,0:T(8,128)(2,1)S(1)} %collective-permute-done.16.refs_0_, bf16[144,1152]{1,0:T(8,128)(2,1)S(1)} %collective-permute-done.17.refs_1_, bf16[1408,576]{1,0:T(8,128)(2,1)S(1)} %input_product_4.1.refs_2_, bf16[1408,432]{1,0:T(8,128)(2,1)S(1)} %input_product_3.1.refs_3_, ...), custom_call_target="tpu_custom_call" | custom-call | flops 1000 | bytes 1000 | tf_op jit(solution)/shard_map/input_product_2/pallas_call | solution.py:299
  70.1 4.0 %all-gather.2.cloned.1.call-done = bf16[16,88,1152]{2,1,0:T(8,128)(2,1)} async-done(((bf16[2,88,1152]{2,1,0:T(8,128)(2,1)}), bf16[16,88,1152]{2,1,0:T(8,128)(2,1)}) %all-gather.2.cloned.1.call-update) | async-done | bytes 3244048 | tf_op jit(solution)/shard_map/all_gather | solution.py:350
  74.1 7.3 %weight_product_0.1 = (bf16[144,2304]{1,0:T(8,128)(2,1)}, bf16[144,2304]{1,0:T(8,128)(2,1)}, bf16[144,2304]{1,0:T(8,128)(2,1)}) custom-call(bf16[1408,1152]{1,0:T(8,128)(2,1)} %bitcast.15, bf16[1408,2304]{1,0:T(8,128)(2,1)} %bitcast.13), custom_call_target="tpu_custom_call" | custom-call | flops 1000 | bytes 1000 | tf_op jit(solution)/shard_map/weight_product_0/pallas_call | solution.py:245
  82.6 2.5 %collective-permute-start.13 = (bf16[144,2304]{1,0:T(8,128)(2,1)}, bf16[144,2304]{1,0:T(8,128)(2,1)}, u32[]{:S(2)}, u32[]{:S(2)}) collective-permute-start(bf16[144,2304]{1,0:T(8,128)(2,1)} %get-tuple-element.50.refs_2_), channel_id=1, source_target_pairs={{0,6},{2,0},{4,2},{6,4},{1,7},{3,1},{5,3},{7,5},{8,14},{10,8},{12,... | collective-permute-start | bytes 1990664 | tf_op jit(solution)/shard_map/ppermute | solution.py:23
  86.2 9.9 %weight_product_432.1 = (bf16[144,2304]{1,0:T(8,128)(2,1)}, bf16[144,2304]{1,0:T(8,128)(2,1)}, bf16[144,2304]{1,0:T(8,128)(2,1)}, bf16[144,2304]{1,0:T(8,128)(2,1)}, bf16[144,2304]{1,0:T(8,128)(2,1)}) custom-call(bf16[1408,1152]{1,0:T(8,128)(2,1)} %bitcast.16, bf16[1408,2304]{1,0:T(8,128)(2,1)} %bitcast.14, f32[8,128]{1,0:T(8,128)} %sent.1.refs_0_), custom_call_target="tpu_custom_call" | custom-call | flops 99999997952 | bytes 1000 | tf_op jit(solution)/shard_map/weight_product_432/pallas_call | solution.py:245
  99.8 2.4 %collective-permute-start.10 = (bf16[144,1152]{1,0:T(8,128)(2,1)}, bf16[144,1152]{1,0:T(8,128)(2,1)S(1)}, u32[]{:S(2)}, u32[]{:S(2)}) collective-permute-start(bf16[144,1152]{1,0:T(8,128)(2,1)} %get-tuple-element.56), channel_id=1, source_target_pairs={{0,6},{2,0},{4,2},{6,4},{1,7},{3,1},{5,3},{7,5},{8,14},{10,8},{12,... | collective-permute-start | bytes 995336 | tf_op jit(solution)/shard_map/ppermute | solution.py:23
  105.1 3.0 %collective-permute-done.10.left_ref = bf16[144,1152]{1,0:T(8,128)(2,1)S(1)} collective-permute-done((bf16[144,1152]{1,0:T(8,128)(2,1)}, bf16[144,1152]{1,0:T(8,128)(2,1)S(1)}, u32[]{:S(2)}, u32[]{:S(2)}) %collective-permute-start.10) | collective-permute-done | bytes 331808 | tf_op jit(solution)/shard_map/ppermute | solution.py:23
  108.1 3.1 %collective-permute-done.9.right_ref = bf16[144,1152]{1,0:T(8,128)(2,1)S(1)} collective-permute-done((bf16[144,1152]{1,0:T(8,128)(2,1)}, bf16[144,1152]{1,0:T(8,128)(2,1)S(1)}, u32[]{:S(2)}, u32[]{:S(2)}) %collective-permute-start.9) | collective-permute-done | bytes 331808 | tf_op jit(solution)/shard_map/ppermute | solution.py:23
  111.9 2.7 %merge.1 = (bf16[144,2304]{1,0:T(8,128)(2,1)}, bf16[144,2304]{1,0:T(8,128)(2,1)}) custom-call(bf16[144,2304]{1,0:T(8,128)(2,1)} %get-tuple-element.52.up_ref, bf16[144,1152]{1,0:T(8,128)(2,1)} %copy-done.4, bf16[144,2304]{1,0:T(8,128)(2,1)} %get-tuple-element.55.down_ref, bf16[144,1152]{1,0:T(8,128)(2,1)} %copy-done.3), custom_call_target="tpu_custom_call" | custom-call | flops 1000 | bytes 1000 | tf_op jit(solution)/shard_map/merge/pallas_call | solution.py:229
  114.6 2.7 %collective-permute-start.12 = (bf16[144,2304]{1,0:T(8,128)(2,1)}, bf16[144,2304]{1,0:T(8,128)(2,1)S(1)}, u32[]{:S(2)}, u32[]{:S(2)}) collective-permute-start(bf16[144,2304]{1,0:T(8,128)(2,1)} %get-tuple-element.58), channel_id=1, source_target_pairs={{0,6},{2,0},{4,2},{6,4},{1,7},{3,1},{5,3},{7,5},{8,14},{10,8},{12,... | collective-permute-start | bytes 1990664 | tf_op jit(solution)/shard_map/ppermute | solution.py:23
  117.3 3.8 %reduce-scatter.2.cloned.1.call-done.x_ref = bf16[176,1152]{1,0:T(8,128)(2,1)} async-done(((bf16[1408,1152]{1,0:T(8,128)(2,1)}), bf16[176,1152]{1,0:T(8,128)(2,1)}) %reduce-scatter.2.cloned.1.call-update) | async-done | bytes 405520 | tf_op jit(solution)/shard_map/reduce_scatter | solution.py:362
  122.9 2.6 %collective-permute-start.19 = (bf16[44,1152]{1,0:T(8,128)(2,1)}, bf16[44,1152]{1,0:T(8,128)(2,1)S(1)}, u32[]{:S(2)}, u32[]{:S(2)}) collective-permute-start(bf16[44,1152]{1,0:T(8,128)(2,1)} %get-tuple-element.64), channel_id=1, source_target_pairs={{0,16},{16,0},{1,17},{17,1},{2,18},{18,2},{3,19},{19,3},{4,20},{20... | collective-permute-start | bytes 304136 | tf_op jit(solution)/shard_map/ppermute | solution.py:23
  125.5 2.9 %collective-permute-start.20 = (bf16[44,1152]{1,0:T(8,128)(2,1)}, bf16[44,1152]{1,0:T(8,128)(2,1)S(1)}, u32[]{:S(2)}, u32[]{:S(2)}) collective-permute-start(bf16[44,1152]{1,0:T(8,128)(2,1)} %get-tuple-element.65), channel_id=1, source_target_pairs={{0,17},{1,16},{16,1},{17,0},{2,19},{3,18},{18,3},{19,2},{4,21},{5,... | collective-permute-start | bytes 304136 | tf_op jit(solution)/shard_map/ppermute | solution.py:27
  133.2 2.4 %join_columns.1 = bf16[44,2304]{1,0:T(8,128)(2,1)} custom-call(bf16[44,1152]{1,0:T(8,128)(2,1)} %get-tuple-element.67.m0_ref, bf16[44,1152]{1,0:T(8,128)(2,1)} %copy-done.5, bf16[44,1152]{1,0:T(8,128)(2,1)} %copy-done.6, bf16[44,1152]{1,0:T(8,128)(2,1)} %copy-done.7), custom_call_target="tpu_custom_call" | custom-call | flops 1000 | bytes 1000 | tf_op jit(solution)/shard_map/join_columns/pallas_call | solution.py:179
  (63 shorter events, 36.9 us)
Async XLA Ops:
  7.2 67.0 %all-gather.2.cloned.1.call-start = ((), (), s32[]{:S(2)}) async-start(), calls=%async_computation.1 | async-start | bytes 3649536 | tf_op jit(solution)/shard_map/all_gather | solution.py:350
  10.1 4.4 %collective-permute-start = (bf16[44,1152]{1,0:T(8,128)(2,1)}, bf16[44,1152]{1,0:T(8,128)(2,1)S(1)}, u32[]{:S(2)}, u32[]{:S(2)}) collective-permute-start(bf16[44,1152]{1,0:T(8,128)(2,1)} %get-tuple-element.39), channel_id=1, source_target_pairs={{0,1},{1,0},{2,3},{3,2},{4,5},{5,4},{6,7},{7,6},{8,9},{9,8},{10,11... | collective-permute-start | bytes 304136 | tf_op jit(solution)/shard_map/ppermute | solution.py:23
  15.4 8.2 %collective-permute-start.1 = (bf16[2,44,1152]{2,1,0:T(8,128)(2,1)S(1)}, bf16[2,44,1152]{2,1,0:T(8,128)(2,1)S(1)}, u32[]{:S(2)}, u32[]{:S(2)}) collective-permute-start(bf16[2,44,1152]{2,1,0:T(8,128)(2,1)S(1)} %pad_maximum_fusion.1), channel_id=1, source_target_pairs={{0,16},{16,0},{1,17},{17,1},{2,18},{18,2},{3,19},{19,3},{4,20},{20... | collective-permute-start | bytes 608264 | tf_op jit(solution)/shard_map/ppermute | solution.py:23
  16.5 17.4 %collective-permute-start.2 = (bf16[144,2304]{1,0:T(8,128)(2,1)}, bf16[144,2304]{1,0:T(8,128)(2,1)S(1)}, u32[]{:S(2)}, u32[]{:S(2)}) collective-permute-start(bf16[144,2304]{1,0:T(8,128)(2,1)} %get-tuple-element.41.refs_0_), channel_id=1, source_target_pairs={{0,2},{2,4},{4,6},{6,0},{1,3},{3,5},{5,7},{7,1},{8,10},{10,12},{12... | collective-permute-start | bytes 1990664 | tf_op jit(solution)/shard_map/ppermute | solution.py:23
  17.8 16.1 %collective-permute-start.3 = (bf16[144,2304]{1,0:T(8,128)(2,1)}, bf16[144,2304]{1,0:T(8,128)(2,1)S(1)}, u32[]{:S(2)}, u32[]{:S(2)}) collective-permute-start(bf16[144,2304]{1,0:T(8,128)(2,1)} %get-tuple-element.41.refs_0_), channel_id=1, source_target_pairs={{0,6},{2,0},{4,2},{6,4},{1,7},{3,1},{5,3},{7,5},{8,14},{10,8},{12,... | collective-permute-start | bytes 1990664 | tf_op jit(solution)/shard_map/ppermute | solution.py:23
  19.2 16.7 %collective-permute-start.4 = (bf16[144,2304]{1,0:T(8,128)(2,1)}, bf16[144,2304]{1,0:T(8,128)(2,1)S(1)}, u32[]{:S(2)}, u32[]{:S(2)}) collective-permute-start(bf16[144,2304]{1,0:T(8,128)(2,1)} %get-tuple-element.41.refs_0_), channel_id=1, source_target_pairs={{0,8},{8,0},{1,9},{9,1},{2,10},{10,2},{3,11},{11,3},{4,12},{12,4},... | collective-permute-start | bytes 1990664 | tf_op jit(solution)/shard_map/ppermute | solution.py:23
  25.5 95.5 %reduce-scatter.2.cloned.1.call-start = ((), (), s32[]{:S(2)}) async-start(), calls=%async_computation.2 | async-start | bytes 3649536 | tf_op jit(solution)/shard_map/reduce_scatter | solution.py:362
  36.0 7.1 %collective-permute-start.7 = (bf16[704,2304]{1,0:T(8,128)(2,1)}, bf16[704,2304]{1,0:T(8,128)(2,1)S(1)}, u32[]{:S(2)}, u32[]{:S(2)}) collective-permute-start(bf16[704,2304]{1,0:T(8,128)(2,1)} %deltas.1), channel_id=1, source_target_pairs={{0,1},{1,0},{2,3},{3,2},{4,5},{5,4},{6,7},{7,6},{8,9},{9,8},{10,11... | collective-permute-start | bytes 9732104 | tf_op jit(solution)/shard_map/ppermute | solution.py:23
  37.4 16.6 %collective-permute-start.5 = (bf16[144,2304]{1,0:T(8,128)(2,1)S(1)}, bf16[144,2304]{1,0:T(8,128)(2,1)S(1)}, u32[]{:S(2)}, u32[]{:S(2)}) collective-permute-start(bf16[144,2304]{1,0:T(8,128)(2,1)S(1)} %collective-permute-done.2.refs_3_), channel_id=1, source_target_pairs={{0,8},{8,0},{1,9},{9,1},{2,10},{10,2},{3,11},{11,3},{4,12},{12,4},... | collective-permute-start | bytes 1990664 | tf_op jit(solution)/shard_map/ppermute | solution.py:23
  38.6 16.8 %collective-permute-start.6 = (bf16[144,2304]{1,0:T(8,128)(2,1)S(1)}, bf16[144,2304]{1,0:T(8,128)(2,1)S(1)}, u32[]{:S(2)}, u32[]{:S(2)}) collective-permute-start(bf16[144,2304]{1,0:T(8,128)(2,1)S(1)} %collective-permute-done.4.refs_1_), channel_id=1, source_target_pairs={{0,6},{2,0},{4,2},{6,4},{1,7},{3,1},{5,3},{7,5},{8,14},{10,8},{12,... | collective-permute-start | bytes 1990664 | tf_op jit(solution)/shard_map/ppermute | solution.py:23
  41.3 18.0 %collective-permute-start.18 = (bf16[144,2304]{1,0:T(8,128)(2,1)S(1)}, bf16[144,2304]{1,0:T(8,128)(2,1)S(1)}, u32[]{:S(2)}, u32[]{:S(2)}) collective-permute-start(bf16[144,2304]{1,0:T(8,128)(2,1)S(1)} %collective-permute-done.2.refs_3_), channel_id=1, source_target_pairs={{0,2},{2,4},{4,6},{6,0},{1,3},{3,5},{5,7},{7,1},{8,10},{10,12},{12... | collective-permute-start | bytes 1990664 | tf_op jit(solution)/shard_map/ppermute | solution.py:23
  55.3 10.9 %collective-permute-start.16 = (bf16[144,1152]{1,0:T(8,128)(2,1)S(1)}, bf16[144,1152]{1,0:T(8,128)(2,1)S(1)}, u32[]{:S(2)}, u32[]{:S(2)}) collective-permute-start(bf16[144,1152]{1,0:T(8,128)(2,1)S(1)} %slice.38), channel_id=1, source_target_pairs={{0,2},{2,4},{4,6},{6,0},{1,3},{3,5},{5,7},{7,1},{8,10},{10,12},{12... | collective-permute-start | bytes 995336 | tf_op jit(solution)/shard_map/ppermute | solution.py:23
  56.3 9.9 %collective-permute-start.17 = (bf16[144,1152]{1,0:T(8,128)(2,1)S(1)}, bf16[144,1152]{1,0:T(8,128)(2,1)S(1)}, u32[]{:S(2)}, u32[]{:S(2)}) collective-permute-start(bf16[144,1152]{1,0:T(8,128)(2,1)S(1)} %slice.39), channel_id=1, source_target_pairs={{0,6},{2,0},{4,2},{6,4},{1,7},{3,1},{5,3},{7,5},{8,14},{10,8},{12,... | collective-permute-start | bytes 995336 | tf_op jit(solution)/shard_map/ppermute | solution.py:23
  81.4 16.1 %collective-permute-start.8 = (bf16[144,2304]{1,0:T(8,128)(2,1)}, bf16[144,2304]{1,0:T(8,128)(2,1)}, u32[]{:S(2)}, u32[]{:S(2)}) collective-permute-start(bf16[144,2304]{1,0:T(8,128)(2,1)} %get-tuple-element.48.refs_0_), channel_id=1, source_target_pairs={{0,8},{8,0},{1,9},{9,1},{2,10},{10,2},{3,11},{11,3},{4,12},{12,4},... | collective-permute-start | bytes 1990664 | tf_op jit(solution)/shard_map/ppermute | solution.py:23
  82.6 19.6 %collective-permute-start.13 = (bf16[144,2304]{1,0:T(8,128)(2,1)}, bf16[144,2304]{1,0:T(8,128)(2,1)}, u32[]{:S(2)}, u32[]{:S(2)}) collective-permute-start(bf16[144,2304]{1,0:T(8,128)(2,1)} %get-tuple-element.50.refs_2_), channel_id=1, source_target_pairs={{0,6},{2,0},{4,2},{6,4},{1,7},{3,1},{5,3},{7,5},{8,14},{10,8},{12,... | collective-permute-start | bytes 1990664 | tf_op jit(solution)/shard_map/ppermute | solution.py:23
  86.2 16.5 %collective-permute-start.14 = (bf16[144,2304]{1,0:T(8,128)(2,1)S(1)}, bf16[144,2304]{1,0:T(8,128)(2,1)S(1)}, u32[]{:S(2)}, u32[]{:S(2)}) collective-permute-start(bf16[144,2304]{1,0:T(8,128)(2,1)S(1)} %copy-done.8), channel_id=1, source_target_pairs={{0,2},{2,4},{4,6},{6,0},{1,3},{3,5},{5,7},{7,1},{8,10},{10,12},{12... | collective-permute-start | bytes 1990664 | tf_op jit(solution)/shard_map/ppermute | solution.py:23
  99.8 8.3 %collective-permute-start.10 = (bf16[144,1152]{1,0:T(8,128)(2,1)}, bf16[144,1152]{1,0:T(8,128)(2,1)S(1)}, u32[]{:S(2)}, u32[]{:S(2)}) collective-permute-start(bf16[144,1152]{1,0:T(8,128)(2,1)} %get-tuple-element.56), channel_id=1, source_target_pairs={{0,6},{2,0},{4,2},{6,4},{1,7},{3,1},{5,3},{7,5},{8,14},{10,8},{12,... | collective-permute-start | bytes 995336 | tf_op jit(solution)/shard_map/ppermute | solution.py:23
  102.2 9.0 %collective-permute-start.9 = (bf16[144,1152]{1,0:T(8,128)(2,1)}, bf16[144,1152]{1,0:T(8,128)(2,1)S(1)}, u32[]{:S(2)}, u32[]{:S(2)}) collective-permute-start(bf16[144,1152]{1,0:T(8,128)(2,1)} %get-tuple-element.54), channel_id=1, source_target_pairs={{0,2},{2,4},{4,6},{6,0},{1,3},{3,5},{5,7},{7,1},{8,10},{10,12},{12... | collective-permute-start | bytes 995336 | tf_op jit(solution)/shard_map/ppermute | solution.py:23
  104.2 24.1 %collective-permute-start.15 = (bf16[144,2304]{1,0:T(8,128)(2,1)S(1)}, bf16[144,2304]{1,0:T(8,128)(2,1)S(1)}, u32[]{:S(2)}, u32[]{:S(2)}) collective-permute-start(bf16[144,2304]{1,0:T(8,128)(2,1)S(1)} %add_convert_fusion), channel_id=1, source_target_pairs={{0,8},{8,0},{1,9},{9,1},{2,10},{10,2},{3,11},{11,3},{4,12},{12,4},... | collective-permute-start | bytes 1990664 | tf_op jit(solution)/shard_map/ppermute | solution.py:23
  114.6 15.2 %collective-permute-start.11 = (bf16[144,2304]{1,0:T(8,128)(2,1)}, bf16[144,2304]{1,0:T(8,128)(2,1)S(1)}, u32[]{:S(2)}, u32[]{:S(2)}) collective-permute-start(bf16[144,2304]{1,0:T(8,128)(2,1)} %get-tuple-element.57), channel_id=1, source_target_pairs={{0,2},{2,4},{4,6},{6,0},{1,3},{3,5},{5,7},{7,1},{8,10},{10,12},{12... | collective-permute-start | bytes 1990664 | tf_op jit(solution)/shard_map/ppermute | solution.py:23
  114.6 15.2 %collective-permute-start.12 = (bf16[144,2304]{1,0:T(8,128)(2,1)}, bf16[144,2304]{1,0:T(8,128)(2,1)S(1)}, u32[]{:S(2)}, u32[]{:S(2)}) collective-permute-start(bf16[144,2304]{1,0:T(8,128)(2,1)} %get-tuple-element.58), channel_id=1, source_target_pairs={{0,6},{2,0},{4,2},{6,4},{1,7},{3,1},{5,3},{7,5},{8,14},{10,8},{12,... | collective-permute-start | bytes 1990664 | tf_op jit(solution)/shard_map/ppermute | solution.py:23
  122.9 8.1 %collective-permute-start.19 = (bf16[44,1152]{1,0:T(8,128)(2,1)}, bf16[44,1152]{1,0:T(8,128)(2,1)S(1)}, u32[]{:S(2)}, u32[]{:S(2)}) collective-permute-start(bf16[44,1152]{1,0:T(8,128)(2,1)} %get-tuple-element.64), channel_id=1, source_target_pairs={{0,16},{16,0},{1,17},{17,1},{2,18},{18,2},{3,19},{19,3},{4,20},{20... | collective-permute-start | bytes 304136 | tf_op jit(solution)/shard_map/ppermute | solution.py:23
  125.5 7.0 %collective-permute-start.20 = (bf16[44,1152]{1,0:T(8,128)(2,1)}, bf16[44,1152]{1,0:T(8,128)(2,1)S(1)}, u32[]{:S(2)}, u32[]{:S(2)}) collective-permute-start(bf16[44,1152]{1,0:T(8,128)(2,1)} %get-tuple-element.65), channel_id=1, source_target_pairs={{0,17},{1,16},{16,1},{17,0},{2,19},{3,18},{18,3},{19,2},{4,21},{5,... | collective-permute-start | bytes 304136 | tf_op jit(solution)/shard_map/ppermute | solution.py:27
  128.3 4.2 %collective-permute-start.21 = (bf16[44,1152]{1,0:T(8,128)(2,1)}, bf16[44,1152]{1,0:T(8,128)(2,1)S(1)}, u32[]{:S(2)}, u32[]{:S(2)}) collective-permute-start(bf16[44,1152]{1,0:T(8,128)(2,1)} %get-tuple-element.66), channel_id=1, source_target_pairs={{0,1},{1,0},{2,3},{3,2},{4,5},{5,4},{6,7},{7,6},{8,9},{9,8},{10,11... | collective-permute-start | bytes 304136 | tf_op jit(solution)/shard_map/ppermute | solution.py:23
  (9 other events, 64.6 us)
Sparse Core Ops, SparseCore 0:
  25.7 48.4 all-gather.1
  76.7 44.3 reduce-scatter.1
